TPU v7x, 32 devices: a whole 2x2x4 slice. The times are simulated.
32 devices in a mesh: dp: 32 (over z, y, x, core).
Axes of the slice: x: 2, y: 2, z: 4, core: 2. Of those that a mesh axis runs over, the one named last changes fastest.
Arguments:
- tokens: bfloat16 [32768, 768], P('dp'), may hold values from -6 to 6
- seg_lengths: int32 [32, 6], P('dp'), may hold values from 24 to 180, as said below
- owner: int32 [32, 5], replicated, may hold values from 0 to 31, as said below
- place: int32 [32, 5], replicated, may hold values from 0 to 4, as said below
- w_qkv: bfloat16 [768, 2304], replicated, may hold values from -0.21875 to 0.21875
- b_qv: float32 [1536], replicated, may hold values from -2 to 2
- w_out: bfloat16 [768, 768], replicated, may hold values from -0.875 to 0.875
- b_out: float32 [768], replicated, may hold values from -2 to 2
- ln1_gain: float32 [768], replicated, may hold values from 0.1 to 1.9
- ln1_bias: float32 [768], replicated, may hold values from -2 to 2
- w_up: bfloat16 [768, 3072], replicated, may hold values from -0.21875 to 0.21875
- b_up: float32 [3072], replicated, may hold values from -2 to 2
- w_down: bfloat16 [3072, 768], replicated, may hold values from -0.109375 to 0.109375
- b_down: float32 [768], replicated, may hold values from -2 to 2
- ln2_gain: float32 [768], replicated, may hold values from 0.1 to 1.9
- ln2_bias: float32 [768], replicated, may hold values from -2 to 2
- w_proj: bfloat16 [768, 128], replicated, may hold values from -0.21875 to 0.21875
Outputs:
- losses: float32 [32], P('dp')
- d_tokens: float32 [32768, 768], P('dp')
- g_w_qkv: float32 [768, 2304], replicated
- g_b_qv: float32 [1536], replicated
- g_w_out: float32 [768, 768], replicated
- g_b_out: float32 [768], replicated
- g_ln1_gain: float32 [768], replicated
- g_ln1_bias: float32 [768], replicated
- g_w_up: float32 [768, 3072], replicated
- g_b_up: float32 [3072], replicated
- g_w_down: float32 [3072, 768], replicated
- g_b_down: float32 [768], replicated
- g_ln2_gain: float32 [768], replicated
- g_ln2_bias: float32 [768], replicated
- g_w_proj: float32 [768, 128], replicated
Inputs may be any that keep to these rules, and one draw needn't show every extreme that they name: `seg_lengths`: entry 0 of a row is its query's length, at least 24, and 32 in some row; entries 1 to 5 are passage lengths of at least 90, and every row has a passage of exactly 180. `owner`: every row's query scores exactly 5 passages, none of them in its own row. `place`: the 5 passages scored by one query have the roles 0 to 4, each once.
All inputs are finite; a program needn't handle non-finite values.
Results may differ from a plain program's by a relative error of at most 0.014.
Values may be sent and summed in bfloat16 or wider, within the bound.
No kernel may reach another device: no remote copies, remote signals or barrier semaphores. Data moves between devices by JAX's collectives and lax.ppermute only.
A program may use at most 384 MiB of HBM per device.

v0:
```python
import jax
import jax.numpy as jnp
from jax import lax
from jax.sharding import PartitionSpec as P

HEADS = 12
QLEN = 32
PLEN = 180


logit_divisor = 0.1
huge_penalty_constant = -1e30
ln_epsilon = 1e-12
norm_epsilon = 1e-06
precise = lax.Precision.HIGHEST


def inner_rows(left, right):
    return lax.dot_general(
        left, right, (((0,), (0,)), ((), ())), preferred_element_type=jnp.float32
    )


def times_transposed(left, right):
    return lax.dot_general(
        left, right, (((1,), (1,)), ((), ())), preferred_element_type=jnp.float32
    )


def layer_stats(resid, gain, shift):
    center = resid - jnp.mean(resid, axis=-1, keepdims=True)
    scale_inv = lax.rsqrt(jnp.mean(center * center, axis=-1, keepdims=True) + ln_epsilon)
    normal = center * scale_inv
    return (normal * gain + shift, normal, scale_inv)


def layer_back(grad_out, gain, normal, scale_inv):
    grad_n = grad_out * gain
    return scale_inv * (
        grad_n
        - jnp.mean(grad_n, axis=-1, keepdims=True)
        - normal * jnp.mean(grad_n * normal, axis=-1, keepdims=True)
    )


def gelu_slope(inner):
    return (
        0.5 * (1.0 + lax.erf(inner * 0.7071067811865476))
        + inner * jnp.exp(-0.5 * inner * inner) * 0.3989422804014327
    )


def body(
    tokens,
    seg_lengths,
    owner,
    place,
    w_qkv,
    b_qv,
    w_out,
    b_out,
    ln1_gain,
    ln1_bias,
    w_up,
    b_up,
    w_down,
    b_down,
    ln2_gain,
    ln2_bias,
    w_proj,
):
    row_count, width = tokens.shape
    head_size = width // HEADS
    out_width = w_proj.shape[1]
    lengths = seg_lengths[0]
    seg_count = lengths.shape[0]
    passages_per = owner.shape[1]
    devices = lax.axis_size("dp")
    device = lax.axis_index("dp")
    position = jnp.arange(row_count, dtype=jnp.int32)
    ends = jnp.cumsum(lengths)
    starts = ends - lengths
    segment = jnp.sum((position[:, None] >= ends[None, :]).astype(jnp.int32), axis=1)
    onehot_seg = segment[:, None] == jnp.arange(seg_count, dtype=jnp.int32)[None, :]
    token_start = jnp.sum(jnp.where(onehot_seg, starts[None, :], 0), axis=1)
    offset = position - token_start
    pad_slot = QLEN + passages_per * PLEN
    token_slot = jnp.where(segment == 0, offset, QLEN + (segment - 1) * PLEN + offset)
    token_slot = jnp.where(segment >= seg_count, pad_slot, token_slot)
    inputs = tokens.astype(jnp.float32)
    bias_all = jnp.concatenate([b_qv[:width], jnp.zeros((width,), jnp.float32), b_qv[width:]])
    packed = (jnp.dot(tokens, w_qkv, preferred_element_type=jnp.float32) + bias_all).astype(
        jnp.bfloat16
    )
    queries = packed[:, :width].reshape(row_count, HEADS, head_size)
    keys_all = packed[:, width : 2 * width].reshape(row_count, HEADS, head_size)
    values = packed[:, 2 * width :].reshape(row_count, HEADS, head_size)
    scale = head_size ** (-0.5)
    block = min(512, row_count)
    windows = []
    for first_row in range(0, row_count, block):
        span = row_count
        key_first = 0
        windows.append((first_row, key_first, span))

    def block_scores(first_row, key_first, span):
        raw = (
            jnp.einsum(
                "qhd,khd->hqk",
                queries[first_row : first_row + block],
                keys_all,
                preferred_element_type=jnp.float32,
            )
            * scale
        )
        same = (
            segment[first_row : first_row + block, None]
            == segment[None, key_first : key_first + span]
        )
        return jnp.where(same[None], raw, huge_penalty_constant)

    attended_parts = []
    log_totals = []
    for first_row, key_first, span in windows:
        scores = block_scores(first_row, key_first, span)
        top = jnp.max(scores, axis=-1, keepdims=True)
        expo = jnp.exp(scores - top)
        summed = jnp.sum(expo, axis=-1, keepdims=True)
        probs = (expo / summed).astype(jnp.bfloat16)
        log_totals.append(top + jnp.log(summed))
        attended_parts.append(
            jnp.einsum("hqk,khd->qhd", probs, values, preferred_element_type=jnp.float32)
        )
    attended = (
        jnp.concatenate(attended_parts, axis=0).reshape(row_count, width).astype(jnp.bfloat16)
    )
    projected = jnp.dot(attended, w_out, preferred_element_type=jnp.float32) + b_out
    hidden, normal_one, inv_one = layer_stats(inputs + projected, ln1_gain, ln1_bias)
    hidden_low = hidden.astype(jnp.bfloat16)
    inner = jnp.dot(hidden_low, w_up, preferred_element_type=jnp.float32) + b_up
    activ = jax.nn.gelu(inner, approximate=False).astype(jnp.bfloat16)
    branch = jnp.dot(activ, w_down, preferred_element_type=jnp.float32) + b_down
    normed, normal_two, inv_two = layer_stats(hidden + branch, ln2_gain, ln2_bias)
    normed_low = normed.astype(jnp.bfloat16)
    embedded = jnp.dot(normed_low, w_proj, preferred_element_type=jnp.float32)
    inv_len = lax.rsqrt(jnp.sum(embedded * embedded, axis=-1, keepdims=True) + norm_epsilon)
    unit = embedded * inv_len
    unit_low = unit.astype(jnp.bfloat16)
    query_slots = jnp.arange(QLEN, dtype=jnp.int32)
    query_valid = query_slots < lengths[0]
    my_query = jnp.where(query_valid[:, None], unit_low[:QLEN], jnp.zeros((), jnp.bfloat16))
    my_length = jnp.full((1, 1), lengths[0], jnp.float32).astype(jnp.bfloat16)
    all_queries, all_lengths = (
        lax.all_gather(my_query[None], "dp", axis=0, tiled=True),
        lax.all_gather(my_length, "dp", axis=0, tiled=True),
    )
    my_owner = owner[device]
    my_place = place[device]
    query_for = all_queries[my_owner]
    length_for = all_lengths[my_owner, 0].astype(jnp.float32)
    passage_slots = jnp.arange(PLEN, dtype=jnp.int32)
    passage_index = jnp.minimum(starts[1:, None] + passage_slots[None, :], row_count - 1)
    document_exists_flag = passage_slots[None, :] < lengths[1:, None]
    passage_vec = jnp.where(
        document_exists_flag[..., None], unit_low[passage_index], jnp.zeros((), jnp.bfloat16)
    )
    matching_logits = jnp.einsum(
        "pid,pjd->pij", query_for, passage_vec, preferred_element_type=jnp.float32
    )
    divided_logits = jnp.where(
        document_exists_flag[:, None, :], matching_logits / logit_divisor, huge_penalty_constant
    )
    score_maximum = jnp.max(divided_logits, axis=-1, keepdims=True)
    spread = jnp.exp(divided_logits - score_maximum)
    exponent_total_sum = jnp.sum(spread, axis=-1, keepdims=True)
    normalized_likelihoods = logit_divisor * (
        score_maximum[..., 0] + jnp.log(exponent_total_sum[..., 0])
    )
    query_mask = query_slots[None, :].astype(jnp.float32) < length_for[:, None]
    score = jnp.sum(jnp.where(query_mask, normalized_likelihoods, 0.0), axis=-1)
    all_scores = lax.all_gather(score, "dp", axis=0, tiled=True)
    table = (
        jnp.zeros((devices, passages_per), jnp.float32)
        .at[owner.reshape(-1), place.reshape(-1)]
        .set(all_scores)
    )
    table_top = jnp.max(table, axis=-1, keepdims=True)
    table_exp = jnp.exp(table - table_top)
    table_sum = jnp.sum(table_exp, axis=-1, keepdims=True)
    loss_all = table_top[:, 0] + jnp.log(table_sum[:, 0]) - table[:, 0]
    losses = lax.dynamic_slice_in_dim(loss_all, device, 1)
    positive = (jnp.arange(passages_per, dtype=jnp.int32) == 0).astype(jnp.float32)
    d_table = table_exp / table_sum - positive[None, :]
    d_score = d_table[my_owner, my_place]
    d_soft = d_score[:, None] * query_mask.astype(jnp.float32)
    d_sims = d_soft[..., None] * (spread / exponent_total_sum)
    d_query_for = jnp.einsum(
        "pij,pjd->pid", d_sims, passage_vec.astype(jnp.float32), precision=precise
    )
    d_passage = jnp.einsum("pij,pid->pjd", d_sims, query_for.astype(jnp.float32), precision=precise)
    owner_flat = owner.reshape(-1)
    match = (owner_flat == device).astype(jnp.float32)[None, :]
    d_my_query = jnp.zeros((1, QLEN * out_width), jnp.float32) + jnp.dot(
        match,
        lax.all_gather(
            d_query_for.reshape(passages_per, QLEN * out_width).astype(jnp.bfloat16),
            "dp",
            axis=0,
            tiled=True,
        ).astype(jnp.float32),
        precision=precise,
    )
    slot_grads = jnp.concatenate(
        [
            d_my_query.reshape(QLEN, out_width),
            d_passage.reshape(passages_per * PLEN, out_width),
            jnp.zeros((1, out_width), jnp.float32),
        ],
        axis=0,
    ).astype(jnp.bfloat16)
    d_unit = slot_grads[token_slot].astype(jnp.float32)
    d_embedded = (
        inv_len * (d_unit - unit * jnp.sum(unit * d_unit, axis=-1, keepdims=True))
    ).astype(jnp.bfloat16)
    g_w_proj = inner_rows(normed_low, d_embedded)
    d_normed = times_transposed(d_embedded, w_proj)
    g_ln2_gain = jnp.sum(d_normed * normal_two, axis=0)
    g_ln2_bias = jnp.sum(d_normed, axis=0)
    d_resid_two = layer_back(d_normed, ln2_gain, normal_two, inv_two)
    d_branch = d_resid_two.astype(jnp.bfloat16)
    g_w_down = inner_rows(activ, d_branch)
    g_b_down = jnp.sum(d_branch.astype(jnp.float32), axis=0)
    d_activ = times_transposed(d_branch, w_down)
    d_inner = (d_activ * gelu_slope(inner)).astype(jnp.bfloat16)
    g_w_up = inner_rows(hidden_low, d_inner)
    g_b_up = jnp.sum(d_inner.astype(jnp.float32), axis=0)
    d_hidden = times_transposed(d_inner, w_up) + d_resid_two
    g_ln1_gain = jnp.sum(d_hidden * normal_one, axis=0)
    g_ln1_bias = jnp.sum(d_hidden, axis=0)
    d_resid_one = layer_back(d_hidden, ln1_gain, normal_one, inv_one)
    d_projected = d_resid_one.astype(jnp.bfloat16)
    g_w_out = inner_rows(attended, d_projected)
    g_b_out = jnp.sum(d_projected.astype(jnp.float32), axis=0)
    d_attended = (
        times_transposed(d_projected, w_out)
        .astype(jnp.bfloat16)
        .reshape(row_count, HEADS, head_size)
    )
    d_queries_parts = []
    key_gradient_accumulated = jnp.zeros((row_count, HEADS, head_size), jnp.float32)
    d_values_total = jnp.zeros((row_count, HEADS, head_size), jnp.float32)
    for window_id in range(len(windows)):
        first_row, key_first, span = windows[window_id]
        scores = block_scores(first_row, key_first, span)
        probs_full = jnp.exp(scores - log_totals[window_id])
        probs_low = probs_full.astype(jnp.bfloat16)
        derivative_lines = d_attended[first_row : first_row + block]
        d_probs = jnp.einsum(
            "qhd,khd->hqk", derivative_lines, values, preferred_element_type=jnp.float32
        )
        d_scores = (
            probs_full * (d_probs - jnp.sum(d_probs * probs_full, axis=-1, keepdims=True))
        ).astype(jnp.bfloat16)
        d_queries_parts.append(
            jnp.einsum("hqk,khd->qhd", d_scores, keys_all, preferred_element_type=jnp.float32)
            * scale
        )
        key_grad = (
            jnp.einsum(
                "hqk,qhd->khd",
                d_scores,
                queries[first_row : first_row + block],
                preferred_element_type=jnp.float32,
            )
            * scale
        )
        value_grad = jnp.einsum(
            "hqk,qhd->khd", probs_low, derivative_lines, preferred_element_type=jnp.float32
        )
        key_gradient_accumulated = key_gradient_accumulated.at[key_first : key_first + span].add(
            key_grad
        )
        d_values_total = d_values_total.at[key_first : key_first + span].add(value_grad)
    d_queries = jnp.concatenate(d_queries_parts, axis=0).reshape(row_count, width)
    d_packed = jnp.concatenate(
        [
            d_queries,
            key_gradient_accumulated.reshape(row_count, width),
            d_values_total.reshape(row_count, width),
        ],
        axis=1,
    ).astype(jnp.bfloat16)
    g_w_qkv = inner_rows(tokens, d_packed)
    packed_sums = jnp.sum(d_packed.astype(jnp.float32), axis=0)
    g_b_qv = jnp.concatenate([packed_sums[:width], packed_sums[2 * width :]])
    d_tokens = times_transposed(d_packed, w_qkv) + d_resid_one
    (
        g_w_qkv,
        g_b_qv,
        g_w_out,
        g_b_out,
        g_ln1_gain,
        g_ln1_bias,
        g_w_up,
        g_b_up,
        g_w_down,
        g_b_down,
        g_ln2_gain,
        g_ln2_bias,
        g_w_proj,
    ) = lax.psum(
        (
            g_w_qkv,
            g_b_qv,
            g_w_out,
            g_b_out,
            g_ln1_gain,
            g_ln1_bias,
            g_w_up,
            g_b_up,
            g_w_down,
            g_b_down,
            g_ln2_gain,
            g_ln2_bias,
            g_w_proj,
        ),
        "dp",
    )
    return (
        losses,
        d_tokens,
        g_w_qkv,
        g_b_qv,
        g_w_out,
        g_b_out,
        g_ln1_gain,
        g_ln1_bias,
        g_w_up,
        g_b_up,
        g_w_down,
        g_b_down,
        g_ln2_gain,
        g_ln2_bias,
        g_w_proj,
    )


def solution(mesh):
    placed = (
        P("dp", None),
        P("dp", None),
        P(),
        P(),
        P(),
        P(),
        P(),
        P(),
        P(),
        P(),
        P(),
        P(),
        P(),
        P(),
        P(),
        P(),
        P(),
    )
    return jax.shard_map(
        body,
        mesh=mesh,
        in_specs=placed,
        out_specs=(
            P("dp"),
            P("dp", None),
            P(),
            P(),
            P(),
            P(),
            P(),
            P(),
            P(),
            P(),
            P(),
            P(),
            P(),
            P(),
            P(),
        ),
        check_vma=False,
    )
```

profile of v0, /device:TPU:0, one launch (start us, length us, event | category | flops | bytes accessed | tf_op | source)
XLA Modules:
  0.0 1105.7 jit_solution(794403253104239357)
XLA Ops:
  16.9 2.6 copy.84
  19.5 5.9 add_convert_fusion
  26.7 1.9 fusion.80
  30.6 42.2 %all-reduce.1 = bf16[32]{0:T(256)(128)(2,1)S(1)} all-reduce(bf16[32]{0:T(256)(128)(2,1)S(1)} %dynamic-update-slice.8), channel_id=1, replica_groups=mesh['dp'=32] {'dp'}, use_global_device_ids=true, to_apply=%add.1 | all-reduce | flops 32 | bytes 128
  82.6 2.6 copy.87
  85.3 2.3 copy.86
  87.5 2.3 copy.88
  89.8 2.6 copy.85
  93.8 14.4 %fusion.29 = (f32[12,512]{1,0:T(8,128)S(1)}, f32[12,512,1024]{2,1,0:T(8,128)}) fusion(pred[512,1024]{1,0:T(8,128)(4,1)S(1)} %get-tuple-element.192, bf16[512,12,64]{0,2,1:T(8,128)(2,1)} %bitcast.137, bf16[1024,12,64]{0,2,1:T(8,128)(2,1)} %bitcast.126), kind=kOutput, calls=%fused_computation.58 | convolution fusion | flops 824174592 | bytes 28073984 | tf_op jit(solution)/shard_map/qhd,khd->hqk/dot_general | solution.py:108
  108.3 12.3 %fusion.1 = f32[12,512]{1,0:T(8,128)S(1)} fusion(f32[12,512]{1,0:T(8,128)S(1)} %get-tuple-element.198, f32[12,512,1024]{2,1,0:T(8,128)} %get-tuple-element.199, pred[512,1024]{1,0:T(8,128)(4,1)S(1)} %get-tuple-element.192), kind=kLoop, calls=%fused_computation.19 | loop fusion | flops 25159680 | bytes 25739264 | tf_op jit(solution)/shard_map/reduce_sum | solution.py:128
  120.6 3.1 copy-done.2
  123.7 9.8 fusion.41
  133.5 12.4 %fusion.28 = (f32[12,512]{1,0:T(8,128)S(1)}, f32[12,512,1024]{2,1,0:T(8,128)}) fusion(pred[512,1024]{1,0:T(8,128)(4,1)} %get-tuple-element.191, bf16[512,12,64]{0,2,1:T(8,128)(2,1)} %bitcast.141, bf16[1024,12,64]{0,2,1:T(8,128)(2,1)S(1)} %bitcast.127), kind=kOutput, calls=%fused_computation.57 | convolution fusion | flops 824174592 | bytes 28073984 | tf_op jit(solution)/shard_map/qhd,khd->hqk/dot_general | solution.py:108
  145.9 13.5 %fusion = f32[12,512]{1,0:T(8,128)S(1)} fusion(f32[12,512]{1,0:T(8,128)S(1)} %get-tuple-element.200, f32[12,512,1024]{2,1,0:T(8,128)} %get-tuple-element.201, pred[512,1024]{1,0:T(8,128)(4,1)} %get-tuple-element.191), kind=kLoop, calls=%fused_computation.18 | loop fusion | flops 25159680 | bytes 25739264 | tf_op jit(solution)/shard_map/reduce_sum | solution.py:128
  159.4 2.4 copy-done.1
  161.8 9.7 fusion.40
  172.9 4.0 fusion.85
  177.4 48.7 %fusion.6 = (bf16[1024,3072]{1,0:T(8,128)(2,1)S(1)}, f32[1024,3072]{1,0:T(8,128)}) fusion(f32[3072]{0:T(1024)S(1)} %copy-done.69, bf16[768,3072]{1,0:T(8,128)(2,1)} %param.43, f32[1024,768]{0,1:T(8,128)S(1)} %get-tuple-element.203, f32[768]{0:T(1024)S(1)} %copy-done.73, f32[768]{0:T(1024)S(1)} %copy-done.63, f32[1024]{0:T(1024)S(1)} %add_rsqrt_fusion.2, ...), kind=kOutput, calls=%fused_computation.26 | convolution fusion | flops 5043388416 | bytes 26765312 | tf_op jit(solution)/shard_map/dot_general | solution.py:140
  226.3 6.0 fusion.86
  236.6 5.0 gather_fusion.2
  241.6 1.7 reshape.695
  243.3 43.8 %all-gather = bf16[1024,128]{1,0:T(8,128)(2,1)} all-gather(bf16[32,128]{1,0:T(8,128)(2,1)} %slice_select_fusion), channel_id=2, replica_groups=mesh['dp'=32] {'dp'}, dimensions={0}, use_global_device_ids=true | all-gather | bytes 270336 | tf_op jit(solution)/shard_map/all_gather | solution.py:154
  287.0 2.2 gather_fusion.1
  292.6 36.8 %all-reduce.2 = f32[160]{0:T(256)} all-reduce(f32[160]{0:T(256)S(1)} %dynamic-update-slice.9), channel_id=1, replica_groups=mesh['dp'=32] {'dp'}, use_global_device_ids=true, to_apply=%add.2 | all-reduce | flops 160 | bytes 1280
  330.2 13.8 %scatter_fusion = f32[32,5]{0,1:T(8,128)S(1)} fusion(f32[32,5]{0,1:T(8,128)S(1)} %broadcast_in_dim.92, s32[160]{0:T(256)S(1)} %bitcast.143, f32[160]{0:T(256)} %all-reduce.2), kind=kCustom, calls=%fused_computation.5 | custom fusion | bytes 3200 | tf_op jit(solution)/shard_map/scatter | solution.py:185
  348.4 2.2 convolution_convert_fusion.2
  356.0 2.4 convolution_convert_fusion.1
  358.4 1.7 reshape.677
  364.4 44.8 %all-gather.4.cloned.1.call-done = bf16[32,5,4096]{2,1,0:T(8,128)(2,1)} async-done(((bf16[1,5,4096]{2,1,0:T(8,128)(2,1)}), bf16[32,5,4096]{2,1,0:T(8,128)(2,1)}) %all-gather.4.cloned.1.call-update) | async-done | bytes 1310736 | tf_op jit(solution)/shard_map/all_gather | solution.py:205
  409.2 2.8 reshape.729
  412.0 1.6 fusion.35
  413.6 1.8 maximum_maximum_fusion
  415.4 5.1 gather_fusion.4
  420.5 1.5 fusion.43
  423.5 2.7 fusion.90
  426.2 3.8 fusion.88
  430.0 3.5 copy.91
  433.5 4.6 multiply_reduce_fusion.2
  438.2 1.7 convert_reduce_fusion.2
  439.9 10.3 fusion.61
  450.3 12.6 %convert_reduce_fusion = (f32[3072]{0:T(1024)}, bf16[1024,3072]{1,0:T(8,128)(2,1)S(1)}) fusion(f32[1024,3072]{1,0:T(8,128)} %get-tuple-element.205, f32[3072]{0:T(1024)S(1)} %copy-done.70, bf16[3072,768]{1,0:T(8,128)(2,1)S(1)} %bitcast.165, f32[1024,768]{0,1:T(8,128)S(1)} %get-tuple-element.176), kind=kOutput, calls=%fused_computation.35 | convolution fusion | flops 4873516032 | bytes 26763264 | tf_op jit(solution)/shard_map/dot_general | solution.py:25
  463.0 6.8 multiply_reduce_fusion.3
  469.8 7.8 fusion.75
  477.6 1.7 convert_reduce_fusion.3
  479.4 2.8 fusion.58
  485.5 13.5 %fusion.13 = f32[12,64,1024]{2,1,0:T(8,128)} fusion(bf16[512,12,64]{0,2,1:T(8,128)(2,1)S(1)} %bitcast.149, f32[12,512]{1,0:T(8,128)S(1)} %copy-done.35, f32[12,512,1024]{2,1,0:T(8,128)} %get-tuple-element.199, pred[512,1024]{1,0:T(8,128)(4,1)S(1)} %copy-done.14), kind=kOutput, calls=%fused_computation.33 | convolution fusion | flops 830472192 | bytes 29646848 | tf_op jit(solution)/shard_map/hqk,qhd->khd/dot_general | solution.py:277
  499.0 18.8 %multiply_reduce_fusion = (f32[12,512]{1,0:T(8,128)}, f32[12,512,1024]{2,1,0:T(8,128)}) fusion(f32[12,512]{1,0:T(8,128)} %log_add_fusion, f32[12,512,1024]{2,1,0:T(8,128)} %get-tuple-element.199, pred[512,1024]{1,0:T(8,128)(4,1)} %copy-done.13, bf16[512,12,64]{0,2,1:T(8,128)(2,1)} %bitcast.150, bf16[1024,12,64]{0,2,1:T(8,128)(2,1)} %bitcast.132), kind=kOutput, calls=%fused_computation.7 | convolution fusion | flops 836757504 | bytes 53264384 | tf_op jit(solution)/shard_map/qhd,khd->hqk/dot_general | solution.py:258
  517.8 18.8 %multiply_reduce_fusion.1 = (f32[12,512]{1,0:T(8,128)}, f32[12,512,1024]{2,1,0:T(8,128)}) fusion(f32[12,512]{1,0:T(8,128)} %log_add_fusion.1, f32[12,512,1024]{2,1,0:T(8,128)} %get-tuple-element.201, pred[512,1024]{1,0:T(8,128)(4,1)} %get-tuple-element.191, bf16[512,12,64]{0,2,1:T(8,128)(2,1)} %bitcast.147, bf16[1024,12,64]{0,2,1:T(8,128)(2,1)} %bitcast.133), kind=kOutput, calls=%fused_computation.10 | convolution fusion | flops 836757504 | bytes 53264384 | tf_op jit(solution)/shard_map/qhd,khd->hqk/dot_general | solution.py:258
  536.6 42.9 %multiply_convert_fusion = (bf16[12,512,1024]{2,1,0:T(8,128)(2,1)}, bf16[12,512,1024]{2,1,0:T(8,128)(2,1)}) fusion(f32[12,512,1024]{2,1,0:T(8,128)} %get-tuple-element.216, f32[12,512]{1,0:T(8,128)} %get-tuple-element.215, f32[12,512]{1,0:T(8,128)} %log_add_fusion, f32[12,512,1024]{2,1,0:T(8,128)} %get-tuple-element.199, pred[512,1024]{1,0:T(8,128)(4,1)} %copy-done.13, ...), kind=kLoop, calls=%fused_computation.6 | loop fusion | flops 75497472 | bytes 126976000 | tf_op jit(solution)/shard_map/convert_element_type | solution.py:263
  579.4 8.7 fusion.38
  588.2 7.0 fusion.89
  595.2 12.9 %add_convert_fusion.1 = bf16[12,64,1024]{2,1,0:T(8,128)(2,1)S(1)} fusion(f32[12,64,1024]{2,1,0:T(8,128)} %fusion.13, bf16[512,12,64]{0,2,1:T(8,128)(2,1)S(1)} %bitcast.148, f32[12,512]{1,0:T(8,128)S(1)} %copy-done.34, f32[12,512,1024]{2,1,0:T(8,128)} %get-tuple-element.201, pred[512,1024]{1,0:T(8,128)(4,1)S(1)} %copy-done.12), kind=kOutput, calls=%fused_computation.66 | convolution fusion | flops 832045056 | bytes 31219712 | tf_op jit(solution)/shard_map/hqk,qhd->khd/dot_general | solution.py:277
  608.0 9.2 fusion.39
  617.3 7.0 multiply_convert_fusion.2
  625.9 9.2 convolution_bitcast_fusion
  637.0 9.4 convolution_add_fusion.1
  646.3 3.6 copy.95
  650.0 2.8 convert_reduce_fusion.1
  652.8 41.2 %all-reduce.3 = (f32[1536]{0:T(1024)}, f32[768]{0:T(1024)}, f32[768]{0:T(1024)}, f32[768]{0:T(1024)}, f32[3072]{0:T(1024)}, /*index=5*/f32[768]{0:T(1024)}, f32[768]{0:T(1024)}, f32[768]{0:T(1024)}) all-reduce(f32[1536]{0:T(1024)S(1)} %pad_maximum_fusion.4, f32[768]{0:T(1024)} %get-tuple-element.177, ...), channel_id=1, replica_groups=mesh['dp'=32] {'dp'}, use_global_device_ids=true, to_apply=%region_27.28 | all-reduce | flops 9216 | bytes 73728 | tf_op jit(solution)/shard_map/psum | solution.py:311
  694.0 380.0 %all-reduce.7.cloned.1.call-done = (f32[768,2304]{0,1:T(8,128)}, f32[768,768]{1,0:T(8,128)}, f32[768,3072]{1,0:T(8,128)}, f32[3072,768]{1,0:T(8,128)}, f32[768,128]{1,0:T(8,128)}) async-done(((f32[768,2304]{0,1:T(8,128)}, f32[768,768]{1,0:T(8,128)}, f32[768,3072]{1,0:T(8,128)}, f32[3072,768]{1,0:T(8,128)}, f32[768,128]{1,0:T(8,128)}), (f32[768,2304]{0,1:T(8,128)}, f32[768,768]{1,0:T(8,128)}, ...) | async-done | bytes 28704784 | tf_op jit(solution)/shard_map/psum | solution.py:311
  1074.0 8.0 copy.96
  1082.0 3.4 copy.115
  1085.3 8.8 copy.116
  1094.1 3.7 copy.117
  (259 shorter events, 56.7 us)
Async XLA Ops:
  7.2 12.3 %copy-start = (bf16[768,2304]{1,0:T(8,128)(2,1)S(1)}, bf16[768,2304]{1,0:T(8,128)(2,1)}, u32[]{:S(2)}) copy-start(bf16[768,2304]{1,0:T(8,128)(2,1)} %param.37) | copy-start | bytes 10616836
  7.2 402.0 %all-gather.4.cloned.1.call-start = ((), (), s32[]{:S(2)}) async-start(), calls=%async_computation | async-start | bytes 2162688 | tf_op jit(solution)/shard_map/all_gather | solution.py:205
  76.6 15.8 %copy-start.37 = (s32[1024]{0:T(1024)}, s32[1024]{0:T(1024)S(1)}, u32[]{:S(2)}) copy-start(s32[1024]{0:T(1024)S(1)} %convert_reduce_fusion.4) | copy-start | bytes 12292
  82.6 9.8 copy-start.56
  82.6 9.8 copy-start.57
  93.8 14.4 %copy-start.13 = (pred[512,1024]{1,0:T(8,128)(4,1)}, pred[512,1024]{1,0:T(8,128)(4,1)S(1)}, u32[]{:S(2)}) copy-start(pred[512,1024]{1,0:T(8,128)(4,1)S(1)} %get-tuple-element.192) | copy-start | bytes 1572868
  108.3 12.4 %copy-start.32 = (f32[12,512]{1,0:T(8,128)}, f32[12,512]{1,0:T(8,128)S(1)}, u32[]{:S(2)}) copy-start(f32[12,512]{1,0:T(8,128)S(1)} %get-tuple-element.198) | copy-start | bytes 73732
  108.3 15.4 %copy-start.2 = (f32[12,512,1024]{2,1,0:T(8,128)S(1)}, f32[12,512,1024]{2,1,0:T(8,128)}, u32[]{:S(2)}) copy-start(f32[12,512,1024]{2,1,0:T(8,128)} %get-tuple-element.199) | copy-start | bytes 75497472
  120.6 12.9 %copy-start.39 = (f32[12,512]{1,0:T(8,128)}, f32[12,512]{1,0:T(8,128)S(1)}, u32[]{:S(2)}) copy-start(f32[12,512]{1,0:T(8,128)S(1)} %fusion.1) | copy-start | bytes 73732
  123.7 9.8 copy-start.6
  145.9 13.5 %copy-start.33 = (f32[12,512]{1,0:T(8,128)}, f32[12,512]{1,0:T(8,128)S(1)}, u32[]{:S(2)}) copy-start(f32[12,512]{1,0:T(8,128)S(1)} %get-tuple-element.200) | copy-start | bytes 73732
  145.9 15.8 %copy-start.1 = (f32[12,512,1024]{2,1,0:T(8,128)S(1)}, f32[12,512,1024]{2,1,0:T(8,128)}, u32[]{:S(2)}) copy-start(f32[12,512,1024]{2,1,0:T(8,128)} %get-tuple-element.201) | copy-start | bytes 75497472
  145.9 15.9 %copy-start.11 = (pred[512,1024]{1,0:T(8,128)(4,1)S(1)}, pred[512,1024]{1,0:T(8,128)(4,1)}, u32[]{:S(2)}) copy-start(pred[512,1024]{1,0:T(8,128)(4,1)} %get-tuple-element.191) | copy-start | bytes 1572868
  161.8 9.7 copy-start.40
  161.8 9.7 copy-start.30
  161.8 11.0 copy-start.71
  172.8 4.1 copy-start.26
  172.8 4.5 copy-start.63
  172.8 4.5 copy-start.69
  172.9 4.5 copy-start.73
  172.9 53.3 %slice-start.3 = ((s8[4718592]{0:T(1024)(128)(4,1)}), s8[4194304]{0:T(1024)(128)(4,1)S(1)}, s32[]{:S(2)}) async-start(s8[4718592]{0:T(1024)(128)(4,1)} %bitcast.162), calls=%async_computation.5 | async-start | bytes 8388608
  176.9 49.2 %copy-start.15 = (f32[1024,768]{0,1:T(8,128)}, f32[1024,768]{0,1:T(8,128)S(1)}, u32[]{:S(2)}) copy-start(f32[1024,768]{0,1:T(8,128)S(1)} %get-tuple-element.203) | copy-start | bytes 9437188
  177.0 49.2 %copy-start.47 = (f32[1024]{0:T(1024)}, f32[1024]{0:T(1024)S(1)}, u32[]{:S(2)}) copy-start(f32[1024]{0:T(1024)S(1)} %broadcast_multiply_fusion.5) | copy-start | bytes 12292
  177.4 48.8 %copy-start.50 = (f32[1024]{0:T(1024)}, f32[1024]{0:T(1024)S(1)}, u32[]{:S(2)}) copy-start(f32[1024]{0:T(1024)S(1)} %add_rsqrt_fusion.2) | copy-start | bytes 12292
  177.4 48.8 %slice-start.4 = ((s8[4718592]{0:T(1024)(128)(4,1)}), s8[524288]{0:T(1024)(128)(4,1)S(1)}, s32[]{:S(2)}) async-start(s8[4718592]{0:T(1024)(128)(4,1)} %bitcast.162), calls=%async_computation.6 | async-start | bytes 1048576
  177.4 48.8 %copy-start.72 = (f32[768]{0:T(1024)S(1)}, f32[768]{0:T(1024)}, u32[]{:S(2)}) copy-start(f32[768]{0:T(1024)} %param.46) | copy-start | bytes 9220
  226.2 6.1 copy-start.76
  226.2 6.5 copy-start.45
  226.3 6.5 copy-start.62
  232.3 3.6 copy-start.67
  232.7 3.9 copy-start.49
  235.9 125.5 %copy-start.38 = (s32[1024]{0:T(1024)S(1)}, s32[1024]{0:T(1024)}, u32[]{:S(2)}) copy-start(s32[1024]{0:T(1024)} %copy-done.37) | copy-start | bytes 12292
  344.0 76.5 %copy-start.3 = (f32[32,5]{0,1:T(8,128)}, f32[32,5]{0,1:T(8,128)S(1)}, u32[]{:S(2)}) copy-start(f32[32,5]{0,1:T(8,128)S(1)} %scatter_fusion) | copy-start | bytes 1924
  350.5 70.0 %copy-start.44 = (f32[1024]{0:T(1024)S(1)}, f32[1024]{0:T(1024)}, u32[]{:S(2)}) copy-start(f32[1024]{0:T(1024)} %copy-done.43) | copy-start | bytes 12292
  352.0 722.0 %all-reduce.7.cloned.1.call-start = ((), (), s32[]{:S(2)}) async-start(), calls=%async_computation.1 | async-start | bytes 57409536 | tf_op jit(solution)/shard_map/psum | solution.py:311
  426.2 7.3 copy-start.42
  426.2 7.3 copy-start.46
  433.5 4.6 copy-start.5
  433.5 4.7 copy-start.8
  438.2 12.1 %slice-start.5 = ((s8[4718592]{0:T(1024)(128)(4,1)}), s8[4194304]{0:T(1024)(128)(4,1)S(1)}, s32[]{:S(2)}) async-start(s8[4718592]{0:T(1024)(128)(4,1)} %bitcast.164), calls=%async_computation.7 | async-start | bytes 8388608
  439.9 10.4 slice-start.6
  439.9 10.4 copy-start.70
  439.9 23.0 %slice-start.7 = ((s8[4718592]{0:T(1024)(128)(4,1)}), s8[4194304]{0:T(1024)(128)(4,1)S(1)}, s32[]{:S(2)}) async-start(s8[4718592]{0:T(1024)(128)(4,1)} %bitcast.166), calls=%async_computation.9 | async-start | bytes 8388608
  450.3 12.6 %copy-start.16 = (f32[1024,768]{0,1:T(8,128)S(1)}, f32[1024,768]{0,1:T(8,128)}, u32[]{:S(2)}) copy-start(f32[1024,768]{0,1:T(8,128)} %copy-done.15) | copy-start | bytes 9437188
  450.3 12.6 %copy-start.48 = (f32[1024]{0:T(1024)S(1)}, f32[1024]{0:T(1024)}, u32[]{:S(2)}) copy-start(f32[1024]{0:T(1024)} %copy-done.47) | copy-start | bytes 12292
  450.3 12.6 %copy-start.51 = (f32[1024]{0:T(1024)S(1)}, f32[1024]{0:T(1024)}, u32[]{:S(2)}) copy-start(f32[1024]{0:T(1024)} %copy-done.50) | copy-start | bytes 12292
  450.3 12.6 %copy-start.64 = (f32[768]{0:T(1024)S(1)}, f32[768]{0:T(1024)}, u32[]{:S(2)}) copy-start(f32[768]{0:T(1024)} %param.41) | copy-start | bytes 9220
  450.3 12.6 %slice-start.8 = ((s8[4718592]{0:T(1024)(128)(4,1)}), s8[524288]{0:T(1024)(128)(4,1)S(1)}, s32[]{:S(2)}) async-start(s8[4718592]{0:T(1024)(128)(4,1)} %bitcast.166), calls=%async_computation.10 | async-start | bytes 1048576
  463.0 6.8 copy-start.74
  482.2 3.3 copy-start.35
  536.6 42.9 %copy-start.7 = (bf16[1024,768]{0,1:T(8,128)(2,1)S(1)}, bf16[1024,768]{0,1:T(8,128)(2,1)}, u32[]{:S(2)}) copy-start(bf16[1024,768]{0,1:T(8,128)(2,1)} %copy.87) | copy-start | bytes 4718596
  579.4 8.7 copy-start.19
  588.1 7.0 copy-start.12
  588.1 7.0 copy-start.23
  588.1 7.0 copy-start.34
  608.0 16.4 %copy-start.28 = (bf16[12,64,1024]{2,1,0:T(8,128)(2,1)}, bf16[12,64,1024]{2,1,0:T(8,128)(2,1)S(1)}, u32[]{:S(2)}) copy-start(bf16[12,64,1024]{2,1,0:T(8,128)(2,1)S(1)} %add_convert_fusion.1) | copy-start | bytes 4718596
  608.0 9.2 copy-start.18
  617.2 8.7 copy-start.25
  646.3 6.5 copy-start.52
  646.3 6.5 copy-start.53
  1082.0 12.1 %slice-start = ((s8[9437184]{0:T(1024)(128)(4,1)}), s8[4194304]{0:T(1024)(128)(4,1)S(1)}, s32[]{:S(2)}) async-start(s8[9437184]{0:T(1024)(128)(4,1)} %bitcast.139), calls=%async_computation.2 | async-start | bytes 8388608
  1085.3 8.8 slice-start.1
  1085.3 8.8 slice-start.2
  1094.1 3.8 copy-start.31
  (24 other events, 31.9 us)
Sparse Core Ops, SparseCore 0:
  352.1 57.0 all-gather.3
  635.2 438.7 all-reduce.6
where the time goes:
time: 1110 us
  waiting for transfers between devices  425 us (38%)
  matrix products  282 us (25%)
  blocking collectives  164 us (15%)
  local copies, waits for them, and re-layouts  112 us (10%)
  other arithmetic  107 us (10%)
  between operations  16.2 us (1%)
    psum x1, waiting for transfers between devices, body(): lax.psum((g_w_qkv, g_b_qv, g_w_out, g_b_out, g_ln1_gain, g_ln1_bias, g_w_...  380 us
    unnamed x2, blocking collectives  79.1 us
    unnamed x187, local copies, waits for them, and re-layouts  50.9 us
    dot_general x1, matrix products, body(): inner = jnp.dot(hidden_low, w_up, preferred_element_type=jnp.float32) + b_up  48.7 us
    all_gather x1, waiting for transfers between devices, body(): lax.all_gather(d_query_for.reshape(passages_per, QLEN * out_width).astype...  44.8 us
    all_gather x1, blocking collectives, body(): lax.all_gather(my_query[None], 'dp', axis=0, tiled=True)  43.8 us
    convert_element_type x1, other arithmetic, body(): d_scores = (probs_full * (d_probs - jnp.sum(d_probs * probs_full, axis=-1...  42.9 us
    psum x1, blocking collectives, body(): lax.psum((g_w_qkv, g_b_qv, g_w_out, g_b_out, g_ln1_gain, g_ln1_bias, g_w_...  41.2 us
  transfers between devices with their start and end apart: 2, of which 2 were waited for; matrix products, arithmetic and copies ran while one was open for 3% of the time, Pallas kernels for 0%

commit v1 on v0

v1 whole, which is shorter than its diff:
```python
import functools

import jax
import jax.numpy as jnp
from jax import lax
from jax.experimental import pallas as pl
from jax.experimental.pallas import tpu as pltpu
from jax.sharding import PartitionSpec as P

HEADS = 12
QLEN = 32
PLEN = 180
QB = 128
WIDTHS = (256, 384, 512, 768, 1024)
PIECES = 16
PORTIONS = 3
NEG = -1e30
LN_EPS = 1e-12
NORM_EPS = 1e-6
f32, bf16, i32 = jnp.float32, jnp.bfloat16, jnp.int32


def nn(a, b):
    return lax.dot_general(a, b, (((1,), (0,)), ((), ())), preferred_element_type=f32)


def nt(a, b):
    return lax.dot_general(a, b, (((1,), (1,)), ((), ())), preferred_element_type=f32)


def tn(a, b):
    return lax.dot_general(a, b, (((0,), (0,)), ((), ())), preferred_element_type=f32)


def params(mib=48):
    return pltpu.CompilerParams(vmem_limit_bytes=mib << 20)


def cost(flops, nbytes):
    return pl.CostEstimate(flops=int(flops), bytes_accessed=int(nbytes), transcendentals=0)


SMEM = pl.BlockSpec(memory_space=pltpu.SMEM)
VMEM = pl.BlockSpec(memory_space=pltpu.VMEM)


def whole(shape):
    return pl.BlockSpec(shape, lambda *g: (0,) * len(shape))


def struct(shape, dtype):
    return jax.ShapeDtypeStruct(shape, dtype)


def segment_ends(lens):
    ends = [lens[0, 0]]
    for s in range(1, lens.shape[1]):
        ends.append(ends[-1] + lens[0, s])
    return ends


def segment_of(ends, position):
    seg = jnp.zeros(position.shape, i32)
    for e in ends:
        seg = seg + (position >= e).astype(i32)
    return seg


def key_window(ends, rows, first):
    lo = jnp.zeros((), i32)
    hi = jnp.asarray(rows, i32)
    for e in ends:
        lo = jnp.where(e <= first, e, lo)
    for e in reversed(ends):
        hi = jnp.where(e >= first + QB, e, hi)
    lo = lax.div(lo, QB) * QB
    need = hi - lo
    cls = jnp.zeros((), i32)
    wide = jnp.asarray(WIDTHS[0], i32)
    for c, w in enumerate(WIDTHS[:-1]):
        if WIDTHS[c + 1] <= rows:
            cls = jnp.where(need > w, c + 1, cls)
            wide = jnp.where(need > w, WIDTHS[c + 1], wide)
    return pl.multiple_of(jnp.minimum(lo, rows - wide), QB), cls


def fill_segments(ends, segq, segk):
    segk[...] = segment_of(ends, lax.broadcasted_iota(i32, segk.shape, 0))
    at = lax.broadcasted_iota(i32, segq.shape, 0) * QB + lax.broadcasted_iota(i32, segq.shape, 1)
    segq[...] = segment_of(ends, at)


def two_heads(x, scale=None):
    lane = lax.broadcasted_iota(i32, x.shape, 1)
    zero = jnp.zeros_like(x)
    if scale is not None:
        x = x * scale
    return jnp.concatenate([jnp.where(lane < 64, x, zero), jnp.where(lane < 64, zero, x)], axis=0)


def pick_heads(t):
    return jnp.concatenate([t[:64, :QB], t[64:, QB:]], axis=0)


def attn_fwd_kernel(lens, tok, wqkv, bqv, packed, out, lse, vt, segq, segk):
    rows, width = tok.shape
    ends = segment_ends(lens)
    fill_segments(ends, segq, segk)
    pairs = width // 128
    for j in range(3 * width // 256):
        at = slice(j * 256, (j + 1) * 256)
        x = nn(tok[...], wqkv[:, at])
        which = j * 256 // width
        if which != 1:
            b0 = j * 256 - (width if which else 0)
            x = x + bqv[b0 : b0 + 256].reshape(1, 256)
        packed[:, at] = x.astype(bf16)
    q = packed.at[:, 0:width]
    k = packed.at[:, width : 2 * width]
    v = packed.at[:, 2 * width : 3 * width]
    for g in range(pairs):
        vt[g] = v[:, g * 128 : (g + 1) * 128].T

    def step(i, carry):
        base = pl.multiple_of(i * QB, QB)
        k0, cls = key_window(ends, rows, base)
        sq = segq[pl.ds(i, 1), :]

        def body(w):
            same = segk[pl.ds(k0, w), :] == sq
            sts = []
            for g in range(pairs):
                sl = slice(g * 128, (g + 1) * 128)
                q2 = two_heads(q[pl.ds(base, QB), sl], jnp.asarray(0.125, bf16))
                sts.append(nt(k[pl.ds(k0, w), sl], q2))
            for g in range(pairs):
                sl = slice(g * 128, (g + 1) * 128)
                st = sts[g]
                ps, ms, ls = [], [], []
                for h in range(2):
                    s = jnp.where(same, st[:, h * QB : (h + 1) * QB], NEG)
                    m = jnp.max(s, axis=0, keepdims=True)
                    p = jnp.exp(s - m)
                    ls.append(jnp.sum(p, axis=0, keepdims=True))
                    ms.append(m)
                    ps.append(p.astype(bf16))
                total = jnp.concatenate(ls, 1)
                top = jnp.concatenate(ms, 1)
                ot = nn(vt[g, :, pl.ds(k0, w)], jnp.concatenate(ps, 1)) * (1.0 / total)
                out[pl.ds(base, QB), sl] = pick_heads(ot).T.astype(bf16)
                lse[g, pl.ds(i, 1), :] = top + jnp.log(total)

        for c, w in enumerate(WIDTHS):
            if w <= rows:
                pl.when(cls == c)(functools.partial(body, w))
        return carry

    lax.fori_loop(0, rows // QB, step, 0)


def attn_bwd_kernel(
    part, lens, packed, do, o, lse, dq, dk, dv, sums, kt, dka, dva, segq, segk
):
    rows = packed.shape[0]
    width = packed.shape[1] // 3
    span = dq.shape[1]
    ends = segment_ends(lens)
    fill_segments(ends, segq, segk)
    pairs = span // 128
    q, k, v = [packed.at[:, i * width + part * span : i * width + (part + 1) * span] for i in range(3)]
    do = do.at[:, part * span : (part + 1) * span]
    o = o.at[:, part * span : (part + 1) * span]
    for g in range(pairs):
        kt[g] = k[:, g * 128 : (g + 1) * 128].T
    dka[...] = jnp.zeros_like(dka)
    dva[...] = jnp.zeros_like(dva)
    head = (
        lax.broadcasted_iota(i32, (8, 128), 0) == lax.broadcasted_iota(i32, (8, 128), 1) // 64
    ).astype(f32)

    def step(i, carry):
        base = pl.multiple_of(i * QB, QB)
        k0, cls = key_window(ends, rows, base)
        sq = segq[pl.ds(i, 1), :]

        def body(w):
            at = pl.ds(k0, w)
            same = segk[at, :] == sq
            for g in range(pairs):
                gs = slice(g * 128, (g + 1) * 128)
                q2 = two_heads(q[pl.ds(base, QB), gs], jnp.asarray(0.125, bf16))
                do_ = do[pl.ds(base, QB), gs]
                do2 = two_heads(do_)
                d8 = lax.dot_general(
                    head,
                    do_.astype(f32) * o[pl.ds(base, QB), gs].astype(f32),
                    (((1,), (1,)), ((), ())),
                    precision=lax.Precision.HIGHEST,
                    preferred_element_type=f32,
                )
                lrow = lse[part * pairs + g, pl.ds(i, 1), :]
                st = nt(k[at, gs], q2)
                dpt = nt(v[at, gs], do2)
                ps, ds = [], []
                for h in range(2):
                    sl = slice(h * QB, (h + 1) * QB)
                    p = jnp.exp(jnp.where(same, st[:, sl] - lrow[:, sl], NEG))
                    ps.append(p.astype(bf16))
                    ds.append((p * (dpt[:, sl] - d8[h : h + 1, :])).astype(bf16))
                p = jnp.concatenate(ps, 1)
                d = jnp.concatenate(ds, 1)
                dka[at, gs] += nn(d, q2)
                dva[at, gs] += nn(p, do2)
                dqt = nn(kt[g, :, pl.ds(k0, w)], d)
                dq[pl.ds(base, QB), gs] = (pick_heads(dqt).T * 0.125).astype(bf16)

        for c, w in enumerate(WIDTHS):
            if w <= rows:
                pl.when(cls == c)(functools.partial(body, w))
        return carry

    lax.fori_loop(0, rows // QB, step, 0)
    dk[...] = dka[...].astype(bf16)
    dvl = dva[...].astype(bf16)
    dv[...] = dvl
    sums[0:1, :] = jnp.sum(dq[...].astype(f32), axis=0, keepdims=True)
    sums[1:2, :] = jnp.sum(dvl.astype(f32), axis=0, keepdims=True)


def segment_scratch(rows):
    return [pltpu.VMEM((rows // QB, QB), i32), pltpu.VMEM((rows, 128), i32)]


def attention(lens, tok, wqkv, bqv):
    rows, width = tok.shape
    pairs = width // 128
    return pl.pallas_call(
        attn_fwd_kernel,
        in_specs=[SMEM, VMEM, VMEM, VMEM],
        out_specs=[VMEM] * 3,
        out_shape=[
            struct((rows, 3 * width), bf16),
            struct((rows, width), bf16),
            struct((pairs, rows // QB, 2 * QB), f32),
        ],
        scratch_shapes=[pltpu.VMEM((pairs, 128, rows), bf16)] + segment_scratch(rows),
        compiler_params=params(32),
        cost_estimate=cost(16e9, 8 * rows * width),
        name="attention_forward",
    )(lens, tok, wqkv, bqv)


def attention_back(part, lens, packed, do, o, lse):
    rows, width = packed.shape[0], packed.shape[1] // 3
    span = width // PORTIONS
    pairs = span // 128
    shp = struct((rows, span), bf16)
    return pl.pallas_call(
        functools.partial(attn_bwd_kernel, part),
        in_specs=[SMEM] + [VMEM] * 4,
        out_specs=[VMEM] * 4,
        out_shape=[shp, shp, shp, struct((8, span), f32)],
        scratch_shapes=[
            pltpu.VMEM((pairs, 128, rows), bf16),
            pltpu.VMEM((rows, span), f32),
            pltpu.VMEM((rows, span), f32),
        ]
        + segment_scratch(rows),
        compiler_params=params(24),
        cost_estimate=cost(10e9, 16 * rows * span),
        name="attention_backward",
    )(lens, packed, do, o, lse)


def normalize(resid):
    center = resid - jnp.mean(resid, axis=-1, keepdims=True)
    inv = lax.rsqrt(jnp.mean(center * center, axis=-1, keepdims=True) + LN_EPS)
    return center * inv, inv


def norm_back(grad, gain, normal, inv):
    dn = grad * gain
    return inv * (
        dn
        - jnp.mean(dn, axis=-1, keepdims=True)
        - normal * jnp.mean(dn * normal, axis=-1, keepdims=True)
    )


def row(v):
    return v[...].reshape(1, -1)


def mid_fwd_kernel(
    lens, att, tok, wo, bo, g1, b1, wu, bu, wd, bd, g2, b2, wp,
    ht, act, slp, n1, i1, n2, i2, nl, emb, ul, msg,
    hid, low, acc, bus,
):
    rows = att.shape[0]
    ff = wu.shape[1]
    chunk = 512
    tile = 256
    tiles = [slice(r, r + tile) for r in range(0, rows, tile)]
    bus[...] = row(bu)
    for r in tiles:
        resid = tok[r, :].astype(f32) + (nn(att[r, :], wo[...]) + row(bo))
        normal, inv = normalize(resid)
        hidden = normal * row(g1) + row(b1)
        hid[r, :] = hidden
        hl = hidden.astype(bf16)
        low[r, :] = hl
        ht[:, r] = hl.T
        n1[r, :] = normal.astype(bf16)
        i1[r, :] = inv
        acc[r, :] = hidden + row(bd)

    def step(c, carry):
        at = pl.ds(pl.multiple_of(c * chunk, chunk), chunk)
        for r in tiles:
            inner = nn(low[r, :], wu[:, at]) + bus[:, at]
            cdf = 0.5 + 0.5 * lax.erf(inner * 0.7071067811865476)
            a = (inner * cdf).astype(bf16)
            act[r, at] = a
            slp[r, at] = (
                cdf + inner * (jnp.exp(inner * inner * -0.5) * 0.3989422804014327)
            ).astype(bf16)
            acc[r, :] += nn(a, wd[at, :])
        return carry

    lax.fori_loop(0, ff // chunk, step, 0)
    for r in tiles:
        normal, inv = normalize(acc[r, :])
        normed = (normal * row(g2) + row(b2)).astype(bf16)
        n2[r, :] = normal.astype(bf16)
        i2[r, :] = inv
        nl[r, :] = normed
        e = nn(normed, wp[...])
        emb[r, :] = e
        ul[r, :] = (e * lax.rsqrt(jnp.sum(e * e, axis=-1, keepdims=True) + NORM_EPS)).astype(bf16)
    count = lens[0, 0]
    slot = lax.broadcasted_iota(i32, (QLEN, ul.shape[1]), 0)
    msg[0, 0:QLEN, :] = jnp.where(slot < count, ul[0:QLEN, :].astype(f32), 0.0).astype(bf16)
    msg[0, QLEN : QLEN + 16, :] = jnp.full((16, ul.shape[1]), count, i32).astype(f32).astype(bf16)


def mid_fwd(lens, att, tok, wo, bo, g1, b1, wu, bu, wd, bd, g2, b2, wp):
    rows, width = att.shape
    ff, out = wu.shape[1], wp.shape[1]
    ins = [lens, att, tok, wo, bo, g1, b1, wu, bu, wd, bd, g2, b2, wp]
    outs = [
        struct((width, rows), bf16),
        struct((rows, ff), bf16),
        struct((rows, ff), bf16),
        struct((rows, width), bf16),
        struct((rows, 1), f32),
        struct((rows, width), bf16),
        struct((rows, 1), f32),
        struct((rows, width), bf16),
        struct((rows, out), f32),
        struct((rows, out), bf16),
        struct((1, QLEN + 16, out), bf16),
    ]
    return pl.pallas_call(
        mid_fwd_kernel,
        in_specs=[SMEM] + [VMEM] * (len(ins) - 1),
        out_specs=[VMEM] * len(outs),
        out_shape=outs,
        scratch_shapes=[
            pltpu.VMEM((rows, width), f32),
            pltpu.VMEM((rows, width), bf16),
            pltpu.VMEM((rows, width), f32),
            pltpu.VMEM((1, ff), f32),
        ],
        compiler_params=params(56),
        cost_estimate=cost(20e9, 40e6),
        name="middle_forward",
    )(*ins)


def relative(device, n):
    bits = n.bit_length() - 1
    at = jnp.zeros((), i32)
    for b in range(bits):
        at = at | (((device >> b) & 1) << (bits - 1 - b))
    return at


def loss_kernel(me, lens, owner, gathered, ul, msg, dpb):
    n, nump = owner.shape
    rows = ul.shape[0]
    total = nump * QLEN
    seg = segment_of(segment_ends(lens), lax.broadcasted_iota(i32, (1, rows), 1))
    rel = [relative(owner[me[0], p] ^ me[0], n) for p in range(nump)]
    qs = [gathered[rel[p], 0:QLEN, :] for p in range(nump)]
    q = jnp.concatenate(qs, axis=0)
    slot = lax.broadcasted_iota(i32, (QLEN, 1), 0).astype(f32)
    valid = jnp.concatenate(
        [
            (slot < gathered[rel[p], QLEN : QLEN + 16, :][0:1, 0:1].astype(f32)).astype(f32)
            for p in range(nump)
        ],
        axis=0,
    )
    group = lax.broadcasted_iota(i32, (total, rows), 0) // QLEN + 1
    x = jnp.where(group == seg, nt(q, ul[...]) * 10.0, NEG)
    top = jnp.max(x, axis=1, keepdims=True)
    e = jnp.exp(x - top)
    sm = jnp.sum(e, axis=1, keepdims=True)
    soft = valid * (0.1 * (top + jnp.log(sm)))
    lane = lax.broadcasted_iota(i32, (1, 128), 1)
    score = jnp.zeros((1, 128), f32)
    for p in range(nump):
        score = score + jnp.where(
            lane == p, jnp.sum(soft[p * QLEN : (p + 1) * QLEN], axis=0, keepdims=True), 0.0
        )
    w = e * (valid / sm)
    wh = w.astype(bf16)
    wl = (w - wh.astype(f32)).astype(bf16)
    msg[0, 0:total, :] = (nn(wh, ul[...]) + nn(wl, ul[...])).astype(bf16)
    hi = score.astype(bf16)
    rest = score - hi.astype(f32)
    mid = rest.astype(bf16)
    lo = (rest - mid.astype(f32)).astype(bf16)
    row = lax.broadcasted_iota(i32, (16, 128), 0)
    tail = jnp.where(row == 0, hi.astype(f32), 0.0)
    tail = tail + jnp.where(row == 1, mid.astype(f32), 0.0)
    tail = tail + jnp.where(row == 2, lo.astype(f32), 0.0)
    msg[0, total : total + 16, :] = tail.astype(bf16)
    dpb[...] = tn(wh, q) + tn(wl, q)


def loss_forward(me, lens, owner, gathered, ul):
    rows, out = ul.shape
    total = owner.shape[1] * QLEN
    smem = pl.BlockSpec(memory_space=pltpu.SMEM)
    vmem = pl.BlockSpec(memory_space=pltpu.VMEM)
    return pl.pallas_call(
        loss_kernel,
        in_specs=[smem] * 3 + [vmem] * 2,
        out_specs=[vmem] * 2,
        out_shape=[struct((1, total + 16, out), bf16), struct((rows, out), f32)],
        compiler_params=params(16),
        cost_estimate=cost(1e9, 2e6),
        name="loss_forward",
    )(me, lens, owner, gathered, ul)


def loss_back_kernel(
    me, lens, owner, place, messages, dpb, emb, nl, n2, i2, g2, wp,
    loss, dr2, dbr, gwp, sums, du, gwpt, inverse,
):
    n, nump = owner.shape
    groups = nump + 1
    rows, width = nl.shape
    total = nump * QLEN
    mine = me[0]

    def note(i, carry):
        for p in range(nump):
            inverse[owner[i, p] * nump + place[i, p]] = i * nump + p
        return carry

    lax.fori_loop(0, n, note, 0)
    group = [mine] + [owner[mine, p] for p in range(nump)]
    plc = [place[mine, p] for p in range(nump)]
    src, col = {}, {}
    for g in range(groups):
        for r in range(nump):
            entry = inverse[group[g] * nump + r]
            src[g, r] = relative(lax.div(entry, nump) ^ mine, n)
            col[g, r] = lax.rem(entry, nump)
    lane = lax.broadcasted_iota(i32, (8, 128), 1)
    sub = lax.broadcasted_iota(i32, (8, 128), 0)
    vals = []
    for r in range(nump):
        a = jnp.zeros((8, 128), f32)
        for g in range(groups):
            t = messages[src[g, r], total : total + 16, :].astype(f32)
            t = t[0:1, :] + t[1:2, :] + t[2:3, :]
            a = jnp.where((sub == g) & (lane == col[g, r]), t, a)
        vals.append(jnp.sum(a, axis=1, keepdims=True))
    top = vals[0]
    for v in vals[1:]:
        top = jnp.maximum(top, v)
    es = [jnp.exp(v - top) for v in vals]
    sm = es[0]
    for e in es[1:]:
        sm = sm + e
    loss[...] = jnp.broadcast_to((top + jnp.log(sm) - vals[0])[0:1], (8, 128))
    dt = [e / sm - (1.0 if r == 0 else 0.0) for r, e in enumerate(es)]
    sub1 = lax.broadcasted_iota(i32, (8, 1), 0)
    place = jnp.zeros((8, 1), i32)
    for p in range(nump):
        place = jnp.where(sub1 == p + 1, plc[p], place)
    dscore = jnp.zeros((8, 1), f32)
    for r in range(nump):
        dscore = jnp.where(place == r, dt[r], dscore)
    dmq = jnp.zeros((QLEN, 128), f32)
    for r in range(nump):
        at = pl.multiple_of(col[0, r] * QLEN, QLEN)
        dmq = dmq + dt[r][0:1] * messages[src[0, r], pl.ds(at, QLEN), :].astype(f32)
    sk = segment_of(segment_ends(lens), lax.broadcasted_iota(i32, (rows, 128), 0))
    scale = jnp.zeros(sk.shape, f32)
    for p in range(nump):
        scale = jnp.where(sk == p + 1, dscore[p + 1 : p + 2], scale)
    du[...] = scale * dpb[...]
    du[0:QLEN, :] = jnp.where(sk[0:QLEN] == 0, dmq, du[0:QLEN, :])

    gwpt[...] = jnp.zeros_like(gwpt)
    sums[...] = jnp.zeros_like(sums)
    tile = 256
    for r0 in range(0, rows, tile):
        r = slice(r0, r0 + tile)
        e = emb[r, :]
        inv = lax.rsqrt(jnp.sum(e * e, axis=-1, keepdims=True) + NORM_EPS)
        unit = e * inv
        d = du[r, :].astype(bf16).astype(f32)
        de = (inv * (d - unit * jnp.sum(unit * d, axis=-1, keepdims=True))).astype(bf16)
        gwpt[...] += tn(de, nl[r, :])
        dn = nt(de, wp[...])
        normal = n2[r, :].astype(f32)
        sums[0:1, :] += jnp.sum(dn * normal, axis=0, keepdims=True)
        sums[1:2, :] += jnp.sum(dn, axis=0, keepdims=True)
        dr = norm_back(dn, row(g2), normal, i2[r, :])
        dr2[r, :] = dr
        db = dr.astype(bf16)
        dbr[r, :] = db
        sums[2:3, :] += jnp.sum(db.astype(f32), axis=0, keepdims=True)
    gwp[...] = gwpt[...].T


def loss_back(me, lens, owner, place, messages, dpb, emb, nl, n2, i2, g2, wp):
    rows, width = nl.shape
    out = wp.shape[1]
    smem = pl.BlockSpec(memory_space=pltpu.SMEM)
    vmem = pl.BlockSpec(memory_space=pltpu.VMEM)
    return pl.pallas_call(
        loss_back_kernel,
        in_specs=[smem] * 4 + [vmem] * 8,
        out_specs=[vmem] * 5,
        out_shape=[
            struct((8, 128), f32),
            struct((rows, width), f32),
            struct((rows, width), bf16),
            struct((width, out), f32),
            struct((8, width), f32),
        ],
        scratch_shapes=[
            pltpu.VMEM((rows, out), f32),
            pltpu.VMEM((out, width), f32),
            pltpu.SMEM((owner.size,), i32),
        ],
        compiler_params=params(32),
        cost_estimate=cost(6e9, 10e6),
        name="loss_backward",
    )(me, lens, owner, place, messages, dpb, emb, nl, n2, i2, g2, wp)


def flip_of(device, dims):
    m = jnp.zeros((), i32)
    for i, d in enumerate(dims[:4]):
        m = m | jnp.where((device & d) != 0, 8 >> i, 0)
    return m


def sides(me, dims, keep, send):
    m = flip_of(me[0], dims)
    half = PIECES // 2
    top, low = lax.div(m, half), lax.rem(m, half)
    return [(keep, top, low), (send, 1 - top, low)]


def down_grad_kernel(dims, me, act, dbr, keep, send):
    pr = keep.shape[1]
    half = PIECES // 2
    for dst, side, low in sides(me, dims, keep, send):
        for t in range(0, half, 2):
            at = pl.multiple_of((side * half + t) * pr, 128)
            g = tn(act[:, pl.ds(at, 2 * pr)], dbr[...])
            dst[t ^ low] = g[:pr]
            dst[(t + 1) ^ low] = g[pr:]


def down_grad(dims, me, act, dbr):
    rows, width = dbr.shape
    buf = struct((PIECES // 2, act.shape[1] // PIECES, width), f32)
    return pl.pallas_call(
        functools.partial(down_grad_kernel, dims),
        in_specs=[SMEM, VMEM, VMEM],
        out_specs=[VMEM] * 2,
        out_shape=[buf, buf],
        compiler_params=params(32),
        cost_estimate=cost(5e9, 17e6),
        name="down_gradient",
    )(me, act, dbr)


def up_grad_kernel(dims, me, dbr, slp, wd, ht, keep, send, din, dsum):
    ff = slp.shape[1]
    pr = keep.shape[1]
    half = PIECES // 2
    chunk = 512

    def step(c, carry):
        at = pl.ds(pl.multiple_of(c * chunk, chunk), chunk)
        d_inner = (nt(dbr[...], wd[at, :]) * slp[:, at].astype(f32)).astype(bf16)
        din[:, at] = d_inner
        dsum[:, at] = jnp.sum(d_inner.astype(f32), axis=0, keepdims=True)
        for dst, side, low in sides(me, dims, keep, send):
            r = pl.ds(pl.multiple_of(side * (half * pr), half * pr), half * pr)
            g = nn(ht[r, :], d_inner)
            for t in range(half):
                dst[t ^ low, :, at] = g[t * pr : (t + 1) * pr]
        return carry

    lax.fori_loop(0, ff // chunk, step, 0)


def up_grad(dims, me, dbr, slp, wd, ht):
    rows, width = dbr.shape
    ff = slp.shape[1]
    buf = struct((PIECES // 2, width // PIECES, ff), f32)
    return pl.pallas_call(
        functools.partial(up_grad_kernel, dims),
        in_specs=[SMEM] + [VMEM] * 4,
        out_specs=[VMEM] * 4,
        out_shape=[buf, buf, struct((rows, ff), bf16), struct((1, ff), f32)],
        compiler_params=params(48),
        cost_estimate=cost(10e9, 30e6),
        name="up_gradient",
    )(me, dbr, slp, wd, ht)


def mid_back_kernel(me, din, wu, dr2, n1, i1, g1, wo, dr1, dpr, dat, sums):
    rows, width = dr2.shape
    sums[...] = jnp.zeros_like(sums)
    tile = 256
    for r0 in range(0, rows, tile):
        r = slice(r0, r0 + tile)
        d = dr2[r, :] + nt(din[r, :], wu[...])
        normal = n1[r, :].astype(f32)
        sums[0:1, :] += jnp.sum(d * normal, axis=0, keepdims=True)
        sums[1:2, :] += jnp.sum(d, axis=0, keepdims=True)
        dr = norm_back(d, row(g1), normal, i1[r, :])
        dr1[r, :] = dr
        low = dr.astype(bf16)
        dpr[r, :] = low
        sums[2:3, :] += jnp.sum(low.astype(f32), axis=0, keepdims=True)
        dat[r, :] = nt(low, wo[...]).astype(bf16)


def mid_back(me, din, wu, dr2, n1, i1, g1, wo):
    rows, width = dr2.shape
    return pl.pallas_call(
        mid_back_kernel,
        in_specs=[SMEM] + [VMEM] * 7,
        out_specs=[VMEM] * 4,
        out_shape=[
            struct((rows, width), f32),
            struct((rows, width), bf16),
            struct((rows, width), bf16),
            struct((8, width), f32),
        ],
        compiler_params=params(40),
        cost_estimate=cost(9e9, 15e6),
        name="middle_backward",
    )(me, din, wu, dr2, n1, i1, g1, wo)


def qkv_grad_kernel(p, dims, me, tok, d0, d1, d2, att, dpr, *rest):
    keep, send = rest[-2:]
    extra = rest[0] if len(rest) == 3 else None
    half = PIECES // 2
    pr = keep.shape[1]
    for dst, side, low in sides(me, dims, keep, send):
        at = pl.ds(pl.multiple_of(side * (half * pr), half * pr), half * pr)
        col = 0
        dpr_own = dpr.at[:, p * 256 : (p + 1) * 256]
        for left, d in ((tok, d0), (tok, d1), (tok, d2), (att, dpr_own)):
            g = tn(left[:, at], d[...])
            for t in range(half):
                dst[t ^ low, :, col : col + 256] = g[t * pr : (t + 1) * pr]
            col += 256
        if extra is not None:
            for t in range(half):
                first = pl.multiple_of((side * half + t) * pr, 16)
                dst[t ^ low, :, col : col + 128] = extra[pl.ds(first, pr), :]


def qkv_grad(p, dims, me, tok, ds, att, dpr, extra):
    rows, width = att.shape
    ins = [me, tok, *ds, att, dpr] + ([] if extra is None else [extra])
    buf = struct((PIECES // 2, width // PIECES, width + 256 + (0 if extra is None else 128)), f32)
    return pl.pallas_call(
        functools.partial(qkv_grad_kernel, p, dims),
        in_specs=[SMEM] + [VMEM] * (len(ins) - 1),
        out_specs=[VMEM] * 2,
        out_shape=[buf, buf],
        compiler_params=params(24),
        cost_estimate=cost(4e9, 8e6),
        name="qkv_gradient",
    )(*ins)


def input_grad_kernel(count, me, *refs):
    ds = refs[:count]
    w, dr1, out = refs[count:]
    tile = 256
    for r0 in range(0, out.shape[0], tile):
        r = slice(r0, r0 + tile)
        acc = dr1[r, :]
        for j, d in enumerate(ds):
            acc = acc + nt(d[r, :], w[:, j * 256 : (j + 1) * 256])
        out[r, :] = acc


def input_grad(me, ds, w, dr1):
    return pl.pallas_call(
        functools.partial(input_grad_kernel, len(ds)),
        in_specs=[SMEM] + [VMEM] * (len(ds) + 2),
        out_specs=VMEM,
        out_shape=struct(dr1.shape, f32),
        compiler_params=params(32),
        cost_estimate=cost(5e9, 15e6),
        name="input_gradient",
    )(me, *ds, w, dr1)


def collect_kernel(s0, s1, s2, dsum, sm1, sm2, out):
    width = out.shape[1]
    for j, s in enumerate((s0, s1, s2)):
        out[0:2, j * 256 : (j + 1) * 256] = s[0:2, :]
    out[2:3, :] = sm1[2:3, :]
    out[3:5, :] = sm1[0:2, :]
    end = 5
    for j in range(dsum.shape[1] // width):
        out[end : end + 1, :] = dsum[:, j * width : (j + 1) * width]
        end += 1
    out[end : end + 1, :] = sm2[2:3, :]
    out[end + 1 : end + 3, :] = sm2[0:2, :]
    out[end + 3 :, :] = jnp.zeros((out.shape[0] - end - 3, width), f32)


def collect(s, dsum, sm1, sm2):
    ins = [*s, dsum, sm1, sm2]
    return pl.pallas_call(
        collect_kernel,
        in_specs=[VMEM] * len(ins),
        out_specs=VMEM,
        out_shape=struct((16, sm1.shape[1]), f32),
        compiler_params=params(16),
        cost_estimate=cost(1e4, 1e5),
        name="collect_vectors",
    )(*ins)


def swap(x, mask, n):
    return lax.ppermute(x, "dp", [(i, i ^ mask) for i in range(n)])


def after(x, *others):
    return lax.optimization_barrier((x,) + others)[0]


def join(x, y):
    which = lax.broadcasted_iota(i32, (2,) + x.shape, 0)
    both = jnp.where(which == 0, x[None], y[None])
    return both.reshape((2 * x.shape[0],) + x.shape[1:])


class Chain:
    def __init__(self, keep, send, dims, n):
        self.keep, self.ready, self.dims, self.n = keep, send, dims, n
        self.at = 0
        self.out = None
        self.recv = None

    def start(self):
        k, dims = self.at, self.dims
        d = dims[k] if k < len(dims) else dims[3 - (k - len(dims))]
        self.recv = swap(self.ready, d, self.n)

    def land(self, *others):
        k, dims = self.at, self.dims
        self.at += 1
        recv = after(self.recv, *others) if others else self.recv
        if k < 4:
            recv = recv.astype(f32)
            half = self.keep.shape[0] // 2
            if k < 3:
                self.ready = (self.keep[half:] + recv[half:]).astype(bf16)
                self.keep = self.keep[:half] + recv[:half]
            else:
                self.ready = (self.keep + recv).astype(bf16)
        elif k < len(dims):
            self.ready = (self.ready.astype(f32) + recv.astype(f32)).astype(bf16)
        elif k == len(dims) + 3:
            self.out = (self.ready, recv)
        else:
            self.ready = join(self.ready, recv)

    def step(self):
        self.start()
        self.land()

    def finish(self):
        while self.out is None:
            self.step()
        return self.out


def sum_all(x, n):
    for b in range(n.bit_length() - 1):
        x = x + swap(x, 1 << b, n)
    return x


def gather_all(x, n):
    for b in reversed(range(n.bit_length() - 1)):
        x = join(x, swap(x, 1 << b, n))
    return x


BATCH = 4


def spread_kernel(dims, cuts, count, me, x, y, *refs):
    outs = refs[-count:]
    low = flip_of(me[0], dims) & (BATCH - 1)
    pr = x.shape[1]

    def put(src):
        for t in range(BATCH):
            col = 0
            for out, cols in zip(outs, cuts):
                out[t * pr : (t + 1) * pr, :] = src[t ^ low, :, col : col + cols].astype(f32)
                col += cols

    j = pl.program_id(0)
    here = PIECES // 2 // BATCH
    pl.when(j < here)(lambda: put(x))
    pl.when(j >= here)(lambda: put(y))


def spread(dims, me, x, y, places, previous, name):
    ins = [me, x, y]
    pr = x.shape[1]
    half = PIECES // 2 // BATCH
    block = (BATCH,) + x.shape[1:]
    specs = [
        pl.BlockSpec(block, lambda j, f: (jnp.minimum(j, half - 1), 0, 0)),
        pl.BlockSpec(block, lambda j, f: (jnp.maximum(j - half, 0), 0, 0)),
    ]
    aliases = {}
    if previous is not None:
        for i, g in enumerate(previous):
            aliases[3 + i] = i
            ins.append(g)
            specs.append(pl.BlockSpec(memory_space=pl.ANY))

    def place(col):
        return lambda j, f: (j ^ lax.div(flip_of(f[0], dims), BATCH), col)

    return pl.pallas_call(
        functools.partial(spread_kernel, dims, [c for c, _, _ in places], len(places)),
        grid_spec=pltpu.PrefetchScalarGridSpec(
            num_scalar_prefetch=1,
            grid=(PIECES // BATCH,),
            in_specs=specs,
            out_specs=[pl.BlockSpec((BATCH * pr, c), place(col)) for c, col, _ in places],
        ),
        out_shape=[struct((PIECES * pr, w), f32) for _, _, w in places],
        input_output_aliases=aliases,
        compiler_params=params(24),
        cost_estimate=cost(1e6, 6 * x.size * 2),
        name=name,
    )(*ins)


def axis_orders(n):
    rest = [1 << i for i in range(1, n.bit_length() - 1)]
    if n == 32:
        x, y, z, far = rest
        return [(1, x, z, y, far), (1, y, x, z, far), (1, z, y, x, far)]
    return [tuple([1] + rest[i:] + rest[:i]) for i in range(PORTIONS)]


def body(
    tokens, seg_lengths, owner, place, w_qkv, b_qv, w_out, b_out, ln1_gain, ln1_bias,
    w_up, b_up, w_down, b_down, ln2_gain, ln2_bias, w_proj,
):
    rows, width = tokens.shape
    ff = w_up.shape[1]
    n = lax.axis_size("dp")
    me = lax.axis_index("dp").astype(i32).reshape(1)
    orders = axis_orders(n)

    packed, attended, lse = attention(seg_lengths, tokens, w_qkv, b_qv)
    ht, act, slp, n1, i1, n2, i2, nl, emb, ul, query = mid_fwd(
        seg_lengths, attended, tokens, w_out, b_out, ln1_gain, ln1_bias, w_up, b_up,
        w_down, b_down, ln2_gain, ln2_bias, w_proj,
    )

    msg, dpb = loss_forward(me, seg_lengths, owner, gather_all(query, n), ul)
    loss, dr2, dbr, gwp, sums2 = loss_back(
        me, seg_lengths, owner, place, gather_all(msg, n), dpb, emb, nl, n2, i2, ln2_gain, w_proj
    )

    down = Chain(*down_grad(orders[0], me, act, dbr), orders[0], n)
    down.start()
    keep, send, din, dsum = up_grad(orders[1], after(me, down.ready), dbr, slp, w_down, ht)
    up = Chain(keep, send, orders[1], n)
    down.land(dsum)
    down.start()
    up.start()
    dr1, dpr, dat, sums1 = mid_back(
        after(me, down.ready, up.ready), din, w_up, dr2, n1, i1, ln1_gain, w_out
    )
    up.land(sums1)
    up.start()
    parts = [
        attention_back(0, after(seg_lengths, up.ready), packed, dat, attended, lse)
    ]
    down.land(parts[0][3])
    down.start()
    parts.append(
        attention_back(1, after(seg_lengths, down.ready), packed, dat, attended, lse)
    )
    down.land(parts[1][3])
    up.land(parts[1][3])
    down.start()
    up.start()
    parts.append(
        attention_back(2, after(seg_lengths, down.ready, up.ready), packed, dat, attended, lse)
    )
    down.land(parts[2][3])
    up.land(parts[2][3])
    down.start()
    up.start()
    held = after(me, down.ready, up.ready)
    vector = collect([x[3] for x in parts], dsum, sums1, sums2)
    more = []
    for p in reversed(range(PORTIONS)):
        keep, send = qkv_grad(
            p, orders[p], held, tokens, [x[p] for x in parts], attended, dpr, gwp if p == 2 else None
        )
        more.append((p, Chain(keep, send, orders[p], n)))
    d_tokens = input_grad(
        after(me, *[c.ready for _, c in more]), [x[p] for p in range(3) for x in parts], w_qkv, dr1
    )
    down.land()
    up.land()

    g_w_down = spread(orders[0], me, *down.finish(), [(width, 0, width)], None, "down_place")[0]
    g_w_up = spread(orders[1], me, *up.finish(), [(ff, 0, ff)], None, "up_place")[0]
    vector = sum_all(vector, n)
    grads = None
    for p, c in more:
        places = [(width, p, 3 * width), (256, p, width)]
        if p == 2:
            places.append((128, 0, 128))
        out = spread(orders[p], me, *c.finish(), places, grads, "qkv_place")
        grads = out[:2]
        if p == 2:
            g_w_proj = out[2]
    g_w_qkv, g_w_out = grads
    at = 5 + ff // width
    return (
        loss[0, 0:1], d_tokens, g_w_qkv, vector[0:2].reshape(-1), g_w_out, vector[2], vector[3],
        vector[4], g_w_up, vector[5:at].reshape(-1), g_w_down, vector[at], vector[at + 1],
        vector[at + 2], g_w_proj,
    )


def solution(mesh):
    whole_rows = P("dp", None)
    return jax.shard_map(
        body,
        mesh=mesh,
        in_specs=(whole_rows, whole_rows) + (P(),) * 15,
        out_specs=(P("dp"), whole_rows) + (P(),) * 13,
        check_vma=False,
    )
```

time: 1110 us -> 422 us (0.38)
  waiting for transfers between devices: 425 us -> 134 us
  matrix products: 282 us -> 0 us
  blocking collectives: 164 us -> 0 us
  Pallas kernels: 0 us -> 163 us
  other arithmetic: 107 us -> 20.4 us
  local copies, waits for them, and re-layouts: 112 us -> 31 us
  starting transfers between devices: 0.08 us -> 66.8 us
  between operations: 16.2 us -> 1.71 us
    psum x1 -> x0, waiting for transfers between devices: 380 us -> none  [body(): lax.psum((g_w_qkv, g_b_qv, g_w_out, g_b_out, g_ln1_gain, g_ln1_bias, g_w_...]
    dot_general x31 -> x0, matrix products: 282 us -> none  [the longest x1 48.7 us: body(): inner = jnp.dot(hidden_low, w_up, preferred_element_type=jnp.float32) + b_up]
    pallas_call x0 -> x20, Pallas kernels: none -> 163 us  [the longest x3 34.5 us: attention_back(): pl.pallas_call(functools.partial(attn_bwd_kernel, part), in_specs=[SMEM]...]
    ppermute x0 -> x60, waiting for transfers between devices: none -> 134 us  [swap(): return lax.ppermute(x, 'dp', [(i, i ^ mask) for i in range(n)])]
    unnamed x2 -> x0, blocking collectives: 79.1 us -> none
    ppermute x0 -> x60, starting transfers between devices: none -> 66.8 us  [swap(): return lax.ppermute(x, 'dp', [(i, i ^ mask) for i in range(n)])]
    all_gather x1 -> x0, waiting for transfers between devices: 44.8 us -> none  [body(): lax.all_gather(d_query_for.reshape(passages_per, QLEN * out_width).astype...]
    all_gather x1 -> x0, blocking collectives: 43.8 us -> none  [body(): lax.all_gather(my_query[None], 'dp', axis=0, tiled=True)]
  transfers between devices with their start and end apart: 2 -> 60, of which waited for: 2 -> 29; matrix products, arithmetic and copies ran while one was open for 3% -> 5% of each run, Pallas kernels for 0% -> 24%
where the time goes in v1:
time: 422 us; the launch traced here: 417 us
  Pallas kernels  163 us (39%)
  waiting for transfers between devices  134 us (32%)
  starting transfers between devices  66.8 us (16%)
  local copies, waits for them, and re-layouts  31 us (7%)
  other arithmetic  20.4 us (5%)
    ppermute x60, waiting for transfers between devices, swap(): return lax.ppermute(x, 'dp', [(i, i ^ mask) for i in range(n)])  134 us
    ppermute x60, starting transfers between devices, swap(): return lax.ppermute(x, 'dp', [(i, i ^ mask) for i in range(n)])  66.8 us
    pallas_call x3, Pallas kernels, attention_back(): pl.pallas_call(functools.partial(attn_bwd_kernel, part), in_specs=[SMEM]...  34.5 us
    pallas_call x1, Pallas kernels, mid_fwd(): pl.pallas_call(mid_fwd_kernel, in_specs=[SMEM] + [VMEM] * (len(ins) - 1),...  28.8 us
    unnamed x100, local copies, waits for them, and re-layouts  28 us
    pallas_call x5, Pallas kernels, spread(): pl.pallas_call(functools.partial(spread_kernel, dims, [c for c, _, _ in p...  25.7 us
    pallas_call x1, Pallas kernels, up_grad(): pl.pallas_call(functools.partial(up_grad_kernel, dims), in_specs=[SMEM] +...  21.3 us
    pallas_call x1, Pallas kernels, attention(): pl.pallas_call(attn_fwd_kernel, in_specs=[SMEM, VMEM, VMEM, VMEM], out_sp...  15.1 us
  transfers between devices with their start and end apart: 60, of which 29 were waited for; matrix products, arithmetic and copies ran while one was open for 5% of the time, Pallas kernels for 24%

profile of v1, /device:TPU:0, one launch (start us, length us, event | category | flops | bytes accessed | tf_op | source)
XLA Modules:
  0.0 417.2 jit_solution(2753310210665408215)
XLA Ops:
  0.7 2.0 copy-done
  5.4 15.1 %attention_forward.1 = (bf16[1024,2304]{1,0:T(8,128)(2,1)S(1)}, bf16[1024,768]{1,0:T(8,128)(2,1)S(1)}, f32[6,8,256]{2,1,0:T(8,128)S(1)}) custom-call(s32[1,6]{1,0:T(1,128)S(1)} %copy-done.9, bf16[1024,768]{1,0:T(8,128)(2,1)S(1)} %copy-done.2, bf16[768,2304]{1,0:T(8,128)(2,1)S(1)} %copy-done, f32[1536]{0:T(1024)S(1)} %copy-done.6), custom_call_target="tpu_custom_call" | custom-call | flops 16000000000 | bytes 6291456 | tf_op jit(solution)/shard_map/attention_forward/pallas_call | solution.py:237
  21.7 2.2 copy-done.39
  23.9 28.8 %middle_forward.1 = (bf16[768,1024]{1,0:T(8,128)(2,1)}, bf16[1024,3072]{1,0:T(8,128)(2,1)}, bf16[1024,3072]{1,0:T(8,128)(2,1)}, bf16[1024,768]{1,0:T(8,128)(2,1)...) custom-call(s32[1,6]{1,0:T(1,128)} %lens.10, ...), custom_call_target="tpu_custom_call" | custom-call | flops 20000000000 | bytes 40000000 | tf_op jit(solution)/shard_map/middle_forward/pallas_call | solution.py:363
  52.7 4.4 %collective-permute-start = (bf16[1,48,128]{2,1,0:T(8,128)(2,1)}, bf16[1,48,128]{2,1,0:T(8,128)(2,1)S(1)}, u32[]{:S(2)}, u32[]{:S(2)}) collective-permute-start(bf16[1,48,128]{2,1,0:T(8,128)(2,1)} %get-tuple-element.86), channel_id=1, source_target_pairs={{0,16},{1,17},{2,18},{3,19},{4,20},{5,21},{6,22},{7,23},{8,24},{9,... | collective-permute-start | bytes 36872 | tf_op jit(solution)/shard_map/ppermute | solution.py:758
  57.1 1.9 collective-permute-done
  59.8 1.9 collective-permute-start.1
  61.8 1.8 collective-permute-done.1
  63.7 1.8 collective-permute-start.2
  65.7 2.1 collective-permute-done.2
  67.9 2.5 collective-permute-start.3
  70.5 2.4 collective-permute-done.3
  74.7 1.9 loss_forward.1
  76.6 2.6 collective-permute-start.5
  79.2 3.4 collective-permute-done.5
  83.3 4.0 collective-permute-done.6
  88.4 4.5 %collective-permute-done.7 = bf16[4,176,128]{2,1,0:T(8,128)(2,1)S(1)} collective-permute-done((bf16[4,176,128]{2,1,0:T(8,128)(2,1)S(1)}, bf16[4,176,128]{2,1,0:T(8,128)(2,1)S(1)}, u32[]{:S(2)}, u32[]{:S(2)}) %collective-permute-start.7) | collective-permute-done | bytes 180256 | tf_op jit(solution)/shard_map/ppermute | solution.py:758
  93.0 1.7 collective-permute-start.8
  94.8 5.8 %collective-permute-done.8 = bf16[8,176,128]{2,1,0:T(8,128)(2,1)S(1)} collective-permute-done((bf16[8,176,128]{2,1,0:T(8,128)(2,1)S(1)}, bf16[8,176,128]{2,1,0:T(8,128)(2,1)S(1)}, u32[]{:S(2)}, u32[]{:S(2)}) %collective-permute-start.8) | collective-permute-done | bytes 360480 | tf_op jit(solution)/shard_map/ppermute | solution.py:758
  100.9 2.1 collective-permute-done.9
  107.2 4.7 %loss_backward.1 = (f32[8,128]{1,0:T(8,128)S(1)}, f32[1024,768]{1,0:T(8,128)S(1)}, bf16[1024,768]{1,0:T(8,128)(2,1)S(1)}, f32[768,128]{1,0:T(8,128)S(1)}, f32[8,768]{1,0:T(8,128)S(1)}) custom-call(s32[1]{0:T(128)} %bitcast.me, s32[1,6]{1,0:T(1,128)S(1)} %copy-done.10, s32[32,5]{1,0:T(8,128)S(1)} %copy.37.owner, s32[32,5]{1,0:T(8,128)S(1)} %copy.38.place, ...), custom_call_target="tpu_custom_call" | custom-call | flops 6000000000 | bytes 10000000 | tf_op jit(solution)/shard_map/loss_backward/pallas_call | solution.py:537
  112.0 5.6 %down_gradient.1 = (f32[8,192,768]{2,1,0:T(8,128)S(1)}, f32[8,192,768]{2,1,0:T(8,128)S(1)}) custom-call(s32[1]{0:T(128)} %bitcast.me, bf16[1024,3072]{1,0:T(8,128)(2,1)S(1)} %bitcast.90, bf16[1024,768]{1,0:T(8,128)(2,1)S(1)} %get-tuple-element.96.dbr), custom_call_target="tpu_custom_call" | custom-call | flops 5000000000 | bytes 17000000 | tf_op jit(solution)/shard_map/down_gradient/pallas_call | solution.py:587
  117.8 21.3 %up_gradient.1 = (f32[8,48,3072]{2,1,0:T(8,128)}, f32[8,48,3072]{2,1,0:T(8,128)}, bf16[1024,3072]{1,0:T(8,128)(2,1)}, f32[1,3072]{1,0:T(1,128)S(1)}) custom-call(s32[1]{0:T(128)} %bitcast.me, bf16[1024,768]{1,0:T(8,128)(2,1)S(1)} %get-tuple-element.96.dbr, bf16[1024,3072]{1,0:T(8,128)(2,1)} %get-tuple-element.100.slp, bf16[3072,768]{1,0:T(8,128)(2,1)} %wd.3, ...), custom_call_target="tpu_custom_call" | custom-call | flops 10000000000 | bytes 30000000 | tf_op jit(solution)/shard_map/up_gradient/pallas_call | solution.py:623
  139.4 3.0 slice_add_fusion.1
  144.2 14.3 %middle_backward.1 = (f32[1024,768]{1,0:T(8,128)S(1)}, bf16[1024,768]{1,0:T(8,128)(2,1)S(1)}, bf16[1024,768]{1,0:T(8,128)(2,1)S(1)}, f32[8,768]{1,0:T(8,128)S(1)}) custom-call(s32[1]{0:T(128)} %bitcast.me, bf16[1024,3072]{1,0:T(8,128)(2,1)} %get-tuple-element.107.din, bf16[768,3072]{1,0:T(8,128)(2,1)} %wu.3, f32[1024,768]{1,0:T(8,128)S(1)} %copy-done.35, ...), custom_call_target="tpu_custom_call" | custom-call | flops 8999999488 | bytes 15000000 | tf_op jit(solution)/shard_map/middle_backward/pallas_call | solution.py:654
  158.6 5.6 %slice_add_fusion = (f32[4,48,3072]{2,1,0:T(8,128)S(1)}, bf16[4,48,3072]{2,1,0:T(8,128)(2,1)S(1)}) fusion(f32[8,48,3072]{2,1,0:T(8,128)} %collective-permute-done.12, f32[8,48,3072]{2,1,0:T(8,128)} %get-tuple-element.104), kind=kLoop, calls=%fused_computation.2 | loop fusion | flops 1769472 | bytes 12976128 | tf_op jit(solution)/shard_map/add | solution.py:792
  165.1 2.3 copy-done.40
  167.4 11.4 %attention_backward.3 = (bf16[1024,256]{1,0:T(8,128)(2,1)S(1)}, bf16[1024,256]{1,0:T(8,128)(2,1)S(1)}, bf16[1024,256]{1,0:T(8,128)(2,1)S(1)}, f32[8,256]{1,0:T(8,128)S(1)}) custom-call(s32[1,6]{1,0:T(1,128)S(1)} %copy-done.10, bf16[1024,2304]{1,0:T(8,128)(2,1)S(1)} %copy-done.40, bf16[1024,768]{1,0:T(8,128)(2,1)S(1)} %get-tuple-element.115.do, ...), custom_call_target="tpu_custom_call" | custom-call | flops 10000000000 | bytes 4194304 | tf_op jit(solution)/shard_map/attention_backward/pallas_call | solution.py:258
  178.9 2.0 convert_element_type.152
  182.4 11.5 %attention_backward.4 = (bf16[1024,256]{1,0:T(8,128)(2,1)S(1)}, bf16[1024,256]{1,0:T(8,128)(2,1)S(1)}, bf16[1024,256]{1,0:T(8,128)(2,1)S(1)}, f32[8,256]{1,0:T(8,128)S(1)}) custom-call(s32[1,6]{1,0:T(1,128)S(1)} %copy-done.10, bf16[1024,2304]{1,0:T(8,128)(2,1)S(1)} %copy-done.40, bf16[1024,768]{1,0:T(8,128)(2,1)S(1)} %get-tuple-element.115.do, ...), custom_call_target="tpu_custom_call" | custom-call | flops 10000000000 | bytes 4194304 | tf_op jit(solution)/shard_map/attention_backward/pallas_call | solution.py:258
  197.6 11.7 %attention_backward.5 = (bf16[1024,256]{1,0:T(8,128)(2,1)S(1)}, bf16[1024,256]{1,0:T(8,128)(2,1)S(1)}, bf16[1024,256]{1,0:T(8,128)(2,1)S(1)}, f32[8,256]{1,0:T(8,128)S(1)}) custom-call(s32[1,6]{1,0:T(1,128)S(1)} %copy-done.10, bf16[1024,2304]{1,0:T(8,128)(2,1)S(1)} %copy-done.40, bf16[1024,768]{1,0:T(8,128)(2,1)S(1)} %get-tuple-element.115.do, ...), custom_call_target="tpu_custom_call" | custom-call | flops 10000000000 | bytes 4194304 | tf_op jit(solution)/shard_map/attention_backward/pallas_call | solution.py:258
  210.5 3.3 collective-permute-start.55
  213.9 6.0 %collective-permute-done.49 = bf16[1,48,3072]{2,1,0:T(8,128)(2,1)S(1)} collective-permute-done((bf16[1,48,3072]{2,1,0:T(8,128)(2,1)S(1)}, bf16[1,48,3072]{2,1,0:T(8,128)(2,1)S(1)}, u32[]{:S(2)}, u32[]{:S(2)}) %collective-permute-start.49) | collective-permute-done | bytes 294944 | tf_op jit(solution)/shard_map/ppermute | solution.py:758
  219.9 2.6 collective-permute-start.50
  222.6 2.0 qkv_gradient.5
  224.7 2.0 qkv_gradient.4
  227.2 13.4 %collective-permute-done.50 = bf16[1,48,3072]{2,1,0:T(8,128)(2,1)S(1)} collective-permute-done((bf16[1,48,3072]{2,1,0:T(8,128)(2,1)S(1)}, bf16[1,48,3072]{2,1,0:T(8,128)(2,1)S(1)}, u32[]{:S(2)}, u32[]{:S(2)}) %collective-permute-start.50) | collective-permute-done | bytes 294944 | tf_op jit(solution)/shard_map/ppermute | solution.py:758
  240.8 2.0 qkv_gradient.3
  243.0 6.5 %collective-permute-done.51 = bf16[1,48,3072]{2,1,0:T(8,128)(2,1)S(1)} collective-permute-done((bf16[1,48,3072]{2,1,0:T(8,128)(2,1)S(1)}, bf16[1,48,3072]{2,1,0:T(8,128)(2,1)S(1)}, u32[]{:S(2)}, u32[]{:S(2)}) %collective-permute-start.51) | collective-permute-done | bytes 294944 | tf_op jit(solution)/shard_map/ppermute | solution.py:758
  250.5 6.9 %collective-permute-done.56 = bf16[1,192,768]{2,1,0:T(8,128)(2,1)S(1)} collective-permute-done((bf16[1,192,768]{2,1,0:T(8,128)(2,1)S(1)}, bf16[1,192,768]{2,1,0:T(8,128)(2,1)S(1)}, u32[]{:S(2)}, u32[]{:S(2)}) %collective-permute-start.56) | collective-permute-done | bytes 294944 | tf_op jit(solution)/shard_map/ppermute | solution.py:758
  259.3 11.6 %collective-permute-done.52 = bf16[2,48,3072]{2,1,0:T(8,128)(2,1)S(1)} collective-permute-done((bf16[2,48,3072]{2,1,0:T(8,128)(2,1)S(1)}, bf16[2,48,3072]{2,1,0:T(8,128)(2,1)S(1)}, u32[]{:S(2)}, u32[]{:S(2)}) %collective-permute-start.52) | collective-permute-done | bytes 589856 | tf_op jit(solution)/shard_map/ppermute | solution.py:758
  277.3 28.1 %collective-permute-done.18 = bf16[4,48,1024]{2,1,0:T(8,128)(2,1)S(1)} collective-permute-done((bf16[4,48,1024]{2,1,0:T(8,128)(2,1)S(1)}, bf16[4,48,1024]{2,1,0:T(8,128)(2,1)S(1)}, u32[]{:S(2)}, u32[]{:S(2)}) %collective-permute-start.18) | collective-permute-done | bytes 393248 | tf_op jit(solution)/shard_map/ppermute | solution.py:758
  306.8 2.1 collective-permute-start.28
  308.9 3.5 collective-permute-done.19
  317.2 3.8 collective-permute-start.21
  322.0 2.2 collective-permute-start.30
  324.7 1.8 bitcast_select_fusion.1.x
  328.3 1.7 collective-permute-start.22
  330.0 5.4 %collective-permute-done.39 = bf16[1,48,1152]{2,1,0:T(8,128)(2,1)S(1)} collective-permute-done((bf16[1,48,1152]{2,1,0:T(8,128)(2,1)S(1)}, bf16[1,48,1152]{2,1,0:T(8,128)(2,1)S(1)}, u32[]{:S(2)}, u32[]{:S(2)}) %collective-permute-start.39) | collective-permute-done | bytes 110624 | tf_op jit(solution)/shard_map/ppermute | solution.py:758
  336.9 3.4 collective-permute-done.40
  343.7 2.6 collective-permute-done.41
  349.5 4.7 %collective-permute-done.23 = bf16[2,48,1024]{2,1,0:T(8,128)(2,1)S(1)} collective-permute-done((bf16[2,48,1024]{2,1,0:T(8,128)(2,1)S(1)}, bf16[2,48,1024]{2,1,0:T(8,128)(2,1)S(1)}, u32[]{:S(2)}, u32[]{:S(2)}) %collective-permute-start.23) | collective-permute-done | bytes 196640 | tf_op jit(solution)/shard_map/ppermute | solution.py:758
  356.9 2.9 collective-permute-done.42
  360.3 3.6 collective-permute-done.47
  363.9 2.4 collective-permute-start.48
  367.9 2.1 collective-permute-done.48
  372.5 2.0 copy-done.1
  374.5 1.9 copy-done.12
  385.8 5.5 %input_gradient.1 = f32[1024,768]{1,0:T(8,128)} custom-call(s32[1]{0:T(128)} %bitcast.me, bf16[1024,256]{1,0:T(8,128)(2,1)S(1)} %copy-done.14, bf16[1024,256]{1,0:T(8,128)(2,1)S(1)} %copy-done.20, bf16[1024,256]{1,0:T(8,128)(2,1)S(1)} %copy-done.26, bf16[1024,256]{1,0:T(8,128)(2,1)S(1)} %copy-done.16, bf16[1024,256]{1,0:T(8,128)(2,1)S(1)} %copy-done.22, ...), custom_call_target="tpu_custom_call" | custom-call | flops 5000000000 | bytes 15000000 | tf_op jit(solution)/shard_map/input_gradient/pallas_call | solution.py:718
  391.3 4.1 qkv_place.3
  395.4 4.1 qkv_place.4
  399.5 4.1 qkv_place.5
  403.6 6.9 %up_place.1 = f32[768,3072]{1,0:T(8,128)} custom-call(s32[1]{0:T(128)} %bitcast.me, bf16[8,48,3072]{2,1,0:T(8,128)(2,1)} %bitcast_select_fusion.1.x, bf16[8,48,3072]{2,1,0:T(8,128)(2,1)} %collective-permute-done.54.y), custom_call_target="tpu_custom_call" | custom-call | flops 1000000 | bytes 14155776 | tf_op jit(solution)/shard_map/up_place/pallas_call | solution.py:864
  410.5 6.5 %down_place.1 = f32[3072,768]{1,0:T(8,128)} custom-call(s32[1]{0:T(128)} %bitcast.me, bf16[8,192,768]{2,1,0:T(8,128)(2,1)S(1)} %bitcast_select_fusion.x, bf16[8,192,768]{2,1,0:T(8,128)(2,1)} %collective-permute-done.59.y), custom_call_target="tpu_custom_call" | custom-call | flops 1000000 | bytes 14155776 | tf_op jit(solution)/shard_map/down_place/pallas_call | solution.py:864
  (254 shorter events, 67.4 us)
Async XLA Ops:
  23.9 49.4 %copy-start.45 = (s32[32,5]{0,1:T(8,128)S(1)}, s32[32,5]{0,1:T(8,128)}, u32[]{:S(2)}) copy-start(s32[32,5]{0,1:T(8,128)} %param.19) | copy-start | bytes 1924
  52.7 6.3 %collective-permute-start = (bf16[1,48,128]{2,1,0:T(8,128)(2,1)}, bf16[1,48,128]{2,1,0:T(8,128)(2,1)S(1)}, u32[]{:S(2)}, u32[]{:S(2)}) collective-permute-start(bf16[1,48,128]{2,1,0:T(8,128)(2,1)} %get-tuple-element.86), channel_id=1, source_target_pairs={{0,16},{1,17},{2,18},{3,19},{4,20},{5,21},{6,22},{7,23},{8,24},{9,... | collective-permute-start | bytes 36872 | tf_op jit(solution)/shard_map/ppermute | solution.py:758
  59.8 3.8 collective-permute-start.1
  63.7 4.1 collective-permute-start.2
  67.9 5.1 %collective-permute-start.3 = (bf16[8,48,128]{2,1,0:T(8,128)(2,1)S(1)}, bf16[8,48,128]{2,1,0:T(8,128)(2,1)S(1)}, u32[]{:S(2)}, u32[]{:S(2)}) collective-permute-start(bf16[8,48,128]{2,1,0:T(8,128)(2,1)S(1)} %bitcast_select_fusion.16), channel_id=1, source_target_pairs={{0,2},{1,3},{2,0},{3,1},{4,6},{5,7},{6,4},{7,5},{8,10},{9,11},{10,... | collective-permute-start | bytes 294920 | tf_op jit(solution)/shard_map/ppermute | solution.py:758
  73.0 1.5 collective-permute-start.4
  76.6 6.0 %collective-permute-start.5 = (bf16[1,176,128]{2,1,0:T(8,128)(2,1)S(1)}, bf16[1,176,128]{2,1,0:T(8,128)(2,1)S(1)}, u32[]{:S(2)}, u32[]{:S(2)}) collective-permute-start(bf16[1,176,128]{2,1,0:T(8,128)(2,1)S(1)} %get-tuple-element.88), channel_id=1, source_target_pairs={{0,16},{1,17},{2,18},{3,19},{4,20},{5,21},{6,22},{7,23},{8,24},{9,... | collective-permute-start | bytes 135176 | tf_op jit(solution)/shard_map/ppermute | solution.py:758
  82.7 4.6 %collective-permute-start.6 = (bf16[2,176,128]{2,1,0:T(8,128)(2,1)S(1)}, bf16[2,176,128]{2,1,0:T(8,128)(2,1)S(1)}, u32[]{:S(2)}, u32[]{:S(2)}) collective-permute-start(bf16[2,176,128]{2,1,0:T(8,128)(2,1)S(1)} %broadcast_select_fusion.5), channel_id=1, source_target_pairs={{0,8},{1,9},{2,10},{3,11},{4,12},{5,13},{6,14},{7,15},{8,0},{9,1},... | collective-permute-start | bytes 270344 | tf_op jit(solution)/shard_map/ppermute | solution.py:758
  87.4 5.6 %collective-permute-start.7 = (bf16[4,176,128]{2,1,0:T(8,128)(2,1)S(1)}, bf16[4,176,128]{2,1,0:T(8,128)(2,1)S(1)}, u32[]{:S(2)}, u32[]{:S(2)}) collective-permute-start(bf16[4,176,128]{2,1,0:T(8,128)(2,1)S(1)} %bitcast_select_fusion.15), channel_id=1, source_target_pairs={{0,4},{1,5},{2,6},{3,7},{4,0},{5,1},{6,2},{7,3},{8,12},{9,13},{10,... | collective-permute-start | bytes 540680 | tf_op jit(solution)/shard_map/ppermute | solution.py:758
  93.0 7.5 %collective-permute-start.8 = (bf16[8,176,128]{2,1,0:T(8,128)(2,1)S(1)}, bf16[8,176,128]{2,1,0:T(8,128)(2,1)S(1)}, u32[]{:S(2)}, u32[]{:S(2)}) collective-permute-start(bf16[8,176,128]{2,1,0:T(8,128)(2,1)S(1)} %bitcast_select_fusion.13), channel_id=1, source_target_pairs={{0,2},{1,3},{2,0},{3,1},{4,6},{5,7},{6,4},{7,5},{8,10},{9,11},{10,... | collective-permute-start | bytes 1081352 | tf_op jit(solution)/shard_map/ppermute | solution.py:758
  100.7 2.3 collective-permute-start.9
  117.6 21.8 %collective-permute-start.10 = (f32[8,192,768]{2,1,0:T(8,128)S(1)}, f32[8,192,768]{2,1,0:T(8,128)}, u32[]{:S(2)}, u32[]{:S(2)}) collective-permute-start(f32[8,192,768]{2,1,0:T(8,128)S(1)} %get-tuple-element.98), channel_id=1, source_target_pairs={{0,1},{1,0},{2,3},{3,2},{4,5},{5,4},{6,7},{7,6},{8,9},{9,8},{10,11... | collective-permute-start | bytes 14155784 | tf_op jit(solution)/shard_map/ppermute | solution.py:758
  139.0 19.5 %collective-permute-start.12 = (f32[8,48,3072]{2,1,0:T(8,128)}, f32[8,48,3072]{2,1,0:T(8,128)}, u32[]{:S(2)}, u32[]{:S(2)}) collective-permute-start(f32[8,48,3072]{2,1,0:T(8,128)} %get-tuple-element.105), channel_id=1, source_target_pairs={{0,1},{1,0},{2,3},{3,2},{4,5},{5,4},{6,7},{7,6},{8,9},{9,8},{10,11... | collective-permute-start | bytes 14155784 | tf_op jit(solution)/shard_map/ppermute | solution.py:758
  142.5 36.4 %collective-permute-start.11 = (bf16[4,192,768]{2,1,0:T(8,128)(2,1)S(1)}, bf16[4,192,768]{2,1,0:T(8,128)(2,1)}, u32[]{:S(2)}, u32[]{:S(2)}) collective-permute-start(bf16[4,192,768]{2,1,0:T(8,128)(2,1)S(1)} %get-tuple-element.164), channel_id=1, source_target_pairs={{0,2},{1,3},{2,0},{3,1},{4,6},{5,7},{6,4},{7,5},{8,10},{9,11},{10,... | collective-permute-start | bytes 3538952 | tf_op jit(solution)/shard_map/ppermute | solution.py:758
  164.2 29.7 %collective-permute-start.15 = (bf16[4,48,3072]{2,1,0:T(8,128)(2,1)S(1)}, bf16[4,48,3072]{2,1,0:T(8,128)(2,1)S(1)}, u32[]{:S(2)}, u32[]{:S(2)}) collective-permute-start(bf16[4,48,3072]{2,1,0:T(8,128)(2,1)S(1)} %get-tuple-element.162), channel_id=1, source_target_pairs={{0,4},{1,5},{2,6},{3,7},{4,0},{5,1},{6,2},{7,3},{8,12},{9,13},{10,... | collective-permute-start | bytes 3538952 | tf_op jit(solution)/shard_map/ppermute | solution.py:758
  178.8 45.8 %copy-start.15 = (bf16[1024,256]{1,0:T(8,128)(2,1)}, bf16[1024,256]{1,0:T(8,128)(2,1)S(1)}, u32[]{:S(2)}) copy-start(bf16[1024,256]{1,0:T(8,128)(2,1)S(1)} %get-tuple-element.134.d0.refs_3_) | copy-start | bytes 1572868
  178.8 62.0 %copy-start.17 = (bf16[1024,256]{1,0:T(8,128)(2,1)}, bf16[1024,256]{1,0:T(8,128)(2,1)S(1)}, u32[]{:S(2)}) copy-start(bf16[1024,256]{1,0:T(8,128)(2,1)S(1)} %get-tuple-element.128.d0.refs_6_) | copy-start | bytes 1572868
  181.2 14.9 %collective-permute-start.13 = (bf16[2,192,768]{2,1,0:T(8,128)(2,1)S(1)}, bf16[2,192,768]{2,1,0:T(8,128)(2,1)S(1)}, u32[]{:S(2)}, u32[]{:S(2)}) collective-permute-start(bf16[2,192,768]{2,1,0:T(8,128)(2,1)S(1)} %get-tuple-element.168), channel_id=1, source_target_pairs={{0,8},{1,9},{2,10},{3,11},{4,12},{5,13},{6,14},{7,15},{8,0},{9,1},... | collective-permute-start | bytes 1769480 | tf_op jit(solution)/shard_map/ppermute | solution.py:758
  193.9 47.0 %copy-start.23 = (bf16[1024,256]{1,0:T(8,128)(2,1)}, bf16[1024,256]{1,0:T(8,128)(2,1)S(1)}, u32[]{:S(2)}) copy-start(bf16[1024,256]{1,0:T(8,128)(2,1)S(1)} %get-tuple-element.129.d1.refs_7_) | copy-start | bytes 1572868
  194.4 14.8 %collective-permute-start.16 = (bf16[2,48,3072]{2,1,0:T(8,128)(2,1)S(1)}, bf16[2,48,3072]{2,1,0:T(8,128)(2,1)S(1)}, u32[]{:S(2)}, u32[]{:S(2)}) collective-permute-start(bf16[2,48,3072]{2,1,0:T(8,128)(2,1)S(1)} %get-tuple-element.166), channel_id=1, source_target_pairs={{0,2},{1,3},{2,0},{3,1},{4,6},{5,7},{6,4},{7,5},{8,10},{9,11},{10,... | collective-permute-start | bytes 1769480 | tf_op jit(solution)/shard_map/ppermute | solution.py:758
  196.3 14.2 %collective-permute-start.14 = (bf16[1,192,768]{2,1,0:T(8,128)(2,1)S(1)}, bf16[1,192,768]{2,1,0:T(8,128)(2,1)S(1)}, u32[]{:S(2)}, u32[]{:S(2)}) collective-permute-start(bf16[1,192,768]{2,1,0:T(8,128)(2,1)S(1)} %fusion.8), channel_id=1, source_target_pairs={{0,4},{1,5},{2,6},{3,7},{4,0},{5,1},{6,2},{7,3},{8,12},{9,13},{10,... | collective-permute-start | bytes 884744 | tf_op jit(solution)/shard_map/ppermute | solution.py:758
  209.4 10.4 %collective-permute-start.49 = (bf16[1,48,3072]{2,1,0:T(8,128)(2,1)S(1)}, bf16[1,48,3072]{2,1,0:T(8,128)(2,1)S(1)}, u32[]{:S(2)}, u32[]{:S(2)}) collective-permute-start(bf16[1,48,3072]{2,1,0:T(8,128)(2,1)S(1)} %fusion.7), channel_id=1, source_target_pairs={{0,8},{1,9},{2,10},{3,11},{4,12},{5,13},{6,14},{7,15},{8,0},{9,1},... | collective-permute-start | bytes 884744 | tf_op jit(solution)/shard_map/ppermute | solution.py:758
  210.4 48.5 %collective-permute-start.44 = (f32[16,768]{1,0:T(8,128)S(1)}, f32[16,768]{1,0:T(8,128)S(1)}, u32[]{:S(2)}, u32[]{:S(2)}) collective-permute-start(f32[16,768]{1,0:T(8,128)S(1)} %collect_vectors.1), channel_id=1, source_target_pairs={{0,1},{1,0},{2,3},{3,2},{4,5},{5,4},{6,7},{7,6},{8,9},{9,8},{10,11... | collective-permute-start | bytes 147464 | tf_op jit(solution)/shard_map/ppermute | solution.py:758
  210.5 32.3 %collective-permute-start.55 = (bf16[1,192,768]{2,1,0:T(8,128)(2,1)S(1)}, bf16[1,192,768]{2,1,0:T(8,128)(2,1)S(1)}, u32[]{:S(2)}, u32[]{:S(2)}) collective-permute-start(bf16[1,192,768]{2,1,0:T(8,128)(2,1)S(1)} %fusion.10), channel_id=1, source_target_pairs={{0,16},{1,17},{2,18},{3,19},{4,20},{5,21},{6,22},{7,23},{8,24},{9,... | collective-permute-start | bytes 884744 | tf_op jit(solution)/shard_map/ppermute | solution.py:758
  219.9 20.6 %collective-permute-start.50 = (bf16[1,48,3072]{2,1,0:T(8,128)(2,1)S(1)}, bf16[1,48,3072]{2,1,0:T(8,128)(2,1)S(1)}, u32[]{:S(2)}, u32[]{:S(2)}) collective-permute-start(bf16[1,48,3072]{2,1,0:T(8,128)(2,1)S(1)} %fusion.6), channel_id=1, source_target_pairs={{0,16},{1,17},{2,18},{3,19},{4,20},{5,21},{6,22},{7,23},{8,24},{9,... | collective-permute-start | bytes 884744 | tf_op jit(solution)/shard_map/ppermute | solution.py:758
  224.5 49.1 %collective-permute-start.17 = (f32[8,48,1024]{2,1,0:T(8,128)S(1)}, f32[8,48,1024]{2,1,0:T(8,128)S(1)}, u32[]{:S(2)}, u32[]{:S(2)}) collective-permute-start(f32[8,48,1024]{2,1,0:T(8,128)S(1)} %get-tuple-element.141), channel_id=1, source_target_pairs={{0,1},{1,0},{2,3},{3,2},{4,5},{5,4},{6,7},{7,6},{8,9},{9,8},{10,11... | collective-permute-start | bytes 4718600 | tf_op jit(solution)/shard_map/ppermute | solution.py:758
  226.6 48.0 %collective-permute-start.26 = (f32[8,48,1024]{2,1,0:T(8,128)S(1)}, f32[8,48,1024]{2,1,0:T(8,128)S(1)}, u32[]{:S(2)}, u32[]{:S(2)}) collective-permute-start(f32[8,48,1024]{2,1,0:T(8,128)S(1)} %get-tuple-element.137), channel_id=1, source_target_pairs={{0,1},{1,0},{2,3},{3,2},{4,5},{5,4},{6,7},{7,6},{8,9},{9,8},{10,11... | collective-permute-start | bytes 4718600 | tf_op jit(solution)/shard_map/ppermute | solution.py:758
  240.6 8.9 %collective-permute-start.51 = (bf16[1,48,3072]{2,1,0:T(8,128)(2,1)S(1)}, bf16[1,48,3072]{2,1,0:T(8,128)(2,1)S(1)}, u32[]{:S(2)}, u32[]{:S(2)}) collective-permute-start(bf16[1,48,3072]{2,1,0:T(8,128)(2,1)S(1)} %add_convert_fusion.3), channel_id=1, source_target_pairs={{0,8},{1,9},{2,10},{3,11},{4,12},{5,13},{6,14},{7,15},{8,0},{9,1},... | collective-permute-start | bytes 884744 | tf_op jit(solution)/shard_map/ppermute | solution.py:758
  242.8 33.3 %collective-permute-start.35 = (f32[8,48,1152]{2,1,0:T(8,128)S(1)}, f32[8,48,1152]{2,1,0:T(8,128)S(1)}, u32[]{:S(2)}, u32[]{:S(2)}) collective-permute-start(f32[8,48,1152]{2,1,0:T(8,128)S(1)} %get-tuple-element.133), channel_id=1, source_target_pairs={{0,1},{1,0},{2,3},{3,2},{4,5},{5,4},{6,7},{7,6},{8,9},{9,8},{10,11... | collective-permute-start | bytes 5308424 | tf_op jit(solution)/shard_map/ppermute | solution.py:758
  249.5 8.0 %collective-permute-start.56 = (bf16[1,192,768]{2,1,0:T(8,128)(2,1)S(1)}, bf16[1,192,768]{2,1,0:T(8,128)(2,1)S(1)}, u32[]{:S(2)}, u32[]{:S(2)}) collective-permute-start(bf16[1,192,768]{2,1,0:T(8,128)(2,1)S(1)} %add_convert_fusion.2), channel_id=1, source_target_pairs={{0,4},{1,5},{2,6},{3,7},{4,0},{5,1},{6,2},{7,3},{8,12},{9,13},{10,... | collective-permute-start | bytes 884744 | tf_op jit(solution)/shard_map/ppermute | solution.py:758
  257.5 13.4 %collective-permute-start.52 = (bf16[2,48,3072]{2,1,0:T(8,128)(2,1)S(1)}, bf16[2,48,3072]{2,1,0:T(8,128)(2,1)S(1)}, u32[]{:S(2)}, u32[]{:S(2)}) collective-permute-start(bf16[2,48,3072]{2,1,0:T(8,128)(2,1)S(1)} %broadcast_select_fusion.1), channel_id=1, source_target_pairs={{0,2},{1,3},{2,0},{3,1},{4,6},{5,7},{6,4},{7,5},{8,10},{9,11},{10,... | collective-permute-start | bytes 1769480 | tf_op jit(solution)/shard_map/ppermute | solution.py:758
  258.8 13.2 %collective-permute-start.57 = (bf16[2,192,768]{2,1,0:T(8,128)(2,1)S(1)}, bf16[2,192,768]{2,1,0:T(8,128)(2,1)S(1)}, u32[]{:S(2)}, u32[]{:S(2)}) collective-permute-start(bf16[2,192,768]{2,1,0:T(8,128)(2,1)S(1)} %broadcast_select_fusion), channel_id=1, source_target_pairs={{0,8},{1,9},{2,10},{3,11},{4,12},{5,13},{6,14},{7,15},{8,0},{9,1},... | collective-permute-start | bytes 1769480 | tf_op jit(solution)/shard_map/ppermute | solution.py:758
  271.0 53.7 %collective-permute-start.53 = (bf16[4,48,3072]{2,1,0:T(8,128)(2,1)S(1)}, bf16[4,48,3072]{2,1,0:T(8,128)(2,1)S(1)}, u32[]{:S(2)}, u32[]{:S(2)}) collective-permute-start(bf16[4,48,3072]{2,1,0:T(8,128)(2,1)S(1)} %bitcast_select_fusion.4), channel_id=1, source_target_pairs={{0,4},{1,5},{2,6},{3,7},{4,0},{5,1},{6,2},{7,3},{8,12},{9,13},{10,... | collective-permute-start | bytes 3538952 | tf_op jit(solution)/shard_map/ppermute | solution.py:758
  272.2 52.1 %collective-permute-start.58 = (bf16[4,192,768]{2,1,0:T(8,128)(2,1)S(1)}, bf16[4,192,768]{2,1,0:T(8,128)(2,1)S(1)}, u32[]{:S(2)}, u32[]{:S(2)}) collective-permute-start(bf16[4,192,768]{2,1,0:T(8,128)(2,1)S(1)} %bitcast_select_fusion.3), channel_id=1, source_target_pairs={{0,2},{1,3},{2,0},{3,1},{4,6},{5,7},{6,4},{7,5},{8,10},{9,11},{10,... | collective-permute-start | bytes 3538952 | tf_op jit(solution)/shard_map/ppermute | solution.py:758
  273.9 31.5 %collective-permute-start.18 = (bf16[4,48,1024]{2,1,0:T(8,128)(2,1)S(1)}, bf16[4,48,1024]{2,1,0:T(8,128)(2,1)S(1)}, u32[]{:S(2)}, u32[]{:S(2)}) collective-permute-start(bf16[4,48,1024]{2,1,0:T(8,128)(2,1)S(1)} %get-tuple-element.174), channel_id=1, source_target_pairs={{0,2},{1,3},{2,0},{3,1},{4,6},{5,7},{6,4},{7,5},{8,10},{9,11},{10,... | collective-permute-start | bytes 1179656 | tf_op jit(solution)/shard_map/ppermute | solution.py:758
  274.9 31.7 %collective-permute-start.27 = (bf16[4,48,1024]{2,1,0:T(8,128)(2,1)S(1)}, bf16[4,48,1024]{2,1,0:T(8,128)(2,1)S(1)}, u32[]{:S(2)}, u32[]{:S(2)}) collective-permute-start(bf16[4,48,1024]{2,1,0:T(8,128)(2,1)S(1)} %get-tuple-element.172), channel_id=1, source_target_pairs={{0,4},{1,5},{2,6},{3,7},{4,0},{5,1},{6,2},{7,3},{8,12},{9,13},{10,... | collective-permute-start | bytes 1179656 | tf_op jit(solution)/shard_map/ppermute | solution.py:758
  276.4 38.9 %collective-permute-start.36 = (bf16[4,48,1152]{2,1,0:T(8,128)(2,1)S(1)}, bf16[4,48,1152]{2,1,0:T(8,128)(2,1)S(1)}, u32[]{:S(2)}, u32[]{:S(2)}) collective-permute-start(bf16[4,48,1152]{2,1,0:T(8,128)(2,1)S(1)} %get-tuple-element.170), channel_id=1, source_target_pairs={{0,8},{1,9},{2,10},{3,11},{4,12},{5,13},{6,14},{7,15},{8,0},{9,1},... | collective-permute-start | bytes 1327112 | tf_op jit(solution)/shard_map/ppermute | solution.py:758
  305.6 6.8 %collective-permute-start.19 = (bf16[2,48,1024]{2,1,0:T(8,128)(2,1)S(1)}, bf16[2,48,1024]{2,1,0:T(8,128)(2,1)S(1)}, u32[]{:S(2)}, u32[]{:S(2)}) collective-permute-start(bf16[2,48,1024]{2,1,0:T(8,128)(2,1)S(1)} %get-tuple-element.180), channel_id=1, source_target_pairs={{0,8},{1,9},{2,10},{3,11},{4,12},{5,13},{6,14},{7,15},{8,0},{9,1},... | collective-permute-start | bytes 589832 | tf_op jit(solution)/shard_map/ppermute | solution.py:758
  306.8 6.7 %collective-permute-start.28 = (bf16[2,48,1024]{2,1,0:T(8,128)(2,1)S(1)}, bf16[2,48,1024]{2,1,0:T(8,128)(2,1)S(1)}, u32[]{:S(2)}, u32[]{:S(2)}) collective-permute-start(bf16[2,48,1024]{2,1,0:T(8,128)(2,1)S(1)} %get-tuple-element.178), channel_id=1, source_target_pairs={{0,2},{1,3},{2,0},{3,1},{4,6},{5,7},{6,4},{7,5},{8,10},{9,11},{10,... | collective-permute-start | bytes 589832 | tf_op jit(solution)/shard_map/ppermute | solution.py:758
  312.5 4.7 %collective-permute-start.20 = (bf16[1,48,1024]{2,1,0:T(8,128)(2,1)S(1)}, bf16[1,48,1024]{2,1,0:T(8,128)(2,1)S(1)}, u32[]{:S(2)}, u32[]{:S(2)}) collective-permute-start(bf16[1,48,1024]{2,1,0:T(8,128)(2,1)S(1)} %fusion.20), channel_id=1, source_target_pairs={{0,4},{1,5},{2,6},{3,7},{4,0},{5,1},{6,2},{7,3},{8,12},{9,13},{10,... | collective-permute-start | bytes 294920 | tf_op jit(solution)/shard_map/ppermute | solution.py:758
  313.6 8.4 %collective-permute-start.29 = (bf16[1,48,1024]{2,1,0:T(8,128)(2,1)S(1)}, bf16[1,48,1024]{2,1,0:T(8,128)(2,1)S(1)}, u32[]{:S(2)}, u32[]{:S(2)}) collective-permute-start(bf16[1,48,1024]{2,1,0:T(8,128)(2,1)S(1)} %fusion.17), channel_id=1, source_target_pairs={{0,8},{1,9},{2,10},{3,11},{4,12},{5,13},{6,14},{7,15},{8,0},{9,1},... | collective-permute-start | bytes 294920 | tf_op jit(solution)/shard_map/ppermute | solution.py:758
  315.4 6.0 %collective-permute-start.37 = (bf16[2,48,1152]{2,1,0:T(8,128)(2,1)S(1)}, bf16[2,48,1152]{2,1,0:T(8,128)(2,1)S(1)}, u32[]{:S(2)}, u32[]{:S(2)}) collective-permute-start(bf16[2,48,1152]{2,1,0:T(8,128)(2,1)S(1)} %get-tuple-element.176), channel_id=1, source_target_pairs={{0,4},{1,5},{2,6},{3,7},{4,0},{5,1},{6,2},{7,3},{8,12},{9,13},{10,... | collective-permute-start | bytes 663560 | tf_op jit(solution)/shard_map/ppermute | solution.py:758
  317.2 11.0 %collective-permute-start.21 = (bf16[1,48,1024]{2,1,0:T(8,128)(2,1)S(1)}, bf16[1,48,1024]{2,1,0:T(8,128)(2,1)S(1)}, u32[]{:S(2)}, u32[]{:S(2)}) collective-permute-start(bf16[1,48,1024]{2,1,0:T(8,128)(2,1)S(1)} %fusion.22), channel_id=1, source_target_pairs={{0,16},{1,17},{2,18},{3,19},{4,20},{5,21},{6,22},{7,23},{8,24},{9,... | collective-permute-start | bytes 294920 | tf_op jit(solution)/shard_map/ppermute | solution.py:758
  321.5 5.5 %collective-permute-start.38 = (bf16[1,48,1152]{2,1,0:T(8,128)(2,1)S(1)}, bf16[1,48,1152]{2,1,0:T(8,128)(2,1)S(1)}, u32[]{:S(2)}, u32[]{:S(2)}) collective-permute-start(bf16[1,48,1152]{2,1,0:T(8,128)(2,1)S(1)} %fusion.14), channel_id=1, source_target_pairs={{0,2},{1,3},{2,0},{3,1},{4,6},{5,7},{6,4},{7,5},{8,10},{9,11},{10,... | collective-permute-start | bytes 331784 | tf_op jit(solution)/shard_map/ppermute | solution.py:758
  322.0 14.8 %collective-permute-start.30 = (bf16[1,48,1024]{2,1,0:T(8,128)(2,1)S(1)}, bf16[1,48,1024]{2,1,0:T(8,128)(2,1)S(1)}, u32[]{:S(2)}, u32[]{:S(2)}) collective-permute-start(bf16[1,48,1024]{2,1,0:T(8,128)(2,1)S(1)} %fusion.19), channel_id=1, source_target_pairs={{0,16},{1,17},{2,18},{3,19},{4,20},{5,21},{6,22},{7,23},{8,24},{9,... | collective-permute-start | bytes 294920 | tf_op jit(solution)/shard_map/ppermute | solution.py:758
  324.6 85.9 %collective-permute-start.59 = (bf16[8,192,768]{2,1,0:T(8,128)(2,1)S(1)}, bf16[8,192,768]{2,1,0:T(8,128)(2,1)}, u32[]{:S(2)}, u32[]{:S(2)}) collective-permute-start(bf16[8,192,768]{2,1,0:T(8,128)(2,1)S(1)} %bitcast_select_fusion.x), channel_id=1, source_target_pairs={{0,1},{1,0},{2,3},{3,2},{4,5},{5,4},{6,7},{7,6},{8,9},{9,8},{10,11... | collective-permute-start | bytes 7077896 | tf_op jit(solution)/shard_map/ppermute | solution.py:758
  326.5 77.0 %collective-permute-start.54 = (bf16[8,48,3072]{2,1,0:T(8,128)(2,1)}, bf16[8,48,3072]{2,1,0:T(8,128)(2,1)}, u32[]{:S(2)}, u32[]{:S(2)}) collective-permute-start(bf16[8,48,3072]{2,1,0:T(8,128)(2,1)} %bitcast_select_fusion.1.x), channel_id=1, source_target_pairs={{0,1},{1,0},{2,3},{3,2},{4,5},{5,4},{6,7},{7,6},{8,9},{9,8},{10,11... | collective-permute-start | bytes 7077896 | tf_op jit(solution)/shard_map/ppermute | solution.py:758
  327.1 8.3 %collective-permute-start.39 = (bf16[1,48,1152]{2,1,0:T(8,128)(2,1)S(1)}, bf16[1,48,1152]{2,1,0:T(8,128)(2,1)S(1)}, u32[]{:S(2)}, u32[]{:S(2)}) collective-permute-start(bf16[1,48,1152]{2,1,0:T(8,128)(2,1)S(1)} %fusion.16), channel_id=1, source_target_pairs={{0,16},{1,17},{2,18},{3,19},{4,20},{5,21},{6,22},{7,23},{8,24},{9,... | collective-permute-start | bytes 331784 | tf_op jit(solution)/shard_map/ppermute | solution.py:758
  328.3 13.0 %collective-permute-start.22 = (bf16[1,48,1024]{2,1,0:T(8,128)(2,1)S(1)}, bf16[1,48,1024]{2,1,0:T(8,128)(2,1)S(1)}, u32[]{:S(2)}, u32[]{:S(2)}) collective-permute-start(bf16[1,48,1024]{2,1,0:T(8,128)(2,1)S(1)} %add_convert_fusion.6), channel_id=1, source_target_pairs={{0,4},{1,5},{2,6},{3,7},{4,0},{5,1},{6,2},{7,3},{8,12},{9,13},{10,... | collective-permute-start | bytes 294920 | tf_op jit(solution)/shard_map/ppermute | solution.py:758
  335.4 4.8 %collective-permute-start.40 = (bf16[1,48,1152]{2,1,0:T(8,128)(2,1)S(1)}, bf16[1,48,1152]{2,1,0:T(8,128)(2,1)S(1)}, u32[]{:S(2)}, u32[]{:S(2)}) collective-permute-start(bf16[1,48,1152]{2,1,0:T(8,128)(2,1)S(1)} %add_convert_fusion.4), channel_id=1, source_target_pairs={{0,2},{1,3},{2,0},{3,1},{4,6},{5,7},{6,4},{7,5},{8,10},{9,11},{10,... | collective-permute-start | bytes 331784 | tf_op jit(solution)/shard_map/ppermute | solution.py:758
  336.8 4.7 %collective-permute-start.31 = (bf16[1,48,1024]{2,1,0:T(8,128)(2,1)S(1)}, bf16[1,48,1024]{2,1,0:T(8,128)(2,1)S(1)}, u32[]{:S(2)}, u32[]{:S(2)}) collective-permute-start(bf16[1,48,1024]{2,1,0:T(8,128)(2,1)S(1)} %add_convert_fusion.5), channel_id=1, source_target_pairs={{0,8},{1,9},{2,10},{3,11},{4,12},{5,13},{6,14},{7,15},{8,0},{9,1},... | collective-permute-start | bytes 294920 | tf_op jit(solution)/shard_map/ppermute | solution.py:758
  340.3 6.0 %collective-permute-start.41 = (bf16[2,48,1152]{2,1,0:T(8,128)(2,1)S(1)}, bf16[2,48,1152]{2,1,0:T(8,128)(2,1)S(1)}, u32[]{:S(2)}, u32[]{:S(2)}) collective-permute-start(bf16[2,48,1152]{2,1,0:T(8,128)(2,1)S(1)} %broadcast_select_fusion.2), channel_id=1, source_target_pairs={{0,4},{1,5},{2,6},{3,7},{4,0},{5,1},{6,2},{7,3},{8,12},{9,13},{10,... | collective-permute-start | bytes 663560 | tf_op jit(solution)/shard_map/ppermute | solution.py:758
  341.6 7.0 %collective-permute-start.32 = (bf16[2,48,1024]{2,1,0:T(8,128)(2,1)S(1)}, bf16[2,48,1024]{2,1,0:T(8,128)(2,1)S(1)}, u32[]{:S(2)}, u32[]{:S(2)}) collective-permute-start(bf16[2,48,1024]{2,1,0:T(8,128)(2,1)S(1)} %get-tuple-element.185), channel_id=1, source_target_pairs={{0,2},{1,3},{2,0},{3,1},{4,6},{5,7},{6,4},{7,5},{8,10},{9,11},{10,... | collective-permute-start | bytes 589832 | tf_op jit(solution)/shard_map/ppermute | solution.py:758
  343.2 4.6 %collective-permute-start.45 = (f32[16,768]{1,0:T(8,128)S(1)}, f32[16,768]{1,0:T(8,128)S(1)}, u32[]{:S(2)}, u32[]{:S(2)}) collective-permute-start(f32[16,768]{1,0:T(8,128)S(1)} %add.171), channel_id=1, source_target_pairs={{0,2},{1,3},{2,0},{3,1},{4,6},{5,7},{6,4},{7,5},{8,10},{9,11},{10,... | collective-permute-start | bytes 147464 | tf_op jit(solution)/shard_map/ppermute | solution.py:758
  346.3 7.8 %collective-permute-start.23 = (bf16[2,48,1024]{2,1,0:T(8,128)(2,1)S(1)}, bf16[2,48,1024]{2,1,0:T(8,128)(2,1)S(1)}, u32[]{:S(2)}, u32[]{:S(2)}) collective-permute-start(bf16[2,48,1024]{2,1,0:T(8,128)(2,1)S(1)} %get-tuple-element.186), channel_id=1, source_target_pairs={{0,8},{1,9},{2,10},{3,11},{4,12},{5,13},{6,14},{7,15},{8,0},{9,1},... | collective-permute-start | bytes 589832 | tf_op jit(solution)/shard_map/ppermute | solution.py:758
  347.8 11.9 %collective-permute-start.42 = (bf16[4,48,1152]{2,1,0:T(8,128)(2,1)S(1)}, bf16[4,48,1152]{2,1,0:T(8,128)(2,1)S(1)}, u32[]{:S(2)}, u32[]{:S(2)}) collective-permute-start(bf16[4,48,1152]{2,1,0:T(8,128)(2,1)S(1)} %bitcast_select_fusion.9), channel_id=1, source_target_pairs={{0,8},{1,9},{2,10},{3,11},{4,12},{5,13},{6,14},{7,15},{8,0},{9,1},... | collective-permute-start | bytes 1327112 | tf_op jit(solution)/shard_map/ppermute | solution.py:758
  348.6 6.8 %collective-permute-start.46 = (f32[16,768]{1,0:T(8,128)S(1)}, f32[16,768]{1,0:T(8,128)S(1)}, u32[]{:S(2)}, u32[]{:S(2)}) collective-permute-start(f32[16,768]{1,0:T(8,128)S(1)} %add.172), channel_id=1, source_target_pairs={{0,4},{1,5},{2,6},{3,7},{4,0},{5,1},{6,2},{7,3},{8,12},{9,13},{10,... | collective-permute-start | bytes 147464 | tf_op jit(solution)/shard_map/ppermute | solution.py:758
  354.3 9.6 %collective-permute-start.33 = (bf16[4,48,1024]{2,1,0:T(8,128)(2,1)S(1)}, bf16[4,48,1024]{2,1,0:T(8,128)(2,1)S(1)}, u32[]{:S(2)}, u32[]{:S(2)}) collective-permute-start(bf16[4,48,1024]{2,1,0:T(8,128)(2,1)S(1)} %get-tuple-element.183), channel_id=1, source_target_pairs={{0,4},{1,5},{2,6},{3,7},{4,0},{5,1},{6,2},{7,3},{8,12},{9,13},{10,... | collective-permute-start | bytes 1179656 | tf_op jit(solution)/shard_map/ppermute | solution.py:758
  355.4 11.0 %collective-permute-start.24 = (bf16[4,48,1024]{2,1,0:T(8,128)(2,1)S(1)}, bf16[4,48,1024]{2,1,0:T(8,128)(2,1)S(1)}, u32[]{:S(2)}, u32[]{:S(2)}) collective-permute-start(bf16[4,48,1024]{2,1,0:T(8,128)(2,1)S(1)} %get-tuple-element.184), channel_id=1, source_target_pairs={{0,2},{1,3},{2,0},{3,1},{4,6},{5,7},{6,4},{7,5},{8,10},{9,11},{10,... | collective-permute-start | bytes 1179656 | tf_op jit(solution)/shard_map/ppermute | solution.py:758
  359.8 4.1 collective-permute-start.47
  363.9 27.4 %collective-permute-start.43 = (bf16[8,48,1152]{2,1,0:T(8,128)(2,1)S(1)}, bf16[8,48,1152]{2,1,0:T(8,128)(2,1)}, u32[]{:S(2)}, u32[]{:S(2)}) collective-permute-start(bf16[8,48,1152]{2,1,0:T(8,128)(2,1)S(1)} %bitcast_select_fusion.5.x), channel_id=1, source_target_pairs={{0,1},{1,0},{2,3},{3,2},{4,5},{5,4},{6,7},{7,6},{8,9},{9,8},{10,11... | collective-permute-start | bytes 2654216 | tf_op jit(solution)/shard_map/ppermute | solution.py:758
  363.9 6.2 %collective-permute-start.48 = (f32[16,768]{1,0:T(8,128)S(1)}, f32[16,768]{1,0:T(8,128)S(1)}, u32[]{:S(2)}, u32[]{:S(2)}) collective-permute-start(f32[16,768]{1,0:T(8,128)S(1)} %add.174), channel_id=1, source_target_pairs={{0,16},{1,17},{2,18},{3,19},{4,20},{5,21},{6,22},{7,23},{8,24},{9,... | collective-permute-start | bytes 147464 | tf_op jit(solution)/shard_map/ppermute | solution.py:758
  367.7 27.7 %collective-permute-start.34 = (bf16[8,48,1024]{2,1,0:T(8,128)(2,1)}, bf16[8,48,1024]{2,1,0:T(8,128)(2,1)}, u32[]{:S(2)}, u32[]{:S(2)}) collective-permute-start(bf16[8,48,1024]{2,1,0:T(8,128)(2,1)} %get-tuple-element.181.x), channel_id=1, source_target_pairs={{0,1},{1,0},{2,3},{3,2},{4,5},{5,4},{6,7},{7,6},{8,9},{9,8},{10,11... | collective-permute-start | bytes 2359304 | tf_op jit(solution)/shard_map/ppermute | solution.py:758
  370.1 29.4 %collective-permute-start.25 = (bf16[8,48,1024]{2,1,0:T(8,128)(2,1)}, bf16[8,48,1024]{2,1,0:T(8,128)(2,1)}, u32[]{:S(2)}, u32[]{:S(2)}) collective-permute-start(bf16[8,48,1024]{2,1,0:T(8,128)(2,1)} %get-tuple-element.182.x), channel_id=1, source_target_pairs={{0,1},{1,0},{2,3},{3,2},{4,5},{5,4},{6,7},{7,6},{8,9},{9,8},{10,11... | collective-permute-start | bytes 2359304 | tf_op jit(solution)/shard_map/ppermute | solution.py:758
  (45 other events, 340.7 us)

commit v2 on v1

--- a/solution.py
+++ b/solution.py
@@ -48,8 +48,22 @@
     return pl.BlockSpec(shape, lambda *g: (0,) * len(shape))
 
 
+def held(shape):
+    return pl.BlockSpec(shape, lambda *g: (0,) * len(shape), pipeline_mode=pl.Buffered(1))
+
+
 def struct(shape, dtype):
     return jax.ShapeDtypeStruct(shape, dtype)
+
+
+def row(v):
+    return v[...].reshape(1, -1)
+
+
+def normalize(resid):
+    center = resid - jnp.mean(resid, axis=-1, keepdims=True)
+    inv = lax.rsqrt(jnp.mean(center * center, axis=-1, keepdims=True) + LN_EPS)
+    return center * inv, inv
 
 
 def segment_ends(lens):
@@ -102,7 +116,10 @@
     return jnp.concatenate([t[:64, :QB], t[64:, QB:]], axis=0)
 
 
-def attn_fwd_kernel(lens, tok, wqkv, bqv, packed, out, lse, vt, segq, segk):
+def attn_fwd_kernel(
+    lens, tok, wqkv, bqv, wo, bo, g1, b1,
+    packed, out, lse, hid, low, ht, n1, i1, vt, segq, segk,
+):
     rows, width = tok.shape
     ends = segment_ends(lens)
     fill_segments(ends, segq, segk)
@@ -156,6 +173,18 @@
         return carry
 
     lax.fori_loop(0, rows // QB, step, 0)
+    tile = 256
+    for r0 in range(0, rows, tile):
+        r = slice(r0, r0 + tile)
+        resid = tok[r, :].astype(f32) + (nn(out[r, :], wo[...]) + row(bo))
+        normal, inv = normalize(resid)
+        hidden = normal * row(g1) + row(b1)
+        hid[r, :] = hidden
+        hl = hidden.astype(bf16)
+        low[r, :] = hl
+        ht[:, r] = hl.T
+        n1[r, :] = normal.astype(bf16)
+        i1[r, :] = inv
 
 
 def attn_bwd_kernel(
@@ -231,23 +260,28 @@
     return [pltpu.VMEM((rows // QB, QB), i32), pltpu.VMEM((rows, 128), i32)]
 
 
-def attention(lens, tok, wqkv, bqv):
+def attention(lens, tok, wqkv, bqv, wo, bo, g1, b1):
     rows, width = tok.shape
     pairs = width // 128
     return pl.pallas_call(
         attn_fwd_kernel,
-        in_specs=[SMEM, VMEM, VMEM, VMEM],
-        out_specs=[VMEM] * 3,
+        in_specs=[SMEM] + [VMEM] * 7,
+        out_specs=[VMEM] * 8,
         out_shape=[
             struct((rows, 3 * width), bf16),
             struct((rows, width), bf16),
             struct((pairs, rows // QB, 2 * QB), f32),
+            struct((rows, width), f32),
+            struct((rows, width), bf16),
+            struct((width, rows), bf16),
+            struct((rows, width), bf16),
+            struct((rows, 1), f32),
         ],
         scratch_shapes=[pltpu.VMEM((pairs, 128, rows), bf16)] + segment_scratch(rows),
         compiler_params=params(32),
-        cost_estimate=cost(16e9, 8 * rows * width),
+        cost_estimate=cost(18e9, 8 * rows * width),
         name="attention_forward",
-    )(lens, tok, wqkv, bqv)
+    )(lens, tok, wqkv, bqv, wo, bo, g1, b1)
 
 
 def attention_back(part, lens, packed, do, o, lse):
@@ -272,12 +306,6 @@
     )(lens, packed, do, o, lse)
 
 
-def normalize(resid):
-    center = resid - jnp.mean(resid, axis=-1, keepdims=True)
-    inv = lax.rsqrt(jnp.mean(center * center, axis=-1, keepdims=True) + LN_EPS)
-    return center * inv, inv
-
-
 def norm_back(grad, gain, normal, inv):
     dn = grad * gain
     return inv * (
@@ -287,72 +315,68 @@
     )
 
 
-def row(v):
-    return v[...].reshape(1, -1)
-
-
-def mid_fwd_kernel(
-    lens, att, tok, wo, bo, g1, b1, wu, bu, wd, bd, g2, b2, wp,
-    ht, act, slp, n1, i1, n2, i2, nl, emb, ul, msg,
-    hid, low, acc, bus,
+FF_CHUNK = 1024
+
+
+def ffn_fwd_kernel(
+    lens, hid, low, wu, bu, wd, bd, g2, b2, wp, act, slp, n2, i2, nl, emb, ul, msg, acc
 ):
-    rows = att.shape[0]
-    ff = wu.shape[1]
-    chunk = 512
+    c = pl.program_id(0)
+    rows = low.shape[0]
+    span = hid.shape[1]
     tile = 256
     tiles = [slice(r, r + tile) for r in range(0, rows, tile)]
-    bus[...] = row(bu)
+
+    @pl.when(c == 0)
+    def _():
+        for r in tiles:
+            acc[r, :] = jnp.broadcast_to(row(bd), acc[r, :].shape)
+
     for r in tiles:
-        resid = tok[r, :].astype(f32) + (nn(att[r, :], wo[...]) + row(bo))
-        normal, inv = normalize(resid)
-        hidden = normal * row(g1) + row(b1)
-        hid[r, :] = hidden
-        hl = hidden.astype(bf16)
-        low[r, :] = hl
-        ht[:, r] = hl.T
-        n1[r, :] = normal.astype(bf16)
-        i1[r, :] = inv
-        acc[r, :] = hidden + row(bd)
-
-    def step(c, carry):
-        at = pl.ds(pl.multiple_of(c * chunk, chunk), chunk)
+        inner = nn(low[r, :], wu[...]) + row(bu)
+        cdf = 0.5 + 0.5 * lax.erf(inner * 0.7071067811865476)
+        a = (inner * cdf).astype(bf16)
+        act[r, :] = a
+        slp[r, :] = (cdf + inner * (jnp.exp(inner * inner * -0.5) * 0.3989422804014327)).astype(bf16)
+        acc[r, :] += nn(a, wd[...])
+    at = pl.ds(pl.multiple_of(c * span, span), span)
+    acc[:, at] += hid[...]
+
+    @pl.when(c == pl.num_programs(0) - 1)
+    def _():
         for r in tiles:
-            inner = nn(low[r, :], wu[:, at]) + bus[:, at]
-            cdf = 0.5 + 0.5 * lax.erf(inner * 0.7071067811865476)
-            a = (inner * cdf).astype(bf16)
-            act[r, at] = a
-            slp[r, at] = (
-                cdf + inner * (jnp.exp(inner * inner * -0.5) * 0.3989422804014327)
+            normal, inv = normalize(acc[r, :])
+            normed = (normal * row(g2) + row(b2)).astype(bf16)
+            n2[r, :] = normal.astype(bf16)
+            i2[r, :] = inv
+            nl[r, :] = normed
+            e = nn(normed, wp[...])
+            emb[r, :] = e
+            ul[r, :] = (
+                e * lax.rsqrt(jnp.sum(e * e, axis=-1, keepdims=True) + NORM_EPS)
             ).astype(bf16)
-            acc[r, :] += nn(a, wd[at, :])
-        return carry
-
-    lax.fori_loop(0, ff // chunk, step, 0)
-    for r in tiles:
-        normal, inv = normalize(acc[r, :])
-        normed = (normal * row(g2) + row(b2)).astype(bf16)
-        n2[r, :] = normal.astype(bf16)
-        i2[r, :] = inv
-        nl[r, :] = normed
-        e = nn(normed, wp[...])
-        emb[r, :] = e
-        ul[r, :] = (e * lax.rsqrt(jnp.sum(e * e, axis=-1, keepdims=True) + NORM_EPS)).astype(bf16)
-    count = lens[0, 0]
-    slot = lax.broadcasted_iota(i32, (QLEN, ul.shape[1]), 0)
-    msg[0, 0:QLEN, :] = jnp.where(slot < count, ul[0:QLEN, :].astype(f32), 0.0).astype(bf16)
-    msg[0, QLEN : QLEN + 16, :] = jnp.full((16, ul.shape[1]), count, i32).astype(f32).astype(bf16)
-
-
-def mid_fwd(lens, att, tok, wo, bo, g1, b1, wu, bu, wd, bd, g2, b2, wp):
-    rows, width = att.shape
+        count = lens[0, 0]
+        slot = lax.broadcasted_iota(i32, (QLEN, ul.shape[1]), 0)
+        msg[0, 0:QLEN, :] = jnp.where(slot < count, ul[0:QLEN, :].astype(f32), 0.0).astype(bf16)
+        msg[0, QLEN : QLEN + 16, :] = (
+            jnp.full((16, ul.shape[1]), count, i32).astype(f32).astype(bf16)
+        )
+
+
+def ffn_fwd(lens, hid, low, wu, bu, wd, bd, g2, b2, wp):
+    rows, width = hid.shape
     ff, out = wu.shape[1], wp.shape[1]
-    ins = [lens, att, tok, wo, bo, g1, b1, wu, bu, wd, bd, g2, b2, wp]
+    steps = ff // FF_CHUNK
+    ins = [lens, hid, low, wu, bu, wd, bd, g2, b2, wp]
+    specs = [held(x.shape) for x in ins]
+    specs[0] = SMEM
+    specs[1] = pl.BlockSpec((rows, width // steps), lambda c: (0, c))
+    specs[3] = pl.BlockSpec((width, FF_CHUNK), lambda c: (0, c))
+    specs[4] = pl.BlockSpec((FF_CHUNK,), lambda c: (c,))
+    specs[5] = pl.BlockSpec((FF_CHUNK, width), lambda c: (c, 0))
     outs = [
-        struct((width, rows), bf16),
         struct((rows, ff), bf16),
         struct((rows, ff), bf16),
-        struct((rows, width), bf16),
-        struct((rows, 1), f32),
         struct((rows, width), bf16),
         struct((rows, 1), f32),
         struct((rows, width), bf16),
@@ -360,20 +384,18 @@
         struct((rows, out), bf16),
         struct((1, QLEN + 16, out), bf16),
     ]
-    return pl.pallas_call(
-        mid_fwd_kernel,
-        in_specs=[SMEM] + [VMEM] * (len(ins) - 1),
-        out_specs=[VMEM] * len(outs),
+    ospecs = [whole(x.shape) for x in outs]
+    ospecs[0] = ospecs[1] = pl.BlockSpec((rows, FF_CHUNK), lambda c: (0, c))
+    return pl.pallas_call(
+        ffn_fwd_kernel,
+        grid=(steps,),
+        in_specs=specs,
+        out_specs=ospecs,
         out_shape=outs,
-        scratch_shapes=[
-            pltpu.VMEM((rows, width), f32),
-            pltpu.VMEM((rows, width), bf16),
-            pltpu.VMEM((rows, width), f32),
-            pltpu.VMEM((1, ff), f32),
-        ],
-        compiler_params=params(56),
-        cost_estimate=cost(20e9, 40e6),
-        name="middle_forward",
+        scratch_shapes=[pltpu.VMEM((rows, width), f32)],
+        compiler_params=params(36),
+        cost_estimate=cost(18e9, 40e6),
+        name="ffn_forward",
     )(*ins)
 
 
@@ -570,129 +592,167 @@
     return [(keep, top, low), (send, 1 - top, low)]
 
 
-def down_grad_kernel(dims, me, act, dbr, keep, send):
-    pr = keep.shape[1]
+def down_grad_kernel(dims, me, act, dbr, gwp, keep, send):
+    pr, width = keep.shape[1], dbr.shape[1]
+    parts = act.shape[1] // width
     half = PIECES // 2
     for dst, side, low in sides(me, dims, keep, send):
         for t in range(0, half, 2):
-            at = pl.multiple_of((side * half + t) * pr, 128)
-            g = tn(act[:, pl.ds(at, 2 * pr)], dbr[...])
-            dst[t ^ low] = g[:pr]
-            dst[(t + 1) ^ low] = g[pr:]
-
-
-def down_grad(dims, me, act, dbr):
+            at = pl.multiple_of((side * half + t) * (pr * parts), 128)
+            g = tn(act[:, pl.ds(at, 2 * pr * parts)], dbr[...])
+            for u in range(2):
+                for i in range(parts):
+                    r = (u * parts + i) * pr
+                    dst[(t + u) ^ low, :, i * width : (i + 1) * width] = g[r : r + pr]
+                first = pl.multiple_of((side * half + t + u) * pr, 16)
+                dst[(t + u) ^ low, :, parts * width :] = gwp[pl.ds(first, pr), :]
+
+
+def down_grad(dims, me, act, dbr, gwp):
     rows, width = dbr.shape
-    buf = struct((PIECES // 2, act.shape[1] // PIECES, width), f32)
+    buf = struct((PIECES // 2, width // PIECES, act.shape[1] + gwp.shape[1]), f32)
     return pl.pallas_call(
         functools.partial(down_grad_kernel, dims),
-        in_specs=[SMEM, VMEM, VMEM],
+        in_specs=[SMEM] + [VMEM] * 3,
         out_specs=[VMEM] * 2,
         out_shape=[buf, buf],
         compiler_params=params(32),
         cost_estimate=cost(5e9, 17e6),
         name="down_gradient",
-    )(me, act, dbr)
+    )(me, act, dbr, gwp)
 
 
 def up_grad_kernel(dims, me, dbr, slp, wd, ht, keep, send, din, dsum):
-    ff = slp.shape[1]
     pr = keep.shape[1]
     half = PIECES // 2
-    chunk = 512
-
-    def step(c, carry):
-        at = pl.ds(pl.multiple_of(c * chunk, chunk), chunk)
-        d_inner = (nt(dbr[...], wd[at, :]) * slp[:, at].astype(f32)).astype(bf16)
-        din[:, at] = d_inner
-        dsum[:, at] = jnp.sum(d_inner.astype(f32), axis=0, keepdims=True)
-        for dst, side, low in sides(me, dims, keep, send):
-            r = pl.ds(pl.multiple_of(side * (half * pr), half * pr), half * pr)
-            g = nn(ht[r, :], d_inner)
-            for t in range(half):
-                dst[t ^ low, :, at] = g[t * pr : (t + 1) * pr]
-        return carry
-
-    lax.fori_loop(0, ff // chunk, step, 0)
+    rows = dbr.shape[0]
+    tile = 256
+    dsum[...] = jnp.zeros_like(dsum)
+    for r0 in range(0, rows, tile):
+        r = slice(r0, r0 + tile)
+        d_inner = (nt(dbr[r, :], wd[...]) * slp[r, :].astype(f32)).astype(bf16)
+        din[r, :] = d_inner
+        dsum[...] += jnp.sum(d_inner.astype(f32), axis=0, keepdims=True)
+    for dst, side, low in sides(me, dims, keep, send):
+        at = pl.multiple_of(side * (half * pr), half * pr)
+        g = nn(ht[pl.ds(at, half * pr), :], din[...])
+        for t in range(half):
+            dst[t ^ low] = g[t * pr : (t + 1) * pr]
 
 
 def up_grad(dims, me, dbr, slp, wd, ht):
     rows, width = dbr.shape
     ff = slp.shape[1]
-    buf = struct((PIECES // 2, width // PIECES, ff), f32)
+    half, pr = PIECES // 2, width // PIECES
+    buf = struct((half, pr, ff), f32)
+    part = pl.BlockSpec((half, pr, FF_CHUNK), lambda c: (0, 0, c))
+    wide = pl.BlockSpec((rows, FF_CHUNK), lambda c: (0, c))
     return pl.pallas_call(
         functools.partial(up_grad_kernel, dims),
-        in_specs=[SMEM] + [VMEM] * 4,
-        out_specs=[VMEM] * 4,
+        grid=(ff // FF_CHUNK,),
+        in_specs=[
+            SMEM,
+            held(dbr.shape),
+            wide,
+            pl.BlockSpec((FF_CHUNK, width), lambda c: (c, 0)),
+            held(ht.shape),
+        ],
+        out_specs=[part, part, wide, pl.BlockSpec((1, FF_CHUNK), lambda c: (0, c))],
         out_shape=[buf, buf, struct((rows, ff), bf16), struct((1, ff), f32)],
-        compiler_params=params(48),
+        compiler_params=params(36),
         cost_estimate=cost(10e9, 30e6),
         name="up_gradient",
     )(me, dbr, slp, wd, ht)
 
 
-def mid_back_kernel(me, din, wu, dr2, n1, i1, g1, wo, dr1, dpr, dat, sums):
-    rows, width = dr2.shape
-    sums[...] = jnp.zeros_like(sums)
-    tile = 256
-    for r0 in range(0, rows, tile):
-        r = slice(r0, r0 + tile)
-        d = dr2[r, :] + nt(din[r, :], wu[...])
-        normal = n1[r, :].astype(f32)
-        sums[0:1, :] += jnp.sum(d * normal, axis=0, keepdims=True)
-        sums[1:2, :] += jnp.sum(d, axis=0, keepdims=True)
-        dr = norm_back(d, row(g1), normal, i1[r, :])
-        dr1[r, :] = dr
-        low = dr.astype(bf16)
-        dpr[r, :] = low
-        sums[2:3, :] += jnp.sum(low.astype(f32), axis=0, keepdims=True)
-        dat[r, :] = nt(low, wo[...]).astype(bf16)
+def mid_back_kernel(me, din, wu, dr2, n1, i1, g1, wo, dr1, dpr, dat, sums, acc):
+    c = pl.program_id(0)
+    rows, width = dr1.shape
+    span = dr2.shape[1]
+
+    @pl.when(c == 0)
+    def _():
+        acc[...] = nt(din[...], wu[...])
+
+    @pl.when(c > 0)
+    def _():
+        acc[...] += nt(din[...], wu[...])
+
+    at = pl.ds(pl.multiple_of(c * span, span), span)
+    acc[:, at] += dr2[...]
+
+    @pl.when(c == pl.num_programs(0) - 1)
+    def _():
+        sums[...] = jnp.zeros_like(sums)
+        tile = 256
+        for r0 in range(0, rows, tile):
+            r = slice(r0, r0 + tile)
+            d = acc[r, :]
+            normal = n1[r, :].astype(f32)
+            sums[0:1, :] += jnp.sum(d * normal, axis=0, keepdims=True)
+            sums[1:2, :] += jnp.sum(d, axis=0, keepdims=True)
+            dr = norm_back(d, row(g1), normal, i1[r, :])
+            dr1[r, :] = dr
+            low = dr.astype(bf16)
+            dpr[r, :] = low
+            sums[2:3, :] += jnp.sum(low.astype(f32), axis=0, keepdims=True)
+            dat[r, :] = nt(low, wo[...]).astype(bf16)
 
 
 def mid_back(me, din, wu, dr2, n1, i1, g1, wo):
     rows, width = dr2.shape
+    ff = din.shape[1]
+    steps = ff // FF_CHUNK
+    ins = [me, din, wu, dr2, n1, i1, g1, wo]
+    specs = [held(x.shape) for x in ins]
+    specs[0] = SMEM
+    specs[1] = pl.BlockSpec((rows, FF_CHUNK), lambda c: (0, c))
+    specs[2] = pl.BlockSpec((width, FF_CHUNK), lambda c: (0, c))
+    specs[3] = pl.BlockSpec((rows, width // steps), lambda c: (0, c))
+    outs = [
+        struct((rows, width), f32),
+        struct((rows, width), bf16),
+        struct((rows, width), bf16),
+        struct((8, width), f32),
+    ]
     return pl.pallas_call(
         mid_back_kernel,
-        in_specs=[SMEM] + [VMEM] * 7,
-        out_specs=[VMEM] * 4,
-        out_shape=[
-            struct((rows, width), f32),
-            struct((rows, width), bf16),
-            struct((rows, width), bf16),
-            struct((8, width), f32),
-        ],
-        compiler_params=params(40),
+        grid=(steps,),
+        in_specs=specs,
+        out_specs=[whole(x.shape) for x in outs],
+        out_shape=outs,
+        scratch_shapes=[pltpu.VMEM((rows, width), f32)],
+        compiler_params=params(36),
         cost_estimate=cost(9e9, 15e6),
         name="middle_backward",
-    )(me, din, wu, dr2, n1, i1, g1, wo)
-
-
-def qkv_grad_kernel(p, dims, me, tok, d0, d1, d2, att, dpr, *rest):
+    )(*ins)
+
+
+def qkv_grad_kernel(dims, has_out, me, tok, d0, d1, d2, *rest):
     keep, send = rest[-2:]
-    extra = rest[0] if len(rest) == 3 else None
+    pairs = [(tok, d0), (tok, d1), (tok, d2)]
+    if has_out:
+        pairs.append(rest[:2])
     half = PIECES // 2
     pr = keep.shape[1]
     for dst, side, low in sides(me, dims, keep, send):
         at = pl.ds(pl.multiple_of(side * (half * pr), half * pr), half * pr)
         col = 0
-        dpr_own = dpr.at[:, p * 256 : (p + 1) * 256]
-        for left, d in ((tok, d0), (tok, d1), (tok, d2), (att, dpr_own)):
+        for left, d in pairs:
             g = tn(left[:, at], d[...])
+            cols = d.shape[1]
             for t in range(half):
-                dst[t ^ low, :, col : col + 256] = g[t * pr : (t + 1) * pr]
-            col += 256
-        if extra is not None:
-            for t in range(half):
-                first = pl.multiple_of((side * half + t) * pr, 16)
-                dst[t ^ low, :, col : col + 128] = extra[pl.ds(first, pr), :]
-
-
-def qkv_grad(p, dims, me, tok, ds, att, dpr, extra):
-    rows, width = att.shape
-    ins = [me, tok, *ds, att, dpr] + ([] if extra is None else [extra])
-    buf = struct((PIECES // 2, width // PIECES, width + 256 + (0 if extra is None else 128)), f32)
-    return pl.pallas_call(
-        functools.partial(qkv_grad_kernel, p, dims),
+                dst[t ^ low, :, col : col + cols] = g[t * pr : (t + 1) * pr]
+            col += cols
+
+
+def qkv_grad(dims, me, tok, ds, outer):
+    rows, width = tok.shape
+    ins = [me, tok, *ds, *outer]
+    cols = sum(d.shape[1] for d in ds) + (width if outer else 0)
+    buf = struct((PIECES // 2, width // PIECES, cols), f32)
+    return pl.pallas_call(
+        functools.partial(qkv_grad_kernel, dims, bool(outer)),
         in_specs=[SMEM] + [VMEM] * (len(ins) - 1),
         out_specs=[VMEM] * 2,
         out_shape=[buf, buf],
@@ -781,9 +841,12 @@
         self.recv = swap(self.ready, d, self.n)
 
     def land(self, *others):
+        if self.recv is None:
+            self.start()
         k, dims = self.at, self.dims
         self.at += 1
         recv = after(self.recv, *others) if others else self.recv
+        self.recv = None
         if k < 4:
             recv = recv.astype(f32)
             half = self.keep.shape[0] // 2
@@ -799,20 +862,32 @@
         else:
             self.ready = join(self.ready, recv)
 
-    def step(self):
-        self.start()
-        self.land()
-
     def finish(self):
         while self.out is None:
-            self.step()
+            self.land()
         return self.out
 
 
-def sum_all(x, n):
-    for b in range(n.bit_length() - 1):
-        x = x + swap(x, 1 << b, n)
-    return x
+class Total:
+    def __init__(self, x, n):
+        self.ready, self.n, self.at, self.recv, self.out = x, n, 0, None, None
+
+    def start(self):
+        self.recv = swap(self.ready, 1 << self.at, self.n)
+
+    def land(self, *others):
+        if self.recv is None:
+            self.start()
+        self.ready = self.ready + (after(self.recv, *others) if others else self.recv)
+        self.recv = None
+        self.at += 1
+        if 1 << self.at == self.n:
+            self.out = self.ready
+
+    def finish(self):
+        while self.out is None:
+            self.land()
+        return self.out
 
 
 def gather_all(x, n):
@@ -824,65 +899,86 @@
 BATCH = 4
 
 
-def spread_kernel(dims, cuts, count, me, x, y, *refs):
-    outs = refs[-count:]
-    low = flip_of(me[0], dims) & (BATCH - 1)
-    pr = x.shape[1]
-
-    def put(src):
-        for t in range(BATCH):
-            col = 0
-            for out, cols in zip(outs, cuts):
-                out[t * pr : (t + 1) * pr, :] = src[t ^ low, :, col : col + cols].astype(f32)
-                col += cols
-
-    j = pl.program_id(0)
+def place_kernel(chains, layout, me, *refs):
+    bufs, outs = refs[: 2 * len(chains)], refs[2 * len(chains) :]
+    a = pl.program_id(0)
     here = PIECES // 2 // BATCH
-    pl.when(j < here)(lambda: put(x))
-    pl.when(j >= here)(lambda: put(y))
-
-
-def spread(dims, me, x, y, places, previous, name):
-    ins = [me, x, y]
-    pr = x.shape[1]
+    for i, dims in enumerate(chains):
+        flip = flip_of(me[0], dims)
+        low = flip & (BATCH - 1)
+        group = a ^ lax.div(flip, BATCH)
+        pr = bufs[2 * i].shape[1]
+
+        def put(src, i=i, low=low, pr=pr):
+            for t in range(BATCH):
+                for which, col, cols, row0, out, out_col, out_rows in layout:
+                    if which == i:
+                        at = t * out_rows + row0
+                        outs[out][at : at + pr, out_col : out_col + cols] = src[
+                            t ^ low, :, col : col + cols
+                        ].astype(f32)
+
+        pl.when(group < here)(functools.partial(put, bufs[2 * i]))
+        pl.when(group >= here)(functools.partial(put, bufs[2 * i + 1]))
+
+
+def put_in_place(chains, me, layout, shapes, name):
     half = PIECES // 2 // BATCH
-    block = (BATCH,) + x.shape[1:]
-    specs = [
-        pl.BlockSpec(block, lambda j, f: (jnp.minimum(j, half - 1), 0, 0)),
-        pl.BlockSpec(block, lambda j, f: (jnp.maximum(j - half, 0), 0, 0)),
-    ]
-    aliases = {}
-    if previous is not None:
-        for i, g in enumerate(previous):
-            aliases[3 + i] = i
-            ins.append(g)
-            specs.append(pl.BlockSpec(memory_space=pl.ANY))
-
-    def place(col):
-        return lambda j, f: (j ^ lax.div(flip_of(f[0], dims), BATCH), col)
-
-    return pl.pallas_call(
-        functools.partial(spread_kernel, dims, [c for c, _, _ in places], len(places)),
+    ins, specs = [me], []
+
+    def block(dims, second):
+        def index(a, f):
+            group = a ^ lax.div(flip_of(f[0], dims), BATCH)
+            return (jnp.maximum(group - half, 0) if second else jnp.minimum(group, half - 1), 0, 0)
+
+        return index
+
+    for c in chains:
+        for second, x in enumerate(c.out):
+            ins.append(x)
+            specs.append(pl.BlockSpec((BATCH,) + x.shape[1:], block(c.dims, second)))
+    return pl.pallas_call(
+        functools.partial(place_kernel, [c.dims for c in chains], layout),
         grid_spec=pltpu.PrefetchScalarGridSpec(
             num_scalar_prefetch=1,
             grid=(PIECES // BATCH,),
             in_specs=specs,
-            out_specs=[pl.BlockSpec((BATCH * pr, c), place(col)) for c, col, _ in places],
+            out_specs=[
+                pl.BlockSpec((r * BATCH // PIECES, w), lambda a, f: (a, 0)) for r, w in shapes
+            ],
         ),
-        out_shape=[struct((PIECES * pr, w), f32) for _, _, w in places],
-        input_output_aliases=aliases,
+        out_shape=[struct(x, f32) for x in shapes],
         compiler_params=params(24),
-        cost_estimate=cost(1e6, 6 * x.size * 2),
+        cost_estimate=cost(1e6, 6 * sum(x.size for x in ins)),
         name=name,
     )(*ins)
+
+
+SCHEDULE = (
+    "+D up +U -D +D mid -U +U E0 q0 +Q0 -D +D E1 -U +U",
+    "-Q0 +Q0 -D +D q1 +Q1 E2 -D +D -Q1 +Q1 q2 +Q2 -U +U",
+    "-Q0 +Q0 -Q2 +Q2 vec +V -Q1 +Q1 -D +D -U +U -V +V in",
+    "-Q0 +Q0 -Q2 +Q2 -Q1 +Q1 -V +V -Q0 +Q0 -D +D -U +U",
+    "-V +V -Q1 +Q1 -Q2 +Q2 -Q0 +Q0 -U +U -Q2 +Q2 -Q1 +Q1",
+    "-D +D -Q0 +Q0 -Q2 +Q2 -Q1 +Q1 -V +V -Q2 +Q2 -Q0 +Q0",
+    "-U +U -Q1 +Q1 -V -Q2 +Q2 -Q1 +Q1 -Q0 +Q0 -Q2 +Q2",
+    "-D +D -Q0 -Q1 -Q2 =Q -U +U -D =D -U =U",
+)
 
 
 def axis_orders(n):
     rest = [1 << i for i in range(1, n.bit_length() - 1)]
     if n == 32:
         x, y, z, far = rest
-        return [(1, x, z, y, far), (1, y, x, z, far), (1, z, y, x, far)]
-    return [tuple([1] + rest[i:] + rest[:i]) for i in range(PORTIONS)]
+        return {
+            "D": (1, x, y, z, far),
+            "U": (1, z, y, x, far),
+            "Q0": (1, y, z, x, far),
+            "Q1": (1, x, y, z, far),
+            "Q2": (1, y, z, x, far),
+        }
+    names = ("D", "U", "Q0", "Q1", "Q2")
+    return {name: tuple([1] + rest[i:] + rest[:i]) for i, name in enumerate(names)}
 
 
 def body(
@@ -895,10 +991,11 @@
     me = lax.axis_index("dp").astype(i32).reshape(1)
     orders = axis_orders(n)
 
-    packed, attended, lse = attention(seg_lengths, tokens, w_qkv, b_qv)
-    ht, act, slp, n1, i1, n2, i2, nl, emb, ul, query = mid_fwd(
-        seg_lengths, attended, tokens, w_out, b_out, ln1_gain, ln1_bias, w_up, b_up,
-        w_down, b_down, ln2_gain, ln2_bias, w_proj,
+    packed, attended, lse, hid, low, ht, n1, i1 = attention(
+        seg_lengths, tokens, w_qkv, b_qv, w_out, b_out, ln1_gain, ln1_bias
+    )
+    act, slp, n2, i2, nl, emb, ul, query = ffn_fwd(
+        seg_lengths, hid, low, w_up, b_up, w_down, b_down, ln2_gain, ln2_bias, w_proj
     )
 
     msg, dpb = loss_forward(me, seg_lengths, owner, gather_all(query, n), ul)
@@ -906,64 +1003,81 @@
         me, seg_lengths, owner, place, gather_all(msg, n), dpb, emb, nl, n2, i2, ln2_gain, w_proj
     )
 
-    down = Chain(*down_grad(orders[0], me, act, dbr), orders[0], n)
-    down.start()
-    keep, send, din, dsum = up_grad(orders[1], after(me, down.ready), dbr, slp, w_down, ht)
-    up = Chain(keep, send, orders[1], n)
-    down.land(dsum)
-    down.start()
-    up.start()
-    dr1, dpr, dat, sums1 = mid_back(
-        after(me, down.ready, up.ready), din, w_up, dr2, n1, i1, ln1_gain, w_out
-    )
-    up.land(sums1)
-    up.start()
-    parts = [
-        attention_back(0, after(seg_lengths, up.ready), packed, dat, attended, lse)
-    ]
-    down.land(parts[0][3])
-    down.start()
-    parts.append(
-        attention_back(1, after(seg_lengths, down.ready), packed, dat, attended, lse)
-    )
-    down.land(parts[1][3])
-    up.land(parts[1][3])
-    down.start()
-    up.start()
-    parts.append(
-        attention_back(2, after(seg_lengths, down.ready, up.ready), packed, dat, attended, lse)
-    )
-    down.land(parts[2][3])
-    up.land(parts[2][3])
-    down.start()
-    up.start()
-    held = after(me, down.ready, up.ready)
-    vector = collect([x[3] for x in parts], dsum, sums1, sums2)
-    more = []
-    for p in reversed(range(PORTIONS)):
-        keep, send = qkv_grad(
-            p, orders[p], held, tokens, [x[p] for x in parts], attended, dpr, gwp if p == 2 else None
-        )
-        more.append((p, Chain(keep, send, orders[p], n)))
-    d_tokens = input_grad(
-        after(me, *[c.ready for _, c in more]), [x[p] for p in range(3) for x in parts], w_qkv, dr1
-    )
-    down.land()
-    up.land()
-
-    g_w_down = spread(orders[0], me, *down.finish(), [(width, 0, width)], None, "down_place")[0]
-    g_w_up = spread(orders[1], me, *up.finish(), [(ff, 0, ff)], None, "up_place")[0]
-    vector = sum_all(vector, n)
-    grads = None
-    for p, c in more:
-        places = [(width, p, 3 * width), (256, p, width)]
-        if p == 2:
-            places.append((128, 0, 128))
-        out = spread(orders[p], me, *c.finish(), places, grads, "qkv_place")
-        grads = out[:2]
-        if p == 2:
-            g_w_proj = out[2]
-    g_w_qkv, g_w_out = grads
+    chains = {"D": Chain(*down_grad(orders["D"], me, act, dbr, gwp), orders["D"], n)}
+    flying = {}
+    parts = []
+    placed = {}
+    last = None
+
+    def now(x):
+        return after(x, *flying.values()) if flying else x
+
+    def finish(name):
+        for other in ("Q0", "Q1", "Q2") if name == "Q" else (name,):
+            chains[other].finish()
+        if name == "D":
+            layout = [(0, i * width, width, i * width // PIECES, 0, 0, ff // PIECES) for i in range(ff // width)]
+            layout.append((0, ff, w_proj.shape[1], 0, 1, 0, width // PIECES))
+            shapes = [(ff, width), w_proj.shape]
+            placed["D"] = put_in_place([chains["D"]], me, layout, shapes, "down_place")
+        elif name == "U":
+            layout = [(0, 0, ff, 0, 0, 0, width // PIECES)]
+            placed["U"] = put_in_place([chains["U"]], me, layout, [(width, ff)], "up_place")
+        else:
+            span = width // PORTIONS
+            layout = [
+                (c, i * span, span, 0, 0, i * width + c * span, width // PIECES)
+                for c in range(PORTIONS)
+                for i in range(3)
+            ]
+            layout.append((0, width, width, 0, 1, 0, width // PIECES))
+            shapes = [(width, 3 * width), (width, width)]
+            own = [chains["Q%d" % j] for j in range(PORTIONS)]
+            placed["Q"] = put_in_place(own, me, layout, shapes, "qkv_place")
+        return placed[name][0]
+
+    for event in " ".join(SCHEDULE).split():
+        if event[0] == "+":
+            name = event[1:]
+            if chains[name].out is None:
+                chains[name].start()
+                flying[name] = chains[name].ready
+        elif event[0] == "-":
+            name = event[1:]
+            if chains[name].out is None:
+                chains[name].land(*([] if last is None else [last]))
+                flying.pop(name, None)
+                last = chains[name].ready
+        elif event[0] == "=":
+            last = finish(event[1:])
+        elif event == "up":
+            keep, send, din, dsum = up_grad(orders["U"], now(me), dbr, slp, w_down, ht)
+            chains["U"] = Chain(keep, send, orders["U"], n)
+            last = dsum
+        elif event == "mid":
+            dr1, dpr, dat, sums1 = mid_back(now(me), din, w_up, dr2, n1, i1, ln1_gain, w_out)
+            last = sums1
+        elif event[0] == "E":
+            j = int(event[1])
+            parts.append(attention_back(j, now(seg_lengths), packed, dat, attended, lse))
+            last = parts[j][3]
+        elif event[0] == "q":
+            j = int(event[1])
+            outer = [attended, dpr] if j == 0 else []
+            name = "Q%d" % j
+            keep, send = qkv_grad(orders[name], now(me), tokens, parts[j][:3], outer)
+            chains[name] = Chain(keep, send, orders[name], n)
+            last = send
+        elif event == "vec":
+            chains["V"] = Total(collect([x[3] for x in parts], dsum, sums1, sums2), n)
+        elif event == "in":
+            ds = [x[i] for i in range(3) for x in parts]
+            d_tokens = input_grad(now(me), ds, w_qkv, dr1)
+            last = d_tokens
+    g_w_down, g_w_proj = placed["D"]
+    g_w_up = placed["U"][0]
+    g_w_qkv, g_w_out = placed["Q"]
+    vector = chains["V"].finish()
     at = 5 + ff // width
     return (
         loss[0, 0:1], d_tokens, g_w_qkv, vector[0:2].reshape(-1), g_w_out, vector[2], vector[3],

time: 422 us -> 369 us (0.87)
  waiting for transfers between devices: 134 us -> 101 us
  Pallas kernels: 163 us -> 141 us
  local copies, waits for them, and re-layouts: 31 us -> 36.7 us
    ppermute x60, waiting for transfers between devices: 134 us -> 101 us  [swap(): return lax.ppermute(x, 'dp', [(i, i ^ mask) for i in range(n)])]
    pallas_call x13 -> x11, Pallas kernels: 117 us -> 93.9 us  [the longest x1 19.2 us: ffn_fwd(): pl.pallas_call(ffn_fwd_kernel, grid=(steps,), in_specs=specs, out_specs=o...]
    unnamed x100 -> x94, local copies, waits for them, and re-layouts: 28 us -> 33.7 us
  transfers between devices with their start and end apart: 60 -> 60, of which waited for: 29 -> 30; matrix products, arithmetic and copies ran while one was open for 5% -> 6% of each run, Pallas kernels for 24% -> 22%
where the time goes in v2:
time: 369 us; the launch traced here: 365 us
  Pallas kernels  141 us (38%)
  waiting for transfers between devices  101 us (27%)
  starting transfers between devices  63.3 us (17%)
  local copies, waits for them, and re-layouts  36.7 us (10%)
  other arithmetic  21.6 us (6%)
    ppermute x60, waiting for transfers between devices, swap(): return lax.ppermute(x, 'dp', [(i, i ^ mask) for i in range(n)])  101 us
    ppermute x60, starting transfers between devices, swap(): return lax.ppermute(x, 'dp', [(i, i ^ mask) for i in range(n)])  63.3 us
    pallas_call x3, Pallas kernels, attention_back(): pl.pallas_call(functools.partial(attn_bwd_kernel, part), in_specs=[SMEM]...  34.3 us
    unnamed x94, local copies, waits for them, and re-layouts  33.7 us
    pallas_call x1, Pallas kernels, ffn_fwd(): pl.pallas_call(ffn_fwd_kernel, grid=(steps,), in_specs=specs, out_specs=o...  19.2 us
    pallas_call x1, Pallas kernels, attention(): pl.pallas_call(attn_fwd_kernel, in_specs=[SMEM] + [VMEM] * 7, out_specs=[...  17.9 us
    pallas_call x3, Pallas kernels, put_in_place(): pl.pallas_call(functools.partial(place_kernel, [c.dims for c in chains],...  17.5 us
    pallas_call x1, Pallas kernels, up_grad(): pl.pallas_call(functools.partial(up_grad_kernel, dims), grid=(ff // FF_CH...  14.7 us
  transfers between devices with their start and end apart: 60, of which 30 were waited for; matrix products, arithmetic and copies ran while one was open for 6% of the time, Pallas kernels for 22%

profile of v2, /device:TPU:0, one launch (start us, length us, event | category | flops | bytes accessed | tf_op | source)
XLA Modules:
  0.0 365.2 jit_solution(3706174433576546330)
XLA Ops:
  0.7 2.1 copy-done.3
  2.8 1.7 copy-done.5
  9.3 17.9 %attention_forward.1 = (bf16[1024,2304]{1,0:T(8,128)(2,1)S(1)}, bf16[1024,768]{1,0:T(8,128)(2,1)S(1)}, f32[6,8,256]{2,1,0:T(8,128)S(1)}, f32[1024,768]{1,0:T(8,1...) custom-call(s32[1,6]{1,0:T(1,128)S(1)} %copy-done.19, ...), custom_call_target="tpu_custom_call" | custom-call | flops 17999998976 | bytes 6291456 | tf_op jit(solution)/shard_map/attention_forward/pallas_call | solution.py:266
  27.2 2.2 copy-done.36
  30.7 19.2 %ffn_forward.1 = (bf16[1024,3072]{1,0:T(8,128)(2,1)}, bf16[1024,3072]{1,0:T(8,128)(2,1)}, bf16[1024,768]{1,0:T(8,128)(2,1)S(1)}, f32[1024,1]{1,0:T(8,128)S(1)}, ...) custom-call(s32[1,6]{1,0:T(1,128)S(1)} %copy-done.20, ...), custom_call_target="tpu_custom_call" | custom-call | flops 17999998976 | bytes 40000000 | tf_op jit(solution)/shard_map/ffn_forward/pallas_call | solution.py:389
  52.3 4.0 %collective-permute-start = (bf16[1,48,128]{2,1,0:T(8,128)(2,1)S(1)}, bf16[1,48,128]{2,1,0:T(8,128)(2,1)S(1)}, u32[]{:S(2)}, u32[]{:S(2)}) collective-permute-start(bf16[1,48,128]{2,1,0:T(8,128)(2,1)S(1)} %get-tuple-element.131), channel_id=1, source_target_pairs={{0,16},{1,17},{2,18},{3,19},{4,20},{5,21},{6,22},{7,23},{8,24},{9,... | collective-permute-start | bytes 36872 | tf_op jit(solution)/shard_map/ppermute | solution.py:818
  56.3 1.7 collective-permute-done
  58.9 2.9 collective-permute-done.1
  61.9 1.5 collective-permute-start.2
  63.6 2.4 collective-permute-done.2
  66.1 1.9 collective-permute-start.3
  68.2 2.6 collective-permute-done.3
  72.5 1.9 loss_forward.1
  74.4 3.0 collective-permute-start.5
  77.4 3.0 collective-permute-done.5
  81.0 4.1 %collective-permute-done.6 = bf16[2,176,128]{2,1,0:T(8,128)(2,1)S(1)} collective-permute-done((bf16[2,176,128]{2,1,0:T(8,128)(2,1)S(1)}, bf16[2,176,128]{2,1,0:T(8,128)(2,1)S(1)}, u32[]{:S(2)}, u32[]{:S(2)}) %collective-permute-start.6) | collective-permute-done | bytes 90144 | tf_op jit(solution)/shard_map/ppermute | solution.py:818
  85.8 4.9 %collective-permute-done.7 = bf16[4,176,128]{2,1,0:T(8,128)(2,1)S(1)} collective-permute-done((bf16[4,176,128]{2,1,0:T(8,128)(2,1)S(1)}, bf16[4,176,128]{2,1,0:T(8,128)(2,1)S(1)}, u32[]{:S(2)}, u32[]{:S(2)}) %collective-permute-start.7) | collective-permute-done | bytes 180256 | tf_op jit(solution)/shard_map/ppermute | solution.py:818
  92.3 6.1 %collective-permute-done.8 = bf16[8,176,128]{2,1,0:T(8,128)(2,1)S(1)} collective-permute-done((bf16[8,176,128]{2,1,0:T(8,128)(2,1)S(1)}, bf16[8,176,128]{2,1,0:T(8,128)(2,1)S(1)}, u32[]{:S(2)}, u32[]{:S(2)}) %collective-permute-start.8) | collective-permute-done | bytes 360480 | tf_op jit(solution)/shard_map/ppermute | solution.py:818
  99.4 2.4 collective-permute-done.9
  104.8 4.9 %loss_backward.1 = (f32[8,128]{1,0:T(8,128)S(1)}, f32[1024,768]{1,0:T(8,128)S(1)}, bf16[1024,768]{1,0:T(8,128)(2,1)S(1)}, f32[768,128]{1,0:T(8,128)S(1)}, f32[8,768]{1,0:T(8,128)S(1)}) custom-call(s32[1]{0:T(128)} %bitcast.me, s32[1,6]{1,0:T(1,128)S(1)} %copy-done.20, s32[32,5]{1,0:T(8,128)S(1)} %copy.33.owner, s32[32,5]{1,0:T(8,128)S(1)} %copy.34.place, ...), custom_call_target="tpu_custom_call" | custom-call | flops 6000000000 | bytes 10000000 | tf_op jit(solution)/shard_map/loss_backward/pallas_call | solution.py:559
  109.8 1.7 copy-done.28
  111.5 3.4 copy-done.21
  114.8 7.7 %down_gradient.1 = (f32[8,48,3200]{2,1,0:T(8,128)S(1)}, f32[8,48,3200]{2,1,0:T(8,128)}) custom-call(s32[1]{0:T(128)} %bitcast.me, bf16[1024,3072]{1,0:T(8,128)(2,1)S(1)} %copy-done.21, bf16[1024,768]{1,0:T(8,128)(2,1)S(1)} %get-tuple-element.141.dbr, f32[768,128]{1,0:T(8,128)S(1)} %get-tuple-element.142.gwp), custom_call_target="tpu_custom_call" | custom-call | flops 5000000000 | bytes 17000000 | tf_op jit(solution)/shard_map/down_gradient/pallas_call | solution.py:614
  122.6 2.3 copy-done
  127.8 14.7 %up_gradient.1 = (f32[8,48,3072]{2,1,0:T(8,128)S(1)}, f32[8,48,3072]{2,1,0:T(8,128)}, bf16[1024,3072]{1,0:T(8,128)(2,1)}, f32[1,3072]{1,0:T(1,128)S(1)}) custom-call(s32[1]{0:T(128)} %bitcast.me, bf16[1024,768]{1,0:T(8,128)(2,1)S(1)} %copy-done.27, bf16[1024,3072]{1,0:T(8,128)(2,1)} %get-tuple-element.146.slp, bf16[3072,768]{1,0:T(8,128)(2,1)S(1)} %copy-done, ...), custom_call_target="tpu_custom_call" | custom-call | flops 10000000000 | bytes 30000000 | tf_op jit(solution)/shard_map/up_gradient/pallas_call | solution.py:650
  142.9 4.9 %slice_add_fusion = (f32[4,48,3200]{2,1,0:T(8,128)}, bf16[4,48,3200]{2,1,0:T(8,128)(2,1)}) fusion(f32[8,48,3200]{2,1,0:T(8,128)} %collective-permute-done.10, f32[8,48,3200]{2,1,0:T(8,128)S(1)} %get-tuple-element.143), kind=kLoop, calls=%fused_computation.1 | loop fusion | flops 1843200 | bytes 13516800 | tf_op jit(solution)/shard_map/add | solution.py:855
  149.2 2.3 copy-done.2
  151.5 11.1 %middle_backward.1 = (f32[1024,768]{1,0:T(8,128)S(1)}, bf16[1024,768]{1,0:T(8,128)(2,1)S(1)}, bf16[1024,768]{1,0:T(8,128)(2,1)S(1)}, f32[8,768]{1,0:T(8,128)S(1)}) custom-call(s32[1]{0:T(128)} %bitcast.me, bf16[1024,3072]{1,0:T(8,128)(2,1)} %get-tuple-element.153.din, bf16[768,3072]{1,0:T(8,128)(2,1)S(1)} %copy-done.2, f32[1024,768]{1,0:T(8,128)S(1)} %copy-done.29, ...), custom_call_target="tpu_custom_call" | custom-call | flops 8999999488 | bytes 15000000 | tf_op jit(solution)/shard_map/middle_backward/pallas_call | solution.py:718
  163.8 4.9 %slice_add_fusion.1 = (f32[4,48,3072]{2,1,0:T(8,128)}, bf16[4,48,3072]{2,1,0:T(8,128)(2,1)}) fusion(f32[8,48,3072]{2,1,0:T(8,128)} %collective-permute-done.11, f32[8,48,3072]{2,1,0:T(8,128)S(1)} %get-tuple-element.150), kind=kLoop, calls=%fused_computation.4 | loop fusion | flops 1769472 | bytes 12976128 | tf_op jit(solution)/shard_map/add | solution.py:855
  169.8 2.3 copy-done.37
  172.1 11.3 %attention_backward.3 = (bf16[1024,256]{1,0:T(8,128)(2,1)S(1)}, bf16[1024,256]{1,0:T(8,128)(2,1)S(1)}, bf16[1024,256]{1,0:T(8,128)(2,1)S(1)}, f32[8,256]{1,0:T(8,128)S(1)}) custom-call(s32[1,6]{1,0:T(1,128)S(1)} %copy-done.20, bf16[1024,2304]{1,0:T(8,128)(2,1)S(1)} %copy-done.37, bf16[1024,768]{1,0:T(8,128)(2,1)S(1)} %get-tuple-element.162.do, ...), custom_call_target="tpu_custom_call" | custom-call | flops 10000000000 | bytes 4194304 | tf_op jit(solution)/shard_map/attention_backward/pallas_call | solution.py:292
  183.5 2.8 qkv_gradient.3
  186.4 1.6 convert_element_type.152
  189.9 11.6 %attention_backward.4 = (bf16[1024,256]{1,0:T(8,128)(2,1)S(1)}, bf16[1024,256]{1,0:T(8,128)(2,1)S(1)}, bf16[1024,256]{1,0:T(8,128)(2,1)S(1)}, f32[8,256]{1,0:T(8,128)S(1)}) custom-call(s32[1,6]{1,0:T(1,128)S(1)} %copy-done.20, bf16[1024,2304]{1,0:T(8,128)(2,1)S(1)} %bitcast.91, bf16[1024,768]{1,0:T(8,128)(2,1)S(1)} %get-tuple-element.162.do, ...), custom_call_target="tpu_custom_call" | custom-call | flops 10000000000 | bytes 4194304 | tf_op jit(solution)/shard_map/attention_backward/pallas_call | solution.py:292
  204.5 1.6 collective-permute-start.15
  209.0 11.4 %attention_backward.5 = (bf16[1024,256]{1,0:T(8,128)(2,1)S(1)}, bf16[1024,256]{1,0:T(8,128)(2,1)S(1)}, bf16[1024,256]{1,0:T(8,128)(2,1)S(1)}, f32[8,256]{1,0:T(8,128)S(1)}) custom-call(s32[1,6]{1,0:T(1,128)S(1)} %copy-done.20, bf16[1024,2304]{1,0:T(8,128)(2,1)S(1)} %bitcast.91, bf16[1024,768]{1,0:T(8,128)(2,1)S(1)} %get-tuple-element.162.do, ...), custom_call_target="tpu_custom_call" | custom-call | flops 10000000000 | bytes 4194304 | tf_op jit(solution)/shard_map/attention_backward/pallas_call | solution.py:292
  221.1 3.5 collective-permute-start.22
  227.9 3.6 collective-permute-done.15
  234.2 4.8 %collective-permute-done.22 = bf16[1,48,3200]{2,1,0:T(8,128)(2,1)S(1)} collective-permute-done((bf16[1,48,3200]{2,1,0:T(8,128)(2,1)S(1)}, bf16[1,48,3200]{2,1,0:T(8,128)(2,1)S(1)}, u32[]{:S(2)}, u32[]{:S(2)}) %collective-permute-start.22) | collective-permute-done | bytes 307232 | tf_op jit(solution)/shard_map/ppermute | solution.py:818
  241.5 2.9 collective-permute-start.34
  245.6 5.6 %input_gradient.1 = f32[1024,768]{1,0:T(8,128)} custom-call(s32[1]{0:T(128)} %bitcast.me, bf16[1024,256]{1,0:T(8,128)(2,1)S(1)} %get-tuple-element.165.d0.refs_0_, bf16[1024,256]{1,0:T(8,128)(2,1)S(1)} %get-tuple-element.178.d0.refs_1_, bf16[1024,256]{1,0:T(8,128)(2,1)S(1)} %get-tuple-element.188.d0.refs_2_, ...), custom_call_target="tpu_custom_call" | custom-call | flops 5000000000 | bytes 15000000 | tf_op jit(solution)/shard_map/input_gradient/pallas_call | solution.py:778
  251.1 1.8 collective-permute-start.35
  253.0 1.6 collective-permute-start.26
  258.6 4.2 %collective-permute-done.35 = bf16[1,48,3200]{2,1,0:T(8,128)(2,1)S(1)} collective-permute-done((bf16[1,48,3200]{2,1,0:T(8,128)(2,1)S(1)}, bf16[1,48,3200]{2,1,0:T(8,128)(2,1)S(1)}, u32[]{:S(2)}, u32[]{:S(2)}) %collective-permute-start.35) | collective-permute-done | bytes 307232 | tf_op jit(solution)/shard_map/ppermute | solution.py:818
  269.0 2.1 collective-permute-start.38
  271.1 2.7 collective-permute-done.30
  273.9 2.1 collective-permute-start.36
  276.1 2.1 collective-permute-done.39
  280.4 2.9 collective-permute-start.45
  286.5 2.3 collective-permute-done.43
  289.0 2.0 collective-permute-done.41
  291.6 1.6 collective-permute-start.47
  293.3 14.5 %collective-permute-done.47 = bf16[2,48,768]{2,1,0:T(8,128)(2,1)S(1)} collective-permute-done((bf16[2,48,768]{2,1,0:T(8,128)(2,1)S(1)}, bf16[2,48,768]{2,1,0:T(8,128)(2,1)S(1)}, u32[]{:S(2)}, u32[]{:S(2)}) %collective-permute-start.47) | collective-permute-done | bytes 147488 | tf_op jit(solution)/shard_map/ppermute | solution.py:818
  308.7 2.1 collective-permute-start.50
  310.8 1.7 collective-permute-start.53
  312.8 4.7 %collective-permute-done.51 = f32[16,768]{1,0:T(8,128)S(1)} collective-permute-done((f32[16,768]{1,0:T(8,128)S(1)}, f32[16,768]{1,0:T(8,128)S(1)}, u32[]{:S(2)}, u32[]{:S(2)}) %collective-permute-start.51) | collective-permute-done | bytes 49184 | tf_op jit(solution)/shard_map/ppermute | solution.py:818
  318.2 2.7 collective-permute-start.57
  321.2 8.8 %collective-permute-done.54 = bf16[4,48,768]{2,1,0:T(8,128)(2,1)S(1)} collective-permute-done((bf16[4,48,768]{2,1,0:T(8,128)(2,1)S(1)}, bf16[4,48,768]{2,1,0:T(8,128)(2,1)S(1)}, u32[]{:S(2)}, u32[]{:S(2)}) %collective-permute-start.54) | collective-permute-done | bytes 294944 | tf_op jit(solution)/shard_map/ppermute | solution.py:818
  330.2 10.9 %collective-permute-done.53 = bf16[4,48,3200]{2,1,0:T(8,128)(2,1)S(1)} collective-permute-done((bf16[4,48,3200]{2,1,0:T(8,128)(2,1)S(1)}, bf16[4,48,3200]{2,1,0:T(8,128)(2,1)S(1)}, u32[]{:S(2)}, u32[]{:S(2)}) %collective-permute-start.53) | collective-permute-done | bytes 1228832 | tf_op jit(solution)/shard_map/ppermute | solution.py:818
  341.5 4.0 %qkv_place.1 = (f32[768,2304]{1,0:T(8,128)}, f32[768,768]{1,0:T(8,128)}) custom-call(s32[1]{0:T(128)} %bitcast.me, bf16[8,48,1536]{2,1,0:T(8,128)(2,1)S(1)} %bitcast_select_fusion.4.refs_0_, bf16[8,48,1536]{2,1,0:T(8,128)(2,1)S(1)} %collective-permute-done.52.refs_1_, bf16[8,48,768]{2,1,0:T(8,128)(2,1)S(1)} %bitcast_select_fusion.8.refs_2_, ...), custom_call_target="tpu_custom_call" | custom-call | flops 1000000 | bytes 14155782 | tf_op jit(solution)/shard_map/qkv_place/pallas_call | solution.py:940
  345.5 2.0 collective-permute-done.57
  347.5 1.7 bitcast_select_fusion.1.refs_0_
  351.6 6.6 %down_place.1 = (f32[3072,768]{1,0:T(8,128)}, f32[768,128]{1,0:T(8,128)}) custom-call(s32[1]{0:T(128)} %bitcast.me, bf16[8,48,3200]{2,1,0:T(8,128)(2,1)S(1)} %bitcast_select_fusion.refs_0_, bf16[8,48,3200]{2,1,0:T(8,128)(2,1)} %collective-permute-done.59.refs_1_), custom_call_target="tpu_custom_call" | custom-call | flops 1000000 | bytes 14745606 | tf_op jit(solution)/shard_map/down_place/pallas_call | solution.py:940
  358.2 6.9 %up_place.1 = f32[768,3072]{1,0:T(8,128)} custom-call(s32[1]{0:T(128)} %bitcast.me, bf16[8,48,3072]{2,1,0:T(8,128)(2,1)} %bitcast_select_fusion.1.refs_0_, bf16[8,48,3072]{2,1,0:T(8,128)(2,1)} %collective-permute-done.58.refs_1_), custom_call_target="tpu_custom_call" | custom-call | flops 1000000 | bytes 14155782 | tf_op jit(solution)/shard_map/up_place/pallas_call | solution.py:940
  (249 shorter events, 65.2 us)
Async XLA Ops:
  0.6 30.0 %copy-start.1 = (bf16[768,3072]{1,0:T(8,128)(2,1)S(1)}, bf16[768,3072]{1,0:T(8,128)(2,1)}, u32[]{:S(2)}) copy-start(bf16[768,3072]{1,0:T(8,128)(2,1)} %wu.3) | copy-start | bytes 14155780
  30.7 40.4 %copy-start.42 = (s32[32,5]{0,1:T(8,128)S(1)}, s32[32,5]{0,1:T(8,128)}, u32[]{:S(2)}) copy-start(s32[32,5]{0,1:T(8,128)} %param.19) | copy-start | bytes 1924
  52.3 5.7 %collective-permute-start = (bf16[1,48,128]{2,1,0:T(8,128)(2,1)S(1)}, bf16[1,48,128]{2,1,0:T(8,128)(2,1)S(1)}, u32[]{:S(2)}, u32[]{:S(2)}) collective-permute-start(bf16[1,48,128]{2,1,0:T(8,128)(2,1)S(1)} %get-tuple-element.131), channel_id=1, source_target_pairs={{0,16},{1,17},{2,18},{3,19},{4,20},{5,21},{6,22},{7,23},{8,24},{9,... | collective-permute-start | bytes 36872 | tf_op jit(solution)/shard_map/ppermute | solution.py:818
  58.0 3.8 %collective-permute-start.1 = (bf16[2,48,128]{2,1,0:T(8,128)(2,1)S(1)}, bf16[2,48,128]{2,1,0:T(8,128)(2,1)S(1)}, u32[]{:S(2)}, u32[]{:S(2)}) collective-permute-start(bf16[2,48,128]{2,1,0:T(8,128)(2,1)S(1)} %broadcast_select_fusion.6), channel_id=1, source_target_pairs={{0,8},{1,9},{2,10},{3,11},{4,12},{5,13},{6,14},{7,15},{8,0},{9,1},... | collective-permute-start | bytes 73736 | tf_op jit(solution)/shard_map/ppermute | solution.py:818
  61.9 4.1 %collective-permute-start.2 = (bf16[4,48,128]{2,1,0:T(8,128)(2,1)S(1)}, bf16[4,48,128]{2,1,0:T(8,128)(2,1)S(1)}, u32[]{:S(2)}, u32[]{:S(2)}) collective-permute-start(bf16[4,48,128]{2,1,0:T(8,128)(2,1)S(1)} %bitcast_select_fusion.17), channel_id=1, source_target_pairs={{0,4},{1,5},{2,6},{3,7},{4,0},{5,1},{6,2},{7,3},{8,12},{9,13},{10,... | collective-permute-start | bytes 147464 | tf_op jit(solution)/shard_map/ppermute | solution.py:818
  66.1 4.7 %collective-permute-start.3 = (bf16[8,48,128]{2,1,0:T(8,128)(2,1)S(1)}, bf16[8,48,128]{2,1,0:T(8,128)(2,1)S(1)}, u32[]{:S(2)}, u32[]{:S(2)}) collective-permute-start(bf16[8,48,128]{2,1,0:T(8,128)(2,1)S(1)} %bitcast_select_fusion.16), channel_id=1, source_target_pairs={{0,2},{1,3},{2,0},{3,1},{4,6},{5,7},{6,4},{7,5},{8,10},{9,11},{10,... | collective-permute-start | bytes 294920 | tf_op jit(solution)/shard_map/ppermute | solution.py:818
  70.9 1.5 collective-permute-start.4
  74.4 24.9 %copy-start.43 = (s32[32,5]{0,1:T(8,128)S(1)}, s32[32,5]{0,1:T(8,128)}, u32[]{:S(2)}) copy-start(s32[32,5]{0,1:T(8,128)} %param.20) | copy-start | bytes 1924
  74.4 6.0 %collective-permute-start.5 = (bf16[1,176,128]{2,1,0:T(8,128)(2,1)S(1)}, bf16[1,176,128]{2,1,0:T(8,128)(2,1)S(1)}, u32[]{:S(2)}, u32[]{:S(2)}) collective-permute-start(bf16[1,176,128]{2,1,0:T(8,128)(2,1)S(1)} %get-tuple-element.133), channel_id=1, source_target_pairs={{0,16},{1,17},{2,18},{3,19},{4,20},{5,21},{6,22},{7,23},{8,24},{9,... | collective-permute-start | bytes 135176 | tf_op jit(solution)/shard_map/ppermute | solution.py:818
  80.5 4.6 %collective-permute-start.6 = (bf16[2,176,128]{2,1,0:T(8,128)(2,1)S(1)}, bf16[2,176,128]{2,1,0:T(8,128)(2,1)S(1)}, u32[]{:S(2)}, u32[]{:S(2)}) collective-permute-start(bf16[2,176,128]{2,1,0:T(8,128)(2,1)S(1)} %broadcast_select_fusion.5), channel_id=1, source_target_pairs={{0,8},{1,9},{2,10},{3,11},{4,12},{5,13},{6,14},{7,15},{8,0},{9,1},... | collective-permute-start | bytes 270344 | tf_op jit(solution)/shard_map/ppermute | solution.py:818
  85.2 5.6 %collective-permute-start.7 = (bf16[4,176,128]{2,1,0:T(8,128)(2,1)S(1)}, bf16[4,176,128]{2,1,0:T(8,128)(2,1)S(1)}, u32[]{:S(2)}, u32[]{:S(2)}) collective-permute-start(bf16[4,176,128]{2,1,0:T(8,128)(2,1)S(1)} %bitcast_select_fusion.15), channel_id=1, source_target_pairs={{0,4},{1,5},{2,6},{3,7},{4,0},{5,1},{6,2},{7,3},{8,12},{9,13},{10,... | collective-permute-start | bytes 540680 | tf_op jit(solution)/shard_map/ppermute | solution.py:818
  90.9 7.5 %collective-permute-start.8 = (bf16[8,176,128]{2,1,0:T(8,128)(2,1)S(1)}, bf16[8,176,128]{2,1,0:T(8,128)(2,1)S(1)}, u32[]{:S(2)}, u32[]{:S(2)}) collective-permute-start(bf16[8,176,128]{2,1,0:T(8,128)(2,1)S(1)} %bitcast_select_fusion.11), channel_id=1, source_target_pairs={{0,2},{1,3},{2,0},{3,1},{4,6},{5,7},{6,4},{7,5},{8,10},{9,11},{10,... | collective-permute-start | bytes 1081352 | tf_op jit(solution)/shard_map/ppermute | solution.py:818
  99.3 2.5 collective-permute-start.9
  122.5 20.4 %collective-permute-start.10 = (f32[8,48,3200]{2,1,0:T(8,128)}, f32[8,48,3200]{2,1,0:T(8,128)}, u32[]{:S(2)}, u32[]{:S(2)}) collective-permute-start(f32[8,48,3200]{2,1,0:T(8,128)} %get-tuple-element.144), channel_id=1, source_target_pairs={{0,1},{1,0},{2,3},{3,2},{4,5},{5,4},{6,7},{7,6},{8,9},{9,8},{10,11... | collective-permute-start | bytes 14745608 | tf_op jit(solution)/shard_map/ppermute | solution.py:818
  142.5 21.2 %collective-permute-start.11 = (f32[8,48,3072]{2,1,0:T(8,128)}, f32[8,48,3072]{2,1,0:T(8,128)}, u32[]{:S(2)}, u32[]{:S(2)}) collective-permute-start(f32[8,48,3072]{2,1,0:T(8,128)} %get-tuple-element.151), channel_id=1, source_target_pairs={{0,1},{1,0},{2,3},{3,2},{4,5},{5,4},{6,7},{7,6},{8,9},{9,8},{10,11... | collective-permute-start | bytes 14155784 | tf_op jit(solution)/shard_map/ppermute | solution.py:818
  147.8 38.5 %collective-permute-start.14 = (bf16[4,48,3200]{2,1,0:T(8,128)(2,1)}, bf16[4,48,3200]{2,1,0:T(8,128)(2,1)}, u32[]{:S(2)}, u32[]{:S(2)}) collective-permute-start(bf16[4,48,3200]{2,1,0:T(8,128)(2,1)} %get-tuple-element.250), channel_id=1, source_target_pairs={{0,2},{1,3},{2,0},{3,1},{4,6},{5,7},{6,4},{7,5},{8,10},{9,11},{10,... | collective-permute-start | bytes 3686408 | tf_op jit(solution)/shard_map/ppermute | solution.py:818
  163.8 26.1 %slice-start = ((s8[4718592]{0:T(1024)(128)(4,1)}), s8[4194304]{0:T(1024)(128)(4,1)S(1)}, s32[]{:S(2)}) async-start(s8[4718592]{0:T(1024)(128)(4,1)} %bitcast.90), calls=%async_computation | async-start | bytes 8388608
  168.7 32.8 %collective-permute-start.13 = (bf16[4,48,3072]{2,1,0:T(8,128)(2,1)}, bf16[4,48,3072]{2,1,0:T(8,128)(2,1)S(1)}, u32[]{:S(2)}, u32[]{:S(2)}) collective-permute-start(bf16[4,48,3072]{2,1,0:T(8,128)(2,1)} %get-tuple-element.252), channel_id=1, source_target_pairs={{0,8},{1,9},{2,10},{3,11},{4,12},{5,13},{6,14},{7,15},{8,0},{9,1},... | collective-permute-start | bytes 3538952 | tf_op jit(solution)/shard_map/ppermute | solution.py:818
  186.3 17.8 %collective-permute-start.12 = (f32[8,48,1536]{2,1,0:T(8,128)S(1)}, f32[8,48,1536]{2,1,0:T(8,128)S(1)}, u32[]{:S(2)}, u32[]{:S(2)}) collective-permute-start(f32[8,48,1536]{2,1,0:T(8,128)S(1)} %get-tuple-element.170), channel_id=1, source_target_pairs={{0,1},{1,0},{2,3},{3,2},{4,5},{5,4},{6,7},{7,6},{8,9},{9,8},{10,11... | collective-permute-start | bytes 7077896 | tf_op jit(solution)/shard_map/ppermute | solution.py:818
  188.6 17.4 %collective-permute-start.17 = (bf16[2,48,3200]{2,1,0:T(8,128)(2,1)S(1)}, bf16[2,48,3200]{2,1,0:T(8,128)(2,1)S(1)}, u32[]{:S(2)}, u32[]{:S(2)}) collective-permute-start(bf16[2,48,3200]{2,1,0:T(8,128)(2,1)S(1)} %get-tuple-element.254), channel_id=1, source_target_pairs={{0,4},{1,5},{2,6},{3,7},{4,0},{5,1},{6,2},{7,3},{8,12},{9,13},{10,... | collective-permute-start | bytes 1843208 | tf_op jit(solution)/shard_map/ppermute | solution.py:818
  203.5 24.1 %collective-permute-start.16 = (bf16[2,48,3072]{2,1,0:T(8,128)(2,1)S(1)}, bf16[2,48,3072]{2,1,0:T(8,128)(2,1)S(1)}, u32[]{:S(2)}, u32[]{:S(2)}) collective-permute-start(bf16[2,48,3072]{2,1,0:T(8,128)(2,1)S(1)} %get-tuple-element.258), channel_id=1, source_target_pairs={{0,4},{1,5},{2,6},{3,7},{4,0},{5,1},{6,2},{7,3},{8,12},{9,13},{10,... | collective-permute-start | bytes 1769480 | tf_op jit(solution)/shard_map/ppermute | solution.py:818
  204.5 27.0 %collective-permute-start.15 = (bf16[4,48,1536]{2,1,0:T(8,128)(2,1)S(1)}, bf16[4,48,1536]{2,1,0:T(8,128)(2,1)S(1)}, u32[]{:S(2)}, u32[]{:S(2)}) collective-permute-start(bf16[4,48,1536]{2,1,0:T(8,128)(2,1)S(1)} %get-tuple-element.256), channel_id=1, source_target_pairs={{0,4},{1,5},{2,6},{3,7},{4,0},{5,1},{6,2},{7,3},{8,12},{9,13},{10,... | collective-permute-start | bytes 1769480 | tf_op jit(solution)/shard_map/ppermute | solution.py:818
  206.2 14.8 %collective-permute-start.18 = (bf16[1,48,3200]{2,1,0:T(8,128)(2,1)S(1)}, bf16[1,48,3200]{2,1,0:T(8,128)(2,1)S(1)}, u32[]{:S(2)}, u32[]{:S(2)}) collective-permute-start(bf16[1,48,3200]{2,1,0:T(8,128)(2,1)S(1)} %fusion.2), channel_id=1, source_target_pairs={{0,8},{1,9},{2,10},{3,11},{4,12},{5,13},{6,14},{7,15},{8,0},{9,1},... | collective-permute-start | bytes 921608 | tf_op jit(solution)/shard_map/ppermute | solution.py:818
  208.9 15.8 %collective-permute-start.19 = (f32[8,48,768]{2,1,0:T(8,128)S(1)}, f32[8,48,768]{2,1,0:T(8,128)S(1)}, u32[]{:S(2)}, u32[]{:S(2)}) collective-permute-start(f32[8,48,768]{2,1,0:T(8,128)S(1)} %get-tuple-element.181), channel_id=1, source_target_pairs={{0,1},{1,0},{2,3},{3,2},{4,5},{5,4},{6,7},{7,6},{8,9},{9,8},{10,11... | collective-permute-start | bytes 3538952 | tf_op jit(solution)/shard_map/ppermute | solution.py:818
  220.3 19.8 %collective-permute-start.24 = (f32[16,768]{1,0:T(8,128)S(1)}, f32[16,768]{1,0:T(8,128)S(1)}, u32[]{:S(2)}, u32[]{:S(2)}) collective-permute-start(f32[16,768]{1,0:T(8,128)S(1)} %collect_vectors.1), channel_id=1, source_target_pairs={{0,1},{1,0},{2,3},{3,2},{4,5},{5,4},{6,7},{7,6},{8,9},{9,8},{10,11... | collective-permute-start | bytes 147464 | tf_op jit(solution)/shard_map/ppermute | solution.py:818
  221.1 17.8 %collective-permute-start.22 = (bf16[1,48,3200]{2,1,0:T(8,128)(2,1)S(1)}, bf16[1,48,3200]{2,1,0:T(8,128)(2,1)S(1)}, u32[]{:S(2)}, u32[]{:S(2)}) collective-permute-start(bf16[1,48,3200]{2,1,0:T(8,128)(2,1)S(1)} %fusion.4), channel_id=1, source_target_pairs={{0,16},{1,17},{2,18},{3,19},{4,20},{5,21},{6,22},{7,23},{8,24},{9,... | collective-permute-start | bytes 921608 | tf_op jit(solution)/shard_map/ppermute | solution.py:818
  224.9 9.2 %collective-permute-start.21 = (bf16[4,48,768]{2,1,0:T(8,128)(2,1)S(1)}, bf16[4,48,768]{2,1,0:T(8,128)(2,1)S(1)}, u32[]{:S(2)}, u32[]{:S(2)}) collective-permute-start(bf16[4,48,768]{2,1,0:T(8,128)(2,1)S(1)} %get-tuple-element.264), channel_id=1, source_target_pairs={{0,2},{1,3},{2,0},{3,1},{4,6},{5,7},{6,4},{7,5},{8,10},{9,11},{10,... | collective-permute-start | bytes 884744 | tf_op jit(solution)/shard_map/ppermute | solution.py:818
  227.6 5.0 %collective-permute-start.20 = (f32[8,48,768]{2,1,0:T(8,128)S(1)}, f32[8,48,768]{2,1,0:T(8,128)S(1)}, u32[]{:S(2)}, u32[]{:S(2)}) collective-permute-start(f32[8,48,768]{2,1,0:T(8,128)S(1)} %get-tuple-element.191), channel_id=1, source_target_pairs={{0,1},{1,0},{2,3},{3,2},{4,5},{5,4},{6,7},{7,6},{8,9},{9,8},{10,11... | collective-permute-start | bytes 3538952 | tf_op jit(solution)/shard_map/ppermute | solution.py:818
  231.5 8.6 %collective-permute-start.23 = (bf16[1,48,3072]{2,1,0:T(8,128)(2,1)S(1)}, bf16[1,48,3072]{2,1,0:T(8,128)(2,1)S(1)}, u32[]{:S(2)}, u32[]{:S(2)}) collective-permute-start(bf16[1,48,3072]{2,1,0:T(8,128)(2,1)S(1)} %fusion.8), channel_id=1, source_target_pairs={{0,2},{1,3},{2,0},{3,1},{4,6},{5,7},{6,4},{7,5},{8,10},{9,11},{10,... | collective-permute-start | bytes 884744 | tf_op jit(solution)/shard_map/ppermute | solution.py:818
  232.6 18.5 %collective-permute-start.25 = (bf16[2,48,1536]{2,1,0:T(8,128)(2,1)S(1)}, bf16[2,48,1536]{2,1,0:T(8,128)(2,1)S(1)}, u32[]{:S(2)}, u32[]{:S(2)}) collective-permute-start(bf16[2,48,1536]{2,1,0:T(8,128)(2,1)S(1)} %get-tuple-element.262), channel_id=1, source_target_pairs={{0,8},{1,9},{2,10},{3,11},{4,12},{5,13},{6,14},{7,15},{8,0},{9,1},... | collective-permute-start | bytes 884744 | tf_op jit(solution)/shard_map/ppermute | solution.py:818
  240.2 15.3 %collective-permute-start.27 = (f32[16,768]{1,0:T(8,128)S(1)}, f32[16,768]{1,0:T(8,128)S(1)}, u32[]{:S(2)}, u32[]{:S(2)}) collective-permute-start(f32[16,768]{1,0:T(8,128)S(1)} %add.157), channel_id=1, source_target_pairs={{0,2},{1,3},{2,0},{3,1},{4,6},{5,7},{6,4},{7,5},{8,10},{9,11},{10,... | collective-permute-start | bytes 147464 | tf_op jit(solution)/shard_map/ppermute | solution.py:818
  241.3 13.4 %collective-permute-start.28 = (bf16[2,48,768]{2,1,0:T(8,128)(2,1)S(1)}, bf16[2,48,768]{2,1,0:T(8,128)(2,1)S(1)}, u32[]{:S(2)}, u32[]{:S(2)}) collective-permute-start(bf16[2,48,768]{2,1,0:T(8,128)(2,1)S(1)} %get-tuple-element.268), channel_id=1, source_target_pairs={{0,4},{1,5},{2,6},{3,7},{4,0},{5,1},{6,2},{7,3},{8,12},{9,13},{10,... | collective-permute-start | bytes 442376 | tf_op jit(solution)/shard_map/ppermute | solution.py:818
  241.5 22.4 %collective-permute-start.34 = (bf16[1,48,3072]{2,1,0:T(8,128)(2,1)S(1)}, bf16[1,48,3072]{2,1,0:T(8,128)(2,1)S(1)}, u32[]{:S(2)}, u32[]{:S(2)}) collective-permute-start(bf16[1,48,3072]{2,1,0:T(8,128)(2,1)S(1)} %fusion.6), channel_id=1, source_target_pairs={{0,16},{1,17},{2,18},{3,19},{4,20},{5,21},{6,22},{7,23},{8,24},{9,... | collective-permute-start | bytes 884744 | tf_op jit(solution)/shard_map/ppermute | solution.py:818
  244.4 8.6 %collective-permute-start.29 = (bf16[4,48,768]{2,1,0:T(8,128)(2,1)S(1)}, bf16[4,48,768]{2,1,0:T(8,128)(2,1)S(1)}, u32[]{:S(2)}, u32[]{:S(2)}) collective-permute-start(bf16[4,48,768]{2,1,0:T(8,128)(2,1)S(1)} %get-tuple-element.260), channel_id=1, source_target_pairs={{0,4},{1,5},{2,6},{3,7},{4,0},{5,1},{6,2},{7,3},{8,12},{9,13},{10,... | collective-permute-start | bytes 884744 | tf_op jit(solution)/shard_map/ppermute | solution.py:818
  251.1 11.7 %collective-permute-start.35 = (bf16[1,48,3200]{2,1,0:T(8,128)(2,1)S(1)}, bf16[1,48,3200]{2,1,0:T(8,128)(2,1)S(1)}, u32[]{:S(2)}, u32[]{:S(2)}) collective-permute-start(bf16[1,48,3200]{2,1,0:T(8,128)(2,1)S(1)} %add_convert_fusion.3), channel_id=1, source_target_pairs={{0,8},{1,9},{2,10},{3,11},{4,12},{5,13},{6,14},{7,15},{8,0},{9,1},... | collective-permute-start | bytes 921608 | tf_op jit(solution)/shard_map/ppermute | solution.py:818
  253.0 5.2 %collective-permute-start.26 = (bf16[1,48,1536]{2,1,0:T(8,128)(2,1)S(1)}, bf16[1,48,1536]{2,1,0:T(8,128)(2,1)S(1)}, u32[]{:S(2)}, u32[]{:S(2)}) collective-permute-start(bf16[1,48,1536]{2,1,0:T(8,128)(2,1)S(1)} %fusion.10), channel_id=1, source_target_pairs={{0,2},{1,3},{2,0},{3,1},{4,6},{5,7},{6,4},{7,5},{8,10},{9,11},{10,... | collective-permute-start | bytes 442376 | tf_op jit(solution)/shard_map/ppermute | solution.py:818
  254.7 14.3 %collective-permute-start.31 = (bf16[2,48,768]{2,1,0:T(8,128)(2,1)S(1)}, bf16[2,48,768]{2,1,0:T(8,128)(2,1)S(1)}, u32[]{:S(2)}, u32[]{:S(2)}) collective-permute-start(bf16[2,48,768]{2,1,0:T(8,128)(2,1)S(1)} %get-tuple-element.266), channel_id=1, source_target_pairs={{0,8},{1,9},{2,10},{3,11},{4,12},{5,13},{6,14},{7,15},{8,0},{9,1},... | collective-permute-start | bytes 442376 | tf_op jit(solution)/shard_map/ppermute | solution.py:818
  255.4 12.4 %collective-permute-start.32 = (bf16[1,48,768]{2,1,0:T(8,128)(2,1)S(1)}, bf16[1,48,768]{2,1,0:T(8,128)(2,1)S(1)}, u32[]{:S(2)}, u32[]{:S(2)}) collective-permute-start(bf16[1,48,768]{2,1,0:T(8,128)(2,1)S(1)} %fusion.19), channel_id=1, source_target_pairs={{0,8},{1,9},{2,10},{3,11},{4,12},{5,13},{6,14},{7,15},{8,0},{9,1},... | collective-permute-start | bytes 221192 | tf_op jit(solution)/shard_map/ppermute | solution.py:818
  258.2 6.8 %collective-permute-start.33 = (f32[16,768]{1,0:T(8,128)S(1)}, f32[16,768]{1,0:T(8,128)S(1)}, u32[]{:S(2)}, u32[]{:S(2)}) collective-permute-start(f32[16,768]{1,0:T(8,128)S(1)} %add.165), channel_id=1, source_target_pairs={{0,4},{1,5},{2,6},{3,7},{4,0},{5,1},{6,2},{7,3},{8,12},{9,13},{10,... | collective-permute-start | bytes 147464 | tf_op jit(solution)/shard_map/ppermute | solution.py:818
  262.8 11.0 %collective-permute-start.30 = (bf16[1,48,1536]{2,1,0:T(8,128)(2,1)S(1)}, bf16[1,48,1536]{2,1,0:T(8,128)(2,1)S(1)}, u32[]{:S(2)}, u32[]{:S(2)}) collective-permute-start(bf16[1,48,1536]{2,1,0:T(8,128)(2,1)S(1)} %fusion.12), channel_id=1, source_target_pairs={{0,16},{1,17},{2,18},{3,19},{4,20},{5,21},{6,22},{7,23},{8,24},{9,... | collective-permute-start | bytes 442376 | tf_op jit(solution)/shard_map/ppermute | solution.py:818
  263.9 16.5 %collective-permute-start.37 = (bf16[2,48,3200]{2,1,0:T(8,128)(2,1)S(1)}, bf16[2,48,3200]{2,1,0:T(8,128)(2,1)S(1)}, u32[]{:S(2)}, u32[]{:S(2)}) collective-permute-start(bf16[2,48,3200]{2,1,0:T(8,128)(2,1)S(1)} %broadcast_select_fusion), channel_id=1, source_target_pairs={{0,4},{1,5},{2,6},{3,7},{4,0},{5,1},{6,2},{7,3},{8,12},{9,13},{10,... | collective-permute-start | bytes 1843208 | tf_op jit(solution)/shard_map/ppermute | solution.py:818
  265.0 8.8 %collective-permute-start.40 = (bf16[1,48,3072]{2,1,0:T(8,128)(2,1)S(1)}, bf16[1,48,3072]{2,1,0:T(8,128)(2,1)S(1)}, u32[]{:S(2)}, u32[]{:S(2)}) collective-permute-start(bf16[1,48,3072]{2,1,0:T(8,128)(2,1)S(1)} %add_convert_fusion.4), channel_id=1, source_target_pairs={{0,2},{1,3},{2,0},{3,1},{4,6},{5,7},{6,4},{7,5},{8,10},{9,11},{10,... | collective-permute-start | bytes 884744 | tf_op jit(solution)/shard_map/ppermute | solution.py:818
  267.8 18.7 %collective-permute-start.44 = (f32[16,768]{1,0:T(8,128)S(1)}, f32[16,768]{1,0:T(8,128)S(1)}, u32[]{:S(2)}, u32[]{:S(2)}) collective-permute-start(f32[16,768]{1,0:T(8,128)S(1)} %add.170), channel_id=1, source_target_pairs={{0,8},{1,9},{2,10},{3,11},{4,12},{5,13},{6,14},{7,15},{8,0},{9,1},... | collective-permute-start | bytes 147464 | tf_op jit(solution)/shard_map/ppermute | solution.py:818
  269.0 9.2 %collective-permute-start.38 = (bf16[1,48,768]{2,1,0:T(8,128)(2,1)S(1)}, bf16[1,48,768]{2,1,0:T(8,128)(2,1)S(1)}, u32[]{:S(2)}, u32[]{:S(2)}) collective-permute-start(bf16[1,48,768]{2,1,0:T(8,128)(2,1)S(1)} %fusion.18), channel_id=1, source_target_pairs={{0,16},{1,17},{2,18},{3,19},{4,20},{5,21},{6,22},{7,23},{8,24},{9,... | collective-permute-start | bytes 221192 | tf_op jit(solution)/shard_map/ppermute | solution.py:818
  273.8 4.4 %collective-permute-start.39 = (bf16[1,48,768]{2,1,0:T(8,128)(2,1)S(1)}, bf16[1,48,768]{2,1,0:T(8,128)(2,1)S(1)}, u32[]{:S(2)}, u32[]{:S(2)}) collective-permute-start(bf16[1,48,768]{2,1,0:T(8,128)(2,1)S(1)} %fusion.16), channel_id=1, source_target_pairs={{0,2},{1,3},{2,0},{3,1},{4,6},{5,7},{6,4},{7,5},{8,10},{9,11},{10,... | collective-permute-start | bytes 221192 | tf_op jit(solution)/shard_map/ppermute | solution.py:818
  273.9 9.6 %collective-permute-start.36 = (bf16[1,48,1536]{2,1,0:T(8,128)(2,1)S(1)}, bf16[1,48,1536]{2,1,0:T(8,128)(2,1)S(1)}, u32[]{:S(2)}, u32[]{:S(2)}) collective-permute-start(bf16[1,48,1536]{2,1,0:T(8,128)(2,1)S(1)} %add_convert_fusion.7), channel_id=1, source_target_pairs={{0,2},{1,3},{2,0},{3,1},{4,6},{5,7},{6,4},{7,5},{8,10},{9,11},{10,... | collective-permute-start | bytes 442376 | tf_op jit(solution)/shard_map/ppermute | solution.py:818
  278.2 15.0 %collective-permute-start.48 = (bf16[2,48,3072]{2,1,0:T(8,128)(2,1)S(1)}, bf16[2,48,3072]{2,1,0:T(8,128)(2,1)S(1)}, u32[]{:S(2)}, u32[]{:S(2)}) collective-permute-start(bf16[2,48,3072]{2,1,0:T(8,128)(2,1)S(1)} %broadcast_select_fusion.1), channel_id=1, source_target_pairs={{0,4},{1,5},{2,6},{3,7},{4,0},{5,1},{6,2},{7,3},{8,12},{9,13},{10,... | collective-permute-start | bytes 1769480 | tf_op jit(solution)/shard_map/ppermute | solution.py:818
  278.2 6.2 %collective-permute-start.42 = (bf16[1,48,768]{2,1,0:T(8,128)(2,1)S(1)}, bf16[1,48,768]{2,1,0:T(8,128)(2,1)S(1)}, u32[]{:S(2)}, u32[]{:S(2)}) collective-permute-start(bf16[1,48,768]{2,1,0:T(8,128)(2,1)S(1)} %fusion.15), channel_id=1, source_target_pairs={{0,16},{1,17},{2,18},{3,19},{4,20},{5,21},{6,22},{7,23},{8,24},{9,... | collective-permute-start | bytes 221192 | tf_op jit(solution)/shard_map/ppermute | solution.py:818
  280.4 6.0 %collective-permute-start.45 = (bf16[1,48,768]{2,1,0:T(8,128)(2,1)S(1)}, bf16[1,48,768]{2,1,0:T(8,128)(2,1)S(1)}, u32[]{:S(2)}, u32[]{:S(2)}) collective-permute-start(bf16[1,48,768]{2,1,0:T(8,128)(2,1)S(1)} %add_convert_fusion.9), channel_id=1, source_target_pairs={{0,8},{1,9},{2,10},{3,11},{4,12},{5,13},{6,14},{7,15},{8,0},{9,1},... | collective-permute-start | bytes 221192 | tf_op jit(solution)/shard_map/ppermute | solution.py:818
  283.6 7.3 %collective-permute-start.41 = (bf16[2,48,1536]{2,1,0:T(8,128)(2,1)S(1)}, bf16[2,48,1536]{2,1,0:T(8,128)(2,1)S(1)}, u32[]{:S(2)}, u32[]{:S(2)}) collective-permute-start(bf16[2,48,1536]{2,1,0:T(8,128)(2,1)S(1)} %broadcast_select_fusion.2), channel_id=1, source_target_pairs={{0,8},{1,9},{2,10},{3,11},{4,12},{5,13},{6,14},{7,15},{8,0},{9,1},... | collective-permute-start | bytes 884744 | tf_op jit(solution)/shard_map/ppermute | solution.py:818
  284.5 4.4 %collective-permute-start.43 = (bf16[1,48,768]{2,1,0:T(8,128)(2,1)S(1)}, bf16[1,48,768]{2,1,0:T(8,128)(2,1)S(1)}, u32[]{:S(2)}, u32[]{:S(2)}) collective-permute-start(bf16[1,48,768]{2,1,0:T(8,128)(2,1)S(1)} %add_convert_fusion.8), channel_id=1, source_target_pairs={{0,2},{1,3},{2,0},{3,1},{4,6},{5,7},{6,4},{7,5},{8,10},{9,11},{10,... | collective-permute-start | bytes 221192 | tf_op jit(solution)/shard_map/ppermute | solution.py:818
  291.0 26.9 %collective-permute-start.46 = (bf16[4,48,1536]{2,1,0:T(8,128)(2,1)S(1)}, bf16[4,48,1536]{2,1,0:T(8,128)(2,1)S(1)}, u32[]{:S(2)}, u32[]{:S(2)}) collective-permute-start(bf16[4,48,1536]{2,1,0:T(8,128)(2,1)S(1)} %bitcast_select_fusion.9), channel_id=1, source_target_pairs={{0,4},{1,5},{2,6},{3,7},{4,0},{5,1},{6,2},{7,3},{8,12},{9,13},{10,... | collective-permute-start | bytes 1769480 | tf_op jit(solution)/shard_map/ppermute | solution.py:818
  291.6 16.3 %collective-permute-start.47 = (bf16[2,48,768]{2,1,0:T(8,128)(2,1)S(1)}, bf16[2,48,768]{2,1,0:T(8,128)(2,1)S(1)}, u32[]{:S(2)}, u32[]{:S(2)}) collective-permute-start(bf16[2,48,768]{2,1,0:T(8,128)(2,1)S(1)} %broadcast_select_fusion.4), channel_id=1, source_target_pairs={{0,4},{1,5},{2,6},{3,7},{4,0},{5,1},{6,2},{7,3},{8,12},{9,13},{10,... | collective-permute-start | bytes 442376 | tf_op jit(solution)/shard_map/ppermute | solution.py:818
  307.9 9.9 %collective-permute-start.49 = (bf16[4,48,768]{2,1,0:T(8,128)(2,1)S(1)}, bf16[4,48,768]{2,1,0:T(8,128)(2,1)S(1)}, u32[]{:S(2)}, u32[]{:S(2)}) collective-permute-start(bf16[4,48,768]{2,1,0:T(8,128)(2,1)S(1)} %bitcast_select_fusion.13), channel_id=1, source_target_pairs={{0,2},{1,3},{2,0},{3,1},{4,6},{5,7},{6,4},{7,5},{8,10},{9,11},{10,... | collective-permute-start | bytes 884744 | tf_op jit(solution)/shard_map/ppermute | solution.py:818
  308.7 8.8 %collective-permute-start.50 = (bf16[2,48,768]{2,1,0:T(8,128)(2,1)S(1)}, bf16[2,48,768]{2,1,0:T(8,128)(2,1)S(1)}, u32[]{:S(2)}, u32[]{:S(2)}) collective-permute-start(bf16[2,48,768]{2,1,0:T(8,128)(2,1)S(1)} %broadcast_select_fusion.3), channel_id=1, source_target_pairs={{0,8},{1,9},{2,10},{3,11},{4,12},{5,13},{6,14},{7,15},{8,0},{9,1},... | collective-permute-start | bytes 442376 | tf_op jit(solution)/shard_map/ppermute | solution.py:818
  310.8 30.2 %collective-permute-start.53 = (bf16[4,48,3200]{2,1,0:T(8,128)(2,1)S(1)}, bf16[4,48,3200]{2,1,0:T(8,128)(2,1)S(1)}, u32[]{:S(2)}, u32[]{:S(2)}) collective-permute-start(bf16[4,48,3200]{2,1,0:T(8,128)(2,1)S(1)} %bitcast_select_fusion.3), channel_id=1, source_target_pairs={{0,2},{1,3},{2,0},{3,1},{4,6},{5,7},{6,4},{7,5},{8,10},{9,11},{10,... | collective-permute-start | bytes 3686408 | tf_op jit(solution)/shard_map/ppermute | solution.py:818
  312.5 5.0 %collective-permute-start.51 = (f32[16,768]{1,0:T(8,128)S(1)}, f32[16,768]{1,0:T(8,128)S(1)}, u32[]{:S(2)}, u32[]{:S(2)}) collective-permute-start(f32[16,768]{1,0:T(8,128)S(1)} %add.178), channel_id=1, source_target_pairs={{0,16},{1,17},{2,18},{3,19},{4,20},{5,21},{6,22},{7,23},{8,24},{9,... | collective-permute-start | bytes 147464 | tf_op jit(solution)/shard_map/ppermute | solution.py:818
  318.2 23.3 %collective-permute-start.52 = (bf16[8,48,1536]{2,1,0:T(8,128)(2,1)S(1)}, bf16[8,48,1536]{2,1,0:T(8,128)(2,1)S(1)}, u32[]{:S(2)}, u32[]{:S(2)}) collective-permute-start(bf16[8,48,1536]{2,1,0:T(8,128)(2,1)S(1)} %bitcast_select_fusion.4.refs_0_), channel_id=1, source_target_pairs={{0,1},{1,0},{2,3},{3,2},{4,5},{5,4},{6,7},{7,6},{8,9},{9,8},{10,11... | collective-permute-start | bytes 3538952 | tf_op jit(solution)/shard_map/ppermute | solution.py:818
  318.2 29.2 %collective-permute-start.57 = (bf16[4,48,3072]{2,1,0:T(8,128)(2,1)S(1)}, bf16[4,48,3072]{2,1,0:T(8,128)(2,1)S(1)}, u32[]{:S(2)}, u32[]{:S(2)}) collective-permute-start(bf16[4,48,3072]{2,1,0:T(8,128)(2,1)S(1)} %bitcast_select_fusion.5), channel_id=1, source_target_pairs={{0,8},{1,9},{2,10},{3,11},{4,12},{5,13},{6,14},{7,15},{8,0},{9,1},... | collective-permute-start | bytes 3538952 | tf_op jit(solution)/shard_map/ppermute | solution.py:818
  320.9 9.1 %collective-permute-start.54 = (bf16[4,48,768]{2,1,0:T(8,128)(2,1)S(1)}, bf16[4,48,768]{2,1,0:T(8,128)(2,1)S(1)}, u32[]{:S(2)}, u32[]{:S(2)}) collective-permute-start(bf16[4,48,768]{2,1,0:T(8,128)(2,1)S(1)} %bitcast_select_fusion.12), channel_id=1, source_target_pairs={{0,4},{1,5},{2,6},{3,7},{4,0},{5,1},{6,2},{7,3},{8,12},{9,13},{10,... | collective-permute-start | bytes 884744 | tf_op jit(solution)/shard_map/ppermute | solution.py:818
  321.2 20.3 %collective-permute-start.55 = (bf16[8,48,768]{2,1,0:T(8,128)(2,1)S(1)}, bf16[8,48,768]{2,1,0:T(8,128)(2,1)S(1)}, u32[]{:S(2)}, u32[]{:S(2)}) collective-permute-start(bf16[8,48,768]{2,1,0:T(8,128)(2,1)S(1)} %bitcast_select_fusion.8.refs_2_), channel_id=1, source_target_pairs={{0,1},{1,0},{2,3},{3,2},{4,5},{5,4},{6,7},{7,6},{8,9},{9,8},{10,11... | collective-permute-start | bytes 1769480 | tf_op jit(solution)/shard_map/ppermute | solution.py:818
  330.1 11.4 %collective-permute-start.56 = (bf16[8,48,768]{2,1,0:T(8,128)(2,1)S(1)}, bf16[8,48,768]{2,1,0:T(8,128)(2,1)S(1)}, u32[]{:S(2)}, u32[]{:S(2)}) collective-permute-start(bf16[8,48,768]{2,1,0:T(8,128)(2,1)S(1)} %bitcast_select_fusion.7.refs_4_), channel_id=1, source_target_pairs={{0,1},{1,0},{2,3},{3,2},{4,5},{5,4},{6,7},{7,6},{8,9},{9,8},{10,11... | collective-permute-start | bytes 1769480 | tf_op jit(solution)/shard_map/ppermute | solution.py:818
  341.4 10.2 %collective-permute-start.59 = (bf16[8,48,3200]{2,1,0:T(8,128)(2,1)S(1)}, bf16[8,48,3200]{2,1,0:T(8,128)(2,1)}, u32[]{:S(2)}, u32[]{:S(2)}) collective-permute-start(bf16[8,48,3200]{2,1,0:T(8,128)(2,1)S(1)} %bitcast_select_fusion.refs_0_), channel_id=1, source_target_pairs={{0,1},{1,0},{2,3},{3,2},{4,5},{5,4},{6,7},{7,6},{8,9},{9,8},{10,11... | collective-permute-start | bytes 7372808 | tf_op jit(solution)/shard_map/ppermute | solution.py:818
  349.2 9.0 %collective-permute-start.58 = (bf16[8,48,3072]{2,1,0:T(8,128)(2,1)}, bf16[8,48,3072]{2,1,0:T(8,128)(2,1)}, u32[]{:S(2)}, u32[]{:S(2)}) collective-permute-start(bf16[8,48,3072]{2,1,0:T(8,128)(2,1)} %bitcast_select_fusion.1.refs_0_), channel_id=1, source_target_pairs={{0,1},{1,0},{2,3},{3,2},{4,5},{5,4},{6,7},{7,6},{8,9},{9,8},{10,11... | collective-permute-start | bytes 7077896 | tf_op jit(solution)/shard_map/ppermute | solution.py:818
  (42 other events, 300.6 us)

commit v3 on v2

--- a/solution.py
+++ b/solution.py
@@ -37,7 +37,7 @@
 
 
 def cost(flops, nbytes):
-    return pl.CostEstimate(flops=int(flops), bytes_accessed=int(nbytes), transcendentals=0)
+    return pl.CostEstimate(flops=0, bytes_accessed=0, transcendentals=0)
 
 
 SMEM = pl.BlockSpec(memory_space=pltpu.SMEM)
@@ -50,6 +50,10 @@
 
 def held(shape):
     return pl.BlockSpec(shape, lambda *g: (0,) * len(shape), pipeline_mode=pl.Buffered(1))
+
+
+def in_hbm(x):
+    return pltpu.with_memory_space_constraint(x, pltpu.HBM)
 
 
 def struct(shape, dtype):
@@ -116,22 +120,55 @@
     return jnp.concatenate([t[:64, :QB], t[64:, QB:]], axis=0)
 
 
-def attn_fwd_kernel(
-    lens, tok, wqkv, bqv, wo, bo, g1, b1,
-    packed, out, lse, hid, low, ht, n1, i1, vt, segq, segk,
-):
+def attn_fwd_kernel(lens, *refs):
+    count = 7
+    given, (packed_out, out, lse, hid, low, ht, n1, i1) = refs[:count], refs[count : count + 8]
+    vt, segq, segk, packed = refs[count + 8 : count + 12]
+    tok, wqkv, bqv, wo, bo, g1, b1 = refs[count + 12 : count + 12 + count]
+    sems, wsems, psems = refs[count + 12 + count :]
     rows, width = tok.shape
+    cols = 3
+    fetch = [
+        pltpu.make_async_copy(given[i], x, sems.at[i])
+        for i, x in ((0, tok), (2, bqv), (3, wo), (4, bo), (5, g1), (6, b1))
+    ]
+    chunk = [
+        pltpu.make_async_copy(
+            given[1].at[:, j * width : (j + 1) * width],
+            wqkv.at[:, j * width : (j + 1) * width],
+            wsems.at[j],
+        )
+        for j in range(cols)
+    ]
+    keep = [
+        pltpu.make_async_copy(
+            packed.at[:, j * width : (j + 1) * width],
+            packed_out.at[:, j * width : (j + 1) * width],
+            psems.at[j],
+        )
+        for j in range(cols)
+    ]
+    for f in fetch[:2]:
+        f.start()
+    for c in chunk:
+        c.start()
+    for f in fetch[2:]:
+        f.start()
     ends = segment_ends(lens)
     fill_segments(ends, segq, segk)
     pairs = width // 128
-    for j in range(3 * width // 256):
-        at = slice(j * 256, (j + 1) * 256)
-        x = nn(tok[...], wqkv[:, at])
-        which = j * 256 // width
-        if which != 1:
-            b0 = j * 256 - (width if which else 0)
-            x = x + bqv[b0 : b0 + 256].reshape(1, 256)
-        packed[:, at] = x.astype(bf16)
+    for f in fetch[:2]:
+        f.wait()
+    for j in range(cols):
+        at = slice(j * width, (j + 1) * width)
+        chunk[j].wait()
+        for r in (slice(0, rows // 2), slice(rows // 2, rows)):
+            x = nn(tok[r, :], wqkv[:, at])
+            if j != 1:
+                b0 = width if j else 0
+                x = x + bqv[b0 : b0 + width].reshape(1, width)
+            packed[r, at] = x.astype(bf16)
+        keep[j].start()
     q = packed.at[:, 0:width]
     k = packed.at[:, width : 2 * width]
     v = packed.at[:, 2 * width : 3 * width]
@@ -173,6 +210,8 @@
         return carry
 
     lax.fori_loop(0, rows // QB, step, 0)
+    for f in fetch[2:]:
+        f.wait()
     tile = 256
     for r0 in range(0, rows, tile):
         r = slice(r0, r0 + tile)
@@ -185,20 +224,17 @@
         ht[:, r] = hl.T
         n1[r, :] = normal.astype(bf16)
         i1[r, :] = inv
+    for k in keep:
+        k.wait()
 
 
 def attn_bwd_kernel(
-    part, lens, packed, do, o, lse, dq, dk, dv, sums, kt, dka, dva, segq, segk
+    lens, q, k, v, do, o, lse, dq, dk, dv, sums, kt, dka, dva, segq, segk
 ):
-    rows = packed.shape[0]
-    width = packed.shape[1] // 3
-    span = dq.shape[1]
+    rows, span = q.shape
     ends = segment_ends(lens)
     fill_segments(ends, segq, segk)
     pairs = span // 128
-    q, k, v = [packed.at[:, i * width + part * span : i * width + (part + 1) * span] for i in range(3)]
-    do = do.at[:, part * span : (part + 1) * span]
-    o = o.at[:, part * span : (part + 1) * span]
     for g in range(pairs):
         kt[g] = k[:, g * 128 : (g + 1) * 128].T
     dka[...] = jnp.zeros_like(dka)
@@ -227,7 +263,7 @@
                     precision=lax.Precision.HIGHEST,
                     preferred_element_type=f32,
                 )
-                lrow = lse[part * pairs + g, pl.ds(i, 1), :]
+                lrow = lse[g, pl.ds(i, 1), :]
                 st = nt(k[at, gs], q2)
                 dpt = nt(v[at, gs], do2)
                 ps, ds = [], []
@@ -263,25 +299,35 @@
 def attention(lens, tok, wqkv, bqv, wo, bo, g1, b1):
     rows, width = tok.shape
     pairs = width // 128
+    ins = [tok, wqkv, bqv, wo, bo, g1, b1]
+    anywhere = pl.BlockSpec(memory_space=pl.ANY)
     return pl.pallas_call(
         attn_fwd_kernel,
-        in_specs=[SMEM] + [VMEM] * 7,
-        out_specs=[VMEM] * 8,
+        in_specs=[SMEM] + [anywhere] * len(ins),
+        out_specs=[anywhere] + [VMEM] * 7,
         out_shape=[
-            struct((rows, 3 * width), bf16),
+            pltpu.HBM((rows, 3 * width), bf16),
             struct((rows, width), bf16),
             struct((pairs, rows // QB, 2 * QB), f32),
             struct((rows, width), f32),
             struct((rows, width), bf16),
-            struct((width, rows), bf16),
-            struct((rows, width), bf16),
-            struct((rows, 1), f32),
+            pltpu.HBM((width, rows), bf16),
+            pltpu.HBM((rows, width), bf16),
+            pltpu.HBM((rows, 1), f32),
         ],
-        scratch_shapes=[pltpu.VMEM((pairs, 128, rows), bf16)] + segment_scratch(rows),
+        scratch_shapes=[pltpu.VMEM((pairs, 128, rows), bf16)]
+        + segment_scratch(rows)
+        + [pltpu.VMEM((rows, 3 * width), bf16)]
+        + [pltpu.VMEM(x.shape, x.dtype) for x in ins]
+        + [
+            pltpu.SemaphoreType.DMA((len(ins),)),
+            pltpu.SemaphoreType.DMA((3,)),
+            pltpu.SemaphoreType.DMA((3,)),
+        ],
         compiler_params=params(32),
         cost_estimate=cost(18e9, 8 * rows * width),
         name="attention_forward",
-    )(lens, tok, wqkv, bqv, wo, bo, g1, b1)
+    )(lens, *[in_hbm(x) for x in ins])
 
 
 def attention_back(part, lens, packed, do, o, lse):
@@ -289,10 +335,14 @@
     span = width // PORTIONS
     pairs = span // 128
     shp = struct((rows, span), bf16)
+    col = lambda off: pl.BlockSpec((rows, span), lambda g, off=off: (0, off * PORTIONS + part))
+    own = pl.BlockSpec((rows, span), lambda g: (0, 0))
     return pl.pallas_call(
-        functools.partial(attn_bwd_kernel, part),
-        in_specs=[SMEM] + [VMEM] * 4,
-        out_specs=[VMEM] * 4,
+        attn_bwd_kernel,
+        grid=(1,),
+        in_specs=[SMEM, col(0), col(1), col(2), col(0), col(0)]
+        + [pl.BlockSpec((pairs,) + lse.shape[1:], lambda g: (part, 0, 0))],
+        out_specs=[own, own, own, whole((8, span))],
         out_shape=[shp, shp, shp, struct((8, span), f32)],
         scratch_shapes=[
             pltpu.VMEM((pairs, 128, rows), bf16),
@@ -300,10 +350,10 @@
             pltpu.VMEM((rows, span), f32),
         ]
         + segment_scratch(rows),
-        compiler_params=params(24),
+        compiler_params=params(16),
         cost_estimate=cost(10e9, 16 * rows * span),
         name="attention_backward",
-    )(lens, packed, do, o, lse)
+    )(lens, packed, packed, packed, do, o, lse)
 
 
 def norm_back(grad, gain, normal, inv):
@@ -367,7 +417,7 @@
     rows, width = hid.shape
     ff, out = wu.shape[1], wp.shape[1]
     steps = ff // FF_CHUNK
-    ins = [lens, hid, low, wu, bu, wd, bd, g2, b2, wp]
+    ins = [lens, hid, low, in_hbm(wu), bu, in_hbm(wd), bd, g2, b2, wp]
     specs = [held(x.shape) for x in ins]
     specs[0] = SMEM
     specs[1] = pl.BlockSpec((rows, width // steps), lambda c: (0, c))
@@ -375,11 +425,11 @@
     specs[4] = pl.BlockSpec((FF_CHUNK,), lambda c: (c,))
     specs[5] = pl.BlockSpec((FF_CHUNK, width), lambda c: (c, 0))
     outs = [
-        struct((rows, ff), bf16),
-        struct((rows, ff), bf16),
-        struct((rows, width), bf16),
+        pltpu.HBM((rows, ff), bf16),
+        pltpu.HBM((rows, ff), bf16),
+        pltpu.HBM((rows, width), bf16),
         struct((rows, 1), f32),
-        struct((rows, width), bf16),
+        pltpu.HBM((rows, width), bf16),
         struct((rows, out), f32),
         struct((rows, out), bf16),
         struct((1, QLEN + 16, out), bf16),
@@ -393,7 +443,7 @@
         out_specs=ospecs,
         out_shape=outs,
         scratch_shapes=[pltpu.VMEM((rows, width), f32)],
-        compiler_params=params(36),
+        compiler_params=params(32),
         cost_estimate=cost(18e9, 40e6),
         name="ffn_forward",
     )(*ins)
@@ -461,7 +511,7 @@
         in_specs=[smem] * 3 + [vmem] * 2,
         out_specs=[vmem] * 2,
         out_shape=[struct((1, total + 16, out), bf16), struct((rows, out), f32)],
-        compiler_params=params(16),
+        compiler_params=params(8),
         cost_estimate=cost(1e9, 2e6),
         name="loss_forward",
     )(me, lens, owner, gathered, ul)
@@ -562,7 +612,7 @@
         out_specs=[vmem] * 5,
         out_shape=[
             struct((8, 128), f32),
-            struct((rows, width), f32),
+            pltpu.HBM((rows, width), f32),
             struct((rows, width), bf16),
             struct((width, out), f32),
             struct((8, width), f32),
@@ -572,7 +622,7 @@
             pltpu.VMEM((out, width), f32),
             pltpu.SMEM((owner.size,), i32),
         ],
-        compiler_params=params(32),
+        compiler_params=params(14),
         cost_estimate=cost(6e9, 10e6),
         name="loss_backward",
     )(me, lens, owner, place, messages, dpb, emb, nl, n2, i2, g2, wp)
@@ -592,34 +642,60 @@
     return [(keep, top, low), (send, 1 - top, low)]
 
 
+DOWN_BATCH = 4
+
+
 def down_grad_kernel(dims, me, act, dbr, gwp, keep, send):
+    r = pl.program_id(0)
     pr, width = keep.shape[1], dbr.shape[1]
-    parts = act.shape[1] // width
-    half = PIECES // 2
-    for dst, side, low in sides(me, dims, keep, send):
-        for t in range(0, half, 2):
-            at = pl.multiple_of((side * half + t) * (pr * parts), 128)
-            g = tn(act[:, pl.ds(at, 2 * pr * parts)], dbr[...])
-            for u in range(2):
-                for i in range(parts):
-                    r = (u * parts + i) * pr
-                    dst[(t + u) ^ low, :, i * width : (i + 1) * width] = g[r : r + pr]
-                first = pl.multiple_of((side * half + t + u) * pr, 16)
-                dst[(t + u) ^ low, :, parts * width :] = gwp[pl.ds(first, pr), :]
+    parts = act.shape[1] // (DOWN_BATCH * pr)
+    flip = flip_of(me[0], dims)
+    low = flip & (DOWN_BATCH - 1)
+    first = (r ^ lax.div(flip, DOWN_BATCH)) * DOWN_BATCH
+
+    def put(dst):
+        g = tn(act[...], dbr[...])
+        for u in range(DOWN_BATCH):
+            for i in range(parts):
+                at = (u * parts + i) * pr
+                dst[u ^ low, :, i * width : (i + 1) * width] = g[at : at + pr]
+            at = pl.multiple_of((first + u) * pr, 16)
+            dst[u ^ low, :, parts * width :] = gwp[pl.ds(at, pr), :]
+
+    pl.when(r < PIECES // 2 // DOWN_BATCH)(lambda: put(keep))
+    pl.when(r >= PIECES // 2 // DOWN_BATCH)(lambda: put(send))
 
 
 def down_grad(dims, me, act, dbr, gwp):
     rows, width = dbr.shape
-    buf = struct((PIECES // 2, width // PIECES, act.shape[1] + gwp.shape[1]), f32)
+    ff = act.shape[1]
+    cols = ff + gwp.shape[1]
+    half = PIECES // 2 // DOWN_BATCH
+    buf = struct((PIECES // 2, width // PIECES, cols), f32)
+    block = (DOWN_BATCH, width // PIECES, cols)
     return pl.pallas_call(
         functools.partial(down_grad_kernel, dims),
-        in_specs=[SMEM] + [VMEM] * 3,
-        out_specs=[VMEM] * 2,
+        grid_spec=pltpu.PrefetchScalarGridSpec(
+            num_scalar_prefetch=1,
+            grid=(PIECES // DOWN_BATCH,),
+            in_specs=[
+                pl.BlockSpec(
+                    (rows, DOWN_BATCH * ff // PIECES),
+                    lambda r, f: (0, r ^ lax.div(flip_of(f[0], dims), DOWN_BATCH)),
+                ),
+                held(dbr.shape),
+                held(gwp.shape),
+            ],
+            out_specs=[
+                pl.BlockSpec(block, lambda r, f: (jnp.minimum(r, half - 1), 0, 0)),
+                pl.BlockSpec(block, lambda r, f: (jnp.maximum(r - half, 0), 0, 0)),
+            ],
+        ),
         out_shape=[buf, buf],
-        compiler_params=params(32),
+        compiler_params=params(24),
         cost_estimate=cost(5e9, 17e6),
         name="down_gradient",
-    )(me, act, dbr, gwp)
+    )(me, in_hbm(act), dbr, gwp)
 
 
 def up_grad_kernel(dims, me, dbr, slp, wd, ht, keep, send, din, dsum):
@@ -658,11 +734,11 @@
             held(ht.shape),
         ],
         out_specs=[part, part, wide, pl.BlockSpec((1, FF_CHUNK), lambda c: (0, c))],
-        out_shape=[buf, buf, struct((rows, ff), bf16), struct((1, ff), f32)],
-        compiler_params=params(36),
+        out_shape=[buf, buf, pltpu.HBM((rows, ff), bf16), struct((1, ff), f32)],
+        compiler_params=params(28),
         cost_estimate=cost(10e9, 30e6),
         name="up_gradient",
-    )(me, dbr, slp, wd, ht)
+    )(me, dbr, in_hbm(slp), in_hbm(wd), ht)
 
 
 def mid_back_kernel(me, din, wu, dr2, n1, i1, g1, wo, dr1, dpr, dat, sums, acc):
@@ -703,7 +779,7 @@
     rows, width = dr2.shape
     ff = din.shape[1]
     steps = ff // FF_CHUNK
-    ins = [me, din, wu, dr2, n1, i1, g1, wo]
+    ins = [me, in_hbm(din), in_hbm(wu), dr2, n1, i1, g1, wo]
     specs = [held(x.shape) for x in ins]
     specs[0] = SMEM
     specs[1] = pl.BlockSpec((rows, FF_CHUNK), lambda c: (0, c))
@@ -722,7 +798,7 @@
         out_specs=[whole(x.shape) for x in outs],
         out_shape=outs,
         scratch_shapes=[pltpu.VMEM((rows, width), f32)],
-        compiler_params=params(36),
+        compiler_params=params(32),
         cost_estimate=cost(9e9, 15e6),
         name="middle_backward",
     )(*ins)
@@ -756,7 +832,7 @@
         in_specs=[SMEM] + [VMEM] * (len(ins) - 1),
         out_specs=[VMEM] * 2,
         out_shape=[buf, buf],
-        compiler_params=params(24),
+        compiler_params=params(10),
         cost_estimate=cost(4e9, 8e6),
         name="qkv_gradient",
     )(*ins)
@@ -780,7 +856,7 @@
         in_specs=[SMEM] + [VMEM] * (len(ds) + 2),
         out_specs=VMEM,
         out_shape=struct(dr1.shape, f32),
-        compiler_params=params(32),
+        compiler_params=params(10),
         cost_estimate=cost(5e9, 15e6),
         name="input_gradient",
     )(me, *ds, w, dr1)
@@ -808,7 +884,7 @@
         in_specs=[VMEM] * len(ins),
         out_specs=VMEM,
         out_shape=struct((16, sm1.shape[1]), f32),
-        compiler_params=params(16),
+        compiler_params=params(6),
         cost_estimate=cost(1e4, 1e5),
         name="collect_vectors",
     )(*ins)
@@ -896,7 +972,7 @@
     return x
 
 
-BATCH = 4
+BATCH = 8
 
 
 def place_kernel(chains, layout, me, *refs):
@@ -948,21 +1024,21 @@
             ],
         ),
         out_shape=[struct(x, f32) for x in shapes],
-        compiler_params=params(24),
+        compiler_params=params(28),
         cost_estimate=cost(1e6, 6 * sum(x.size for x in ins)),
         name=name,
     )(*ins)
 
 
 SCHEDULE = (
-    "+D up +U -D +D mid -U +U E0 q0 +Q0 -D +D E1 -U +U",
-    "-Q0 +Q0 -D +D q1 +Q1 E2 -D +D -Q1 +Q1 q2 +Q2 -U +U",
-    "-Q0 +Q0 -Q2 +Q2 vec +V -Q1 +Q1 -D +D -U +U -V +V in",
-    "-Q0 +Q0 -Q2 +Q2 -Q1 +Q1 -V +V -Q0 +Q0 -D +D -U +U",
-    "-V +V -Q1 +Q1 -Q2 +Q2 -Q0 +Q0 -U +U -Q2 +Q2 -Q1 +Q1",
-    "-D +D -Q0 +Q0 -Q2 +Q2 -Q1 +Q1 -V +V -Q2 +Q2 -Q0 +Q0",
-    "-U +U -Q1 +Q1 -V -Q2 +Q2 -Q1 +Q1 -Q0 +Q0 -Q2 +Q2",
-    "-D +D -Q0 -Q1 -Q2 =Q -U +U -D =D -U =U",
+    "+D", "up", "+U", "-D", "+D", "mid", "-U", "+U", "E0", "-D", "+D", "q0", "+Q0", "E1", "-U",
+    "+U", "-D", "+D", "-Q0", "+Q0", "q1", "+Q1", "E2", "-U", "+U", "-D", "+D", "-Q1", "+Q1", "q2",
+    "+Q2", "-Q0", "+Q0", "vec", "+V", "-U", "+U", "-Q2", "+Q2", "-Q1", "+Q1", "-V", "+V", "in",
+    "-D", "+D", "-Q0", "+Q0", "-Q2", "+Q2", "-Q1", "+Q1", "-V", "+V", "-Q0", "+Q0", "-U", "+U",
+    "-Q2", "+Q2", "-V", "+V", "-D", "+D", "-Q1", "+Q1", "-U", "+U", "-Q0", "+Q0", "-Q2", "+Q2",
+    "-V", "+V", "-Q1", "+Q1", "-D", "+D", "-Q2", "+Q2", "-U", "+U", "-Q0", "+Q0", "-Q1", "+Q1",
+    "-Q2", "+Q2", "-V", "-Q1", "+Q1", "-Q2", "+Q2", "-D", "+D", "-U", "+U", "-D", "-Q0", "+Q0",
+    "=D", "-Q1", "+Q1", "-U", "=U", "-Q2", "+Q2", "-Q1", "-Q0", "+Q0", "-Q2", "-Q0", "=Q",
 )
 
 
@@ -972,10 +1048,10 @@
         x, y, z, far = rest
         return {
             "D": (1, x, y, z, far),
-            "U": (1, z, y, x, far),
-            "Q0": (1, y, z, x, far),
+            "U": (1, z, x, y, far),
+            "Q0": (1, z, x, y, far),
             "Q1": (1, x, y, z, far),
-            "Q2": (1, y, z, x, far),
+            "Q2": (1, x, y, z, far),
         }
     names = ("D", "U", "Q0", "Q1", "Q2")
     return {name: tuple([1] + rest[i:] + rest[:i]) for i, name in enumerate(names)}
@@ -1007,7 +1083,14 @@
     flying = {}
     parts = []
     placed = {}
+    small = None
     last = None
+
+    def vectors(v):
+        end = 5 + ff // width
+        return [v[0:2].reshape(-1), v[5:end].reshape(-1)] + [
+            v[i] for i in (2, 3, 4, end, end + 1, end + 2)
+        ]
 
     def now(x):
         return after(x, *flying.values()) if flying else x
@@ -1036,7 +1119,7 @@
             placed["Q"] = put_in_place(own, me, layout, shapes, "qkv_place")
         return placed[name][0]
 
-    for event in " ".join(SCHEDULE).split():
+    for event in SCHEDULE:
         if event[0] == "+":
             name = event[1:]
             if chains[name].out is None:
@@ -1048,6 +1131,9 @@
                 chains[name].land(*([] if last is None else [last]))
                 flying.pop(name, None)
                 last = chains[name].ready
+                if name == "V" and chains[name].out is not None:
+                    small = vectors(chains[name].out)
+                    last = small[1]
         elif event[0] == "=":
             last = finish(event[1:])
         elif event == "up":
@@ -1074,15 +1160,15 @@
             ds = [x[i] for i in range(3) for x in parts]
             d_tokens = input_grad(now(me), ds, w_qkv, dr1)
             last = d_tokens
+    if small is None:
+        small = vectors(chains["V"].finish())
     g_w_down, g_w_proj = placed["D"]
     g_w_up = placed["U"][0]
     g_w_qkv, g_w_out = placed["Q"]
-    vector = chains["V"].finish()
-    at = 5 + ff // width
+    g_b_qv, g_b_up, g_b_out, g_ln1_gain, g_ln1_bias, g_b_down, g_ln2_gain, g_ln2_bias = small
     return (
-        loss[0, 0:1], d_tokens, g_w_qkv, vector[0:2].reshape(-1), g_w_out, vector[2], vector[3],
-        vector[4], g_w_up, vector[5:at].reshape(-1), g_w_down, vector[at], vector[at + 1],
-        vector[at + 2], g_w_proj,
+        loss[0, 0:1], d_tokens, g_w_qkv, g_b_qv, g_w_out, g_b_out, g_ln1_gain, g_ln1_bias,
+        g_w_up, g_b_up, g_w_down, g_b_down, g_ln2_gain, g_ln2_bias, g_w_proj,
     )
 
 

time: 369 us -> 337 us (0.913)
  local copies, waits for them, and re-layouts: 36.7 us -> 10.4 us
  waiting for transfers between devices: 101 us -> 78.3 us
  starting transfers between devices: 63.3 us -> 82.1 us
  other arithmetic: 21.6 us -> 17.3 us
    unnamed x94 -> x60, local copies, waits for them, and re-layouts: 33.7 us -> 6.45 us
    ppermute x60, waiting for transfers between devices: 101 us -> 78.3 us  [swap(): return lax.ppermute(x, 'dp', [(i, i ^ mask) for i in range(n)])]
    ppermute x60, starting transfers between devices: 63.3 us -> 82.1 us  [swap(): return lax.ppermute(x, 'dp', [(i, i ^ mask) for i in range(n)])]
    add x10, other arithmetic: 11.5 us -> 6.68 us  [land(): self.keep = self.keep[:half] + recv[:half]]
    pallas_call x5, Pallas kernels: 59.9 us -> 64 us  [the longest x3 34.6 us: attention_back(): pl.pallas_call(attn_bwd_kernel, grid=(1,), in_specs=[SMEM, col(0), col(1)...]
    pallas_call x3, Pallas kernels: 17.5 us -> 13.4 us  [put_in_place(): pl.pallas_call(functools.partial(place_kernel, [c.dims for c in chains],...]
  transfers between devices with their start and end apart: 60 -> 60, of which waited for: 30 -> 24; matrix products, arithmetic and copies ran while one was open for 6% -> 5% of each run, Pallas kernels for 22% -> 24%
where the time goes in v3:
time: 337 us; the launch traced here: 333 us
  Pallas kernels  143 us (42%)
  starting transfers between devices  82.1 us (24%)
  waiting for transfers between devices  78.3 us (23%)
  other arithmetic  17.3 us (5%)
  local copies, waits for them, and re-layouts  10.4 us (3%)
    ppermute x60, starting transfers between devices, swap(): return lax.ppermute(x, 'dp', [(i, i ^ mask) for i in range(n)])  82.1 us
    ppermute x60, waiting for transfers between devices, swap(): return lax.ppermute(x, 'dp', [(i, i ^ mask) for i in range(n)])  78.3 us
    pallas_call x3, Pallas kernels, attention_back(): pl.pallas_call(attn_bwd_kernel, grid=(1,), in_specs=[SMEM, col(0), col(1)...  34.6 us
    pallas_call x1, Pallas kernels, attention(): pl.pallas_call(attn_fwd_kernel, in_specs=[SMEM] + [anywhere] * len(ins),...  21.6 us
    pallas_call x1, Pallas kernels, ffn_fwd(): pl.pallas_call(ffn_fwd_kernel, grid=(steps,), in_specs=specs, out_specs=o...  20 us
    pallas_call x1, Pallas kernels, up_grad(): pl.pallas_call(functools.partial(up_grad_kernel, dims), grid=(ff // FF_CH...  15 us
    pallas_call x3, Pallas kernels, put_in_place(): pl.pallas_call(functools.partial(place_kernel, [c.dims for c in chains],...  13.4 us
    pallas_call x1, Pallas kernels, mid_back(): pl.pallas_call(mid_back_kernel, grid=(steps,), in_specs=specs, out_specs=...  11 us
  transfers between devices with their start and end apart: 60, of which 24 were waited for; matrix products, arithmetic and copies ran while one was open for 5% of the time, Pallas kernels for 24%

profile of v3, /device:TPU:0, one launch (start us, length us, event | category | flops | bytes accessed | tf_op | source)
XLA Modules:
  0.0 332.9 jit_solution(5127532720704973857)
XLA Ops:
  1.4 21.6 %attention_forward.1 = (bf16[1024,2304]{1,0:T(8,128)(2,1)}, bf16[1024,768]{1,0:T(8,128)(2,1)S(1)}, f32[6,8,256]{2,1,0:T(8,128)S(1)}, f32[1024,768]{1,0:T(8,128)S...) custom-call(s32[1,6]{1,0:T(1,128)S(1)} %copy-done.16, ...), custom_call_target="tpu_custom_call" | custom-call | tf_op jit(solution)/shard_map/attention_forward/pallas_call | solution.py:304
  23.0 20.0 %ffn_forward.1 = (bf16[1024,3072]{1,0:T(8,128)(2,1)}, bf16[1024,3072]{1,0:T(8,128)(2,1)}, bf16[1024,768]{1,0:T(8,128)(2,1)}, f32[1024,1]{1,0:T(8,128)S(1)}, bf16...) custom-call(s32[1,6]{1,0:T(1,128)S(1)} %copy-done.16, ...), custom_call_target="tpu_custom_call" | custom-call | tf_op jit(solution)/shard_map/ffn_forward/pallas_call | solution.py:439
  44.6 4.0 %collective-permute-start = (bf16[1,48,128]{2,1,0:T(8,128)(2,1)S(1)}, bf16[1,48,128]{2,1,0:T(8,128)(2,1)S(1)}, u32[]{:S(2)}, u32[]{:S(2)}) collective-permute-start(bf16[1,48,128]{2,1,0:T(8,128)(2,1)S(1)} %get-tuple-element.131), channel_id=1, source_target_pairs={{0,16},{1,17},{2,18},{3,19},{4,20},{5,21},{6,22},{7,23},{8,24},{9,... | collective-permute-start | bytes 36872 | tf_op jit(solution)/shard_map/ppermute | solution.py:894
  48.6 1.7 collective-permute-done
  50.4 1.9 collective-permute-start.1
  52.5 1.7 collective-permute-done.1
  54.3 1.9 collective-permute-start.2
  56.3 2.1 collective-permute-done.2
  58.5 2.3 collective-permute-start.3
  60.9 2.4 collective-permute-done.3
  65.1 1.9 loss_forward.1
  67.0 2.8 collective-permute-start.5
  69.8 2.2 collective-permute-done.5
  72.1 2.1 collective-permute-start.6
  74.2 2.5 collective-permute-done.6
  76.8 2.2 collective-permute-start.7
  79.0 3.5 %collective-permute-done.7 = bf16[4,176,128]{2,1,0:T(8,128)(2,1)S(1)} collective-permute-done((bf16[4,176,128]{2,1,0:T(8,128)(2,1)S(1)}, bf16[4,176,128]{2,1,0:T(8,128)(2,1)S(1)}, u32[]{:S(2)}, u32[]{:S(2)}) %collective-permute-start.7) | collective-permute-done | bytes 180256 | tf_op jit(solution)/shard_map/ppermute | solution.py:894
  82.6 2.0 collective-permute-start.8
  84.6 5.5 %collective-permute-done.8 = bf16[8,176,128]{2,1,0:T(8,128)(2,1)S(1)} collective-permute-done((bf16[8,176,128]{2,1,0:T(8,128)(2,1)S(1)}, bf16[8,176,128]{2,1,0:T(8,128)(2,1)S(1)}, u32[]{:S(2)}, u32[]{:S(2)}) %collective-permute-start.8) | collective-permute-done | bytes 360480 | tf_op jit(solution)/shard_map/ppermute | solution.py:894
  91.2 2.4 collective-permute-done.9
  96.3 6.3 %loss_backward.1 = (f32[8,128]{1,0:T(8,128)S(1)}, f32[1024,768]{1,0:T(8,128)}, bf16[1024,768]{1,0:T(8,128)(2,1)S(1)}, f32[768,128]{1,0:T(8,128)S(1)}, f32[8,768]{1,0:T(8,128)S(1)}) custom-call(s32[1]{0:T(128)} %bitcast.me, s32[1,6]{1,0:T(1,128)S(1)} %copy-done.17, s32[32,5]{1,0:T(8,128)S(1)} %copy.33.owner, s32[32,5]{1,0:T(8,128)S(1)} %copy.34.place, ...), custom_call_target="tpu_custom_call" | custom-call | tf_op jit(solution)/shard_map/loss_backward/pallas_call | solution.py:609
  102.6 7.8 %down_gradient.1 = (f32[8,48,3200]{2,1,0:T(8,128)S(1)}, f32[8,48,3200]{2,1,0:T(8,128)S(1)}) custom-call(s32[1]{0:T(128)} %bitcast.me, bf16[1024,3072]{1,0:T(8,128)(2,1)} %get-tuple-element.140.act, bf16[1024,768]{1,0:T(8,128)(2,1)S(1)} %get-tuple-element.141.dbr, f32[768,128]{1,0:T(8,128)S(1)} %get-tuple-element.142.gwp), custom_call_target="tpu_custom_call" | custom-call | tf_op jit(solution)/shard_map/down_gradient/pallas_call | solution.py:676
  110.6 15.0 %up_gradient.1 = (f32[8,48,3072]{2,1,0:T(8,128)S(1)}, f32[8,48,3072]{2,1,0:T(8,128)}, bf16[1024,3072]{1,0:T(8,128)(2,1)}, f32[1,3072]{1,0:T(1,128)S(1)}) custom-call(s32[1]{0:T(128)} %bitcast.me, bf16[1024,768]{1,0:T(8,128)(2,1)S(1)} %get-tuple-element.141.dbr, bf16[1024,3072]{1,0:T(8,128)(2,1)} %get-tuple-element.146.slp, bf16[3072,768]{1,0:T(8,128)(2,1)} %wd.3, ...), custom_call_target="tpu_custom_call" | custom-call | tf_op jit(solution)/shard_map/up_gradient/pallas_call | solution.py:726
  126.5 1.9 collective-permute-start.11
  128.8 11.0 %middle_backward.1 = (f32[1024,768]{1,0:T(8,128)S(1)}, bf16[1024,768]{1,0:T(8,128)(2,1)S(1)}, bf16[1024,768]{1,0:T(8,128)(2,1)S(1)}, f32[8,768]{1,0:T(8,128)S(1)}) custom-call(s32[1]{0:T(128)} %bitcast.me, bf16[1024,3072]{1,0:T(8,128)(2,1)} %get-tuple-element.153.din, bf16[768,3072]{1,0:T(8,128)(2,1)} %wu.3, f32[1024,768]{1,0:T(8,128)S(1)} %copy-done.3, ...), custom_call_target="tpu_custom_call" | custom-call | tf_op jit(solution)/shard_map/middle_backward/pallas_call | solution.py:794
  139.9 4.5 %slice_add_fusion.1 = (f32[4,48,3072]{2,1,0:T(8,128)}, bf16[4,48,3072]{2,1,0:T(8,128)(2,1)S(1)}) fusion(f32[8,48,3072]{2,1,0:T(8,128)} %collective-permute-done.12, f32[8,48,3072]{2,1,0:T(8,128)S(1)} %get-tuple-element.150), kind=kLoop, calls=%fused_computation.4 | loop fusion | flops 1769472 | bytes 12976128 | tf_op jit(solution)/shard_map/add | solution.py:931
  144.4 1.9 collective-permute-start.14
  146.3 11.5 %attention_backward.3 = (bf16[1024,256]{1,0:T(8,128)(2,1)S(1)}, bf16[1024,256]{1,0:T(8,128)(2,1)S(1)}, bf16[1024,256]{1,0:T(8,128)(2,1)S(1)}, f32[8,256]{1,0:T(8,128)S(1)}) custom-call(s32[1,6]{1,0:T(1,128)S(1)} %copy-done.17, bf16[1024,2304]{1,0:T(8,128)(2,1)S(1)} %bitcast.89, bf16[1024,2304]{1,0:T(8,128)(2,1)S(1)} %bitcast.89, ...), custom_call_target="tpu_custom_call" | custom-call | tf_op jit(solution)/shard_map/attention_backward/pallas_call | solution.py:340
  159.4 2.8 qkv_gradient.3
  163.5 11.7 %attention_backward.4 = (bf16[1024,256]{1,0:T(8,128)(2,1)S(1)}, bf16[1024,256]{1,0:T(8,128)(2,1)S(1)}, bf16[1024,256]{1,0:T(8,128)(2,1)S(1)}, f32[8,256]{1,0:T(8,128)S(1)}) custom-call(s32[1,6]{1,0:T(1,128)S(1)} %copy-done.17, bf16[1024,2304]{1,0:T(8,128)(2,1)S(1)} %bitcast.89, bf16[1024,2304]{1,0:T(8,128)(2,1)S(1)} %bitcast.89, ...), custom_call_target="tpu_custom_call" | custom-call | tf_op jit(solution)/shard_map/attention_backward/pallas_call | solution.py:340
  177.2 1.6 collective-permute-start.16
  183.1 11.5 %attention_backward.5 = (bf16[1024,256]{1,0:T(8,128)(2,1)S(1)}, bf16[1024,256]{1,0:T(8,128)(2,1)S(1)}, bf16[1024,256]{1,0:T(8,128)(2,1)S(1)}, f32[8,256]{1,0:T(8,128)S(1)}) custom-call(s32[1,6]{1,0:T(1,128)S(1)} %copy-done.17, bf16[1024,2304]{1,0:T(8,128)(2,1)S(1)} %bitcast.89, bf16[1024,2304]{1,0:T(8,128)(2,1)S(1)} %bitcast.89, ...), custom_call_target="tpu_custom_call" | custom-call | tf_op jit(solution)/shard_map/attention_backward/pallas_call | solution.py:340
  196.8 3.0 collective-permute-start.25
  202.5 1.8 collective-permute-done.20
  204.3 1.8 collective-permute-start.24
  206.2 2.7 collective-permute-start.31
  210.2 2.1 collective-permute-start.28
  212.4 5.5 %input_gradient.1 = f32[1024,768]{1,0:T(8,128)} custom-call(s32[1]{0:T(128)} %bitcast.me, bf16[1024,256]{1,0:T(8,128)(2,1)S(1)} %get-tuple-element.167.d0.refs_0_, bf16[1024,256]{1,0:T(8,128)(2,1)S(1)} %get-tuple-element.179.d0.refs_1_, bf16[1024,256]{1,0:T(8,128)(2,1)S(1)} %get-tuple-element.190.d0.refs_2_, ...), custom_call_target="tpu_custom_call" | custom-call | tf_op jit(solution)/shard_map/input_gradient/pallas_call | solution.py:854
  217.9 3.0 collective-permute-done.25
  222.2 5.8 %collective-permute-done.29 = bf16[4,48,768]{2,1,0:T(8,128)(2,1)S(1)} collective-permute-done((bf16[4,48,768]{2,1,0:T(8,128)(2,1)S(1)}, bf16[4,48,768]{2,1,0:T(8,128)(2,1)S(1)}, u32[]{:S(2)}, u32[]{:S(2)}) %collective-permute-start.29) | collective-permute-done | bytes 294944 | tf_op jit(solution)/shard_map/ppermute | solution.py:894
  231.5 2.2 collective-permute-done.26
  238.3 2.8 collective-permute-start.39
  242.6 3.4 %collective-permute-done.32 = bf16[1,48,3072]{2,1,0:T(8,128)(2,1)S(1)} collective-permute-done((bf16[1,48,3072]{2,1,0:T(8,128)(2,1)S(1)}, bf16[1,48,3072]{2,1,0:T(8,128)(2,1)S(1)}, u32[]{:S(2)}, u32[]{:S(2)}) %collective-permute-start.32) | collective-permute-done | bytes 294944 | tf_op jit(solution)/shard_map/ppermute | solution.py:894
  246.9 2.1 collective-permute-start.38
  251.2 4.2 %collective-permute-start.47 = (bf16[1,48,768]{2,1,0:T(8,128)(2,1)S(1)}, bf16[1,48,768]{2,1,0:T(8,128)(2,1)S(1)}, u32[]{:S(2)}, u32[]{:S(2)}) collective-permute-start(bf16[1,48,768]{2,1,0:T(8,128)(2,1)S(1)} %add_convert_fusion.9), channel_id=1, source_target_pairs={{0,8},{1,9},{2,10},{3,11},{4,12},{5,13},{6,14},{7,15},{8,0},{9,1},... | collective-permute-start | bytes 221192 | tf_op jit(solution)/shard_map/ppermute | solution.py:894
  255.4 2.2 collective-permute-done.41
  258.3 2.6 collective-permute-start.46
  261.0 3.4 %collective-permute-start.54 = (bf16[4,48,3072]{2,1,0:T(8,128)(2,1)S(1)}, bf16[4,48,3072]{2,1,0:T(8,128)(2,1)}, u32[]{:S(2)}, u32[]{:S(2)}) collective-permute-start(bf16[4,48,3072]{2,1,0:T(8,128)(2,1)S(1)} %bitcast_select_fusion.5), channel_id=1, source_target_pairs={{0,8},{1,9},{2,10},{3,11},{4,12},{5,13},{6,14},{7,15},{8,0},{9,1},... | collective-permute-start | bytes 3538952 | tf_op jit(solution)/shard_map/ppermute | solution.py:894
  266.9 1.8 collective-permute-start.50
  268.6 14.9 %collective-permute-done.50 = f32[16,768]{1,0:T(8,128)S(1)} collective-permute-done((f32[16,768]{1,0:T(8,128)S(1)}, f32[16,768]{1,0:T(8,128)S(1)}, u32[]{:S(2)}, u32[]{:S(2)}) %collective-permute-start.50) | collective-permute-done | bytes 49184 | tf_op jit(solution)/shard_map/ppermute | solution.py:894
  285.3 1.6 bitcast_select_fusion.refs_0_
  287.0 1.6 bitcast_select_fusion.1.refs_0_
  289.2 1.7 collective-permute-start.44
  290.9 7.3 %collective-permute-done.44 = bf16[2,48,1536]{2,1,0:T(8,128)(2,1)S(1)} collective-permute-done((bf16[2,48,1536]{2,1,0:T(8,128)(2,1)S(1)}, bf16[2,48,1536]{2,1,0:T(8,128)(2,1)S(1)}, u32[]{:S(2)}, u32[]{:S(2)}) %collective-permute-start.44) | collective-permute-done | bytes 294944 | tf_op jit(solution)/shard_map/ppermute | solution.py:894
  298.3 3.8 %collective-permute-start.51 = (bf16[4,48,1536]{2,1,0:T(8,128)(2,1)S(1)}, bf16[4,48,1536]{2,1,0:T(8,128)(2,1)S(1)}, u32[]{:S(2)}, u32[]{:S(2)}) collective-permute-start(bf16[4,48,1536]{2,1,0:T(8,128)(2,1)S(1)} %bitcast_select_fusion.9), channel_id=1, source_target_pairs={{0,8},{1,9},{2,10},{3,11},{4,12},{5,13},{6,14},{7,15},{8,0},{9,1},... | collective-permute-start | bytes 1769480 | tf_op jit(solution)/shard_map/ppermute | solution.py:894
  302.1 1.7 collective-permute-start.52
  303.8 4.1 %down_place.1 = (f32[3072,768]{1,0:T(8,128)}, f32[768,128]{1,0:T(8,128)}) custom-call(s32[1]{0:T(128)} %bitcast.me, bf16[8,48,3200]{2,1,0:T(8,128)(2,1)S(1)} %bitcast_select_fusion.refs_0_, bf16[8,48,3200]{2,1,0:T(8,128)(2,1)S(1)} %collective-permute-done.53.refs_1_), custom_call_target="tpu_custom_call" | custom-call | tf_op jit(solution)/shard_map/down_place/pallas_call | solution.py:1016
  307.9 2.0 collective-permute-done.52
  310.1 4.7 %collective-permute-done.51 = bf16[4,48,1536]{2,1,0:T(8,128)(2,1)S(1)} collective-permute-done((bf16[4,48,1536]{2,1,0:T(8,128)(2,1)S(1)}, bf16[4,48,1536]{2,1,0:T(8,128)(2,1)S(1)}, u32[]{:S(2)}, u32[]{:S(2)}) %collective-permute-start.51) | collective-permute-done | bytes 589856 | tf_op jit(solution)/shard_map/ppermute | solution.py:894
  315.1 1.8 collective-permute-start.56
  317.1 4.0 %up_place.1 = f32[768,3072]{1,0:T(8,128)} custom-call(s32[1]{0:T(128)} %bitcast.me, bf16[8,48,3072]{2,1,0:T(8,128)(2,1)S(1)} %bitcast_select_fusion.1.refs_0_, bf16[8,48,3072]{2,1,0:T(8,128)(2,1)S(1)} %collective-permute-done.57.refs_1_), custom_call_target="tpu_custom_call" | custom-call | tf_op jit(solution)/shard_map/up_place/pallas_call | solution.py:1016
  321.1 3.4 %collective-permute-done.56 = bf16[4,48,768]{2,1,0:T(8,128)(2,1)S(1)} collective-permute-done((bf16[4,48,768]{2,1,0:T(8,128)(2,1)S(1)}, bf16[4,48,768]{2,1,0:T(8,128)(2,1)S(1)}, u32[]{:S(2)}, u32[]{:S(2)}) %collective-permute-start.56) | collective-permute-done | bytes 294944 | tf_op jit(solution)/shard_map/ppermute | solution.py:894
  325.9 1.5 slice_reduce_fusion
  327.4 5.3 %qkv_place.1 = (f32[768,2304]{1,0:T(8,128)}, f32[768,768]{1,0:T(8,128)}) custom-call(s32[1]{0:T(128)} %bitcast.me, bf16[8,48,1536]{2,1,0:T(8,128)(2,1)S(1)} %bitcast_select_fusion.4.refs_0_, bf16[8,48,1536]{2,1,0:T(8,128)(2,1)S(1)} %collective-permute-done.55.refs_1_, bf16[8,48,768]{2,1,0:T(8,128)(2,1)S(1)} %bitcast_select_fusion.8.refs_2_, ...), custom_call_target="tpu_custom_call" | custom-call | tf_op jit(solution)/shard_map/qkv_place/pallas_call | solution.py:1016
  (216 shorter events, 47.1 us)
Async XLA Ops:
  0.6 22.3 %copy-start.8 = (bf16[768,128]{1,0:T(8,128)(2,1)S(1)}, bf16[768,128]{1,0:T(8,128)(2,1)}, u32[]{:S(2)}) copy-start(bf16[768,128]{1,0:T(8,128)(2,1)} %wp.3) | copy-start | bytes 589828
  1.4 21.6 %copy-start.22 = (f32[768]{0:T(1024)S(1)}, f32[768]{0:T(1024)}, u32[]{:S(2)}) copy-start(f32[768]{0:T(1024)} %b2.1) | copy-start | bytes 9220
  23.0 40.7 %copy-start.25 = (s32[32,5]{0,1:T(8,128)S(1)}, s32[32,5]{0,1:T(8,128)}, u32[]{:S(2)}) copy-start(s32[32,5]{0,1:T(8,128)} %param.19) | copy-start | bytes 1924
  44.6 5.7 %collective-permute-start = (bf16[1,48,128]{2,1,0:T(8,128)(2,1)S(1)}, bf16[1,48,128]{2,1,0:T(8,128)(2,1)S(1)}, u32[]{:S(2)}, u32[]{:S(2)}) collective-permute-start(bf16[1,48,128]{2,1,0:T(8,128)(2,1)S(1)} %get-tuple-element.131), channel_id=1, source_target_pairs={{0,16},{1,17},{2,18},{3,19},{4,20},{5,21},{6,22},{7,23},{8,24},{9,... | collective-permute-start | bytes 36872 | tf_op jit(solution)/shard_map/ppermute | solution.py:894
  50.4 3.8 %collective-permute-start.1 = (bf16[2,48,128]{2,1,0:T(8,128)(2,1)S(1)}, bf16[2,48,128]{2,1,0:T(8,128)(2,1)S(1)}, u32[]{:S(2)}, u32[]{:S(2)}) collective-permute-start(bf16[2,48,128]{2,1,0:T(8,128)(2,1)S(1)} %broadcast_select_fusion.6), channel_id=1, source_target_pairs={{0,8},{1,9},{2,10},{3,11},{4,12},{5,13},{6,14},{7,15},{8,0},{9,1},... | collective-permute-start | bytes 73736 | tf_op jit(solution)/shard_map/ppermute | solution.py:894
  54.3 4.1 %collective-permute-start.2 = (bf16[4,48,128]{2,1,0:T(8,128)(2,1)S(1)}, bf16[4,48,128]{2,1,0:T(8,128)(2,1)S(1)}, u32[]{:S(2)}, u32[]{:S(2)}) collective-permute-start(bf16[4,48,128]{2,1,0:T(8,128)(2,1)S(1)} %bitcast_select_fusion.17), channel_id=1, source_target_pairs={{0,4},{1,5},{2,6},{3,7},{4,0},{5,1},{6,2},{7,3},{8,12},{9,13},{10,... | collective-permute-start | bytes 147464 | tf_op jit(solution)/shard_map/ppermute | solution.py:894
  58.5 4.9 %collective-permute-start.3 = (bf16[8,48,128]{2,1,0:T(8,128)(2,1)S(1)}, bf16[8,48,128]{2,1,0:T(8,128)(2,1)S(1)}, u32[]{:S(2)}, u32[]{:S(2)}) collective-permute-start(bf16[8,48,128]{2,1,0:T(8,128)(2,1)S(1)} %bitcast_select_fusion.16), channel_id=1, source_target_pairs={{0,2},{1,3},{2,0},{3,1},{4,6},{5,7},{6,4},{7,5},{8,10},{9,11},{10,... | collective-permute-start | bytes 294920 | tf_op jit(solution)/shard_map/ppermute | solution.py:894
  63.5 1.5 collective-permute-start.4
  67.0 24.1 %copy-start.26 = (s32[32,5]{0,1:T(8,128)S(1)}, s32[32,5]{0,1:T(8,128)}, u32[]{:S(2)}) copy-start(s32[32,5]{0,1:T(8,128)} %param.20) | copy-start | bytes 1924
  67.0 5.0 %collective-permute-start.5 = (bf16[1,176,128]{2,1,0:T(8,128)(2,1)S(1)}, bf16[1,176,128]{2,1,0:T(8,128)(2,1)S(1)}, u32[]{:S(2)}, u32[]{:S(2)}) collective-permute-start(bf16[1,176,128]{2,1,0:T(8,128)(2,1)S(1)} %get-tuple-element.133), channel_id=1, source_target_pairs={{0,16},{1,17},{2,18},{3,19},{4,20},{5,21},{6,22},{7,23},{8,24},{9,... | collective-permute-start | bytes 135176 | tf_op jit(solution)/shard_map/ppermute | solution.py:894
  72.1 4.6 %collective-permute-start.6 = (bf16[2,176,128]{2,1,0:T(8,128)(2,1)S(1)}, bf16[2,176,128]{2,1,0:T(8,128)(2,1)S(1)}, u32[]{:S(2)}, u32[]{:S(2)}) collective-permute-start(bf16[2,176,128]{2,1,0:T(8,128)(2,1)S(1)} %broadcast_select_fusion.5), channel_id=1, source_target_pairs={{0,8},{1,9},{2,10},{3,11},{4,12},{5,13},{6,14},{7,15},{8,0},{9,1},... | collective-permute-start | bytes 270344 | tf_op jit(solution)/shard_map/ppermute | solution.py:894
  76.8 5.7 %collective-permute-start.7 = (bf16[4,176,128]{2,1,0:T(8,128)(2,1)S(1)}, bf16[4,176,128]{2,1,0:T(8,128)(2,1)S(1)}, u32[]{:S(2)}, u32[]{:S(2)}) collective-permute-start(bf16[4,176,128]{2,1,0:T(8,128)(2,1)S(1)} %bitcast_select_fusion.15), channel_id=1, source_target_pairs={{0,4},{1,5},{2,6},{3,7},{4,0},{5,1},{6,2},{7,3},{8,12},{9,13},{10,... | collective-permute-start | bytes 540680 | tf_op jit(solution)/shard_map/ppermute | solution.py:894
  82.6 7.5 %collective-permute-start.8 = (bf16[8,176,128]{2,1,0:T(8,128)(2,1)S(1)}, bf16[8,176,128]{2,1,0:T(8,128)(2,1)S(1)}, u32[]{:S(2)}, u32[]{:S(2)}) collective-permute-start(bf16[8,176,128]{2,1,0:T(8,128)(2,1)S(1)} %bitcast_select_fusion.11), channel_id=1, source_target_pairs={{0,2},{1,3},{2,0},{3,1},{4,6},{5,7},{6,4},{7,5},{8,10},{9,11},{10,... | collective-permute-start | bytes 1081352 | tf_op jit(solution)/shard_map/ppermute | solution.py:894
  91.1 2.5 collective-permute-start.9
  110.4 15.6 %collective-permute-start.10 = (f32[8,48,3200]{2,1,0:T(8,128)S(1)}, f32[8,48,3200]{2,1,0:T(8,128)S(1)}, u32[]{:S(2)}, u32[]{:S(2)}) collective-permute-start(f32[8,48,3200]{2,1,0:T(8,128)S(1)} %get-tuple-element.144), channel_id=1, source_target_pairs={{0,1},{1,0},{2,3},{3,2},{4,5},{5,4},{6,7},{7,6},{8,9},{9,8},{10,11... | collective-permute-start | bytes 14745608 | tf_op jit(solution)/shard_map/ppermute | solution.py:894
  125.6 14.2 %collective-permute-start.12 = (f32[8,48,3072]{2,1,0:T(8,128)}, f32[8,48,3072]{2,1,0:T(8,128)}, u32[]{:S(2)}, u32[]{:S(2)}) collective-permute-start(f32[8,48,3072]{2,1,0:T(8,128)} %get-tuple-element.151), channel_id=1, source_target_pairs={{0,1},{1,0},{2,3},{3,2},{4,5},{5,4},{6,7},{7,6},{8,9},{9,8},{10,11... | collective-permute-start | bytes 14155784 | tf_op jit(solution)/shard_map/ppermute | solution.py:894
  126.5 31.3 %collective-permute-start.11 = (bf16[4,48,3200]{2,1,0:T(8,128)(2,1)S(1)}, bf16[4,48,3200]{2,1,0:T(8,128)(2,1)S(1)}, u32[]{:S(2)}, u32[]{:S(2)}) collective-permute-start(bf16[4,48,3200]{2,1,0:T(8,128)(2,1)S(1)} %get-tuple-element.250), channel_id=1, source_target_pairs={{0,2},{1,3},{2,0},{3,1},{4,6},{5,7},{6,4},{7,5},{8,10},{9,11},{10,... | collective-permute-start | bytes 3686408 | tf_op jit(solution)/shard_map/ppermute | solution.py:894
  144.4 30.8 %collective-permute-start.14 = (bf16[4,48,3072]{2,1,0:T(8,128)(2,1)S(1)}, bf16[4,48,3072]{2,1,0:T(8,128)(2,1)S(1)}, u32[]{:S(2)}, u32[]{:S(2)}) collective-permute-start(bf16[4,48,3072]{2,1,0:T(8,128)(2,1)S(1)} %get-tuple-element.252), channel_id=1, source_target_pairs={{0,8},{1,9},{2,10},{3,11},{4,12},{5,13},{6,14},{7,15},{8,0},{9,1},... | collective-permute-start | bytes 3538952 | tf_op jit(solution)/shard_map/ppermute | solution.py:894
  162.2 18.2 %collective-permute-start.17 = (f32[8,48,1536]{2,1,0:T(8,128)S(1)}, f32[8,48,1536]{2,1,0:T(8,128)S(1)}, u32[]{:S(2)}, u32[]{:S(2)}) collective-permute-start(f32[8,48,1536]{2,1,0:T(8,128)S(1)} %get-tuple-element.171), channel_id=1, source_target_pairs={{0,1},{1,0},{2,3},{3,2},{4,5},{5,4},{6,7},{7,6},{8,9},{9,8},{10,11... | collective-permute-start | bytes 7077896 | tf_op jit(solution)/shard_map/ppermute | solution.py:894
  162.2 16.5 %collective-permute-start.13 = (bf16[2,48,3200]{2,1,0:T(8,128)(2,1)S(1)}, bf16[2,48,3200]{2,1,0:T(8,128)(2,1)S(1)}, u32[]{:S(2)}, u32[]{:S(2)}) collective-permute-start(bf16[2,48,3200]{2,1,0:T(8,128)(2,1)S(1)} %get-tuple-element.254), channel_id=1, source_target_pairs={{0,4},{1,5},{2,6},{3,7},{4,0},{5,1},{6,2},{7,3},{8,12},{9,13},{10,... | collective-permute-start | bytes 1843208 | tf_op jit(solution)/shard_map/ppermute | solution.py:894
  177.2 17.4 %collective-permute-start.16 = (bf16[2,48,3072]{2,1,0:T(8,128)(2,1)S(1)}, bf16[2,48,3072]{2,1,0:T(8,128)(2,1)S(1)}, u32[]{:S(2)}, u32[]{:S(2)}) collective-permute-start(bf16[2,48,3072]{2,1,0:T(8,128)(2,1)S(1)} %get-tuple-element.258), channel_id=1, source_target_pairs={{0,2},{1,3},{2,0},{3,1},{4,6},{5,7},{6,4},{7,5},{8,10},{9,11},{10,... | collective-permute-start | bytes 1769480 | tf_op jit(solution)/shard_map/ppermute | solution.py:894
  178.9 17.8 %collective-permute-start.15 = (bf16[1,48,3200]{2,1,0:T(8,128)(2,1)S(1)}, bf16[1,48,3200]{2,1,0:T(8,128)(2,1)S(1)}, u32[]{:S(2)}, u32[]{:S(2)}) collective-permute-start(bf16[1,48,3200]{2,1,0:T(8,128)(2,1)S(1)} %fusion.2), channel_id=1, source_target_pairs={{0,8},{1,9},{2,10},{3,11},{4,12},{5,13},{6,14},{7,15},{8,0},{9,1},... | collective-permute-start | bytes 921608 | tf_op jit(solution)/shard_map/ppermute | solution.py:894
  180.8 21.3 %collective-permute-start.18 = (bf16[4,48,1536]{2,1,0:T(8,128)(2,1)S(1)}, bf16[4,48,1536]{2,1,0:T(8,128)(2,1)S(1)}, u32[]{:S(2)}, u32[]{:S(2)}) collective-permute-start(bf16[4,48,1536]{2,1,0:T(8,128)(2,1)S(1)} %get-tuple-element.256), channel_id=1, source_target_pairs={{0,8},{1,9},{2,10},{3,11},{4,12},{5,13},{6,14},{7,15},{8,0},{9,1},... | collective-permute-start | bytes 1769480 | tf_op jit(solution)/shard_map/ppermute | solution.py:894
  183.0 16.8 %collective-permute-start.19 = (f32[8,48,768]{2,1,0:T(8,128)S(1)}, f32[8,48,768]{2,1,0:T(8,128)S(1)}, u32[]{:S(2)}, u32[]{:S(2)}) collective-permute-start(f32[8,48,768]{2,1,0:T(8,128)S(1)} %get-tuple-element.182), channel_id=1, source_target_pairs={{0,1},{1,0},{2,3},{3,2},{4,5},{5,4},{6,7},{7,6},{8,9},{9,8},{10,11... | collective-permute-start | bytes 3538952 | tf_op jit(solution)/shard_map/ppermute | solution.py:894
  194.6 15.6 %collective-permute-start.23 = (f32[16,768]{1,0:T(8,128)S(1)}, f32[16,768]{1,0:T(8,128)S(1)}, u32[]{:S(2)}, u32[]{:S(2)}) collective-permute-start(f32[16,768]{1,0:T(8,128)S(1)} %collect_vectors.1), channel_id=1, source_target_pairs={{0,1},{1,0},{2,3},{3,2},{4,5},{5,4},{6,7},{7,6},{8,9},{9,8},{10,11... | collective-permute-start | bytes 147464 | tf_op jit(solution)/shard_map/ppermute | solution.py:894
  195.3 9.0 %collective-permute-start.20 = (bf16[1,48,3072]{2,1,0:T(8,128)(2,1)S(1)}, bf16[1,48,3072]{2,1,0:T(8,128)(2,1)S(1)}, u32[]{:S(2)}, u32[]{:S(2)}) collective-permute-start(bf16[1,48,3072]{2,1,0:T(8,128)(2,1)S(1)} %fusion.8), channel_id=1, source_target_pairs={{0,4},{1,5},{2,6},{3,7},{4,0},{5,1},{6,2},{7,3},{8,12},{9,13},{10,... | collective-permute-start | bytes 884744 | tf_op jit(solution)/shard_map/ppermute | solution.py:894
  196.8 24.1 %collective-permute-start.25 = (bf16[1,48,3200]{2,1,0:T(8,128)(2,1)S(1)}, bf16[1,48,3200]{2,1,0:T(8,128)(2,1)S(1)}, u32[]{:S(2)}, u32[]{:S(2)}) collective-permute-start(bf16[1,48,3200]{2,1,0:T(8,128)(2,1)S(1)} %fusion.4), channel_id=1, source_target_pairs={{0,16},{1,17},{2,18},{3,19},{4,20},{5,21},{6,22},{7,23},{8,24},{9,... | collective-permute-start | bytes 921608 | tf_op jit(solution)/shard_map/ppermute | solution.py:894
  200.0 10.0 %collective-permute-start.22 = (bf16[4,48,768]{2,1,0:T(8,128)(2,1)S(1)}, bf16[4,48,768]{2,1,0:T(8,128)(2,1)S(1)}, u32[]{:S(2)}, u32[]{:S(2)}) collective-permute-start(bf16[4,48,768]{2,1,0:T(8,128)(2,1)S(1)} %get-tuple-element.264), channel_id=1, source_target_pairs={{0,2},{1,3},{2,0},{3,1},{4,6},{5,7},{6,4},{7,5},{8,10},{9,11},{10,... | collective-permute-start | bytes 884744 | tf_op jit(solution)/shard_map/ppermute | solution.py:894
  202.1 4.0 %collective-permute-start.21 = (f32[8,48,768]{2,1,0:T(8,128)S(1)}, f32[8,48,768]{2,1,0:T(8,128)S(1)}, u32[]{:S(2)}, u32[]{:S(2)}) collective-permute-start(f32[8,48,768]{2,1,0:T(8,128)S(1)} %get-tuple-element.193), channel_id=1, source_target_pairs={{0,1},{1,0},{2,3},{3,2},{4,5},{5,4},{6,7},{7,6},{8,9},{9,8},{10,11... | collective-permute-start | bytes 3538952 | tf_op jit(solution)/shard_map/ppermute | solution.py:894
  204.3 17.7 %collective-permute-start.24 = (bf16[2,48,1536]{2,1,0:T(8,128)(2,1)S(1)}, bf16[2,48,1536]{2,1,0:T(8,128)(2,1)S(1)}, u32[]{:S(2)}, u32[]{:S(2)}) collective-permute-start(bf16[2,48,1536]{2,1,0:T(8,128)(2,1)S(1)} %get-tuple-element.262), channel_id=1, source_target_pairs={{0,2},{1,3},{2,0},{3,1},{4,6},{5,7},{6,4},{7,5},{8,10},{9,11},{10,... | collective-permute-start | bytes 884744 | tf_op jit(solution)/shard_map/ppermute | solution.py:894
  206.2 28.2 %collective-permute-start.31 = (bf16[1,48,3072]{2,1,0:T(8,128)(2,1)S(1)}, bf16[1,48,3072]{2,1,0:T(8,128)(2,1)S(1)}, u32[]{:S(2)}, u32[]{:S(2)}) collective-permute-start(bf16[1,48,3072]{2,1,0:T(8,128)(2,1)S(1)} %fusion.6), channel_id=1, source_target_pairs={{0,16},{1,17},{2,18},{3,19},{4,20},{5,21},{6,22},{7,23},{8,24},{9,... | collective-permute-start | bytes 884744 | tf_op jit(solution)/shard_map/ppermute | solution.py:894
  210.2 20.2 %collective-permute-start.27 = (f32[16,768]{1,0:T(8,128)S(1)}, f32[16,768]{1,0:T(8,128)S(1)}, u32[]{:S(2)}, u32[]{:S(2)}) collective-permute-start(f32[16,768]{1,0:T(8,128)S(1)} %add.156), channel_id=1, source_target_pairs={{0,2},{1,3},{2,0},{3,1},{4,6},{5,7},{6,4},{7,5},{8,10},{9,11},{10,... | collective-permute-start | bytes 147464 | tf_op jit(solution)/shard_map/ppermute | solution.py:894
  210.2 18.5 %collective-permute-start.28 = (bf16[2,48,768]{2,1,0:T(8,128)(2,1)S(1)}, bf16[2,48,768]{2,1,0:T(8,128)(2,1)S(1)}, u32[]{:S(2)}, u32[]{:S(2)}) collective-permute-start(bf16[2,48,768]{2,1,0:T(8,128)(2,1)S(1)} %get-tuple-element.268), channel_id=1, source_target_pairs={{0,4},{1,5},{2,6},{3,7},{4,0},{5,1},{6,2},{7,3},{8,12},{9,13},{10,... | collective-permute-start | bytes 442376 | tf_op jit(solution)/shard_map/ppermute | solution.py:894
  220.9 7.1 %collective-permute-start.29 = (bf16[4,48,768]{2,1,0:T(8,128)(2,1)S(1)}, bf16[4,48,768]{2,1,0:T(8,128)(2,1)S(1)}, u32[]{:S(2)}, u32[]{:S(2)}) collective-permute-start(bf16[4,48,768]{2,1,0:T(8,128)(2,1)S(1)} %get-tuple-element.260), channel_id=1, source_target_pairs={{0,2},{1,3},{2,0},{3,1},{4,6},{5,7},{6,4},{7,5},{8,10},{9,11},{10,... | collective-permute-start | bytes 884744 | tf_op jit(solution)/shard_map/ppermute | solution.py:894
  222.0 19.1 %collective-permute-start.34 = (bf16[1,48,3200]{2,1,0:T(8,128)(2,1)S(1)}, bf16[1,48,3200]{2,1,0:T(8,128)(2,1)S(1)}, u32[]{:S(2)}, u32[]{:S(2)}) collective-permute-start(bf16[1,48,3200]{2,1,0:T(8,128)(2,1)S(1)} %add_convert_fusion.3), channel_id=1, source_target_pairs={{0,8},{1,9},{2,10},{3,11},{4,12},{5,13},{6,14},{7,15},{8,0},{9,1},... | collective-permute-start | bytes 921608 | tf_op jit(solution)/shard_map/ppermute | solution.py:894
  228.0 5.7 %collective-permute-start.26 = (bf16[1,48,1536]{2,1,0:T(8,128)(2,1)S(1)}, bf16[1,48,1536]{2,1,0:T(8,128)(2,1)S(1)}, u32[]{:S(2)}, u32[]{:S(2)}) collective-permute-start(bf16[1,48,1536]{2,1,0:T(8,128)(2,1)S(1)} %fusion.10), channel_id=1, source_target_pairs={{0,4},{1,5},{2,6},{3,7},{4,0},{5,1},{6,2},{7,3},{8,12},{9,13},{10,... | collective-permute-start | bytes 442376 | tf_op jit(solution)/shard_map/ppermute | solution.py:894
  228.8 7.2 %collective-permute-start.36 = (bf16[2,48,768]{2,1,0:T(8,128)(2,1)S(1)}, bf16[2,48,768]{2,1,0:T(8,128)(2,1)S(1)}, u32[]{:S(2)}, u32[]{:S(2)}) collective-permute-start(bf16[2,48,768]{2,1,0:T(8,128)(2,1)S(1)} %get-tuple-element.266), channel_id=1, source_target_pairs={{0,4},{1,5},{2,6},{3,7},{4,0},{5,1},{6,2},{7,3},{8,12},{9,13},{10,... | collective-permute-start | bytes 442376 | tf_op jit(solution)/shard_map/ppermute | solution.py:894
  230.3 11.1 %collective-permute-start.33 = (bf16[1,48,768]{2,1,0:T(8,128)(2,1)S(1)}, bf16[1,48,768]{2,1,0:T(8,128)(2,1)S(1)}, u32[]{:S(2)}, u32[]{:S(2)}) collective-permute-start(bf16[1,48,768]{2,1,0:T(8,128)(2,1)S(1)} %fusion.19), channel_id=1, source_target_pairs={{0,8},{1,9},{2,10},{3,11},{4,12},{5,13},{6,14},{7,15},{8,0},{9,1},... | collective-permute-start | bytes 221192 | tf_op jit(solution)/shard_map/ppermute | solution.py:894
  233.7 4.6 %collective-permute-start.35 = (f32[16,768]{1,0:T(8,128)S(1)}, f32[16,768]{1,0:T(8,128)S(1)}, u32[]{:S(2)}, u32[]{:S(2)}) collective-permute-start(f32[16,768]{1,0:T(8,128)S(1)} %add.165), channel_id=1, source_target_pairs={{0,4},{1,5},{2,6},{3,7},{4,0},{5,1},{6,2},{7,3},{8,12},{9,13},{10,... | collective-permute-start | bytes 147464 | tf_op jit(solution)/shard_map/ppermute | solution.py:894
  234.4 12.5 %collective-permute-start.30 = (bf16[1,48,1536]{2,1,0:T(8,128)(2,1)S(1)}, bf16[1,48,1536]{2,1,0:T(8,128)(2,1)S(1)}, u32[]{:S(2)}, u32[]{:S(2)}) collective-permute-start(bf16[1,48,1536]{2,1,0:T(8,128)(2,1)S(1)} %fusion.12), channel_id=1, source_target_pairs={{0,16},{1,17},{2,18},{3,19},{4,20},{5,21},{6,22},{7,23},{8,24},{9,... | collective-permute-start | bytes 442376 | tf_op jit(solution)/shard_map/ppermute | solution.py:894
  236.0 10.0 %collective-permute-start.32 = (bf16[1,48,3072]{2,1,0:T(8,128)(2,1)S(1)}, bf16[1,48,3072]{2,1,0:T(8,128)(2,1)S(1)}, u32[]{:S(2)}, u32[]{:S(2)}) collective-permute-start(bf16[1,48,3072]{2,1,0:T(8,128)(2,1)S(1)} %add_convert_fusion.4), channel_id=1, source_target_pairs={{0,4},{1,5},{2,6},{3,7},{4,0},{5,1},{6,2},{7,3},{8,12},{9,13},{10,... | collective-permute-start | bytes 884744 | tf_op jit(solution)/shard_map/ppermute | solution.py:894
  238.3 10.7 %collective-permute-start.39 = (bf16[1,48,768]{2,1,0:T(8,128)(2,1)S(1)}, bf16[1,48,768]{2,1,0:T(8,128)(2,1)S(1)}, u32[]{:S(2)}, u32[]{:S(2)}) collective-permute-start(bf16[1,48,768]{2,1,0:T(8,128)(2,1)S(1)} %fusion.16), channel_id=1, source_target_pairs={{0,8},{1,9},{2,10},{3,11},{4,12},{5,13},{6,14},{7,15},{8,0},{9,1},... | collective-permute-start | bytes 221192 | tf_op jit(solution)/shard_map/ppermute | solution.py:894
  241.2 8.7 %collective-permute-start.43 = (f32[16,768]{1,0:T(8,128)S(1)}, f32[16,768]{1,0:T(8,128)S(1)}, u32[]{:S(2)}, u32[]{:S(2)}) collective-permute-start(f32[16,768]{1,0:T(8,128)S(1)} %add.171), channel_id=1, source_target_pairs={{0,8},{1,9},{2,10},{3,11},{4,12},{5,13},{6,14},{7,15},{8,0},{9,1},... | collective-permute-start | bytes 147464 | tf_op jit(solution)/shard_map/ppermute | solution.py:894
  241.4 16.2 %collective-permute-start.41 = (bf16[2,48,3200]{2,1,0:T(8,128)(2,1)S(1)}, bf16[2,48,3200]{2,1,0:T(8,128)(2,1)S(1)}, u32[]{:S(2)}, u32[]{:S(2)}) collective-permute-start(bf16[2,48,3200]{2,1,0:T(8,128)(2,1)S(1)} %broadcast_select_fusion), channel_id=1, source_target_pairs={{0,4},{1,5},{2,6},{3,7},{4,0},{5,1},{6,2},{7,3},{8,12},{9,13},{10,... | collective-permute-start | bytes 1843208 | tf_op jit(solution)/shard_map/ppermute | solution.py:894
  246.0 5.3 %collective-permute-start.42 = (bf16[1,48,768]{2,1,0:T(8,128)(2,1)S(1)}, bf16[1,48,768]{2,1,0:T(8,128)(2,1)S(1)}, u32[]{:S(2)}, u32[]{:S(2)}) collective-permute-start(bf16[1,48,768]{2,1,0:T(8,128)(2,1)S(1)} %fusion.18), channel_id=1, source_target_pairs={{0,16},{1,17},{2,18},{3,19},{4,20},{5,21},{6,22},{7,23},{8,24},{9,... | collective-permute-start | bytes 221192 | tf_op jit(solution)/shard_map/ppermute | solution.py:894
  246.9 13.9 %collective-permute-start.38 = (bf16[2,48,3072]{2,1,0:T(8,128)(2,1)S(1)}, bf16[2,48,3072]{2,1,0:T(8,128)(2,1)S(1)}, u32[]{:S(2)}, u32[]{:S(2)}) collective-permute-start(bf16[2,48,3072]{2,1,0:T(8,128)(2,1)S(1)} %broadcast_select_fusion.1), channel_id=1, source_target_pairs={{0,2},{1,3},{2,0},{3,1},{4,6},{5,7},{6,4},{7,5},{8,10},{9,11},{10,... | collective-permute-start | bytes 1769480 | tf_op jit(solution)/shard_map/ppermute | solution.py:894
  249.0 15.4 %collective-permute-start.37 = (bf16[1,48,1536]{2,1,0:T(8,128)(2,1)S(1)}, bf16[1,48,1536]{2,1,0:T(8,128)(2,1)S(1)}, u32[]{:S(2)}, u32[]{:S(2)}) collective-permute-start(bf16[1,48,1536]{2,1,0:T(8,128)(2,1)S(1)} %add_convert_fusion.7), channel_id=1, source_target_pairs={{0,4},{1,5},{2,6},{3,7},{4,0},{5,1},{6,2},{7,3},{8,12},{9,13},{10,... | collective-permute-start | bytes 442376 | tf_op jit(solution)/shard_map/ppermute | solution.py:894
  249.8 8.4 %collective-permute-start.40 = (bf16[1,48,768]{2,1,0:T(8,128)(2,1)S(1)}, bf16[1,48,768]{2,1,0:T(8,128)(2,1)S(1)}, u32[]{:S(2)}, u32[]{:S(2)}) collective-permute-start(bf16[1,48,768]{2,1,0:T(8,128)(2,1)S(1)} %fusion.15), channel_id=1, source_target_pairs={{0,16},{1,17},{2,18},{3,19},{4,20},{5,21},{6,22},{7,23},{8,24},{9,... | collective-permute-start | bytes 221192 | tf_op jit(solution)/shard_map/ppermute | solution.py:894
  251.2 13.3 %collective-permute-start.47 = (bf16[1,48,768]{2,1,0:T(8,128)(2,1)S(1)}, bf16[1,48,768]{2,1,0:T(8,128)(2,1)S(1)}, u32[]{:S(2)}, u32[]{:S(2)}) collective-permute-start(bf16[1,48,768]{2,1,0:T(8,128)(2,1)S(1)} %add_convert_fusion.9), channel_id=1, source_target_pairs={{0,8},{1,9},{2,10},{3,11},{4,12},{5,13},{6,14},{7,15},{8,0},{9,1},... | collective-permute-start | bytes 221192 | tf_op jit(solution)/shard_map/ppermute | solution.py:894
  257.8 27.5 %collective-permute-start.45 = (bf16[4,48,3200]{2,1,0:T(8,128)(2,1)S(1)}, bf16[4,48,3200]{2,1,0:T(8,128)(2,1)}, u32[]{:S(2)}, u32[]{:S(2)}) collective-permute-start(bf16[4,48,3200]{2,1,0:T(8,128)(2,1)S(1)} %bitcast_select_fusion.3), channel_id=1, source_target_pairs={{0,2},{1,3},{2,0},{3,1},{4,6},{5,7},{6,4},{7,5},{8,10},{9,11},{10,... | collective-permute-start | bytes 3686408 | tf_op jit(solution)/shard_map/ppermute | solution.py:894
  258.3 7.2 %collective-permute-start.46 = (bf16[1,48,768]{2,1,0:T(8,128)(2,1)S(1)}, bf16[1,48,768]{2,1,0:T(8,128)(2,1)S(1)}, u32[]{:S(2)}, u32[]{:S(2)}) collective-permute-start(bf16[1,48,768]{2,1,0:T(8,128)(2,1)S(1)} %add_convert_fusion.8), channel_id=1, source_target_pairs={{0,8},{1,9},{2,10},{3,11},{4,12},{5,13},{6,14},{7,15},{8,0},{9,1},... | collective-permute-start | bytes 221192 | tf_op jit(solution)/shard_map/ppermute | solution.py:894
  261.0 26.0 %collective-permute-start.54 = (bf16[4,48,3072]{2,1,0:T(8,128)(2,1)S(1)}, bf16[4,48,3072]{2,1,0:T(8,128)(2,1)}, u32[]{:S(2)}, u32[]{:S(2)}) collective-permute-start(bf16[4,48,3072]{2,1,0:T(8,128)(2,1)S(1)} %bitcast_select_fusion.5), channel_id=1, source_target_pairs={{0,8},{1,9},{2,10},{3,11},{4,12},{5,13},{6,14},{7,15},{8,0},{9,1},... | collective-permute-start | bytes 3538952 | tf_op jit(solution)/shard_map/ppermute | solution.py:894
  264.6 19.6 %collective-permute-start.49 = (bf16[2,48,768]{2,1,0:T(8,128)(2,1)S(1)}, bf16[2,48,768]{2,1,0:T(8,128)(2,1)}, u32[]{:S(2)}, u32[]{:S(2)}) collective-permute-start(bf16[2,48,768]{2,1,0:T(8,128)(2,1)S(1)} %broadcast_select_fusion.4), channel_id=1, source_target_pairs={{0,4},{1,5},{2,6},{3,7},{4,0},{5,1},{6,2},{7,3},{8,12},{9,13},{10,... | collective-permute-start | bytes 442376 | tf_op jit(solution)/shard_map/ppermute | solution.py:894
  265.5 19.7 %collective-permute-start.48 = (bf16[2,48,768]{2,1,0:T(8,128)(2,1)S(1)}, bf16[2,48,768]{2,1,0:T(8,128)(2,1)S(1)}, u32[]{:S(2)}, u32[]{:S(2)}) collective-permute-start(bf16[2,48,768]{2,1,0:T(8,128)(2,1)S(1)} %broadcast_select_fusion.3), channel_id=1, source_target_pairs={{0,4},{1,5},{2,6},{3,7},{4,0},{5,1},{6,2},{7,3},{8,12},{9,13},{10,... | collective-permute-start | bytes 442376 | tf_op jit(solution)/shard_map/ppermute | solution.py:894
  266.9 16.7 %collective-permute-start.50 = (f32[16,768]{1,0:T(8,128)S(1)}, f32[16,768]{1,0:T(8,128)S(1)}, u32[]{:S(2)}, u32[]{:S(2)}) collective-permute-start(f32[16,768]{1,0:T(8,128)S(1)} %add.176), channel_id=1, source_target_pairs={{0,16},{1,17},{2,18},{3,19},{4,20},{5,21},{6,22},{7,23},{8,24},{9,... | collective-permute-start | bytes 147464 | tf_op jit(solution)/shard_map/ppermute | solution.py:894
  286.9 16.9 %collective-permute-start.53 = (bf16[8,48,3200]{2,1,0:T(8,128)(2,1)S(1)}, bf16[8,48,3200]{2,1,0:T(8,128)(2,1)S(1)}, u32[]{:S(2)}, u32[]{:S(2)}) collective-permute-start(bf16[8,48,3200]{2,1,0:T(8,128)(2,1)S(1)} %bitcast_select_fusion.refs_0_), channel_id=1, source_target_pairs={{0,1},{1,0},{2,3},{3,2},{4,5},{5,4},{6,7},{7,6},{8,9},{9,8},{10,11... | collective-permute-start | bytes 7372808 | tf_op jit(solution)/shard_map/ppermute | solution.py:894
  288.6 28.5 %collective-permute-start.57 = (bf16[8,48,3072]{2,1,0:T(8,128)(2,1)S(1)}, bf16[8,48,3072]{2,1,0:T(8,128)(2,1)S(1)}, u32[]{:S(2)}, u32[]{:S(2)}) collective-permute-start(bf16[8,48,3072]{2,1,0:T(8,128)(2,1)S(1)} %bitcast_select_fusion.1.refs_0_), channel_id=1, source_target_pairs={{0,1},{1,0},{2,3},{3,2},{4,5},{5,4},{6,7},{7,6},{8,9},{9,8},{10,11... | collective-permute-start | bytes 7077896 | tf_op jit(solution)/shard_map/ppermute | solution.py:894
  289.2 9.0 %collective-permute-start.44 = (bf16[2,48,1536]{2,1,0:T(8,128)(2,1)S(1)}, bf16[2,48,1536]{2,1,0:T(8,128)(2,1)S(1)}, u32[]{:S(2)}, u32[]{:S(2)}) collective-permute-start(bf16[2,48,1536]{2,1,0:T(8,128)(2,1)S(1)} %broadcast_select_fusion.2), channel_id=1, source_target_pairs={{0,2},{1,3},{2,0},{3,1},{4,6},{5,7},{6,4},{7,5},{8,10},{9,11},{10,... | collective-permute-start | bytes 884744 | tf_op jit(solution)/shard_map/ppermute | solution.py:894
  298.3 16.5 %collective-permute-start.51 = (bf16[4,48,1536]{2,1,0:T(8,128)(2,1)S(1)}, bf16[4,48,1536]{2,1,0:T(8,128)(2,1)S(1)}, u32[]{:S(2)}, u32[]{:S(2)}) collective-permute-start(bf16[4,48,1536]{2,1,0:T(8,128)(2,1)S(1)} %bitcast_select_fusion.9), channel_id=1, source_target_pairs={{0,8},{1,9},{2,10},{3,11},{4,12},{5,13},{6,14},{7,15},{8,0},{9,1},... | collective-permute-start | bytes 1769480 | tf_op jit(solution)/shard_map/ppermute | solution.py:894
  302.1 7.9 %collective-permute-start.52 = (bf16[4,48,768]{2,1,0:T(8,128)(2,1)S(1)}, bf16[4,48,768]{2,1,0:T(8,128)(2,1)S(1)}, u32[]{:S(2)}, u32[]{:S(2)}) collective-permute-start(bf16[4,48,768]{2,1,0:T(8,128)(2,1)S(1)} %bitcast_select_fusion.13), channel_id=1, source_target_pairs={{0,2},{1,3},{2,0},{3,1},{4,6},{5,7},{6,4},{7,5},{8,10},{9,11},{10,... | collective-permute-start | bytes 884744 | tf_op jit(solution)/shard_map/ppermute | solution.py:894
  315.0 12.4 %collective-permute-start.55 = (bf16[8,48,1536]{2,1,0:T(8,128)(2,1)S(1)}, bf16[8,48,1536]{2,1,0:T(8,128)(2,1)S(1)}, u32[]{:S(2)}, u32[]{:S(2)}) collective-permute-start(bf16[8,48,1536]{2,1,0:T(8,128)(2,1)S(1)} %bitcast_select_fusion.4.refs_0_), channel_id=1, source_target_pairs={{0,1},{1,0},{2,3},{3,2},{4,5},{5,4},{6,7},{7,6},{8,9},{9,8},{10,11... | collective-permute-start | bytes 3538952 | tf_op jit(solution)/shard_map/ppermute | solution.py:894
  315.1 9.4 %collective-permute-start.56 = (bf16[4,48,768]{2,1,0:T(8,128)(2,1)S(1)}, bf16[4,48,768]{2,1,0:T(8,128)(2,1)S(1)}, u32[]{:S(2)}, u32[]{:S(2)}) collective-permute-start(bf16[4,48,768]{2,1,0:T(8,128)(2,1)S(1)} %bitcast_select_fusion.12), channel_id=1, source_target_pairs={{0,2},{1,3},{2,0},{3,1},{4,6},{5,7},{6,4},{7,5},{8,10},{9,11},{10,... | collective-permute-start | bytes 884744 | tf_op jit(solution)/shard_map/ppermute | solution.py:894
  316.9 10.5 %collective-permute-start.58 = (bf16[8,48,768]{2,1,0:T(8,128)(2,1)S(1)}, bf16[8,48,768]{2,1,0:T(8,128)(2,1)}, u32[]{:S(2)}, u32[]{:S(2)}) collective-permute-start(bf16[8,48,768]{2,1,0:T(8,128)(2,1)S(1)} %bitcast_select_fusion.8.refs_2_), channel_id=1, source_target_pairs={{0,1},{1,0},{2,3},{3,2},{4,5},{5,4},{6,7},{7,6},{8,9},{9,8},{10,11... | collective-permute-start | bytes 1769480 | tf_op jit(solution)/shard_map/ppermute | solution.py:894
  324.7 2.7 collective-permute-start.59
  (26 other events, 179.1 us)

commit v4 on v3

--- a/solution.py
+++ b/solution.py
@@ -908,6 +908,7 @@
     def __init__(self, keep, send, dims, n):
         self.keep, self.ready, self.dims, self.n = keep, send, dims, n
         self.at = 0
+        self.steps = len(dims) + 4
         self.out = None
         self.recv = None
 
@@ -972,60 +973,49 @@
     return x
 
 
-BATCH = 8
-
-
-def place_kernel(chains, layout, me, *refs):
-    bufs, outs = refs[: 2 * len(chains)], refs[2 * len(chains) :]
-    a = pl.program_id(0)
-    here = PIECES // 2 // BATCH
+def place_kernel(chains, layout, count, me, *refs):
+    bufs, outs = refs[: len(chains)], refs[-count:]
+    half = PIECES // 2
     for i, dims in enumerate(chains):
-        flip = flip_of(me[0], dims)
-        low = flip & (BATCH - 1)
-        group = a ^ lax.div(flip, BATCH)
-        pr = bufs[2 * i].shape[1]
-
-        def put(src, i=i, low=low, pr=pr):
-            for t in range(BATCH):
-                for which, col, cols, row0, out, out_col, out_rows in layout:
-                    if which == i:
-                        at = t * out_rows + row0
-                        outs[out][at : at + pr, out_col : out_col + cols] = src[
-                            t ^ low, :, col : col + cols
-                        ].astype(f32)
-
-        pl.when(group < here)(functools.partial(put, bufs[2 * i]))
-        pl.when(group >= here)(functools.partial(put, bufs[2 * i + 1]))
-
-
-def put_in_place(chains, me, layout, shapes, name):
-    half = PIECES // 2 // BATCH
-    ins, specs = [me], []
-
-    def block(dims, second):
-        def index(a, f):
-            group = a ^ lax.div(flip_of(f[0], dims), BATCH)
-            return (jnp.maximum(group - half, 0) if second else jnp.minimum(group, half - 1), 0, 0)
-
-        return index
-
-    for c in chains:
-        for second, x in enumerate(c.out):
-            ins.append(x)
-            specs.append(pl.BlockSpec((BATCH,) + x.shape[1:], block(c.dims, second)))
+        low = flip_of(me[0], dims) & (half - 1)
+        pr = bufs[i].shape[1]
+        for t in range(half):
+            for which, col, cols, row0, out, out_col, out_rows in layout:
+                if which == i:
+                    at = t * out_rows + row0
+                    outs[out][at : at + pr, out_col : out_col + cols] = bufs[i][
+                        t ^ low, :, col : col + cols
+                    ].astype(f32)
+
+
+def put_in_place(chains, me, layout, shapes, previous, name):
+    bufs = [c.ready if previous is None else c.out[1] for c in chains]
+    ins = [me, *bufs]
+    specs = [pl.BlockSpec(x.shape, lambda a, f: (0, 0, 0)) for x in bufs]
+    aliases = {}
+    if previous is not None:
+        for i, g in enumerate(previous):
+            aliases[len(ins)] = i
+            ins.append(g)
+            specs.append(pl.BlockSpec(memory_space=pl.ANY))
+    dims = chains[0].dims
+
+    def spot(a, f):
+        own = lax.div(flip_of(f[0], dims), PIECES // 2)
+        return (own if previous is None else 1 - own, 0)
+
     return pl.pallas_call(
-        functools.partial(place_kernel, [c.dims for c in chains], layout),
+        functools.partial(place_kernel, [c.dims for c in chains], layout, len(shapes)),
         grid_spec=pltpu.PrefetchScalarGridSpec(
             num_scalar_prefetch=1,
-            grid=(PIECES // BATCH,),
+            grid=(1,),
             in_specs=specs,
-            out_specs=[
-                pl.BlockSpec((r * BATCH // PIECES, w), lambda a, f: (a, 0)) for r, w in shapes
-            ],
+            out_specs=[pl.BlockSpec((r // 2, w), spot) for r, w in shapes],
         ),
         out_shape=[struct(x, f32) for x in shapes],
+        input_output_aliases=aliases,
         compiler_params=params(28),
-        cost_estimate=cost(1e6, 6 * sum(x.size for x in ins)),
+        cost_estimate=cost(0, 0),
         name=name,
     )(*ins)
 
@@ -1036,9 +1026,10 @@
     "+Q2", "-Q0", "+Q0", "vec", "+V", "-U", "+U", "-Q2", "+Q2", "-Q1", "+Q1", "-V", "+V", "in",
     "-D", "+D", "-Q0", "+Q0", "-Q2", "+Q2", "-Q1", "+Q1", "-V", "+V", "-Q0", "+Q0", "-U", "+U",
     "-Q2", "+Q2", "-V", "+V", "-D", "+D", "-Q1", "+Q1", "-U", "+U", "-Q0", "+Q0", "-Q2", "+Q2",
-    "-V", "+V", "-Q1", "+Q1", "-D", "+D", "-Q2", "+Q2", "-U", "+U", "-Q0", "+Q0", "-Q1", "+Q1",
-    "-Q2", "+Q2", "-V", "-Q1", "+Q1", "-Q2", "+Q2", "-D", "+D", "-U", "+U", "-D", "-Q0", "+Q0",
-    "=D", "-Q1", "+Q1", "-U", "=U", "-Q2", "+Q2", "-Q1", "-Q0", "+Q0", "-Q2", "-Q0", "=Q",
+    "-V", "+V", "-Q1", "+Q1", "-D", "-Q2", "+Q2", "-Q0", "+Q0", "-V", "-U", "-Q1", "+Q1", "-Q2",
+    "+Q2", "~U", "+U", "-Q0", "+Q0", "-Q1", "+Q1", "-Q2", "+Q2", "~D", "+D", "-Q0", "+Q0", "-Q1",
+    "+Q1", "-U", "+U", "<U", "-Q2", "+Q2", "-D", "+D", "<D", "<Q", "-U", "=U", "-Q0", "-Q1", "-Q2",
+    "=Q", "-D", "=D",
 )
 
 
@@ -1049,9 +1040,9 @@
         return {
             "D": (1, x, y, z, far),
             "U": (1, z, x, y, far),
-            "Q0": (1, z, x, y, far),
-            "Q1": (1, x, y, z, far),
-            "Q2": (1, x, y, z, far),
+            "Q0": (1, y, x, z, far),
+            "Q1": (1, y, x, z, far),
+            "Q2": (1, y, x, z, far),
         }
     names = ("D", "U", "Q0", "Q1", "Q2")
     return {name: tuple([1] + rest[i:] + rest[:i]) for i, name in enumerate(names)}
@@ -1095,28 +1086,42 @@
     def now(x):
         return after(x, *flying.values()) if flying else x
 
-    def finish(name):
-        for other in ("Q0", "Q1", "Q2") if name == "Q" else (name,):
-            chains[other].finish()
+    members = {"Q": ["Q0", "Q1", "Q2"]}
+    begun = {}
+
+    def layout_of(name):
         if name == "D":
             layout = [(0, i * width, width, i * width // PIECES, 0, 0, ff // PIECES) for i in range(ff // width)]
             layout.append((0, ff, w_proj.shape[1], 0, 1, 0, width // PIECES))
-            shapes = [(ff, width), w_proj.shape]
-            placed["D"] = put_in_place([chains["D"]], me, layout, shapes, "down_place")
-        elif name == "U":
-            layout = [(0, 0, ff, 0, 0, 0, width // PIECES)]
-            placed["U"] = put_in_place([chains["U"]], me, layout, [(width, ff)], "up_place")
-        else:
-            span = width // PORTIONS
-            layout = [
-                (c, i * span, span, 0, 0, i * width + c * span, width // PIECES)
-                for c in range(PORTIONS)
-                for i in range(3)
-            ]
-            layout.append((0, width, width, 0, 1, 0, width // PIECES))
-            shapes = [(width, 3 * width), (width, width)]
-            own = [chains["Q%d" % j] for j in range(PORTIONS)]
-            placed["Q"] = put_in_place(own, me, layout, shapes, "qkv_place")
+            return layout, [(ff, width), w_proj.shape], "down_place"
+        if name == "U":
+            return [(0, 0, ff, 0, 0, 0, width // PIECES)], [(width, ff)], "up_place"
+        span = width // PORTIONS
+        layout = [
+            (c, i * span, span, 0, 0, i * width + c * span, width // PIECES)
+            for c in range(PORTIONS)
+            for i in range(3)
+        ]
+        layout.append((0, width, width, 0, 1, 0, width // PIECES))
+        return layout, [(width, 3 * width), (width, width)], "qkv_place"
+
+    def begin(name):
+        layout, shapes, title = layout_of(name)
+        own = [chains[q] for q in members.get(name, [name])]
+        for c in own:
+            while c.at < c.steps - 1:
+                c.land()
+        begun[name] = put_in_place(own, me, layout, shapes, None, title)
+        return begun[name][0]
+
+    def finish(name):
+        if name not in begun:
+            begin(name)
+        layout, shapes, title = layout_of(name)
+        own = [chains[q] for q in members.get(name, [name])]
+        for c in own:
+            c.finish()
+        placed[name] = put_in_place(own, me, layout, shapes, begun[name], title)
         return placed[name][0]
 
     for event in SCHEDULE:
@@ -1128,12 +1133,17 @@
         elif event[0] == "-":
             name = event[1:]
             if chains[name].out is None:
-                chains[name].land(*([] if last is None else [last]))
+                chains[name].land(*(last if isinstance(last, list) else [last] if last is not None else []))
                 flying.pop(name, None)
                 last = chains[name].ready
                 if name == "V" and chains[name].out is not None:
                     small = vectors(chains[name].out)
-                    last = small[1]
+                    last = small
+        elif event[0] == "~":
+            c = chains[event[1:]]
+            c.ready = after(c.ready, *(last if isinstance(last, list) else [last]))
+        elif event[0] == "<":
+            last = begin(event[1:])
         elif event[0] == "=":
             last = finish(event[1:])
         elif event == "up":

time: 337 us -> 332 us (0.985)
  starting transfers between devices: 82.1 us -> 71.2 us
  waiting for transfers between devices: 78.3 us -> 83.8 us
    ppermute x60, starting transfers between devices: 82.1 us -> 71.2 us  [swap(): return lax.ppermute(x, 'dp', [(i, i ^ mask) for i in range(n)])]
    ppermute x60, waiting for transfers between devices: 78.3 us -> 83.8 us  [swap(): return lax.ppermute(x, 'dp', [(i, i ^ mask) for i in range(n)])]
    pallas_call x3 -> x6, Pallas kernels: 13.4 us -> 14.8 us  [put_in_place(): pl.pallas_call(functools.partial(place_kernel, [c.dims for c in chains],...]
  transfers between devices with their start and end apart: 60 -> 60, of which waited for: 24 -> 26; matrix products, arithmetic and copies ran while one was open for 5% -> 5% of each run, Pallas kernels for 24% -> 26%
where the time goes in v4:
time: 332 us; the launch traced here: 328 us
  Pallas kernels  144 us (43%)
  waiting for transfers between devices  83.8 us (25%)
  starting transfers between devices  71.2 us (21%)
  other arithmetic  17.9 us (5%)
  local copies, waits for them, and re-layouts  9.32 us (3%)
    ppermute x60, waiting for transfers between devices, swap(): return lax.ppermute(x, 'dp', [(i, i ^ mask) for i in range(n)])  83.8 us
    ppermute x60, starting transfers between devices, swap(): return lax.ppermute(x, 'dp', [(i, i ^ mask) for i in range(n)])  71.2 us
    pallas_call x3, Pallas kernels, attention_back(): pl.pallas_call(attn_bwd_kernel, grid=(1,), in_specs=[SMEM, col(0), col(1)...  34.6 us
    pallas_call x1, Pallas kernels, attention(): pl.pallas_call(attn_fwd_kernel, in_specs=[SMEM] + [anywhere] * len(ins),...  21.6 us
    pallas_call x1, Pallas kernels, ffn_fwd(): pl.pallas_call(ffn_fwd_kernel, grid=(steps,), in_specs=specs, out_specs=o...  20 us
    pallas_call x1, Pallas kernels, up_grad(): pl.pallas_call(functools.partial(up_grad_kernel, dims), grid=(ff // FF_CH...  15 us
    pallas_call x6, Pallas kernels, put_in_place(): pl.pallas_call(functools.partial(place_kernel, [c.dims for c in chains],...  14.8 us
    pallas_call x1, Pallas kernels, mid_back(): pl.pallas_call(mid_back_kernel, grid=(steps,), in_specs=specs, out_specs=...  11 us
  transfers between devices with their start and end apart: 60, of which 26 were waited for; matrix products, arithmetic and copies ran while one was open for 5% of the time, Pallas kernels for 26%

profile of v4, /device:TPU:0, one launch (start us, length us, event | category | flops | bytes accessed | tf_op | source)
XLA Modules:
  0.0 328.3 jit_solution(15657228426704230355)
XLA Ops:
  1.4 21.6 %attention_forward.1 = (bf16[1024,2304]{1,0:T(8,128)(2,1)}, bf16[1024,768]{1,0:T(8,128)(2,1)S(1)}, f32[6,8,256]{2,1,0:T(8,128)S(1)}, f32[1024,768]{1,0:T(8,128)S...) custom-call(s32[1,6]{1,0:T(1,128)S(1)} %copy-done.16, ...), custom_call_target="tpu_custom_call" | custom-call | tf_op jit(solution)/shard_map/attention_forward/pallas_call | solution.py:304
  23.0 20.0 %ffn_forward.1 = (bf16[1024,3072]{1,0:T(8,128)(2,1)}, bf16[1024,3072]{1,0:T(8,128)(2,1)}, bf16[1024,768]{1,0:T(8,128)(2,1)}, f32[1024,1]{1,0:T(8,128)S(1)}, bf16...) custom-call(s32[1,6]{1,0:T(1,128)S(1)} %copy-done.16, ...), custom_call_target="tpu_custom_call" | custom-call | tf_op jit(solution)/shard_map/ffn_forward/pallas_call | solution.py:439
  44.6 4.0 %collective-permute-start = (bf16[1,48,128]{2,1,0:T(8,128)(2,1)S(1)}, bf16[1,48,128]{2,1,0:T(8,128)(2,1)S(1)}, u32[]{:S(2)}, u32[]{:S(2)}) collective-permute-start(bf16[1,48,128]{2,1,0:T(8,128)(2,1)S(1)} %get-tuple-element.137), channel_id=1, source_target_pairs={{0,16},{1,17},{2,18},{3,19},{4,20},{5,21},{6,22},{7,23},{8,24},{9,... | collective-permute-start | bytes 36872 | tf_op jit(solution)/shard_map/ppermute | solution.py:894
  48.7 1.7 collective-permute-done
  50.4 1.9 collective-permute-start.1
  52.5 1.7 collective-permute-done.1
  54.3 1.9 collective-permute-start.2
  56.3 2.1 collective-permute-done.2
  58.5 1.9 collective-permute-start.3
  60.6 2.6 collective-permute-done.3
  64.9 1.9 loss_forward.1
  66.8 3.0 collective-permute-start.5
  69.8 2.0 collective-permute-done.5
  71.9 2.0 collective-permute-start.6
  73.9 2.6 collective-permute-done.6
  76.6 2.4 collective-permute-start.7
  79.0 3.5 %collective-permute-done.7 = bf16[4,176,128]{2,1,0:T(8,128)(2,1)S(1)} collective-permute-done((bf16[4,176,128]{2,1,0:T(8,128)(2,1)S(1)}, bf16[4,176,128]{2,1,0:T(8,128)(2,1)S(1)}, u32[]{:S(2)}, u32[]{:S(2)}) %collective-permute-start.7) | collective-permute-done | bytes 180256 | tf_op jit(solution)/shard_map/ppermute | solution.py:894
  82.6 2.2 collective-permute-start.8
  84.8 5.4 %collective-permute-done.8 = bf16[8,176,128]{2,1,0:T(8,128)(2,1)S(1)} collective-permute-done((bf16[8,176,128]{2,1,0:T(8,128)(2,1)S(1)}, bf16[8,176,128]{2,1,0:T(8,128)(2,1)S(1)}, u32[]{:S(2)}, u32[]{:S(2)}) %collective-permute-start.8) | collective-permute-done | bytes 360480 | tf_op jit(solution)/shard_map/ppermute | solution.py:894
  91.3 2.4 collective-permute-done.9
  93.8 1.5 bitcast_select_fusion.2.messages
  96.4 6.3 %loss_backward.1 = (f32[8,128]{1,0:T(8,128)S(1)}, f32[1024,768]{1,0:T(8,128)}, bf16[1024,768]{1,0:T(8,128)(2,1)S(1)}, f32[768,128]{1,0:T(8,128)S(1)}, f32[8,768]{1,0:T(8,128)S(1)}) custom-call(s32[1]{0:T(128)} %bitcast.me, s32[1,6]{1,0:T(1,128)S(1)} %copy-done.17, s32[32,5]{1,0:T(8,128)S(1)} %copy.38.owner, s32[32,5]{1,0:T(8,128)S(1)} %copy.39.place, ...), custom_call_target="tpu_custom_call" | custom-call | tf_op jit(solution)/shard_map/loss_backward/pallas_call | solution.py:609
  102.7 7.8 %down_gradient.1 = (f32[8,48,3200]{2,1,0:T(8,128)S(1)}, f32[8,48,3200]{2,1,0:T(8,128)S(1)}) custom-call(s32[1]{0:T(128)} %bitcast.me, bf16[1024,3072]{1,0:T(8,128)(2,1)} %get-tuple-element.146.act, bf16[1024,768]{1,0:T(8,128)(2,1)S(1)} %get-tuple-element.147.dbr, f32[768,128]{1,0:T(8,128)S(1)} %get-tuple-element.148.gwp), custom_call_target="tpu_custom_call" | custom-call | tf_op jit(solution)/shard_map/down_gradient/pallas_call | solution.py:676
  110.7 15.0 %up_gradient.1 = (f32[8,48,3072]{2,1,0:T(8,128)S(1)}, f32[8,48,3072]{2,1,0:T(8,128)}, bf16[1024,3072]{1,0:T(8,128)(2,1)}, f32[1,3072]{1,0:T(1,128)S(1)}) custom-call(s32[1]{0:T(128)} %bitcast.me, bf16[1024,768]{1,0:T(8,128)(2,1)S(1)} %get-tuple-element.147.dbr, bf16[1024,3072]{1,0:T(8,128)(2,1)} %get-tuple-element.152.slp, bf16[3072,768]{1,0:T(8,128)(2,1)} %wd.3, ...), custom_call_target="tpu_custom_call" | custom-call | tf_op jit(solution)/shard_map/up_gradient/pallas_call | solution.py:726
  126.6 2.1 collective-permute-start.11
  128.9 11.0 %middle_backward.1 = (f32[1024,768]{1,0:T(8,128)S(1)}, bf16[1024,768]{1,0:T(8,128)(2,1)S(1)}, bf16[1024,768]{1,0:T(8,128)(2,1)S(1)}, f32[8,768]{1,0:T(8,128)S(1)}) custom-call(s32[1]{0:T(128)} %bitcast.me, bf16[1024,3072]{1,0:T(8,128)(2,1)} %get-tuple-element.159.din, bf16[768,3072]{1,0:T(8,128)(2,1)} %wu.3, f32[1024,768]{1,0:T(8,128)S(1)} %copy-done.3, ...), custom_call_target="tpu_custom_call" | custom-call | tf_op jit(solution)/shard_map/middle_backward/pallas_call | solution.py:794
  140.0 4.5 %slice_add_fusion.1 = (f32[4,48,3072]{2,1,0:T(8,128)}, bf16[4,48,3072]{2,1,0:T(8,128)(2,1)S(1)}) fusion(f32[8,48,3072]{2,1,0:T(8,128)} %collective-permute-done.12, f32[8,48,3072]{2,1,0:T(8,128)S(1)} %get-tuple-element.156), kind=kLoop, calls=%fused_computation.4 | loop fusion | flops 1769472 | bytes 12976128 | tf_op jit(solution)/shard_map/add | solution.py:932
  146.0 11.5 %attention_backward.3 = (bf16[1024,256]{1,0:T(8,128)(2,1)S(1)}, bf16[1024,256]{1,0:T(8,128)(2,1)S(1)}, bf16[1024,256]{1,0:T(8,128)(2,1)S(1)}, f32[8,256]{1,0:T(8,128)S(1)}) custom-call(s32[1,6]{1,0:T(1,128)S(1)} %copy-done.17, bf16[1024,2304]{1,0:T(8,128)(2,1)S(1)} %bitcast.89, bf16[1024,2304]{1,0:T(8,128)(2,1)S(1)} %bitcast.89, ...), custom_call_target="tpu_custom_call" | custom-call | tf_op jit(solution)/shard_map/attention_backward/pallas_call | solution.py:340
  159.1 2.8 qkv_gradient.3
  162.0 1.6 collective-permute-start.13
  163.6 11.7 %attention_backward.4 = (bf16[1024,256]{1,0:T(8,128)(2,1)S(1)}, bf16[1024,256]{1,0:T(8,128)(2,1)S(1)}, bf16[1024,256]{1,0:T(8,128)(2,1)S(1)}, f32[8,256]{1,0:T(8,128)S(1)}) custom-call(s32[1,6]{1,0:T(1,128)S(1)} %copy-done.17, bf16[1024,2304]{1,0:T(8,128)(2,1)S(1)} %bitcast.89, bf16[1024,2304]{1,0:T(8,128)(2,1)S(1)} %bitcast.89, ...), custom_call_target="tpu_custom_call" | custom-call | tf_op jit(solution)/shard_map/attention_backward/pallas_call | solution.py:340
  178.8 1.8 collective-permute-start.15
  183.1 11.5 %attention_backward.5 = (bf16[1024,256]{1,0:T(8,128)(2,1)S(1)}, bf16[1024,256]{1,0:T(8,128)(2,1)S(1)}, bf16[1024,256]{1,0:T(8,128)(2,1)S(1)}, f32[8,256]{1,0:T(8,128)S(1)}) custom-call(s32[1,6]{1,0:T(1,128)S(1)} %copy-done.17, bf16[1024,2304]{1,0:T(8,128)(2,1)S(1)} %bitcast.89, bf16[1024,2304]{1,0:T(8,128)(2,1)S(1)} %bitcast.89, ...), custom_call_target="tpu_custom_call" | custom-call | tf_op jit(solution)/shard_map/attention_backward/pallas_call | solution.py:340
  195.3 1.9 collective-permute-start.20
  197.4 2.2 collective-permute-start.25
  201.2 1.5 qkv_gradient.5
  203.0 2.2 collective-permute-done.20
  205.2 2.0 collective-permute-start.24
  207.4 1.9 collective-permute-start.31
  210.9 2.0 collective-permute-start.27
  213.0 5.5 %input_gradient.1 = f32[1024,768]{1,0:T(8,128)} custom-call(s32[1]{0:T(128)} %bitcast.me, bf16[1024,256]{1,0:T(8,128)(2,1)S(1)} %get-tuple-element.173.d0.refs_0_, bf16[1024,256]{1,0:T(8,128)(2,1)S(1)} %get-tuple-element.185.d0.refs_1_, bf16[1024,256]{1,0:T(8,128)(2,1)S(1)} %get-tuple-element.196.d0.refs_2_, ...), custom_call_target="tpu_custom_call" | custom-call | tf_op jit(solution)/shard_map/input_gradient/pallas_call | solution.py:854
  218.6 1.9 collective-permute-done.25
  222.1 6.7 %collective-permute-done.29 = bf16[4,48,768]{2,1,0:T(8,128)(2,1)S(1)} collective-permute-done((bf16[4,48,768]{2,1,0:T(8,128)(2,1)S(1)}, bf16[4,48,768]{2,1,0:T(8,128)(2,1)S(1)}, u32[]{:S(2)}, u32[]{:S(2)}) %collective-permute-start.29) | collective-permute-done | bytes 294944 | tf_op jit(solution)/shard_map/ppermute | solution.py:894
  230.1 1.9 collective-permute-start.33
  232.0 4.3 %collective-permute-done.26 = bf16[1,48,1536]{2,1,0:T(8,128)(2,1)S(1)} collective-permute-done((bf16[1,48,1536]{2,1,0:T(8,128)(2,1)S(1)}, bf16[1,48,1536]{2,1,0:T(8,128)(2,1)S(1)}, u32[]{:S(2)}, u32[]{:S(2)}) %collective-permute-start.26) | collective-permute-done | bytes 147488 | tf_op jit(solution)/shard_map/ppermute | solution.py:894
  240.4 1.8 collective-permute-start.38
  243.7 5.0 %collective-permute-done.32 = bf16[1,48,3072]{2,1,0:T(8,128)(2,1)S(1)} collective-permute-done((bf16[1,48,3072]{2,1,0:T(8,128)(2,1)S(1)}, bf16[1,48,3072]{2,1,0:T(8,128)(2,1)S(1)}, u32[]{:S(2)}, u32[]{:S(2)}) %collective-permute-start.32) | collective-permute-done | bytes 294944 | tf_op jit(solution)/shard_map/ppermute | solution.py:894
  248.7 1.7 collective-permute-start.41
  252.5 3.0 collective-permute-start.39
  256.5 3.6 %collective-permute-done.40 = bf16[2,48,3200]{2,1,0:T(8,128)(2,1)S(1)} collective-permute-done((bf16[2,48,3200]{2,1,0:T(8,128)(2,1)S(1)}, bf16[2,48,3200]{2,1,0:T(8,128)(2,1)S(1)}, u32[]{:S(2)}, u32[]{:S(2)}) %collective-permute-start.40) | collective-permute-done | bytes 614432 | tf_op jit(solution)/shard_map/ppermute | solution.py:894
  260.2 2.5 collective-permute-start.45
  273.0 2.2 collective-permute-done.50
  275.2 1.5 collective-permute-done.49
  277.9 1.7 collective-permute-start.52
  282.6 13.2 %collective-permute-done.48 = bf16[4,48,1536]{2,1,0:T(8,128)(2,1)S(1)} collective-permute-done((bf16[4,48,1536]{2,1,0:T(8,128)(2,1)S(1)}, bf16[4,48,1536]{2,1,0:T(8,128)(2,1)S(1)}, u32[]{:S(2)}, u32[]{:S(2)}) %collective-permute-start.48) | collective-permute-done | bytes 589856 | tf_op jit(solution)/shard_map/ppermute | solution.py:894
  296.0 5.9 %collective-permute-done.53 = bf16[4,48,768]{2,1,0:T(8,128)(2,1)S(1)} collective-permute-done((bf16[4,48,768]{2,1,0:T(8,128)(2,1)S(1)}, bf16[4,48,768]{2,1,0:T(8,128)(2,1)S(1)}, u32[]{:S(2)}, u32[]{:S(2)}) %collective-permute-start.53) | collective-permute-done | bytes 294944 | tf_op jit(solution)/shard_map/ppermute | solution.py:894
  302.1 1.9 collective-permute-done.52
  304.4 2.5 up_place.2.refs_1_
  309.2 2.3 qkv_place.2
  311.6 6.6 %collective-permute-done.56.refs_1_ = bf16[8,48,768]{2,1,0:T(8,128)(2,1)S(1)} collective-permute-done((bf16[8,48,768]{2,1,0:T(8,128)(2,1)S(1)}, bf16[8,48,768]{2,1,0:T(8,128)(2,1)S(1)}, u32[]{:S(2)}, u32[]{:S(2)}) %collective-permute-start.56) | collective-permute-done | bytes 589856 | tf_op jit(solution)/shard_map/ppermute | solution.py:894
  318.2 2.5 down_place.2
  320.7 2.5 up_place.3
  323.2 2.4 qkv_place.3
  325.6 2.5 down_place.3
  (216 shorter events, 51.2 us)
Async XLA Ops:
  0.6 22.3 %copy-start.8 = (bf16[768,128]{1,0:T(8,128)(2,1)S(1)}, bf16[768,128]{1,0:T(8,128)(2,1)}, u32[]{:S(2)}) copy-start(bf16[768,128]{1,0:T(8,128)(2,1)} %wp.3) | copy-start | bytes 589828
  1.4 21.6 %copy-start.22 = (f32[768]{0:T(1024)S(1)}, f32[768]{0:T(1024)}, u32[]{:S(2)}) copy-start(f32[768]{0:T(1024)} %b2.1) | copy-start | bytes 9220
  23.0 40.5 %copy-start.24 = (s32[32,5]{0,1:T(8,128)S(1)}, s32[32,5]{0,1:T(8,128)}, u32[]{:S(2)}) copy-start(s32[32,5]{0,1:T(8,128)} %param.19) | copy-start | bytes 1924
  44.6 5.7 %collective-permute-start = (bf16[1,48,128]{2,1,0:T(8,128)(2,1)S(1)}, bf16[1,48,128]{2,1,0:T(8,128)(2,1)S(1)}, u32[]{:S(2)}, u32[]{:S(2)}) collective-permute-start(bf16[1,48,128]{2,1,0:T(8,128)(2,1)S(1)} %get-tuple-element.137), channel_id=1, source_target_pairs={{0,16},{1,17},{2,18},{3,19},{4,20},{5,21},{6,22},{7,23},{8,24},{9,... | collective-permute-start | bytes 36872 | tf_op jit(solution)/shard_map/ppermute | solution.py:894
  50.4 3.8 %collective-permute-start.1 = (bf16[2,48,128]{2,1,0:T(8,128)(2,1)S(1)}, bf16[2,48,128]{2,1,0:T(8,128)(2,1)S(1)}, u32[]{:S(2)}, u32[]{:S(2)}) collective-permute-start(bf16[2,48,128]{2,1,0:T(8,128)(2,1)S(1)} %broadcast_select_fusion.6), channel_id=1, source_target_pairs={{0,8},{1,9},{2,10},{3,11},{4,12},{5,13},{6,14},{7,15},{8,0},{9,1},... | collective-permute-start | bytes 73736 | tf_op jit(solution)/shard_map/ppermute | solution.py:894
  54.3 4.1 %collective-permute-start.2 = (bf16[4,48,128]{2,1,0:T(8,128)(2,1)S(1)}, bf16[4,48,128]{2,1,0:T(8,128)(2,1)S(1)}, u32[]{:S(2)}, u32[]{:S(2)}) collective-permute-start(bf16[4,48,128]{2,1,0:T(8,128)(2,1)S(1)} %bitcast_select_fusion.17), channel_id=1, source_target_pairs={{0,4},{1,5},{2,6},{3,7},{4,0},{5,1},{6,2},{7,3},{8,12},{9,13},{10,... | collective-permute-start | bytes 147464 | tf_op jit(solution)/shard_map/ppermute | solution.py:894
  58.5 4.7 %collective-permute-start.3 = (bf16[8,48,128]{2,1,0:T(8,128)(2,1)S(1)}, bf16[8,48,128]{2,1,0:T(8,128)(2,1)S(1)}, u32[]{:S(2)}, u32[]{:S(2)}) collective-permute-start(bf16[8,48,128]{2,1,0:T(8,128)(2,1)S(1)} %bitcast_select_fusion.16), channel_id=1, source_target_pairs={{0,2},{1,3},{2,0},{3,1},{4,6},{5,7},{6,4},{7,5},{8,10},{9,11},{10,... | collective-permute-start | bytes 294920 | tf_op jit(solution)/shard_map/ppermute | solution.py:894
  63.3 1.5 collective-permute-start.4
  66.8 24.4 %copy-start.25 = (s32[32,5]{0,1:T(8,128)S(1)}, s32[32,5]{0,1:T(8,128)}, u32[]{:S(2)}) copy-start(s32[32,5]{0,1:T(8,128)} %param.20) | copy-start | bytes 1924
  66.8 5.0 %collective-permute-start.5 = (bf16[1,176,128]{2,1,0:T(8,128)(2,1)S(1)}, bf16[1,176,128]{2,1,0:T(8,128)(2,1)S(1)}, u32[]{:S(2)}, u32[]{:S(2)}) collective-permute-start(bf16[1,176,128]{2,1,0:T(8,128)(2,1)S(1)} %get-tuple-element.139), channel_id=1, source_target_pairs={{0,16},{1,17},{2,18},{3,19},{4,20},{5,21},{6,22},{7,23},{8,24},{9,... | collective-permute-start | bytes 135176 | tf_op jit(solution)/shard_map/ppermute | solution.py:894
  71.9 4.6 %collective-permute-start.6 = (bf16[2,176,128]{2,1,0:T(8,128)(2,1)S(1)}, bf16[2,176,128]{2,1,0:T(8,128)(2,1)S(1)}, u32[]{:S(2)}, u32[]{:S(2)}) collective-permute-start(bf16[2,176,128]{2,1,0:T(8,128)(2,1)S(1)} %broadcast_select_fusion.5), channel_id=1, source_target_pairs={{0,8},{1,9},{2,10},{3,11},{4,12},{5,13},{6,14},{7,15},{8,0},{9,1},... | collective-permute-start | bytes 270344 | tf_op jit(solution)/shard_map/ppermute | solution.py:894
  76.6 5.9 %collective-permute-start.7 = (bf16[4,176,128]{2,1,0:T(8,128)(2,1)S(1)}, bf16[4,176,128]{2,1,0:T(8,128)(2,1)S(1)}, u32[]{:S(2)}, u32[]{:S(2)}) collective-permute-start(bf16[4,176,128]{2,1,0:T(8,128)(2,1)S(1)} %bitcast_select_fusion.15), channel_id=1, source_target_pairs={{0,4},{1,5},{2,6},{3,7},{4,0},{5,1},{6,2},{7,3},{8,12},{9,13},{10,... | collective-permute-start | bytes 540680 | tf_op jit(solution)/shard_map/ppermute | solution.py:894
  82.6 7.6 %collective-permute-start.8 = (bf16[8,176,128]{2,1,0:T(8,128)(2,1)S(1)}, bf16[8,176,128]{2,1,0:T(8,128)(2,1)S(1)}, u32[]{:S(2)}, u32[]{:S(2)}) collective-permute-start(bf16[8,176,128]{2,1,0:T(8,128)(2,1)S(1)} %bitcast_select_fusion.11), channel_id=1, source_target_pairs={{0,2},{1,3},{2,0},{3,1},{4,6},{5,7},{6,4},{7,5},{8,10},{9,11},{10,... | collective-permute-start | bytes 1081352 | tf_op jit(solution)/shard_map/ppermute | solution.py:894
  91.2 2.5 collective-permute-start.9
  110.5 15.6 %collective-permute-start.10 = (f32[8,48,3200]{2,1,0:T(8,128)S(1)}, f32[8,48,3200]{2,1,0:T(8,128)S(1)}, u32[]{:S(2)}, u32[]{:S(2)}) collective-permute-start(f32[8,48,3200]{2,1,0:T(8,128)S(1)} %get-tuple-element.150), channel_id=1, source_target_pairs={{0,1},{1,0},{2,3},{3,2},{4,5},{5,4},{6,7},{7,6},{8,9},{9,8},{10,11... | collective-permute-start | bytes 14745608 | tf_op jit(solution)/shard_map/ppermute | solution.py:894
  125.7 14.2 %collective-permute-start.12 = (f32[8,48,3072]{2,1,0:T(8,128)}, f32[8,48,3072]{2,1,0:T(8,128)}, u32[]{:S(2)}, u32[]{:S(2)}) collective-permute-start(f32[8,48,3072]{2,1,0:T(8,128)} %get-tuple-element.157), channel_id=1, source_target_pairs={{0,1},{1,0},{2,3},{3,2},{4,5},{5,4},{6,7},{7,6},{8,9},{9,8},{10,11... | collective-permute-start | bytes 14155784 | tf_op jit(solution)/shard_map/ppermute | solution.py:894
  126.6 30.9 %collective-permute-start.11 = (bf16[4,48,3200]{2,1,0:T(8,128)(2,1)S(1)}, bf16[4,48,3200]{2,1,0:T(8,128)(2,1)S(1)}, u32[]{:S(2)}, u32[]{:S(2)}) collective-permute-start(bf16[4,48,3200]{2,1,0:T(8,128)(2,1)S(1)} %get-tuple-element.262), channel_id=1, source_target_pairs={{0,2},{1,3},{2,0},{3,1},{4,6},{5,7},{6,4},{7,5},{8,10},{9,11},{10,... | collective-permute-start | bytes 3686408 | tf_op jit(solution)/shard_map/ppermute | solution.py:894
  144.5 30.7 %collective-permute-start.14 = (bf16[4,48,3072]{2,1,0:T(8,128)(2,1)S(1)}, bf16[4,48,3072]{2,1,0:T(8,128)(2,1)S(1)}, u32[]{:S(2)}, u32[]{:S(2)}) collective-permute-start(bf16[4,48,3072]{2,1,0:T(8,128)(2,1)S(1)} %get-tuple-element.264), channel_id=1, source_target_pairs={{0,8},{1,9},{2,10},{3,11},{4,12},{5,13},{6,14},{7,15},{8,0},{9,1},... | collective-permute-start | bytes 3538952 | tf_op jit(solution)/shard_map/ppermute | solution.py:894
  161.9 18.7 %collective-permute-start.17 = (f32[8,48,1536]{2,1,0:T(8,128)S(1)}, f32[8,48,1536]{2,1,0:T(8,128)S(1)}, u32[]{:S(2)}, u32[]{:S(2)}) collective-permute-start(f32[8,48,1536]{2,1,0:T(8,128)S(1)} %get-tuple-element.177), channel_id=1, source_target_pairs={{0,1},{1,0},{2,3},{3,2},{4,5},{5,4},{6,7},{7,6},{8,9},{9,8},{10,11... | collective-permute-start | bytes 7077896 | tf_op jit(solution)/shard_map/ppermute | solution.py:894
  162.0 16.7 %collective-permute-start.13 = (bf16[2,48,3200]{2,1,0:T(8,128)(2,1)S(1)}, bf16[2,48,3200]{2,1,0:T(8,128)(2,1)S(1)}, u32[]{:S(2)}, u32[]{:S(2)}) collective-permute-start(bf16[2,48,3200]{2,1,0:T(8,128)(2,1)S(1)} %get-tuple-element.266), channel_id=1, source_target_pairs={{0,4},{1,5},{2,6},{3,7},{4,0},{5,1},{6,2},{7,3},{8,12},{9,13},{10,... | collective-permute-start | bytes 1843208 | tf_op jit(solution)/shard_map/ppermute | solution.py:894
  177.2 17.4 %collective-permute-start.16 = (bf16[2,48,3072]{2,1,0:T(8,128)(2,1)S(1)}, bf16[2,48,3072]{2,1,0:T(8,128)(2,1)S(1)}, u32[]{:S(2)}, u32[]{:S(2)}) collective-permute-start(bf16[2,48,3072]{2,1,0:T(8,128)(2,1)S(1)} %get-tuple-element.270), channel_id=1, source_target_pairs={{0,2},{1,3},{2,0},{3,1},{4,6},{5,7},{6,4},{7,5},{8,10},{9,11},{10,... | collective-permute-start | bytes 1769480 | tf_op jit(solution)/shard_map/ppermute | solution.py:894
  178.8 18.5 %collective-permute-start.15 = (bf16[1,48,3200]{2,1,0:T(8,128)(2,1)S(1)}, bf16[1,48,3200]{2,1,0:T(8,128)(2,1)S(1)}, u32[]{:S(2)}, u32[]{:S(2)}) collective-permute-start(bf16[1,48,3200]{2,1,0:T(8,128)(2,1)S(1)} %fusion.2), channel_id=1, source_target_pairs={{0,8},{1,9},{2,10},{3,11},{4,12},{5,13},{6,14},{7,15},{8,0},{9,1},... | collective-permute-start | bytes 921608 | tf_op jit(solution)/shard_map/ppermute | solution.py:894
  181.0 21.6 %collective-permute-start.18 = (bf16[4,48,1536]{2,1,0:T(8,128)(2,1)S(1)}, bf16[4,48,1536]{2,1,0:T(8,128)(2,1)S(1)}, u32[]{:S(2)}, u32[]{:S(2)}) collective-permute-start(bf16[4,48,1536]{2,1,0:T(8,128)(2,1)S(1)} %get-tuple-element.268), channel_id=1, source_target_pairs={{0,4},{1,5},{2,6},{3,7},{4,0},{5,1},{6,2},{7,3},{8,12},{9,13},{10,... | collective-permute-start | bytes 1769480 | tf_op jit(solution)/shard_map/ppermute | solution.py:894
  183.0 16.5 %collective-permute-start.19 = (f32[8,48,768]{2,1,0:T(8,128)S(1)}, f32[8,48,768]{2,1,0:T(8,128)S(1)}, u32[]{:S(2)}, u32[]{:S(2)}) collective-permute-start(f32[8,48,768]{2,1,0:T(8,128)S(1)} %get-tuple-element.188), channel_id=1, source_target_pairs={{0,1},{1,0},{2,3},{3,2},{4,5},{5,4},{6,7},{7,6},{8,9},{9,8},{10,11... | collective-permute-start | bytes 3538952 | tf_op jit(solution)/shard_map/ppermute | solution.py:894
  194.6 16.3 %collective-permute-start.23 = (f32[16,768]{1,0:T(8,128)S(1)}, f32[16,768]{1,0:T(8,128)S(1)}, u32[]{:S(2)}, u32[]{:S(2)}) collective-permute-start(f32[16,768]{1,0:T(8,128)S(1)} %collect_vectors.1), channel_id=1, source_target_pairs={{0,1},{1,0},{2,3},{3,2},{4,5},{5,4},{6,7},{7,6},{8,9},{9,8},{10,11... | collective-permute-start | bytes 147464 | tf_op jit(solution)/shard_map/ppermute | solution.py:894
  195.3 9.9 %collective-permute-start.20 = (bf16[1,48,3072]{2,1,0:T(8,128)(2,1)S(1)}, bf16[1,48,3072]{2,1,0:T(8,128)(2,1)S(1)}, u32[]{:S(2)}, u32[]{:S(2)}) collective-permute-start(bf16[1,48,3072]{2,1,0:T(8,128)(2,1)S(1)} %fusion.8), channel_id=1, source_target_pairs={{0,4},{1,5},{2,6},{3,7},{4,0},{5,1},{6,2},{7,3},{8,12},{9,13},{10,... | collective-permute-start | bytes 884744 | tf_op jit(solution)/shard_map/ppermute | solution.py:894
  197.4 23.1 %collective-permute-start.25 = (bf16[1,48,3200]{2,1,0:T(8,128)(2,1)S(1)}, bf16[1,48,3200]{2,1,0:T(8,128)(2,1)S(1)}, u32[]{:S(2)}, u32[]{:S(2)}) collective-permute-start(bf16[1,48,3200]{2,1,0:T(8,128)(2,1)S(1)} %fusion.4), channel_id=1, source_target_pairs={{0,16},{1,17},{2,18},{3,19},{4,20},{5,21},{6,22},{7,23},{8,24},{9,... | collective-permute-start | bytes 921608 | tf_op jit(solution)/shard_map/ppermute | solution.py:894
  199.7 11.1 %collective-permute-start.22 = (bf16[4,48,768]{2,1,0:T(8,128)(2,1)S(1)}, bf16[4,48,768]{2,1,0:T(8,128)(2,1)S(1)}, u32[]{:S(2)}, u32[]{:S(2)}) collective-permute-start(bf16[4,48,768]{2,1,0:T(8,128)(2,1)S(1)} %get-tuple-element.276), channel_id=1, source_target_pairs={{0,4},{1,5},{2,6},{3,7},{4,0},{5,1},{6,2},{7,3},{8,12},{9,13},{10,... | collective-permute-start | bytes 884744 | tf_op jit(solution)/shard_map/ppermute | solution.py:894
  202.7 4.7 %collective-permute-start.21 = (f32[8,48,768]{2,1,0:T(8,128)S(1)}, f32[8,48,768]{2,1,0:T(8,128)S(1)}, u32[]{:S(2)}, u32[]{:S(2)}) collective-permute-start(f32[8,48,768]{2,1,0:T(8,128)S(1)} %get-tuple-element.199), channel_id=1, source_target_pairs={{0,1},{1,0},{2,3},{3,2},{4,5},{5,4},{6,7},{7,6},{8,9},{9,8},{10,11... | collective-permute-start | bytes 3538952 | tf_op jit(solution)/shard_map/ppermute | solution.py:894
  205.2 16.5 %collective-permute-start.24 = (bf16[2,48,1536]{2,1,0:T(8,128)(2,1)S(1)}, bf16[2,48,1536]{2,1,0:T(8,128)(2,1)S(1)}, u32[]{:S(2)}, u32[]{:S(2)}) collective-permute-start(bf16[2,48,1536]{2,1,0:T(8,128)(2,1)S(1)} %get-tuple-element.274), channel_id=1, source_target_pairs={{0,2},{1,3},{2,0},{3,1},{4,6},{5,7},{6,4},{7,5},{8,10},{9,11},{10,... | collective-permute-start | bytes 884744 | tf_op jit(solution)/shard_map/ppermute | solution.py:894
  207.4 29.8 %collective-permute-start.31 = (bf16[1,48,3072]{2,1,0:T(8,128)(2,1)S(1)}, bf16[1,48,3072]{2,1,0:T(8,128)(2,1)S(1)}, u32[]{:S(2)}, u32[]{:S(2)}) collective-permute-start(bf16[1,48,3072]{2,1,0:T(8,128)(2,1)S(1)} %fusion.6), channel_id=1, source_target_pairs={{0,16},{1,17},{2,18},{3,19},{4,20},{5,21},{6,22},{7,23},{8,24},{9,... | collective-permute-start | bytes 884744 | tf_op jit(solution)/shard_map/ppermute | solution.py:894
  210.9 19.1 %collective-permute-start.27 = (f32[16,768]{1,0:T(8,128)S(1)}, f32[16,768]{1,0:T(8,128)S(1)}, u32[]{:S(2)}, u32[]{:S(2)}) collective-permute-start(f32[16,768]{1,0:T(8,128)S(1)} %add.156), channel_id=1, source_target_pairs={{0,2},{1,3},{2,0},{3,1},{4,6},{5,7},{6,4},{7,5},{8,10},{9,11},{10,... | collective-permute-start | bytes 147464 | tf_op jit(solution)/shard_map/ppermute | solution.py:894
  212.9 16.2 %collective-permute-start.28 = (bf16[2,48,768]{2,1,0:T(8,128)(2,1)S(1)}, bf16[2,48,768]{2,1,0:T(8,128)(2,1)S(1)}, u32[]{:S(2)}, u32[]{:S(2)}) collective-permute-start(bf16[2,48,768]{2,1,0:T(8,128)(2,1)S(1)} %get-tuple-element.280), channel_id=1, source_target_pairs={{0,2},{1,3},{2,0},{3,1},{4,6},{5,7},{6,4},{7,5},{8,10},{9,11},{10,... | collective-permute-start | bytes 442376 | tf_op jit(solution)/shard_map/ppermute | solution.py:894
  220.5 8.4 %collective-permute-start.29 = (bf16[4,48,768]{2,1,0:T(8,128)(2,1)S(1)}, bf16[4,48,768]{2,1,0:T(8,128)(2,1)S(1)}, u32[]{:S(2)}, u32[]{:S(2)}) collective-permute-start(bf16[4,48,768]{2,1,0:T(8,128)(2,1)S(1)} %get-tuple-element.272), channel_id=1, source_target_pairs={{0,4},{1,5},{2,6},{3,7},{4,0},{5,1},{6,2},{7,3},{8,12},{9,13},{10,... | collective-permute-start | bytes 884744 | tf_op jit(solution)/shard_map/ppermute | solution.py:894
  221.7 20.4 %collective-permute-start.34 = (bf16[1,48,3200]{2,1,0:T(8,128)(2,1)S(1)}, bf16[1,48,3200]{2,1,0:T(8,128)(2,1)S(1)}, u32[]{:S(2)}, u32[]{:S(2)}) collective-permute-start(bf16[1,48,3200]{2,1,0:T(8,128)(2,1)S(1)} %add_convert_fusion.3), channel_id=1, source_target_pairs={{0,8},{1,9},{2,10},{3,11},{4,12},{5,13},{6,14},{7,15},{8,0},{9,1},... | collective-permute-start | bytes 921608 | tf_op jit(solution)/shard_map/ppermute | solution.py:894
  228.8 7.5 %collective-permute-start.26 = (bf16[1,48,1536]{2,1,0:T(8,128)(2,1)S(1)}, bf16[1,48,1536]{2,1,0:T(8,128)(2,1)S(1)}, u32[]{:S(2)}, u32[]{:S(2)}) collective-permute-start(bf16[1,48,1536]{2,1,0:T(8,128)(2,1)S(1)} %fusion.10), channel_id=1, source_target_pairs={{0,8},{1,9},{2,10},{3,11},{4,12},{5,13},{6,14},{7,15},{8,0},{9,1},... | collective-permute-start | bytes 442376 | tf_op jit(solution)/shard_map/ppermute | solution.py:894
  229.1 9.5 %collective-permute-start.36 = (bf16[2,48,768]{2,1,0:T(8,128)(2,1)S(1)}, bf16[2,48,768]{2,1,0:T(8,128)(2,1)S(1)}, u32[]{:S(2)}, u32[]{:S(2)}) collective-permute-start(bf16[2,48,768]{2,1,0:T(8,128)(2,1)S(1)} %get-tuple-element.278), channel_id=1, source_target_pairs={{0,2},{1,3},{2,0},{3,1},{4,6},{5,7},{6,4},{7,5},{8,10},{9,11},{10,... | collective-permute-start | bytes 442376 | tf_op jit(solution)/shard_map/ppermute | solution.py:894
  230.1 12.6 %collective-permute-start.33 = (bf16[1,48,768]{2,1,0:T(8,128)(2,1)S(1)}, bf16[1,48,768]{2,1,0:T(8,128)(2,1)S(1)}, u32[]{:S(2)}, u32[]{:S(2)}) collective-permute-start(bf16[1,48,768]{2,1,0:T(8,128)(2,1)S(1)} %fusion.19), channel_id=1, source_target_pairs={{0,8},{1,9},{2,10},{3,11},{4,12},{5,13},{6,14},{7,15},{8,0},{9,1},... | collective-permute-start | bytes 221192 | tf_op jit(solution)/shard_map/ppermute | solution.py:894
  236.3 4.1 %collective-permute-start.35 = (f32[16,768]{1,0:T(8,128)S(1)}, f32[16,768]{1,0:T(8,128)S(1)}, u32[]{:S(2)}, u32[]{:S(2)}) collective-permute-start(f32[16,768]{1,0:T(8,128)S(1)} %add.165), channel_id=1, source_target_pairs={{0,4},{1,5},{2,6},{3,7},{4,0},{5,1},{6,2},{7,3},{8,12},{9,13},{10,... | collective-permute-start | bytes 147464 | tf_op jit(solution)/shard_map/ppermute | solution.py:894
  237.2 13.2 %collective-permute-start.30 = (bf16[1,48,1536]{2,1,0:T(8,128)(2,1)S(1)}, bf16[1,48,1536]{2,1,0:T(8,128)(2,1)S(1)}, u32[]{:S(2)}, u32[]{:S(2)}) collective-permute-start(bf16[1,48,1536]{2,1,0:T(8,128)(2,1)S(1)} %fusion.12), channel_id=1, source_target_pairs={{0,16},{1,17},{2,18},{3,19},{4,20},{5,21},{6,22},{7,23},{8,24},{9,... | collective-permute-start | bytes 442376 | tf_op jit(solution)/shard_map/ppermute | solution.py:894
  238.7 10.0 %collective-permute-start.32 = (bf16[1,48,3072]{2,1,0:T(8,128)(2,1)S(1)}, bf16[1,48,3072]{2,1,0:T(8,128)(2,1)S(1)}, u32[]{:S(2)}, u32[]{:S(2)}) collective-permute-start(bf16[1,48,3072]{2,1,0:T(8,128)(2,1)S(1)} %add_convert_fusion.4), channel_id=1, source_target_pairs={{0,4},{1,5},{2,6},{3,7},{4,0},{5,1},{6,2},{7,3},{8,12},{9,13},{10,... | collective-permute-start | bytes 884744 | tf_op jit(solution)/shard_map/ppermute | solution.py:894
  240.4 11.5 %collective-permute-start.38 = (bf16[1,48,768]{2,1,0:T(8,128)(2,1)S(1)}, bf16[1,48,768]{2,1,0:T(8,128)(2,1)S(1)}, u32[]{:S(2)}, u32[]{:S(2)}) collective-permute-start(bf16[1,48,768]{2,1,0:T(8,128)(2,1)S(1)} %fusion.16), channel_id=1, source_target_pairs={{0,8},{1,9},{2,10},{3,11},{4,12},{5,13},{6,14},{7,15},{8,0},{9,1},... | collective-permute-start | bytes 221192 | tf_op jit(solution)/shard_map/ppermute | solution.py:894
  242.2 10.4 %collective-permute-start.42 = (f32[16,768]{1,0:T(8,128)S(1)}, f32[16,768]{1,0:T(8,128)S(1)}, u32[]{:S(2)}, u32[]{:S(2)}) collective-permute-start(f32[16,768]{1,0:T(8,128)S(1)} %add.171), channel_id=1, source_target_pairs={{0,8},{1,9},{2,10},{3,11},{4,12},{5,13},{6,14},{7,15},{8,0},{9,1},... | collective-permute-start | bytes 147464 | tf_op jit(solution)/shard_map/ppermute | solution.py:894
  242.6 17.5 %collective-permute-start.40 = (bf16[2,48,3200]{2,1,0:T(8,128)(2,1)S(1)}, bf16[2,48,3200]{2,1,0:T(8,128)(2,1)S(1)}, u32[]{:S(2)}, u32[]{:S(2)}) collective-permute-start(bf16[2,48,3200]{2,1,0:T(8,128)(2,1)S(1)} %broadcast_select_fusion), channel_id=1, source_target_pairs={{0,4},{1,5},{2,6},{3,7},{4,0},{5,1},{6,2},{7,3},{8,12},{9,13},{10,... | collective-permute-start | bytes 1843208 | tf_op jit(solution)/shard_map/ppermute | solution.py:894
  248.7 7.8 %collective-permute-start.41 = (bf16[1,48,768]{2,1,0:T(8,128)(2,1)S(1)}, bf16[1,48,768]{2,1,0:T(8,128)(2,1)S(1)}, u32[]{:S(2)}, u32[]{:S(2)}) collective-permute-start(bf16[1,48,768]{2,1,0:T(8,128)(2,1)S(1)} %fusion.18), channel_id=1, source_target_pairs={{0,16},{1,17},{2,18},{3,19},{4,20},{5,21},{6,22},{7,23},{8,24},{9,... | collective-permute-start | bytes 221192 | tf_op jit(solution)/shard_map/ppermute | solution.py:894
  250.5 15.6 %collective-permute-start.46 = (bf16[2,48,3072]{2,1,0:T(8,128)(2,1)S(1)}, bf16[2,48,3072]{2,1,0:T(8,128)(2,1)}, u32[]{:S(2)}, u32[]{:S(2)}) collective-permute-start(bf16[2,48,3072]{2,1,0:T(8,128)(2,1)S(1)} %broadcast_select_fusion.1), channel_id=1, source_target_pairs={{0,2},{1,3},{2,0},{3,1},{4,6},{5,7},{6,4},{7,5},{8,10},{9,11},{10,... | collective-permute-start | bytes 1769480 | tf_op jit(solution)/shard_map/ppermute | solution.py:894
  251.9 11.0 %collective-permute-start.37 = (bf16[1,48,1536]{2,1,0:T(8,128)(2,1)S(1)}, bf16[1,48,1536]{2,1,0:T(8,128)(2,1)S(1)}, u32[]{:S(2)}, u32[]{:S(2)}) collective-permute-start(bf16[1,48,1536]{2,1,0:T(8,128)(2,1)S(1)} %add_convert_fusion.7), channel_id=1, source_target_pairs={{0,8},{1,9},{2,10},{3,11},{4,12},{5,13},{6,14},{7,15},{8,0},{9,1},... | collective-permute-start | bytes 442376 | tf_op jit(solution)/shard_map/ppermute | solution.py:894
  252.5 10.3 %collective-permute-start.39 = (bf16[1,48,768]{2,1,0:T(8,128)(2,1)S(1)}, bf16[1,48,768]{2,1,0:T(8,128)(2,1)S(1)}, u32[]{:S(2)}, u32[]{:S(2)}) collective-permute-start(bf16[1,48,768]{2,1,0:T(8,128)(2,1)S(1)} %fusion.15), channel_id=1, source_target_pairs={{0,16},{1,17},{2,18},{3,19},{4,20},{5,21},{6,22},{7,23},{8,24},{9,... | collective-permute-start | bytes 221192 | tf_op jit(solution)/shard_map/ppermute | solution.py:894
  256.5 6.5 %collective-permute-start.47 = (f32[16,768]{1,0:T(8,128)S(1)}, f32[16,768]{1,0:T(8,128)S(1)}, u32[]{:S(2)}, u32[]{:S(2)}) collective-permute-start(f32[16,768]{1,0:T(8,128)S(1)} %add.176), channel_id=1, source_target_pairs={{0,16},{1,17},{2,18},{3,19},{4,20},{5,21},{6,22},{7,23},{8,24},{9,... | collective-permute-start | bytes 147464 | tf_op jit(solution)/shard_map/ppermute | solution.py:894
  260.2 7.2 %collective-permute-start.45 = (bf16[1,48,768]{2,1,0:T(8,128)(2,1)S(1)}, bf16[1,48,768]{2,1,0:T(8,128)(2,1)}, u32[]{:S(2)}, u32[]{:S(2)}) collective-permute-start(bf16[1,48,768]{2,1,0:T(8,128)(2,1)S(1)} %add_convert_fusion.9), channel_id=1, source_target_pairs={{0,8},{1,9},{2,10},{3,11},{4,12},{5,13},{6,14},{7,15},{8,0},{9,1},... | collective-permute-start | bytes 221192 | tf_op jit(solution)/shard_map/ppermute | solution.py:894
  263.1 6.3 %collective-permute-start.44 = (bf16[1,48,768]{2,1,0:T(8,128)(2,1)S(1)}, bf16[1,48,768]{2,1,0:T(8,128)(2,1)}, u32[]{:S(2)}, u32[]{:S(2)}) collective-permute-start(bf16[1,48,768]{2,1,0:T(8,128)(2,1)S(1)} %add_convert_fusion.8), channel_id=1, source_target_pairs={{0,8},{1,9},{2,10},{3,11},{4,12},{5,13},{6,14},{7,15},{8,0},{9,1},... | collective-permute-start | bytes 221192 | tf_op jit(solution)/shard_map/ppermute | solution.py:894
  263.2 8.7 %collective-permute-start.43 = (bf16[2,48,1536]{2,1,0:T(8,128)(2,1)S(1)}, bf16[2,48,1536]{2,1,0:T(8,128)(2,1)}, u32[]{:S(2)}, u32[]{:S(2)}) collective-permute-start(bf16[2,48,1536]{2,1,0:T(8,128)(2,1)S(1)} %broadcast_select_fusion.2), channel_id=1, source_target_pairs={{0,2},{1,3},{2,0},{3,1},{4,6},{5,7},{6,4},{7,5},{8,10},{9,11},{10,... | collective-permute-start | bytes 884744 | tf_op jit(solution)/shard_map/ppermute | solution.py:894
  268.3 6.8 %collective-permute-start.50 = (bf16[2,48,768]{2,1,0:T(8,128)(2,1)S(1)}, bf16[2,48,768]{2,1,0:T(8,128)(2,1)S(1)}, u32[]{:S(2)}, u32[]{:S(2)}) collective-permute-start(bf16[2,48,768]{2,1,0:T(8,128)(2,1)S(1)} %broadcast_select_fusion.4), channel_id=1, source_target_pairs={{0,2},{1,3},{2,0},{3,1},{4,6},{5,7},{6,4},{7,5},{8,10},{9,11},{10,... | collective-permute-start | bytes 442376 | tf_op jit(solution)/shard_map/ppermute | solution.py:894
  270.4 6.3 %collective-permute-start.49 = (bf16[2,48,768]{2,1,0:T(8,128)(2,1)S(1)}, bf16[2,48,768]{2,1,0:T(8,128)(2,1)S(1)}, u32[]{:S(2)}, u32[]{:S(2)}) collective-permute-start(bf16[2,48,768]{2,1,0:T(8,128)(2,1)S(1)} %broadcast_select_fusion.3), channel_id=1, source_target_pairs={{0,2},{1,3},{2,0},{3,1},{4,6},{5,7},{6,4},{7,5},{8,10},{9,11},{10,... | collective-permute-start | bytes 442376 | tf_op jit(solution)/shard_map/ppermute | solution.py:894
  276.8 30.3 %collective-permute-start.58 = (bf16[4,48,3200]{2,1,0:T(8,128)(2,1)S(1)}, bf16[4,48,3200]{2,1,0:T(8,128)(2,1)S(1)}, u32[]{:S(2)}, u32[]{:S(2)}) collective-permute-start(bf16[4,48,3200]{2,1,0:T(8,128)(2,1)S(1)} %bitcast_select_fusion.3), channel_id=1, source_target_pairs={{0,2},{1,3},{2,0},{3,1},{4,6},{5,7},{6,4},{7,5},{8,10},{9,11},{10,... | collective-permute-start | bytes 3686408 | tf_op jit(solution)/shard_map/ppermute | solution.py:894
  277.9 26.1 %collective-permute-start.52 = (bf16[4,48,3072]{2,1,0:T(8,128)(2,1)S(1)}, bf16[4,48,3072]{2,1,0:T(8,128)(2,1)S(1)}, u32[]{:S(2)}, u32[]{:S(2)}) collective-permute-start(bf16[4,48,3072]{2,1,0:T(8,128)(2,1)S(1)} %bitcast_select_fusion.5), channel_id=1, source_target_pairs={{0,8},{1,9},{2,10},{3,11},{4,12},{5,13},{6,14},{7,15},{8,0},{9,1},... | collective-permute-start | bytes 3538952 | tf_op jit(solution)/shard_map/ppermute | solution.py:894
  279.6 16.3 %collective-permute-start.48 = (bf16[4,48,1536]{2,1,0:T(8,128)(2,1)S(1)}, bf16[4,48,1536]{2,1,0:T(8,128)(2,1)S(1)}, u32[]{:S(2)}, u32[]{:S(2)}) collective-permute-start(bf16[4,48,1536]{2,1,0:T(8,128)(2,1)S(1)} %bitcast_select_fusion.9), channel_id=1, source_target_pairs={{0,4},{1,5},{2,6},{3,7},{4,0},{5,1},{6,2},{7,3},{8,12},{9,13},{10,... | collective-permute-start | bytes 1769480 | tf_op jit(solution)/shard_map/ppermute | solution.py:894
  280.6 21.4 %collective-permute-start.53 = (bf16[4,48,768]{2,1,0:T(8,128)(2,1)S(1)}, bf16[4,48,768]{2,1,0:T(8,128)(2,1)S(1)}, u32[]{:S(2)}, u32[]{:S(2)}) collective-permute-start(bf16[4,48,768]{2,1,0:T(8,128)(2,1)S(1)} %bitcast_select_fusion.13), channel_id=1, source_target_pairs={{0,4},{1,5},{2,6},{3,7},{4,0},{5,1},{6,2},{7,3},{8,12},{9,13},{10,... | collective-permute-start | bytes 884744 | tf_op jit(solution)/shard_map/ppermute | solution.py:894
  281.6 25.3 %collective-permute-start.55 = (bf16[4,48,768]{2,1,0:T(8,128)(2,1)S(1)}, bf16[4,48,768]{2,1,0:T(8,128)(2,1)S(1)}, u32[]{:S(2)}, u32[]{:S(2)}) collective-permute-start(bf16[4,48,768]{2,1,0:T(8,128)(2,1)S(1)} %bitcast_select_fusion.12), channel_id=1, source_target_pairs={{0,4},{1,5},{2,6},{3,7},{4,0},{5,1},{6,2},{7,3},{8,12},{9,13},{10,... | collective-permute-start | bytes 884744 | tf_op jit(solution)/shard_map/ppermute | solution.py:894
  307.6 18.1 %collective-permute-start.59 = (bf16[8,48,3200]{2,1,0:T(8,128)(2,1)S(1)}, bf16[8,48,3200]{2,1,0:T(8,128)(2,1)S(1)}, u32[]{:S(2)}, u32[]{:S(2)}) collective-permute-start(bf16[8,48,3200]{2,1,0:T(8,128)(2,1)S(1)} %bitcast_select_fusion.refs_0_), channel_id=1, source_target_pairs={{0,1},{1,0},{2,3},{3,2},{4,5},{5,4},{6,7},{7,6},{8,9},{9,8},{10,11... | collective-permute-start | bytes 7372808 | tf_op jit(solution)/shard_map/ppermute | solution.py:894
  307.6 13.1 %collective-permute-start.54 = (bf16[8,48,3072]{2,1,0:T(8,128)(2,1)S(1)}, bf16[8,48,3072]{2,1,0:T(8,128)(2,1)S(1)}, u32[]{:S(2)}, u32[]{:S(2)}) collective-permute-start(bf16[8,48,3072]{2,1,0:T(8,128)(2,1)S(1)} %bitcast_select_fusion.1.refs_0_), channel_id=1, source_target_pairs={{0,1},{1,0},{2,3},{3,2},{4,5},{5,4},{6,7},{7,6},{8,9},{9,8},{10,11... | collective-permute-start | bytes 7077896 | tf_op jit(solution)/shard_map/ppermute | solution.py:894
  308.1 15.1 %collective-permute-start.51 = (bf16[8,48,1536]{2,1,0:T(8,128)(2,1)S(1)}, bf16[8,48,1536]{2,1,0:T(8,128)(2,1)S(1)}, u32[]{:S(2)}, u32[]{:S(2)}) collective-permute-start(bf16[8,48,1536]{2,1,0:T(8,128)(2,1)S(1)} %bitcast_select_fusion.4.refs_0_), channel_id=1, source_target_pairs={{0,1},{1,0},{2,3},{3,2},{4,5},{5,4},{6,7},{7,6},{8,9},{9,8},{10,11... | collective-permute-start | bytes 3538952 | tf_op jit(solution)/shard_map/ppermute | solution.py:894
  308.2 10.0 %collective-permute-start.56 = (bf16[8,48,768]{2,1,0:T(8,128)(2,1)S(1)}, bf16[8,48,768]{2,1,0:T(8,128)(2,1)S(1)}, u32[]{:S(2)}, u32[]{:S(2)}) collective-permute-start(bf16[8,48,768]{2,1,0:T(8,128)(2,1)S(1)} %bitcast_select_fusion.8.refs_1_), channel_id=1, source_target_pairs={{0,1},{1,0},{2,3},{3,2},{4,5},{5,4},{6,7},{7,6},{8,9},{9,8},{10,11... | collective-permute-start | bytes 1769480 | tf_op jit(solution)/shard_map/ppermute | solution.py:894
  308.6 12.1 %collective-permute-start.57 = (bf16[8,48,768]{2,1,0:T(8,128)(2,1)S(1)}, bf16[8,48,768]{2,1,0:T(8,128)(2,1)S(1)}, u32[]{:S(2)}, u32[]{:S(2)}) collective-permute-start(bf16[8,48,768]{2,1,0:T(8,128)(2,1)S(1)} %bitcast_select_fusion.7.refs_2_), channel_id=1, source_target_pairs={{0,1},{1,0},{2,3},{3,2},{4,5},{5,4},{6,7},{7,6},{8,9},{9,8},{10,11... | collective-permute-start | bytes 1769480 | tf_op jit(solution)/shard_map/ppermute | solution.py:894
  (24 other events, 163.8 us)

commit v5 on v4

--- a/solution.py
+++ b/solution.py
@@ -698,6 +698,9 @@
     )(me, in_hbm(act), dbr, gwp)
 
 
+UP_CHUNK = 512
+
+
 def up_grad_kernel(dims, me, dbr, slp, wd, ht, keep, send, din, dsum):
     pr = keep.shape[1]
     half = PIECES // 2
@@ -721,19 +724,19 @@
     ff = slp.shape[1]
     half, pr = PIECES // 2, width // PIECES
     buf = struct((half, pr, ff), f32)
-    part = pl.BlockSpec((half, pr, FF_CHUNK), lambda c: (0, 0, c))
-    wide = pl.BlockSpec((rows, FF_CHUNK), lambda c: (0, c))
+    part = pl.BlockSpec((half, pr, UP_CHUNK), lambda c: (0, 0, c))
+    wide = pl.BlockSpec((rows, UP_CHUNK), lambda c: (0, c))
     return pl.pallas_call(
         functools.partial(up_grad_kernel, dims),
-        grid=(ff // FF_CHUNK,),
+        grid=(ff // UP_CHUNK,),
         in_specs=[
             SMEM,
             held(dbr.shape),
             wide,
-            pl.BlockSpec((FF_CHUNK, width), lambda c: (c, 0)),
+            pl.BlockSpec((UP_CHUNK, width), lambda c: (c, 0)),
             held(ht.shape),
         ],
-        out_specs=[part, part, wide, pl.BlockSpec((1, FF_CHUNK), lambda c: (0, c))],
+        out_specs=[part, part, wide, pl.BlockSpec((1, UP_CHUNK), lambda c: (0, c))],
         out_shape=[buf, buf, pltpu.HBM((rows, ff), bf16), struct((1, ff), f32)],
         compiler_params=params(28),
         cost_estimate=cost(10e9, 30e6),

time: 332 us -> 332 us (level)
  transfers between devices with their start and end apart: 60 -> 60, of which waited for: 26 -> 24; matrix products, arithmetic and copies ran while one was open for 5% -> 5% of each run, Pallas kernels for 26% -> 26%
where the time goes in v5:
time: 332 us; the launch traced here: 328 us
  Pallas kernels  144 us (43%)
  waiting for transfers between devices  81.8 us (25%)
  starting transfers between devices  73.3 us (22%)
  other arithmetic  17.9 us (5%)
  local copies, waits for them, and re-layouts  9.36 us (3%)
    ppermute x60, waiting for transfers between devices, swap(): return lax.ppermute(x, 'dp', [(i, i ^ mask) for i in range(n)])  81.8 us
    ppermute x60, starting transfers between devices, swap(): return lax.ppermute(x, 'dp', [(i, i ^ mask) for i in range(n)])  73.3 us
    pallas_call x3, Pallas kernels, attention_back(): pl.pallas_call(attn_bwd_kernel, grid=(1,), in_specs=[SMEM, col(0), col(1)...  34.6 us
    pallas_call x1, Pallas kernels, attention(): pl.pallas_call(attn_fwd_kernel, in_specs=[SMEM] + [anywhere] * len(ins),...  21.5 us
    pallas_call x1, Pallas kernels, ffn_fwd(): pl.pallas_call(ffn_fwd_kernel, grid=(steps,), in_specs=specs, out_specs=o...  20 us
    pallas_call x6, Pallas kernels, put_in_place(): pl.pallas_call(functools.partial(place_kernel, [c.dims for c in chains],...  14.8 us
    pallas_call x1, Pallas kernels, up_grad(): pl.pallas_call(functools.partial(up_grad_kernel, dims), grid=(ff // UP_CH...  14.7 us
    pallas_call x1, Pallas kernels, mid_back(): pl.pallas_call(mid_back_kernel, grid=(steps,), in_specs=specs, out_specs=...  10.8 us
  transfers between devices with their start and end apart: 60, of which 24 were waited for; matrix products, arithmetic and copies ran while one was open for 5% of the time, Pallas kernels for 26%

profile of v5, /device:TPU:0, one launch (start us, length us, event | category | flops | bytes accessed | tf_op | source)
XLA Modules:
  0.0 327.9 jit_solution(411670418214458147)
XLA Ops:
  1.4 21.5 %attention_forward.1 = (bf16[1024,2304]{1,0:T(8,128)(2,1)}, bf16[1024,768]{1,0:T(8,128)(2,1)S(1)}, f32[6,8,256]{2,1,0:T(8,128)S(1)}, f32[1024,768]{1,0:T(8,128)S...) custom-call(s32[1,6]{1,0:T(1,128)S(1)} %copy-done.16, ...), custom_call_target="tpu_custom_call" | custom-call | tf_op jit(solution)/shard_map/attention_forward/pallas_call | solution.py:304
  23.0 20.0 %ffn_forward.1 = (bf16[1024,3072]{1,0:T(8,128)(2,1)}, bf16[1024,3072]{1,0:T(8,128)(2,1)}, bf16[1024,768]{1,0:T(8,128)(2,1)}, f32[1024,1]{1,0:T(8,128)S(1)}, bf16...) custom-call(s32[1,6]{1,0:T(1,128)S(1)} %copy-done.16, ...), custom_call_target="tpu_custom_call" | custom-call | tf_op jit(solution)/shard_map/ffn_forward/pallas_call | solution.py:439
  44.5 4.0 %collective-permute-start = (bf16[1,48,128]{2,1,0:T(8,128)(2,1)S(1)}, bf16[1,48,128]{2,1,0:T(8,128)(2,1)S(1)}, u32[]{:S(2)}, u32[]{:S(2)}) collective-permute-start(bf16[1,48,128]{2,1,0:T(8,128)(2,1)S(1)} %get-tuple-element.137), channel_id=1, source_target_pairs={{0,16},{1,17},{2,18},{3,19},{4,20},{5,21},{6,22},{7,23},{8,24},{9,... | collective-permute-start | bytes 36872 | tf_op jit(solution)/shard_map/ppermute | solution.py:897
  48.6 1.7 collective-permute-done
  50.3 1.9 collective-permute-start.1
  52.4 1.8 collective-permute-done.1
  54.2 1.9 collective-permute-start.2
  56.3 2.1 collective-permute-done.2
  58.4 1.9 collective-permute-start.3
  60.5 2.6 collective-permute-done.3
  64.8 1.9 loss_forward.1
  66.8 3.0 collective-permute-start.5
  69.8 2.0 collective-permute-done.5
  71.9 2.0 collective-permute-start.6
  73.8 2.6 collective-permute-done.6
  76.6 2.4 collective-permute-start.7
  79.0 3.5 %collective-permute-done.7 = bf16[4,176,128]{2,1,0:T(8,128)(2,1)S(1)} collective-permute-done((bf16[4,176,128]{2,1,0:T(8,128)(2,1)S(1)}, bf16[4,176,128]{2,1,0:T(8,128)(2,1)S(1)}, u32[]{:S(2)}, u32[]{:S(2)}) %collective-permute-start.7) | collective-permute-done | bytes 180256 | tf_op jit(solution)/shard_map/ppermute | solution.py:897
  82.5 2.1 collective-permute-start.8
  84.6 5.4 %collective-permute-done.8 = bf16[8,176,128]{2,1,0:T(8,128)(2,1)S(1)} collective-permute-done((bf16[8,176,128]{2,1,0:T(8,128)(2,1)S(1)}, bf16[8,176,128]{2,1,0:T(8,128)(2,1)S(1)}, u32[]{:S(2)}, u32[]{:S(2)}) %collective-permute-start.8) | collective-permute-done | bytes 360480 | tf_op jit(solution)/shard_map/ppermute | solution.py:897
  91.1 2.4 collective-permute-done.9
  93.6 1.5 bitcast_select_fusion.2.messages
  96.2 6.3 %loss_backward.1 = (f32[8,128]{1,0:T(8,128)S(1)}, f32[1024,768]{1,0:T(8,128)}, bf16[1024,768]{1,0:T(8,128)(2,1)S(1)}, f32[768,128]{1,0:T(8,128)S(1)}, f32[8,768]{1,0:T(8,128)S(1)}) custom-call(s32[1]{0:T(128)} %bitcast.me, s32[1,6]{1,0:T(1,128)S(1)} %copy-done.17, s32[32,5]{1,0:T(8,128)S(1)} %copy.38.owner, s32[32,5]{1,0:T(8,128)S(1)} %copy.39.place, ...), custom_call_target="tpu_custom_call" | custom-call | tf_op jit(solution)/shard_map/loss_backward/pallas_call | solution.py:609
  102.5 7.8 %down_gradient.1 = (f32[8,48,3200]{2,1,0:T(8,128)S(1)}, f32[8,48,3200]{2,1,0:T(8,128)S(1)}) custom-call(s32[1]{0:T(128)} %bitcast.me, bf16[1024,3072]{1,0:T(8,128)(2,1)} %get-tuple-element.146.act, bf16[1024,768]{1,0:T(8,128)(2,1)S(1)} %get-tuple-element.147.dbr, f32[768,128]{1,0:T(8,128)S(1)} %get-tuple-element.148.gwp), custom_call_target="tpu_custom_call" | custom-call | tf_op jit(solution)/shard_map/down_gradient/pallas_call | solution.py:676
  110.5 14.7 %up_gradient.1 = (f32[8,48,3072]{2,1,0:T(8,128)S(1)}, f32[8,48,3072]{2,1,0:T(8,128)}, bf16[1024,3072]{1,0:T(8,128)(2,1)}, f32[1,3072]{1,0:T(1,128)S(1)}) custom-call(s32[1]{0:T(128)} %bitcast.me, bf16[1024,768]{1,0:T(8,128)(2,1)S(1)} %get-tuple-element.147.dbr, bf16[1024,3072]{1,0:T(8,128)(2,1)} %get-tuple-element.152.slp, bf16[3072,768]{1,0:T(8,128)(2,1)} %wd.3, ...), custom_call_target="tpu_custom_call" | custom-call | tf_op jit(solution)/shard_map/up_gradient/pallas_call | solution.py:729
  126.1 2.1 collective-permute-start.11
  128.4 10.8 %middle_backward.1 = (f32[1024,768]{1,0:T(8,128)S(1)}, bf16[1024,768]{1,0:T(8,128)(2,1)S(1)}, bf16[1024,768]{1,0:T(8,128)(2,1)S(1)}, f32[8,768]{1,0:T(8,128)S(1)}) custom-call(s32[1]{0:T(128)} %bitcast.me, bf16[1024,3072]{1,0:T(8,128)(2,1)} %get-tuple-element.159.din, bf16[768,3072]{1,0:T(8,128)(2,1)} %wu.3, f32[1024,768]{1,0:T(8,128)S(1)} %copy-done.3, ...), custom_call_target="tpu_custom_call" | custom-call | tf_op jit(solution)/shard_map/middle_backward/pallas_call | solution.py:797
  139.3 4.5 %slice_add_fusion.1 = (f32[4,48,3072]{2,1,0:T(8,128)}, bf16[4,48,3072]{2,1,0:T(8,128)(2,1)S(1)}) fusion(f32[8,48,3072]{2,1,0:T(8,128)} %collective-permute-done.12, f32[8,48,3072]{2,1,0:T(8,128)S(1)} %get-tuple-element.156), kind=kLoop, calls=%fused_computation.4 | loop fusion | flops 1769472 | bytes 12976128 | tf_op jit(solution)/shard_map/add | solution.py:935
  143.8 1.6 collective-permute-start.14
  145.4 11.5 %attention_backward.3 = (bf16[1024,256]{1,0:T(8,128)(2,1)S(1)}, bf16[1024,256]{1,0:T(8,128)(2,1)S(1)}, bf16[1024,256]{1,0:T(8,128)(2,1)S(1)}, f32[8,256]{1,0:T(8,128)S(1)}) custom-call(s32[1,6]{1,0:T(1,128)S(1)} %copy-done.17, bf16[1024,2304]{1,0:T(8,128)(2,1)S(1)} %bitcast.89, bf16[1024,2304]{1,0:T(8,128)(2,1)S(1)} %bitcast.89, ...), custom_call_target="tpu_custom_call" | custom-call | tf_op jit(solution)/shard_map/attention_backward/pallas_call | solution.py:340
  158.5 2.8 qkv_gradient.3
  161.3 1.6 collective-permute-start.13
  162.9 11.7 %attention_backward.4 = (bf16[1024,256]{1,0:T(8,128)(2,1)S(1)}, bf16[1024,256]{1,0:T(8,128)(2,1)S(1)}, bf16[1024,256]{1,0:T(8,128)(2,1)S(1)}, f32[8,256]{1,0:T(8,128)S(1)}) custom-call(s32[1,6]{1,0:T(1,128)S(1)} %copy-done.17, bf16[1024,2304]{1,0:T(8,128)(2,1)S(1)} %bitcast.89, bf16[1024,2304]{1,0:T(8,128)(2,1)S(1)} %bitcast.89, ...), custom_call_target="tpu_custom_call" | custom-call | tf_op jit(solution)/shard_map/attention_backward/pallas_call | solution.py:340
  182.4 11.5 %attention_backward.5 = (bf16[1024,256]{1,0:T(8,128)(2,1)S(1)}, bf16[1024,256]{1,0:T(8,128)(2,1)S(1)}, bf16[1024,256]{1,0:T(8,128)(2,1)S(1)}, f32[8,256]{1,0:T(8,128)S(1)}) custom-call(s32[1,6]{1,0:T(1,128)S(1)} %copy-done.17, bf16[1024,2304]{1,0:T(8,128)(2,1)S(1)} %bitcast.89, bf16[1024,2304]{1,0:T(8,128)(2,1)S(1)} %bitcast.89, ...), custom_call_target="tpu_custom_call" | custom-call | tf_op jit(solution)/shard_map/attention_backward/pallas_call | solution.py:340
  195.8 3.7 %collective-permute-start.25 = (bf16[1,48,3200]{2,1,0:T(8,128)(2,1)S(1)}, bf16[1,48,3200]{2,1,0:T(8,128)(2,1)S(1)}, u32[]{:S(2)}, u32[]{:S(2)}) collective-permute-start(bf16[1,48,3200]{2,1,0:T(8,128)(2,1)S(1)} %fusion.4), channel_id=1, source_target_pairs={{0,16},{1,17},{2,18},{3,19},{4,20},{5,21},{6,22},{7,23},{8,24},{9,... | collective-permute-start | bytes 921608 | tf_op jit(solution)/shard_map/ppermute | solution.py:897
  202.4 2.1 collective-permute-done.20
  206.1 3.7 %collective-permute-start.31 = (bf16[1,48,3072]{2,1,0:T(8,128)(2,1)S(1)}, bf16[1,48,3072]{2,1,0:T(8,128)(2,1)S(1)}, u32[]{:S(2)}, u32[]{:S(2)}) collective-permute-start(bf16[1,48,3072]{2,1,0:T(8,128)(2,1)S(1)} %fusion.6), channel_id=1, source_target_pairs={{0,16},{1,17},{2,18},{3,19},{4,20},{5,21},{6,22},{7,23},{8,24},{9,... | collective-permute-start | bytes 884744 | tf_op jit(solution)/shard_map/ppermute | solution.py:897
  212.2 5.5 %input_gradient.1 = f32[1024,768]{1,0:T(8,128)} custom-call(s32[1]{0:T(128)} %bitcast.me, bf16[1024,256]{1,0:T(8,128)(2,1)S(1)} %get-tuple-element.173.d0.refs_0_, bf16[1024,256]{1,0:T(8,128)(2,1)S(1)} %get-tuple-element.185.d0.refs_1_, bf16[1024,256]{1,0:T(8,128)(2,1)S(1)} %get-tuple-element.196.d0.refs_2_, ...), custom_call_target="tpu_custom_call" | custom-call | tf_op jit(solution)/shard_map/input_gradient/pallas_call | solution.py:857
  217.8 2.1 collective-permute-done.25
  221.4 6.8 %collective-permute-done.29 = bf16[4,48,768]{2,1,0:T(8,128)(2,1)S(1)} collective-permute-done((bf16[4,48,768]{2,1,0:T(8,128)(2,1)S(1)}, bf16[4,48,768]{2,1,0:T(8,128)(2,1)S(1)}, u32[]{:S(2)}, u32[]{:S(2)}) %collective-permute-start.29) | collective-permute-done | bytes 294944 | tf_op jit(solution)/shard_map/ppermute | solution.py:897
  229.4 2.0 collective-permute-start.33
  231.4 4.3 %collective-permute-done.26 = bf16[1,48,1536]{2,1,0:T(8,128)(2,1)S(1)} collective-permute-done((bf16[1,48,1536]{2,1,0:T(8,128)(2,1)S(1)}, bf16[1,48,1536]{2,1,0:T(8,128)(2,1)S(1)}, u32[]{:S(2)}, u32[]{:S(2)}) %collective-permute-start.26) | collective-permute-done | bytes 147488 | tf_op jit(solution)/shard_map/ppermute | solution.py:897
  239.8 1.8 collective-permute-start.38
  243.0 5.0 %collective-permute-done.32 = bf16[1,48,3072]{2,1,0:T(8,128)(2,1)S(1)} collective-permute-done((bf16[1,48,3072]{2,1,0:T(8,128)(2,1)S(1)}, bf16[1,48,3072]{2,1,0:T(8,128)(2,1)S(1)}, u32[]{:S(2)}, u32[]{:S(2)}) %collective-permute-start.32) | collective-permute-done | bytes 294944 | tf_op jit(solution)/shard_map/ppermute | solution.py:897
  248.0 1.7 collective-permute-start.41
  249.8 1.7 collective-permute-start.46
  252.5 3.0 collective-permute-start.39
  256.2 3.3 %collective-permute-done.40 = bf16[2,48,3200]{2,1,0:T(8,128)(2,1)S(1)} collective-permute-done((bf16[2,48,3200]{2,1,0:T(8,128)(2,1)S(1)}, bf16[2,48,3200]{2,1,0:T(8,128)(2,1)S(1)}, u32[]{:S(2)}, u32[]{:S(2)}) %collective-permute-start.40) | collective-permute-done | bytes 614432 | tf_op jit(solution)/shard_map/ppermute | solution.py:897
  259.5 2.5 collective-permute-start.45
  262.5 1.7 collective-permute-start.43
  269.7 1.7 collective-permute-start.49
  272.5 2.0 collective-permute-done.50
  276.1 1.7 collective-permute-start.58
  277.8 1.7 collective-permute-start.52
  279.9 1.6 collective-permute-start.53
  281.9 13.8 %collective-permute-done.48 = bf16[4,48,1536]{2,1,0:T(8,128)(2,1)S(1)} collective-permute-done((bf16[4,48,1536]{2,1,0:T(8,128)(2,1)S(1)}, bf16[4,48,1536]{2,1,0:T(8,128)(2,1)S(1)}, u32[]{:S(2)}, u32[]{:S(2)}) %collective-permute-start.48) | collective-permute-done | bytes 589856 | tf_op jit(solution)/shard_map/ppermute | solution.py:897
  295.9 5.8 %collective-permute-done.53 = bf16[4,48,768]{2,1,0:T(8,128)(2,1)S(1)} collective-permute-done((bf16[4,48,768]{2,1,0:T(8,128)(2,1)S(1)}, bf16[4,48,768]{2,1,0:T(8,128)(2,1)S(1)}, u32[]{:S(2)}, u32[]{:S(2)}) %collective-permute-start.53) | collective-permute-done | bytes 294944 | tf_op jit(solution)/shard_map/ppermute | solution.py:897
  301.9 1.7 collective-permute-done.52
  304.0 2.5 up_place.2.refs_1_
  308.8 2.3 qkv_place.2
  311.1 6.6 %collective-permute-done.56.refs_1_ = bf16[8,48,768]{2,1,0:T(8,128)(2,1)S(1)} collective-permute-done((bf16[8,48,768]{2,1,0:T(8,128)(2,1)S(1)}, bf16[8,48,768]{2,1,0:T(8,128)(2,1)S(1)}, u32[]{:S(2)}, u32[]{:S(2)}) %collective-permute-start.56) | collective-permute-done | bytes 589856 | tf_op jit(solution)/shard_map/ppermute | solution.py:897
  317.7 2.5 down_place.2
  320.3 2.5 up_place.3
  322.8 2.4 qkv_place.3
  325.1 2.5 down_place.3
  (216 shorter events, 49.0 us)
Async XLA Ops:
  0.6 22.3 %copy-start.8 = (bf16[768,128]{1,0:T(8,128)(2,1)S(1)}, bf16[768,128]{1,0:T(8,128)(2,1)}, u32[]{:S(2)}) copy-start(bf16[768,128]{1,0:T(8,128)(2,1)} %wp.3) | copy-start | bytes 589828
  1.4 21.6 %copy-start.22 = (f32[768]{0:T(1024)S(1)}, f32[768]{0:T(1024)}, u32[]{:S(2)}) copy-start(f32[768]{0:T(1024)} %b2.1) | copy-start | bytes 9220
  23.0 40.5 %copy-start.24 = (s32[32,5]{0,1:T(8,128)S(1)}, s32[32,5]{0,1:T(8,128)}, u32[]{:S(2)}) copy-start(s32[32,5]{0,1:T(8,128)} %param.19) | copy-start | bytes 1924
  44.5 5.7 %collective-permute-start = (bf16[1,48,128]{2,1,0:T(8,128)(2,1)S(1)}, bf16[1,48,128]{2,1,0:T(8,128)(2,1)S(1)}, u32[]{:S(2)}, u32[]{:S(2)}) collective-permute-start(bf16[1,48,128]{2,1,0:T(8,128)(2,1)S(1)} %get-tuple-element.137), channel_id=1, source_target_pairs={{0,16},{1,17},{2,18},{3,19},{4,20},{5,21},{6,22},{7,23},{8,24},{9,... | collective-permute-start | bytes 36872 | tf_op jit(solution)/shard_map/ppermute | solution.py:897
  50.3 3.8 %collective-permute-start.1 = (bf16[2,48,128]{2,1,0:T(8,128)(2,1)S(1)}, bf16[2,48,128]{2,1,0:T(8,128)(2,1)S(1)}, u32[]{:S(2)}, u32[]{:S(2)}) collective-permute-start(bf16[2,48,128]{2,1,0:T(8,128)(2,1)S(1)} %broadcast_select_fusion.6), channel_id=1, source_target_pairs={{0,8},{1,9},{2,10},{3,11},{4,12},{5,13},{6,14},{7,15},{8,0},{9,1},... | collective-permute-start | bytes 73736 | tf_op jit(solution)/shard_map/ppermute | solution.py:897
  54.2 4.1 %collective-permute-start.2 = (bf16[4,48,128]{2,1,0:T(8,128)(2,1)S(1)}, bf16[4,48,128]{2,1,0:T(8,128)(2,1)S(1)}, u32[]{:S(2)}, u32[]{:S(2)}) collective-permute-start(bf16[4,48,128]{2,1,0:T(8,128)(2,1)S(1)} %bitcast_select_fusion.17), channel_id=1, source_target_pairs={{0,4},{1,5},{2,6},{3,7},{4,0},{5,1},{6,2},{7,3},{8,12},{9,13},{10,... | collective-permute-start | bytes 147464 | tf_op jit(solution)/shard_map/ppermute | solution.py:897
  58.4 4.7 %collective-permute-start.3 = (bf16[8,48,128]{2,1,0:T(8,128)(2,1)S(1)}, bf16[8,48,128]{2,1,0:T(8,128)(2,1)S(1)}, u32[]{:S(2)}, u32[]{:S(2)}) collective-permute-start(bf16[8,48,128]{2,1,0:T(8,128)(2,1)S(1)} %bitcast_select_fusion.16), channel_id=1, source_target_pairs={{0,2},{1,3},{2,0},{3,1},{4,6},{5,7},{6,4},{7,5},{8,10},{9,11},{10,... | collective-permute-start | bytes 294920 | tf_op jit(solution)/shard_map/ppermute | solution.py:897
  63.2 1.5 collective-permute-start.4
  66.8 24.3 %copy-start.25 = (s32[32,5]{0,1:T(8,128)S(1)}, s32[32,5]{0,1:T(8,128)}, u32[]{:S(2)}) copy-start(s32[32,5]{0,1:T(8,128)} %param.20) | copy-start | bytes 1924
  66.8 5.0 %collective-permute-start.5 = (bf16[1,176,128]{2,1,0:T(8,128)(2,1)S(1)}, bf16[1,176,128]{2,1,0:T(8,128)(2,1)S(1)}, u32[]{:S(2)}, u32[]{:S(2)}) collective-permute-start(bf16[1,176,128]{2,1,0:T(8,128)(2,1)S(1)} %get-tuple-element.139), channel_id=1, source_target_pairs={{0,16},{1,17},{2,18},{3,19},{4,20},{5,21},{6,22},{7,23},{8,24},{9,... | collective-permute-start | bytes 135176 | tf_op jit(solution)/shard_map/ppermute | solution.py:897
  71.9 4.6 %collective-permute-start.6 = (bf16[2,176,128]{2,1,0:T(8,128)(2,1)S(1)}, bf16[2,176,128]{2,1,0:T(8,128)(2,1)S(1)}, u32[]{:S(2)}, u32[]{:S(2)}) collective-permute-start(bf16[2,176,128]{2,1,0:T(8,128)(2,1)S(1)} %broadcast_select_fusion.5), channel_id=1, source_target_pairs={{0,8},{1,9},{2,10},{3,11},{4,12},{5,13},{6,14},{7,15},{8,0},{9,1},... | collective-permute-start | bytes 270344 | tf_op jit(solution)/shard_map/ppermute | solution.py:897
  76.6 5.9 %collective-permute-start.7 = (bf16[4,176,128]{2,1,0:T(8,128)(2,1)S(1)}, bf16[4,176,128]{2,1,0:T(8,128)(2,1)S(1)}, u32[]{:S(2)}, u32[]{:S(2)}) collective-permute-start(bf16[4,176,128]{2,1,0:T(8,128)(2,1)S(1)} %bitcast_select_fusion.15), channel_id=1, source_target_pairs={{0,4},{1,5},{2,6},{3,7},{4,0},{5,1},{6,2},{7,3},{8,12},{9,13},{10,... | collective-permute-start | bytes 540680 | tf_op jit(solution)/shard_map/ppermute | solution.py:897
  82.5 7.5 %collective-permute-start.8 = (bf16[8,176,128]{2,1,0:T(8,128)(2,1)S(1)}, bf16[8,176,128]{2,1,0:T(8,128)(2,1)S(1)}, u32[]{:S(2)}, u32[]{:S(2)}) collective-permute-start(bf16[8,176,128]{2,1,0:T(8,128)(2,1)S(1)} %bitcast_select_fusion.11), channel_id=1, source_target_pairs={{0,2},{1,3},{2,0},{3,1},{4,6},{5,7},{6,4},{7,5},{8,10},{9,11},{10,... | collective-permute-start | bytes 1081352 | tf_op jit(solution)/shard_map/ppermute | solution.py:897
  91.0 2.5 collective-permute-start.9
  110.3 15.3 %collective-permute-start.10 = (f32[8,48,3200]{2,1,0:T(8,128)S(1)}, f32[8,48,3200]{2,1,0:T(8,128)S(1)}, u32[]{:S(2)}, u32[]{:S(2)}) collective-permute-start(f32[8,48,3200]{2,1,0:T(8,128)S(1)} %get-tuple-element.150), channel_id=1, source_target_pairs={{0,1},{1,0},{2,3},{3,2},{4,5},{5,4},{6,7},{7,6},{8,9},{9,8},{10,11... | collective-permute-start | bytes 14745608 | tf_op jit(solution)/shard_map/ppermute | solution.py:897
  125.2 14.0 %collective-permute-start.12 = (f32[8,48,3072]{2,1,0:T(8,128)}, f32[8,48,3072]{2,1,0:T(8,128)}, u32[]{:S(2)}, u32[]{:S(2)}) collective-permute-start(f32[8,48,3072]{2,1,0:T(8,128)} %get-tuple-element.157), channel_id=1, source_target_pairs={{0,1},{1,0},{2,3},{3,2},{4,5},{5,4},{6,7},{7,6},{8,9},{9,8},{10,11... | collective-permute-start | bytes 14155784 | tf_op jit(solution)/shard_map/ppermute | solution.py:897
  126.1 30.8 %collective-permute-start.11 = (bf16[4,48,3200]{2,1,0:T(8,128)(2,1)S(1)}, bf16[4,48,3200]{2,1,0:T(8,128)(2,1)S(1)}, u32[]{:S(2)}, u32[]{:S(2)}) collective-permute-start(bf16[4,48,3200]{2,1,0:T(8,128)(2,1)S(1)} %get-tuple-element.262), channel_id=1, source_target_pairs={{0,2},{1,3},{2,0},{3,1},{4,6},{5,7},{6,4},{7,5},{8,10},{9,11},{10,... | collective-permute-start | bytes 3686408 | tf_op jit(solution)/shard_map/ppermute | solution.py:897
  143.8 30.8 %collective-permute-start.14 = (bf16[4,48,3072]{2,1,0:T(8,128)(2,1)S(1)}, bf16[4,48,3072]{2,1,0:T(8,128)(2,1)S(1)}, u32[]{:S(2)}, u32[]{:S(2)}) collective-permute-start(bf16[4,48,3072]{2,1,0:T(8,128)(2,1)S(1)} %get-tuple-element.264), channel_id=1, source_target_pairs={{0,8},{1,9},{2,10},{3,11},{4,12},{5,13},{6,14},{7,15},{8,0},{9,1},... | collective-permute-start | bytes 3538952 | tf_op jit(solution)/shard_map/ppermute | solution.py:897
  161.3 18.1 %collective-permute-start.17 = (f32[8,48,1536]{2,1,0:T(8,128)S(1)}, f32[8,48,1536]{2,1,0:T(8,128)S(1)}, u32[]{:S(2)}, u32[]{:S(2)}) collective-permute-start(f32[8,48,1536]{2,1,0:T(8,128)S(1)} %get-tuple-element.177), channel_id=1, source_target_pairs={{0,1},{1,0},{2,3},{3,2},{4,5},{5,4},{6,7},{7,6},{8,9},{9,8},{10,11... | collective-permute-start | bytes 7077896 | tf_op jit(solution)/shard_map/ppermute | solution.py:897
  161.3 16.6 %collective-permute-start.13 = (bf16[2,48,3200]{2,1,0:T(8,128)(2,1)S(1)}, bf16[2,48,3200]{2,1,0:T(8,128)(2,1)S(1)}, u32[]{:S(2)}, u32[]{:S(2)}) collective-permute-start(bf16[2,48,3200]{2,1,0:T(8,128)(2,1)S(1)} %get-tuple-element.266), channel_id=1, source_target_pairs={{0,4},{1,5},{2,6},{3,7},{4,0},{5,1},{6,2},{7,3},{8,12},{9,13},{10,... | collective-permute-start | bytes 1843208 | tf_op jit(solution)/shard_map/ppermute | solution.py:897
  176.6 17.3 %collective-permute-start.16 = (bf16[2,48,3072]{2,1,0:T(8,128)(2,1)S(1)}, bf16[2,48,3072]{2,1,0:T(8,128)(2,1)S(1)}, u32[]{:S(2)}, u32[]{:S(2)}) collective-permute-start(bf16[2,48,3072]{2,1,0:T(8,128)(2,1)S(1)} %get-tuple-element.270), channel_id=1, source_target_pairs={{0,2},{1,3},{2,0},{3,1},{4,6},{5,7},{6,4},{7,5},{8,10},{9,11},{10,... | collective-permute-start | bytes 1769480 | tf_op jit(solution)/shard_map/ppermute | solution.py:897
  178.1 17.6 %collective-permute-start.15 = (bf16[1,48,3200]{2,1,0:T(8,128)(2,1)S(1)}, bf16[1,48,3200]{2,1,0:T(8,128)(2,1)S(1)}, u32[]{:S(2)}, u32[]{:S(2)}) collective-permute-start(bf16[1,48,3200]{2,1,0:T(8,128)(2,1)S(1)} %fusion.2), channel_id=1, source_target_pairs={{0,8},{1,9},{2,10},{3,11},{4,12},{5,13},{6,14},{7,15},{8,0},{9,1},... | collective-permute-start | bytes 921608 | tf_op jit(solution)/shard_map/ppermute | solution.py:897
  179.8 22.2 %collective-permute-start.18 = (bf16[4,48,1536]{2,1,0:T(8,128)(2,1)S(1)}, bf16[4,48,1536]{2,1,0:T(8,128)(2,1)S(1)}, u32[]{:S(2)}, u32[]{:S(2)}) collective-permute-start(bf16[4,48,1536]{2,1,0:T(8,128)(2,1)S(1)} %get-tuple-element.268), channel_id=1, source_target_pairs={{0,4},{1,5},{2,6},{3,7},{4,0},{5,1},{6,2},{7,3},{8,12},{9,13},{10,... | collective-permute-start | bytes 1769480 | tf_op jit(solution)/shard_map/ppermute | solution.py:897
  182.3 17.2 %collective-permute-start.19 = (f32[8,48,768]{2,1,0:T(8,128)S(1)}, f32[8,48,768]{2,1,0:T(8,128)S(1)}, u32[]{:S(2)}, u32[]{:S(2)}) collective-permute-start(f32[8,48,768]{2,1,0:T(8,128)S(1)} %get-tuple-element.188), channel_id=1, source_target_pairs={{0,1},{1,0},{2,3},{3,2},{4,5},{5,4},{6,7},{7,6},{8,9},{9,8},{10,11... | collective-permute-start | bytes 3538952 | tf_op jit(solution)/shard_map/ppermute | solution.py:897
  193.8 16.3 %collective-permute-start.23 = (f32[16,768]{1,0:T(8,128)S(1)}, f32[16,768]{1,0:T(8,128)S(1)}, u32[]{:S(2)}, u32[]{:S(2)}) collective-permute-start(f32[16,768]{1,0:T(8,128)S(1)} %collect_vectors.1), channel_id=1, source_target_pairs={{0,1},{1,0},{2,3},{3,2},{4,5},{5,4},{6,7},{7,6},{8,9},{9,8},{10,11... | collective-permute-start | bytes 147464 | tf_op jit(solution)/shard_map/ppermute | solution.py:897
  194.6 9.9 %collective-permute-start.20 = (bf16[1,48,3072]{2,1,0:T(8,128)(2,1)S(1)}, bf16[1,48,3072]{2,1,0:T(8,128)(2,1)S(1)}, u32[]{:S(2)}, u32[]{:S(2)}) collective-permute-start(bf16[1,48,3072]{2,1,0:T(8,128)(2,1)S(1)} %fusion.8), channel_id=1, source_target_pairs={{0,4},{1,5},{2,6},{3,7},{4,0},{5,1},{6,2},{7,3},{8,12},{9,13},{10,... | collective-permute-start | bytes 884744 | tf_op jit(solution)/shard_map/ppermute | solution.py:897
  195.8 24.1 %collective-permute-start.25 = (bf16[1,48,3200]{2,1,0:T(8,128)(2,1)S(1)}, bf16[1,48,3200]{2,1,0:T(8,128)(2,1)S(1)}, u32[]{:S(2)}, u32[]{:S(2)}) collective-permute-start(bf16[1,48,3200]{2,1,0:T(8,128)(2,1)S(1)} %fusion.4), channel_id=1, source_target_pairs={{0,16},{1,17},{2,18},{3,19},{4,20},{5,21},{6,22},{7,23},{8,24},{9,... | collective-permute-start | bytes 921608 | tf_op jit(solution)/shard_map/ppermute | solution.py:897
  199.6 10.3 %collective-permute-start.22 = (bf16[4,48,768]{2,1,0:T(8,128)(2,1)S(1)}, bf16[4,48,768]{2,1,0:T(8,128)(2,1)S(1)}, u32[]{:S(2)}, u32[]{:S(2)}) collective-permute-start(bf16[4,48,768]{2,1,0:T(8,128)(2,1)S(1)} %get-tuple-element.276), channel_id=1, source_target_pairs={{0,4},{1,5},{2,6},{3,7},{4,0},{5,1},{6,2},{7,3},{8,12},{9,13},{10,... | collective-permute-start | bytes 884744 | tf_op jit(solution)/shard_map/ppermute | solution.py:897
  202.0 4.1 %collective-permute-start.21 = (f32[8,48,768]{2,1,0:T(8,128)S(1)}, f32[8,48,768]{2,1,0:T(8,128)S(1)}, u32[]{:S(2)}, u32[]{:S(2)}) collective-permute-start(f32[8,48,768]{2,1,0:T(8,128)S(1)} %get-tuple-element.199), channel_id=1, source_target_pairs={{0,1},{1,0},{2,3},{3,2},{4,5},{5,4},{6,7},{7,6},{8,9},{9,8},{10,11... | collective-permute-start | bytes 3538952 | tf_op jit(solution)/shard_map/ppermute | solution.py:897
  204.5 16.5 %collective-permute-start.24 = (bf16[2,48,1536]{2,1,0:T(8,128)(2,1)S(1)}, bf16[2,48,1536]{2,1,0:T(8,128)(2,1)S(1)}, u32[]{:S(2)}, u32[]{:S(2)}) collective-permute-start(bf16[2,48,1536]{2,1,0:T(8,128)(2,1)S(1)} %get-tuple-element.274), channel_id=1, source_target_pairs={{0,2},{1,3},{2,0},{3,1},{4,6},{5,7},{6,4},{7,5},{8,10},{9,11},{10,... | collective-permute-start | bytes 884744 | tf_op jit(solution)/shard_map/ppermute | solution.py:897
  206.1 30.4 %collective-permute-start.31 = (bf16[1,48,3072]{2,1,0:T(8,128)(2,1)S(1)}, bf16[1,48,3072]{2,1,0:T(8,128)(2,1)S(1)}, u32[]{:S(2)}, u32[]{:S(2)}) collective-permute-start(bf16[1,48,3072]{2,1,0:T(8,128)(2,1)S(1)} %fusion.6), channel_id=1, source_target_pairs={{0,16},{1,17},{2,18},{3,19},{4,20},{5,21},{6,22},{7,23},{8,24},{9,... | collective-permute-start | bytes 884744 | tf_op jit(solution)/shard_map/ppermute | solution.py:897
  210.1 19.2 %collective-permute-start.27 = (f32[16,768]{1,0:T(8,128)S(1)}, f32[16,768]{1,0:T(8,128)S(1)}, u32[]{:S(2)}, u32[]{:S(2)}) collective-permute-start(f32[16,768]{1,0:T(8,128)S(1)} %add.156), channel_id=1, source_target_pairs={{0,2},{1,3},{2,0},{3,1},{4,6},{5,7},{6,4},{7,5},{8,10},{9,11},{10,... | collective-permute-start | bytes 147464 | tf_op jit(solution)/shard_map/ppermute | solution.py:897
  211.6 16.8 %collective-permute-start.28 = (bf16[2,48,768]{2,1,0:T(8,128)(2,1)S(1)}, bf16[2,48,768]{2,1,0:T(8,128)(2,1)S(1)}, u32[]{:S(2)}, u32[]{:S(2)}) collective-permute-start(bf16[2,48,768]{2,1,0:T(8,128)(2,1)S(1)} %get-tuple-element.280), channel_id=1, source_target_pairs={{0,2},{1,3},{2,0},{3,1},{4,6},{5,7},{6,4},{7,5},{8,10},{9,11},{10,... | collective-permute-start | bytes 442376 | tf_op jit(solution)/shard_map/ppermute | solution.py:897
  219.9 8.4 %collective-permute-start.29 = (bf16[4,48,768]{2,1,0:T(8,128)(2,1)S(1)}, bf16[4,48,768]{2,1,0:T(8,128)(2,1)S(1)}, u32[]{:S(2)}, u32[]{:S(2)}) collective-permute-start(bf16[4,48,768]{2,1,0:T(8,128)(2,1)S(1)} %get-tuple-element.272), channel_id=1, source_target_pairs={{0,4},{1,5},{2,6},{3,7},{4,0},{5,1},{6,2},{7,3},{8,12},{9,13},{10,... | collective-permute-start | bytes 884744 | tf_op jit(solution)/shard_map/ppermute | solution.py:897
  221.0 20.6 %collective-permute-start.34 = (bf16[1,48,3200]{2,1,0:T(8,128)(2,1)S(1)}, bf16[1,48,3200]{2,1,0:T(8,128)(2,1)S(1)}, u32[]{:S(2)}, u32[]{:S(2)}) collective-permute-start(bf16[1,48,3200]{2,1,0:T(8,128)(2,1)S(1)} %add_convert_fusion.3), channel_id=1, source_target_pairs={{0,8},{1,9},{2,10},{3,11},{4,12},{5,13},{6,14},{7,15},{8,0},{9,1},... | collective-permute-start | bytes 921608 | tf_op jit(solution)/shard_map/ppermute | solution.py:897
  228.2 7.5 %collective-permute-start.26 = (bf16[1,48,1536]{2,1,0:T(8,128)(2,1)S(1)}, bf16[1,48,1536]{2,1,0:T(8,128)(2,1)S(1)}, u32[]{:S(2)}, u32[]{:S(2)}) collective-permute-start(bf16[1,48,1536]{2,1,0:T(8,128)(2,1)S(1)} %fusion.10), channel_id=1, source_target_pairs={{0,8},{1,9},{2,10},{3,11},{4,12},{5,13},{6,14},{7,15},{8,0},{9,1},... | collective-permute-start | bytes 442376 | tf_op jit(solution)/shard_map/ppermute | solution.py:897
  228.4 9.6 %collective-permute-start.36 = (bf16[2,48,768]{2,1,0:T(8,128)(2,1)S(1)}, bf16[2,48,768]{2,1,0:T(8,128)(2,1)S(1)}, u32[]{:S(2)}, u32[]{:S(2)}) collective-permute-start(bf16[2,48,768]{2,1,0:T(8,128)(2,1)S(1)} %get-tuple-element.278), channel_id=1, source_target_pairs={{0,2},{1,3},{2,0},{3,1},{4,6},{5,7},{6,4},{7,5},{8,10},{9,11},{10,... | collective-permute-start | bytes 442376 | tf_op jit(solution)/shard_map/ppermute | solution.py:897
  229.4 12.7 %collective-permute-start.33 = (bf16[1,48,768]{2,1,0:T(8,128)(2,1)S(1)}, bf16[1,48,768]{2,1,0:T(8,128)(2,1)S(1)}, u32[]{:S(2)}, u32[]{:S(2)}) collective-permute-start(bf16[1,48,768]{2,1,0:T(8,128)(2,1)S(1)} %fusion.19), channel_id=1, source_target_pairs={{0,8},{1,9},{2,10},{3,11},{4,12},{5,13},{6,14},{7,15},{8,0},{9,1},... | collective-permute-start | bytes 221192 | tf_op jit(solution)/shard_map/ppermute | solution.py:897
  235.7 4.1 %collective-permute-start.35 = (f32[16,768]{1,0:T(8,128)S(1)}, f32[16,768]{1,0:T(8,128)S(1)}, u32[]{:S(2)}, u32[]{:S(2)}) collective-permute-start(f32[16,768]{1,0:T(8,128)S(1)} %add.165), channel_id=1, source_target_pairs={{0,4},{1,5},{2,6},{3,7},{4,0},{5,1},{6,2},{7,3},{8,12},{9,13},{10,... | collective-permute-start | bytes 147464 | tf_op jit(solution)/shard_map/ppermute | solution.py:897
  236.6 13.2 %collective-permute-start.30 = (bf16[1,48,1536]{2,1,0:T(8,128)(2,1)S(1)}, bf16[1,48,1536]{2,1,0:T(8,128)(2,1)S(1)}, u32[]{:S(2)}, u32[]{:S(2)}) collective-permute-start(bf16[1,48,1536]{2,1,0:T(8,128)(2,1)S(1)} %fusion.12), channel_id=1, source_target_pairs={{0,16},{1,17},{2,18},{3,19},{4,20},{5,21},{6,22},{7,23},{8,24},{9,... | collective-permute-start | bytes 442376 | tf_op jit(solution)/shard_map/ppermute | solution.py:897
  238.0 10.0 %collective-permute-start.32 = (bf16[1,48,3072]{2,1,0:T(8,128)(2,1)S(1)}, bf16[1,48,3072]{2,1,0:T(8,128)(2,1)S(1)}, u32[]{:S(2)}, u32[]{:S(2)}) collective-permute-start(bf16[1,48,3072]{2,1,0:T(8,128)(2,1)S(1)} %add_convert_fusion.4), channel_id=1, source_target_pairs={{0,4},{1,5},{2,6},{3,7},{4,0},{5,1},{6,2},{7,3},{8,12},{9,13},{10,... | collective-permute-start | bytes 884744 | tf_op jit(solution)/shard_map/ppermute | solution.py:897
  239.8 11.8 %collective-permute-start.38 = (bf16[1,48,768]{2,1,0:T(8,128)(2,1)S(1)}, bf16[1,48,768]{2,1,0:T(8,128)(2,1)S(1)}, u32[]{:S(2)}, u32[]{:S(2)}) collective-permute-start(bf16[1,48,768]{2,1,0:T(8,128)(2,1)S(1)} %fusion.16), channel_id=1, source_target_pairs={{0,8},{1,9},{2,10},{3,11},{4,12},{5,13},{6,14},{7,15},{8,0},{9,1},... | collective-permute-start | bytes 221192 | tf_op jit(solution)/shard_map/ppermute | solution.py:897
  241.6 10.9 %collective-permute-start.42 = (f32[16,768]{1,0:T(8,128)S(1)}, f32[16,768]{1,0:T(8,128)S(1)}, u32[]{:S(2)}, u32[]{:S(2)}) collective-permute-start(f32[16,768]{1,0:T(8,128)S(1)} %add.171), channel_id=1, source_target_pairs={{0,8},{1,9},{2,10},{3,11},{4,12},{5,13},{6,14},{7,15},{8,0},{9,1},... | collective-permute-start | bytes 147464 | tf_op jit(solution)/shard_map/ppermute | solution.py:897
  242.1 17.4 %collective-permute-start.40 = (bf16[2,48,3200]{2,1,0:T(8,128)(2,1)S(1)}, bf16[2,48,3200]{2,1,0:T(8,128)(2,1)S(1)}, u32[]{:S(2)}, u32[]{:S(2)}) collective-permute-start(bf16[2,48,3200]{2,1,0:T(8,128)(2,1)S(1)} %broadcast_select_fusion), channel_id=1, source_target_pairs={{0,4},{1,5},{2,6},{3,7},{4,0},{5,1},{6,2},{7,3},{8,12},{9,13},{10,... | collective-permute-start | bytes 1843208 | tf_op jit(solution)/shard_map/ppermute | solution.py:897
  248.0 8.2 %collective-permute-start.41 = (bf16[1,48,768]{2,1,0:T(8,128)(2,1)S(1)}, bf16[1,48,768]{2,1,0:T(8,128)(2,1)S(1)}, u32[]{:S(2)}, u32[]{:S(2)}) collective-permute-start(bf16[1,48,768]{2,1,0:T(8,128)(2,1)S(1)} %fusion.18), channel_id=1, source_target_pairs={{0,16},{1,17},{2,18},{3,19},{4,20},{5,21},{6,22},{7,23},{8,24},{9,... | collective-permute-start | bytes 221192 | tf_op jit(solution)/shard_map/ppermute | solution.py:897
  249.8 16.2 %collective-permute-start.46 = (bf16[2,48,3072]{2,1,0:T(8,128)(2,1)S(1)}, bf16[2,48,3072]{2,1,0:T(8,128)(2,1)}, u32[]{:S(2)}, u32[]{:S(2)}) collective-permute-start(bf16[2,48,3072]{2,1,0:T(8,128)(2,1)S(1)} %broadcast_select_fusion.1), channel_id=1, source_target_pairs={{0,2},{1,3},{2,0},{3,1},{4,6},{5,7},{6,4},{7,5},{8,10},{9,11},{10,... | collective-permute-start | bytes 1769480 | tf_op jit(solution)/shard_map/ppermute | solution.py:897
  251.6 10.6 %collective-permute-start.37 = (bf16[1,48,1536]{2,1,0:T(8,128)(2,1)S(1)}, bf16[1,48,1536]{2,1,0:T(8,128)(2,1)S(1)}, u32[]{:S(2)}, u32[]{:S(2)}) collective-permute-start(bf16[1,48,1536]{2,1,0:T(8,128)(2,1)S(1)} %add_convert_fusion.7), channel_id=1, source_target_pairs={{0,8},{1,9},{2,10},{3,11},{4,12},{5,13},{6,14},{7,15},{8,0},{9,1},... | collective-permute-start | bytes 442376 | tf_op jit(solution)/shard_map/ppermute | solution.py:897
  252.5 9.7 %collective-permute-start.39 = (bf16[1,48,768]{2,1,0:T(8,128)(2,1)S(1)}, bf16[1,48,768]{2,1,0:T(8,128)(2,1)S(1)}, u32[]{:S(2)}, u32[]{:S(2)}) collective-permute-start(bf16[1,48,768]{2,1,0:T(8,128)(2,1)S(1)} %fusion.15), channel_id=1, source_target_pairs={{0,16},{1,17},{2,18},{3,19},{4,20},{5,21},{6,22},{7,23},{8,24},{9,... | collective-permute-start | bytes 221192 | tf_op jit(solution)/shard_map/ppermute | solution.py:897
  256.1 6.2 %collective-permute-start.47 = (f32[16,768]{1,0:T(8,128)S(1)}, f32[16,768]{1,0:T(8,128)S(1)}, u32[]{:S(2)}, u32[]{:S(2)}) collective-permute-start(f32[16,768]{1,0:T(8,128)S(1)} %add.176), channel_id=1, source_target_pairs={{0,16},{1,17},{2,18},{3,19},{4,20},{5,21},{6,22},{7,23},{8,24},{9,... | collective-permute-start | bytes 147464 | tf_op jit(solution)/shard_map/ppermute | solution.py:897
  259.5 7.8 %collective-permute-start.45 = (bf16[1,48,768]{2,1,0:T(8,128)(2,1)S(1)}, bf16[1,48,768]{2,1,0:T(8,128)(2,1)}, u32[]{:S(2)}, u32[]{:S(2)}) collective-permute-start(bf16[1,48,768]{2,1,0:T(8,128)(2,1)S(1)} %add_convert_fusion.9), channel_id=1, source_target_pairs={{0,8},{1,9},{2,10},{3,11},{4,12},{5,13},{6,14},{7,15},{8,0},{9,1},... | collective-permute-start | bytes 221192 | tf_op jit(solution)/shard_map/ppermute | solution.py:897
  262.4 6.3 %collective-permute-start.44 = (bf16[1,48,768]{2,1,0:T(8,128)(2,1)S(1)}, bf16[1,48,768]{2,1,0:T(8,128)(2,1)}, u32[]{:S(2)}, u32[]{:S(2)}) collective-permute-start(bf16[1,48,768]{2,1,0:T(8,128)(2,1)S(1)} %add_convert_fusion.8), channel_id=1, source_target_pairs={{0,8},{1,9},{2,10},{3,11},{4,12},{5,13},{6,14},{7,15},{8,0},{9,1},... | collective-permute-start | bytes 221192 | tf_op jit(solution)/shard_map/ppermute | solution.py:897
  262.5 8.9 %collective-permute-start.43 = (bf16[2,48,1536]{2,1,0:T(8,128)(2,1)S(1)}, bf16[2,48,1536]{2,1,0:T(8,128)(2,1)}, u32[]{:S(2)}, u32[]{:S(2)}) collective-permute-start(bf16[2,48,1536]{2,1,0:T(8,128)(2,1)S(1)} %broadcast_select_fusion.2), channel_id=1, source_target_pairs={{0,2},{1,3},{2,0},{3,1},{4,6},{5,7},{6,4},{7,5},{8,10},{9,11},{10,... | collective-permute-start | bytes 884744 | tf_op jit(solution)/shard_map/ppermute | solution.py:897
  268.3 6.2 %collective-permute-start.50 = (bf16[2,48,768]{2,1,0:T(8,128)(2,1)S(1)}, bf16[2,48,768]{2,1,0:T(8,128)(2,1)S(1)}, u32[]{:S(2)}, u32[]{:S(2)}) collective-permute-start(bf16[2,48,768]{2,1,0:T(8,128)(2,1)S(1)} %broadcast_select_fusion.4), channel_id=1, source_target_pairs={{0,2},{1,3},{2,0},{3,1},{4,6},{5,7},{6,4},{7,5},{8,10},{9,11},{10,... | collective-permute-start | bytes 442376 | tf_op jit(solution)/shard_map/ppermute | solution.py:897
  269.7 6.3 %collective-permute-start.49 = (bf16[2,48,768]{2,1,0:T(8,128)(2,1)S(1)}, bf16[2,48,768]{2,1,0:T(8,128)(2,1)S(1)}, u32[]{:S(2)}, u32[]{:S(2)}) collective-permute-start(bf16[2,48,768]{2,1,0:T(8,128)(2,1)S(1)} %broadcast_select_fusion.3), channel_id=1, source_target_pairs={{0,2},{1,3},{2,0},{3,1},{4,6},{5,7},{6,4},{7,5},{8,10},{9,11},{10,... | collective-permute-start | bytes 442376 | tf_op jit(solution)/shard_map/ppermute | solution.py:897
  276.1 30.5 %collective-permute-start.58 = (bf16[4,48,3200]{2,1,0:T(8,128)(2,1)S(1)}, bf16[4,48,3200]{2,1,0:T(8,128)(2,1)S(1)}, u32[]{:S(2)}, u32[]{:S(2)}) collective-permute-start(bf16[4,48,3200]{2,1,0:T(8,128)(2,1)S(1)} %bitcast_select_fusion.3), channel_id=1, source_target_pairs={{0,2},{1,3},{2,0},{3,1},{4,6},{5,7},{6,4},{7,5},{8,10},{9,11},{10,... | collective-permute-start | bytes 3686408 | tf_op jit(solution)/shard_map/ppermute | solution.py:897
  277.8 25.7 %collective-permute-start.52 = (bf16[4,48,3072]{2,1,0:T(8,128)(2,1)S(1)}, bf16[4,48,3072]{2,1,0:T(8,128)(2,1)S(1)}, u32[]{:S(2)}, u32[]{:S(2)}) collective-permute-start(bf16[4,48,3072]{2,1,0:T(8,128)(2,1)S(1)} %bitcast_select_fusion.5), channel_id=1, source_target_pairs={{0,8},{1,9},{2,10},{3,11},{4,12},{5,13},{6,14},{7,15},{8,0},{9,1},... | collective-permute-start | bytes 3538952 | tf_op jit(solution)/shard_map/ppermute | solution.py:897
  279.5 16.3 %collective-permute-start.48 = (bf16[4,48,1536]{2,1,0:T(8,128)(2,1)S(1)}, bf16[4,48,1536]{2,1,0:T(8,128)(2,1)S(1)}, u32[]{:S(2)}, u32[]{:S(2)}) collective-permute-start(bf16[4,48,1536]{2,1,0:T(8,128)(2,1)S(1)} %bitcast_select_fusion.9), channel_id=1, source_target_pairs={{0,4},{1,5},{2,6},{3,7},{4,0},{5,1},{6,2},{7,3},{8,12},{9,13},{10,... | collective-permute-start | bytes 1769480 | tf_op jit(solution)/shard_map/ppermute | solution.py:897
  279.9 21.8 %collective-permute-start.53 = (bf16[4,48,768]{2,1,0:T(8,128)(2,1)S(1)}, bf16[4,48,768]{2,1,0:T(8,128)(2,1)S(1)}, u32[]{:S(2)}, u32[]{:S(2)}) collective-permute-start(bf16[4,48,768]{2,1,0:T(8,128)(2,1)S(1)} %bitcast_select_fusion.13), channel_id=1, source_target_pairs={{0,4},{1,5},{2,6},{3,7},{4,0},{5,1},{6,2},{7,3},{8,12},{9,13},{10,... | collective-permute-start | bytes 884744 | tf_op jit(solution)/shard_map/ppermute | solution.py:897
  281.5 25.0 %collective-permute-start.55 = (bf16[4,48,768]{2,1,0:T(8,128)(2,1)S(1)}, bf16[4,48,768]{2,1,0:T(8,128)(2,1)S(1)}, u32[]{:S(2)}, u32[]{:S(2)}) collective-permute-start(bf16[4,48,768]{2,1,0:T(8,128)(2,1)S(1)} %bitcast_select_fusion.12), channel_id=1, source_target_pairs={{0,4},{1,5},{2,6},{3,7},{4,0},{5,1},{6,2},{7,3},{8,12},{9,13},{10,... | collective-permute-start | bytes 884744 | tf_op jit(solution)/shard_map/ppermute | solution.py:897
  307.1 18.1 %collective-permute-start.59 = (bf16[8,48,3200]{2,1,0:T(8,128)(2,1)S(1)}, bf16[8,48,3200]{2,1,0:T(8,128)(2,1)S(1)}, u32[]{:S(2)}, u32[]{:S(2)}) collective-permute-start(bf16[8,48,3200]{2,1,0:T(8,128)(2,1)S(1)} %bitcast_select_fusion.refs_0_), channel_id=1, source_target_pairs={{0,1},{1,0},{2,3},{3,2},{4,5},{5,4},{6,7},{7,6},{8,9},{9,8},{10,11... | collective-permute-start | bytes 7372808 | tf_op jit(solution)/shard_map/ppermute | solution.py:897
  307.2 13.1 %collective-permute-start.54 = (bf16[8,48,3072]{2,1,0:T(8,128)(2,1)S(1)}, bf16[8,48,3072]{2,1,0:T(8,128)(2,1)S(1)}, u32[]{:S(2)}, u32[]{:S(2)}) collective-permute-start(bf16[8,48,3072]{2,1,0:T(8,128)(2,1)S(1)} %bitcast_select_fusion.1.refs_0_), channel_id=1, source_target_pairs={{0,1},{1,0},{2,3},{3,2},{4,5},{5,4},{6,7},{7,6},{8,9},{9,8},{10,11... | collective-permute-start | bytes 7077896 | tf_op jit(solution)/shard_map/ppermute | solution.py:897
  307.7 15.1 %collective-permute-start.51 = (bf16[8,48,1536]{2,1,0:T(8,128)(2,1)S(1)}, bf16[8,48,1536]{2,1,0:T(8,128)(2,1)S(1)}, u32[]{:S(2)}, u32[]{:S(2)}) collective-permute-start(bf16[8,48,1536]{2,1,0:T(8,128)(2,1)S(1)} %bitcast_select_fusion.4.refs_0_), channel_id=1, source_target_pairs={{0,1},{1,0},{2,3},{3,2},{4,5},{5,4},{6,7},{7,6},{8,9},{9,8},{10,11... | collective-permute-start | bytes 3538952 | tf_op jit(solution)/shard_map/ppermute | solution.py:897
  307.7 10.0 %collective-permute-start.56 = (bf16[8,48,768]{2,1,0:T(8,128)(2,1)S(1)}, bf16[8,48,768]{2,1,0:T(8,128)(2,1)S(1)}, u32[]{:S(2)}, u32[]{:S(2)}) collective-permute-start(bf16[8,48,768]{2,1,0:T(8,128)(2,1)S(1)} %bitcast_select_fusion.8.refs_1_), channel_id=1, source_target_pairs={{0,1},{1,0},{2,3},{3,2},{4,5},{5,4},{6,7},{7,6},{8,9},{9,8},{10,11... | collective-permute-start | bytes 1769480 | tf_op jit(solution)/shard_map/ppermute | solution.py:897
  308.2 12.1 %collective-permute-start.57 = (bf16[8,48,768]{2,1,0:T(8,128)(2,1)S(1)}, bf16[8,48,768]{2,1,0:T(8,128)(2,1)S(1)}, u32[]{:S(2)}, u32[]{:S(2)}) collective-permute-start(bf16[8,48,768]{2,1,0:T(8,128)(2,1)S(1)} %bitcast_select_fusion.7.refs_2_), channel_id=1, source_target_pairs={{0,1},{1,0},{2,3},{3,2},{4,5},{5,4},{6,7},{7,6},{8,9},{9,8},{10,11... | collective-permute-start | bytes 1769480 | tf_op jit(solution)/shard_map/ppermute | solution.py:897
  (24 other events, 162.4 us)
